TPU v7x, 512 devices: a whole 4x8x8 slice. The times are simulated.
512 devices in a mesh: dp: 32 (over x, y), mp: 16 (over z, core).
Axes of the slice: x: 4, y: 8, z: 8, core: 2. Of those that a mesh axis runs over, the one named last changes fastest.
Arguments:
- tokens: bfloat16 [8192, 2432], P('dp', 'mp'), may hold values from -6 to 6
- route: int32 [8192, 1], P('dp'), may hold values from 0 to 31; in each aligned block of 256 rows (0 to 255, 256 to 511, ...) at most 16 rows name the same one
- tsteps: int32 [32], replicated, may hold values from 0 to 27
- mod_table: bfloat16 [28, 3, 2432], replicated, may hold values from -10 to 10
- w_qkv: bfloat16 [2432, 3, 2048], P(None, None, 'mp'), may hold values from -0.125 to 0.125
- qk_gain: float32 [2, 64], replicated, may hold values from 0.1 to 1.9
- context: bfloat16 [32, 2, 333, 2048], P('dp', None, None, 'mp'), may hold values from -43 to 43
- w_out: bfloat16 [2048, 2432], P('mp'), may hold values from -0.125 to 0.125
Outputs:
- mixed: bfloat16 [8192, 2432], P('dp', 'mp')
Inputs may be any that keep to these rules, and one draw needn't show every extreme that they name: `route`: one index of dp holds at most 16 rows of one request; some request reaches 16; every request has rows.
All inputs are finite; a program needn't handle non-finite values.
Results may differ from a plain program's by a relative error of at most 0.024.
Values may be sent and summed in bfloat16 or wider, within the bound.
No kernel may reach another device: no remote copies, remote signals or barrier semaphores. Data moves between devices by JAX's collectives and lax.ppermute only.
A program may use at most 64 MiB of HBM per device.

v0:
```python
import jax
import jax.numpy as jnp
from jax import lax
from jax.sharding import PartitionSpec as P

HD = 64
TXT = 333
TSTEPS = 28
REQ_DEV = 1


EPS = 1e-06


def modulate(values, shift_rows, scale_rows):
    widened = values.astype(jnp.float32)
    center = jnp.mean(widened, axis=-1, keepdims=True)
    spread = jnp.mean(jnp.square(widened - center), axis=-1, keepdims=True)
    normed = (widened - center) * lax.rsqrt(spread + EPS)
    return (normed * (1.0 + scale_rows) + shift_rows).astype(jnp.bfloat16)


def rms_scaled(values, gain_row):
    return values * lax.rsqrt(jnp.mean(jnp.square(values), axis=-1, keepdims=True) + EPS) * gain_row


def project_heads(hidden, w_qkv, qk_gain, head_count):
    count = hidden.shape[0]
    mixed = jnp.dot(hidden, w_qkv.reshape(w_qkv.shape[0], -1), preferred_element_type=jnp.float32)
    mixed = mixed.reshape(count, 3, head_count, HD)
    queries = rms_scaled(mixed[:, 0], qk_gain[0])
    keys_img = rms_scaled(mixed[:, 1], qk_gain[1])
    return jnp.stack([queries, keys_img, mixed[:, 2]], axis=1).astype(jnp.bfloat16)


def attend(stacked, valid, context, sources, cap_size, head_count):
    span = sources * cap_size
    grid = stacked.reshape(sources, REQ_DEV, cap_size, 3, head_count, HD)
    grid = grid.transpose(1, 0, 2, 3, 4, 5).reshape(REQ_DEV, span, 3, head_count, HD)
    live = valid.reshape(sources, REQ_DEV, cap_size).transpose(1, 0, 2).reshape(REQ_DEV, span)
    ctx_heads = context.reshape(REQ_DEV, 2, TXT, head_count, HD)
    factor = HD ** (-0.5)
    block_count = 1
    while span % block_count != 0 or span // block_count > 512:
        block_count = block_count + 1
    block_rows = span // block_count
    query_blocks = grid[:, :, 0].reshape(REQ_DEV, block_count, block_rows, head_count, HD)
    query_blocks = query_blocks.transpose(1, 0, 2, 3, 4)
    keys_img = grid[:, :, 1]
    values_img = grid[:, :, 2]

    def one_block(queries):
        own = (
            jnp.einsum("rshd,rthd->rhst", queries, keys_img, preferred_element_type=jnp.float32)
            * factor
        )
        own = jnp.where(live[:, None, None, :] > 0, own, -1e30)
        far = (
            jnp.einsum(
                "rshd,rthd->rhst", queries, ctx_heads[:, 0], preferred_element_type=jnp.float32
            )
            * factor
        )
        top = jnp.maximum(
            jnp.max(own, axis=-1, keepdims=True), jnp.max(far, axis=-1, keepdims=True)
        )
        own_weights = jnp.exp(own - top)
        far_weights = jnp.exp(far - top)
        total = jnp.sum(own_weights, axis=-1, keepdims=True) + jnp.sum(
            far_weights, axis=-1, keepdims=True
        )
        own_probs = (own_weights / total).astype(jnp.bfloat16)
        far_probs = (far_weights / total).astype(jnp.bfloat16)
        result = jnp.einsum(
            "rhst,rthd->rshd", own_probs, values_img, preferred_element_type=jnp.float32
        )
        result = result + jnp.einsum(
            "rhst,rthd->rshd", far_probs, ctx_heads[:, 1], preferred_element_type=jnp.float32
        )
        return result.astype(jnp.bfloat16)

    blocks_out = lax.map(one_block, query_blocks)
    result = blocks_out.transpose(1, 0, 2, 3, 4).reshape(
        REQ_DEV, sources, cap_size, head_count * HD
    )
    return result.transpose(1, 0, 2, 3).reshape(span * REQ_DEV, head_count * HD)


def body(tokens, route, tsteps, mod_table, w_qkv, qk_gain, context, w_out):
    row_count = tokens.shape[0]
    width = tokens.shape[1]
    sources = lax.axis_size("dp")
    requests_all = sources * REQ_DEV
    cap_size = max(2, 2 * row_count // (REQ_DEV * sources))
    slot_count = requests_all * cap_size
    head_count = w_qkv.shape[2] // HD
    request = route[:, 0]
    onehot = (request[:, None] == jnp.arange(requests_all, dtype=jnp.int32)[None, :]).astype(
        jnp.int32
    )
    rank = jnp.sum(jnp.cumsum(onehot, axis=0) * onehot, axis=1) - 1
    position = request * cap_size + rank
    hits = position[None, :] == jnp.arange(slot_count, dtype=jnp.int32)[:, None]
    place = hits.astype(jnp.bfloat16)
    valid_send = jnp.any(hits, axis=1).astype(jnp.int32)
    column_start = lax.axis_index("mp") * width
    gate_table = lax.dynamic_slice_in_dim(mod_table[:, 2, :], column_start, width, 1)
    own_steps = lax.dynamic_slice_in_dim(tsteps, lax.axis_index("dp") * REQ_DEV, REQ_DEV)
    pick = (own_steps[:, None] == jnp.arange(TSTEPS, dtype=jnp.int32)[None, :]).astype(jnp.bfloat16)
    send_rows = jnp.dot(place, tokens, preferred_element_type=jnp.float32).astype(jnp.bfloat16)
    arrived, valid = (
        lax.all_to_all(send_rows, "dp", split_axis=0, concat_axis=0, tiled=True),
        lax.all_to_all(valid_send, "dp", split_axis=0, concat_axis=0, tiled=True),
    )
    whole = lax.all_gather(arrived, "mp", axis=1, tiled=True)
    full_width = whole.shape[1]
    shift_req = jnp.dot(pick, mod_table[:, 0, :], preferred_element_type=jnp.float32)
    scale_req = jnp.dot(pick, mod_table[:, 1, :], preferred_element_type=jnp.float32)
    grid = whole.reshape(sources, REQ_DEV, cap_size, full_width)
    hidden = modulate(grid, shift_req[None, :, None, :], scale_req[None, :, None, :])
    stacked = project_heads(hidden.reshape(slot_count, full_width), w_qkv, qk_gain, head_count)
    attn_slots = attend(stacked, valid, context, sources, cap_size, head_count)
    partial_term = jnp.dot(attn_slots, w_out, preferred_element_type=jnp.float32)
    out_sum = lax.psum_scatter(
        partial_term.astype(jnp.bfloat16), "mp", scatter_dimension=1, tiled=True
    ).astype(jnp.float32)
    gate_req = jnp.dot(pick, gate_table, preferred_element_type=jnp.float32)
    finished = arrived.astype(jnp.float32).reshape(sources, REQ_DEV, cap_size, width)
    finished = finished + gate_req[None, :, None, :] * out_sum.reshape(
        sources, REQ_DEV, cap_size, width
    )
    finished = finished.astype(jnp.bfloat16).reshape(slot_count, width)
    returned = lax.all_to_all(finished, "dp", split_axis=0, concat_axis=0, tiled=True)
    return jnp.dot(place.T, returned, preferred_element_type=jnp.float32).astype(jnp.bfloat16)


def solution(mesh):
    return jax.shard_map(
        body,
        mesh=mesh,
        in_specs=(
            P("dp", "mp"),
            P("dp", None),
            P(),
            P(),
            P(None, None, "mp"),
            P(),
            P("dp", None, None, "mp"),
            P("mp", None),
        ),
        out_specs=P("dp", "mp"),
        check_vma=False,
    )
```

profile of v0, /device:TPU:8, one launch (start us, length us, event | category | flops | bytes accessed | tf_op | source)
XLA Modules:
  0.0 177.6 jit_solution(6722144475132627363)
XLA Ops:
  6.6 0.8 fusion.32
  7.4 0.6 reduce-window.6
  8.2 0.8 fusion.31
  9.0 0.7 add_add_fusion
  9.7 1.1 convolution_convert_fusion.1
  11.0 22.3 %all_to_all.27 = bf16[32,16,152]{2,1,0:T(8,128)(2,1)S(1)} all-to-all(bf16[32,16,152]{2,1,0:T(8,128)(2,1)S(1)} %bitcast.99), channel_id=1, replica_groups=mesh['dp'=32,'mp'=16] {'dp'}, dimensions={0} | all-to-all | bytes 311296 | tf_op jit(solution)/shard_map/all_to_all | solution.py:112
  33.2 0.8 copy.29
  34.2 0.7 reshape.328
  34.9 4.6 %all-to-all-start.1 = ((s32[32,16,1]{1,2,0:T(1,128)}), s32[32,16,1]{1,2,0:T(1,128)S(1)}, u32[]{:S(2)}, u32[]{:S(2)}) async-start(s32[32,16,1]{1,2,0:T(1,128)} %bitcast.19), calls=%async_computation.1 | async-start | bytes 32768 | tf_op jit(solution)/shard_map/all_to_all | solution.py:113
  39.5 1.3 dynamic_slice.11
  40.8 1.7 convolution_reduce_fusion.1
  42.5 0.8 convolution_reduce_fusion
  43.3 2.2 %copy.30 = bf16[2432,3,128]{0,2,1:T(8,128)(2,1)} copy(bf16[2432,3,128]{2,0,1:T(8,128)(2,1)S(1)} %copy-done.2) | data formatting | bytes 3735552 | tf_op args[4]
  45.8 2.2 %all-to-all-done.1 = s32[32,16,1]{1,2,0:T(1,128)S(1)} async-done(((s32[32,16,1]{1,2,0:T(1,128)}), s32[32,16,1]{1,2,0:T(1,128)S(1)}, u32[]{:S(2)}, u32[]{:S(2)}) %all-to-all-start.1) | async-done | bytes 2080 | tf_op jit(solution)/shard_map/all_to_all | solution.py:113
  48.2 28.6 %all-gather.2.cloned.1.call-done = bf16[512,2432]{0,1:T(8,128)(2,1)} async-done(((bf16[512,152]{0,1:T(8,128)(2,1)}), bf16[512,2432]{0,1:T(8,128)(2,1)}) %all-gather.2.cloned.1.call-update) | async-done | bytes 2490384 | tf_op jit(solution)/shard_map/all_gather | solution.py:115
  76.8 2.2 %convert_reduce_fusion = f32[512]{0:T(512)S(1)} fusion(bf16[512,2432]{0,1:T(8,128)(2,1)} %all-gather.2.cloned.1.call-done), kind=kLoop, calls=%fused_computation.1 | loop fusion | flops 2489856 | bytes 2492416 | tf_op jit(solution)/shard_map/reduce_sum | solution.py:17
  79.0 0.2 copy-done.1
  79.2 0.7 fusion.2
  80.0 1.3 fusion.7
  81.4 0.4 fusion.47
  81.8 0.6 fusion.9
  82.4 0.2 fusion.11
  82.6 0.5 fusion.10
  83.1 0.7 fusion.14
  83.9 0.4 fusion.13
  84.2 2.3 %convolution_convert_fusion = bf16[512,2432]{0,1:T(8,128)(2,1)} fusion(bf16[512,128]{0,1:T(8,128)(2,1)S(1)} %bitcast.102, bf16[128,2432]{1,0:T(8,128)(2,1)S(1)} %copy-done), kind=kOutput, calls=%fused_computation.8 | convolution fusion | flops 320012288 | bytes 3244032 | tf_op jit(solution)/shard_map/dot_general | solution.py:123
  86.6 0.9 slice-done
  87.5 0.8 fusion.33
  88.3 59.9 %reduce-scatter.2.cloned.1.call-done = bf16[512,152]{0,1:T(8,128)(2,1)} async-done(((bf16[512,2432]{0,1:T(8,128)(2,1)}), bf16[512,152]{0,1:T(8,128)(2,1)}) %reduce-scatter.2.cloned.1.call-update) | async-done | bytes 155664 | tf_op jit(solution)/shard_map/reduce_scatter | solution.py:124
  148.2 1.0 copy.35
  149.3 20.5 %all_to_all.28 = bf16[32,16,152]{2,1,0:T(8,128)(2,1)S(1)} all-to-all(bf16[32,16,152]{2,1,0:T(8,128)(2,1)S(1)} %add_convert_fusion), channel_id=1, replica_groups=mesh['dp'=32,'mp'=16] {'dp'}, dimensions={0} | all-to-all | bytes 311296 | tf_op jit(solution)/shard_map/all_to_all | solution.py:133
  169.8 0.9 convolution_convert_fusion.2
  (36 shorter events, 1.2 us)
Async XLA Ops:
  6.5 77.7 %copy-start = (bf16[128,2432]{1,0:T(8,128)(2,1)S(1)}, bf16[128,2432]{1,0:T(8,128)(2,1)}, u32[]{:S(2)}) copy-start(bf16[128,2432]{1,0:T(8,128)(2,1)} %param.15) | copy-start | bytes 1867780
  6.5 36.0 %copy-start.4 = (bf16[28,3,2432]{2,0,1:T(8,128)(2,1)S(1)}, bf16[28,3,2432]{2,0,1:T(8,128)(2,1)}, u32[]{:S(2)}) copy-start(bf16[28,3,2432]{2,0,1:T(8,128)(2,1)} %param.11) | copy-start | bytes 1225732
  6.5 36.0 %copy-start.6 = (f32[2,64]{1,0:T(2,128)S(1)}, f32[2,64]{1,0:T(2,128)}, u32[]{:S(2)}) copy-start(f32[2,64]{1,0:T(2,128)} %param.13) | copy-start | bytes 1540
  6.5 36.8 %copy-start.2 = (bf16[2432,3,128]{2,0,1:T(8,128)(2,1)S(1)}, bf16[2432,3,128]{2,0,1:T(8,128)(2,1)}, u32[]{:S(2)}) copy-start(bf16[2432,3,128]{2,0,1:T(8,128)(2,1)} %param.12) | copy-start | bytes 5603332
  6.5 70.2 %all-gather.2.cloned.1.call-start = ((), (), s32[]{:S(2)}) async-start(), calls=%async_computation.4 | async-start | bytes 2646016 | tf_op jit(solution)/shard_map/all_gather | solution.py:115
  34.0 11.5 %copy-start.5 = (bf16[1,2,333,128]{3,1,2,0:T(2,128)(2,1)S(1)}, bf16[1,2,333,128]{3,1,2,0:T(2,128)(2,1)}, u32[]{:S(2)}) copy-start(bf16[1,2,333,128]{3,1,2,0:T(2,128)(2,1)} %param.14) | copy-start | bytes 511492
  34.9 13.1 %all-to-all-start.1 = ((s32[32,16,1]{1,2,0:T(1,128)}), s32[32,16,1]{1,2,0:T(1,128)S(1)}, u32[]{:S(2)}, u32[]{:S(2)}) async-start(s32[32,16,1]{1,2,0:T(1,128)} %bitcast.19), calls=%async_computation.1 | async-start | bytes 32768 | tf_op jit(solution)/shard_map/all_to_all | solution.py:113
  39.5 108.7 %reduce-scatter.2.cloned.1.call-start = ((), (), s32[]{:S(2)}) async-start(), calls=%async_computation.5 | async-start | bytes 2646016 | tf_op jit(solution)/shard_map/reduce_scatter | solution.py:124
  76.8 2.5 %copy-start.1 = (bf16[512,2432]{0,1:T(8,128)(2,1)S(1)}, bf16[512,2432]{0,1:T(8,128)(2,1)}, u32[]{:S(2)}) copy-start(bf16[512,2432]{0,1:T(8,128)(2,1)} %all-gather.2.cloned.1.call-done) | copy-start | bytes 7471108
  76.8 3.2 %copy-start.3 = (bf16[2432,3,128]{0,2,1:T(8,128)(2,1)S(1)}, bf16[2432,3,128]{0,2,1:T(8,128)(2,1)}, u32[]{:S(2)}) copy-start(bf16[2432,3,128]{0,2,1:T(8,128)(2,1)} %copy.30) | copy-start | bytes 5603332
  86.5 0.9 slice-start
Sparse Core Ops, SparseCore 0:
  34.1 42.5 all-gather.1
  86.7 61.4 reduce-scatter.1
where the time goes:
time: 178 us
  waiting for transfers between devices  90.8 us (51%)
  blocking collectives  42.8 us (24%)
  between operations  13.6 us (8%)
  matrix products  11.1 us (6%)
  local copies, waits for them, and re-layouts  7.73 us (4%)
  other arithmetic  7 us (4%)
  starting transfers between devices  4.64 us (3%)
    reduce_scatter x1, waiting for transfers between devices, body(): lax.psum_scatter(partial_term.astype(jnp.bfloat16), 'mp', scatter_dimensi...  59.9 us
    all_gather x1, waiting for transfers between devices, body(): whole = lax.all_gather(arrived, 'mp', axis=1, tiled=True)  28.6 us
    all_to_all x1, blocking collectives, body(): lax.all_to_all(send_rows, 'dp', split_axis=0, concat_axis=0, tiled=True)  22.3 us
    all_to_all x1, blocking collectives, body(): lax.all_to_all(finished, 'dp', split_axis=0, concat_axis=0, tiled=True)  20.5 us
    all_to_all x1, starting transfers between devices, body(): lax.all_to_all(valid_send, 'dp', split_axis=0, concat_axis=0, tiled=True)  4.56 us
  transfers between devices with their start and end apart: 3, of which 3 were waited for; matrix products, arithmetic and copies ran while one was open for 5% of the time, Pallas kernels for 0%

commit v1 on v0

v1 whole, which is shorter than its diff:
```python
import jax
import jax.numpy as jnp
from jax import lax
from jax.sharding import PartitionSpec as P

HD = 64
TXT = 333
TSTEPS = 28
EPS = 1e-06
DEAD = 1e30


def rms_scaled(values, gain_row):
    return values * lax.rsqrt(jnp.mean(jnp.square(values), axis=-1, keepdims=True) + EPS) * gain_row


def attend(slots, context, head_count):
    span = slots.shape[0]
    grid = slots.reshape(span, 3, head_count, HD)
    live = slots[:, head_count * HD] < DEAD * 0.5
    ctx_heads = context.reshape(2, TXT, head_count, HD)
    factor = HD ** (-0.5)
    queries, keys_img, values_img = grid[:, 0], grid[:, 1], grid[:, 2]
    own = jnp.einsum("shd,thd->hst", queries, keys_img, preferred_element_type=jnp.float32) * factor
    own = jnp.where(live[None, None, :], own, -1e30)
    far = jnp.einsum("shd,thd->hst", queries, ctx_heads[0], preferred_element_type=jnp.float32) * factor
    top = jnp.maximum(jnp.max(own, axis=-1, keepdims=True), jnp.max(far, axis=-1, keepdims=True))
    own_weights = jnp.exp(own - top)
    far_weights = jnp.exp(far - top)
    total = jnp.sum(own_weights, axis=-1, keepdims=True) + jnp.sum(far_weights, axis=-1, keepdims=True)
    own_probs = (own_weights / total).astype(jnp.bfloat16)
    far_probs = (far_weights / total).astype(jnp.bfloat16)
    result = jnp.einsum("hst,thd->shd", own_probs, values_img, preferred_element_type=jnp.float32)
    result = result + jnp.einsum("hst,thd->shd", far_probs, ctx_heads[1], preferred_element_type=jnp.float32)
    return result.astype(jnp.bfloat16).reshape(span, head_count * HD)


def body(tokens, route, tsteps, mod_table, w_qkv, qk_gain, context, w_out):
    rows, width = tokens.shape
    requests = lax.axis_size("dp")
    parts = lax.axis_size("mp")
    chips = parts // 2
    cap = max(2, 2 * rows // requests)
    slots = requests * cap
    depth = w_qkv.shape[0]
    heads = w_qkv.shape[2] // HD
    inner = heads * HD
    core = lax.axis_index("mp") % 2
    along_z = [[2 * z + c for z in range(chips)] for c in range(2)]
    sibling = [(i, i ^ 1) for i in range(parts)]

    tokens_t = tokens.T
    own_half = lax.all_to_all(
        jnp.broadcast_to(tokens_t, (chips, width, rows)), "mp", 0, 0, axis_index_groups=along_z, tiled=True
    )
    other_half = lax.ppermute(own_half, "mp", sibling)

    request = route[:, 0]
    same = request[:, None] == request[None, :]
    before = jnp.arange(rows)[None, :] < jnp.arange(rows)[:, None]
    rank = jnp.sum((same & before).astype(jnp.int32), axis=1)
    position = request * cap + rank
    hits = position[None, :] == jnp.arange(slots, dtype=jnp.int32)[:, None]
    place = hits.astype(jnp.bfloat16)
    filled = jnp.any(hits, axis=1)
    step_of = jnp.dot(
        (request[:, None] == jnp.arange(requests, dtype=jnp.int32)[None, :]).astype(jnp.float32),
        tsteps.astype(jnp.float32),
    )
    pick = (step_of[:, None] == jnp.arange(TSTEPS, dtype=jnp.float32)[None, :]).astype(jnp.bfloat16)

    first = jnp.where(core == 0, own_half, other_half)
    second = jnp.where(core == 0, other_half, own_half)
    whole = jnp.stack([first, second], axis=1).reshape(depth, rows).astype(jnp.float32)
    shift_t = jnp.einsum("td,rt->dr", mod_table[:, 0], pick, preferred_element_type=jnp.float32)
    scale_t = jnp.einsum("td,rt->dr", mod_table[:, 1], pick, preferred_element_type=jnp.float32)
    center = jnp.mean(whole, axis=0, keepdims=True)
    spread = jnp.mean(jnp.square(whole - center), axis=0, keepdims=True)
    hidden = ((whole - center) * lax.rsqrt(spread + EPS) * (1.0 + scale_t) + shift_t).astype(jnp.bfloat16)
    proj = jnp.einsum("dr,dk->rk", hidden, w_qkv.reshape(depth, 3 * inner), preferred_element_type=jnp.float32)
    proj = proj.reshape(rows, 3, heads, HD)
    packed = jnp.stack(
        [rms_scaled(proj[:, 0], qk_gain[0]), rms_scaled(proj[:, 1], qk_gain[1]), proj[:, 2]], axis=1
    ).astype(jnp.bfloat16).reshape(rows, 3 * inner)
    send = jnp.dot(place, packed, preferred_element_type=jnp.float32).astype(jnp.bfloat16)
    is_key = (jnp.arange(3 * inner) >= inner) & (jnp.arange(3 * inner) < 2 * inner)
    send = jnp.where(is_key[None, :] & ~filled[:, None], jnp.bfloat16(DEAD), send)
    arrived = lax.all_to_all(send.reshape(requests, cap, 3 * inner), "dp", 0, 0, tiled=True)

    attn = attend(arrived.reshape(slots, 3 * inner), context[0], heads)
    returned = lax.all_to_all(attn.reshape(requests, cap, inner), "dp", 0, 0, tiled=True).reshape(slots, inner)
    attn_rows = jnp.einsum("sr,sk->rk", place, returned, preferred_element_type=jnp.float32).astype(jnp.bfloat16)

    partial = jnp.einsum("kd,rk->dr", w_out, attn_rows, preferred_element_type=jnp.float32)
    partial = partial.reshape(chips, 2, width, rows)
    keep = jnp.where(core == 0, partial[:, 0], partial[:, 1])
    give = jnp.where(core == 0, partial[:, 1], partial[:, 0]).astype(jnp.bfloat16)
    paired = (keep + lax.ppermute(give, "mp", sibling).astype(jnp.float32)).astype(jnp.bfloat16)
    spread_out = lax.all_to_all(paired, "mp", 0, 0, axis_index_groups=along_z, tiled=True)
    out_sum = jnp.sum(spread_out.astype(jnp.float32), axis=0)

    gate_table = lax.dynamic_slice_in_dim(mod_table[:, 2, :], lax.axis_index("mp") * width, width, 1)
    gate_t = jnp.einsum("td,rt->dr", gate_table, pick, preferred_element_type=jnp.float32)
    return (tokens_t.astype(jnp.float32) + gate_t * out_sum).astype(jnp.bfloat16).T


def solution(mesh):
    return jax.shard_map(
        body,
        mesh=mesh,
        in_specs=(
            P("dp", "mp"),
            P("dp", None),
            P(),
            P(),
            P(None, None, "mp"),
            P(),
            P("dp", None, None, "mp"),
            P("mp", None),
        ),
        out_specs=P("dp", "mp"),
        check_vma=False,
    )
```

time: 178 us -> 129 us (0.72)
  the two profiles are of different devices: /device:TPU:8 before, /device:TPU:1 now
where the time goes in v1:
time: 129 us
  waiting for transfers between devices  48.9 us (38%)
  starting transfers between devices  30.7 us (24%)
  local copies, waits for them, and re-layouts  16.3 us (13%)
  blocking collectives  16.3 us (13%)
  matrix products  12.6 us (10%)
  other arithmetic  3.65 us (3%)
    all_to_all x1, waiting for transfers between devices, body(): lax.all_to_all(paired, 'mp', 0, 0, axis_index_groups=along_z, tiled=True)  20 us
    all_to_all x1, blocking collectives, body(): lax.all_to_all(attn.reshape(requests, cap, inner), 'dp', 0, 0, tiled=True)  16.3 us
    all_to_all x1, waiting for transfers between devices, body(): lax.all_to_all(jnp.broadcast_to(tokens_t, (chips, width, rows)), 'mp', 0,...  15.6 us
    all_to_all x1, waiting for transfers between devices, body(): lax.all_to_all(send.reshape(requests, cap, 3 * inner), 'dp', 0, 0, tiled=...  11.7 us
    all_to_all x1, starting transfers between devices, body(): lax.all_to_all(jnp.broadcast_to(tokens_t, (chips, width, rows)), 'mp', 0,...  10.9 us
    all_to_all x1, starting transfers between devices, body(): lax.all_to_all(send.reshape(requests, cap, 3 * inner), 'dp', 0, 0, tiled=...  9.67 us
    unnamed x22, local copies, waits for them, and re-layouts  5.67 us
    convert_element_type x2, local copies, waits for them, and re-layouts, body(): jnp.stack([first, second], axis=1).reshape(depth, rows).astype(jnp.float32)  4.89 us
  transfers between devices with their start and end apart: 5, of which 4 were waited for; matrix products, arithmetic and copies ran while one was open for 6% of the time, Pallas kernels for 0%

profile of v1, /device:TPU:1, one launch (start us, length us, event | category | flops | bytes accessed | tf_op | source)
XLA Modules:
  0.0 128.7 jit_solution(5823642437429879125)
XLA Ops:
  0.0 1.8 %broadcast_in_dim.14 = bf16[8,152,256]{2,1,0:T(8,128)(2,1)} broadcast(bf16[152,256]{1,0:T(8,128)(2,1)} %bitcast.107), dimensions={1,2} | broadcast | bytes 700416 | tf_op jit(solution)/shard_map/broadcast_in_dim | solution.py:54
  1.8 10.9 %all-to-all-start = ((bf16[8,152,256]{2,1,0:T(8,128)(2,1)}), bf16[8,152,256]{2,1,0:T(8,128)(2,1)S(1)}, u32[]{:S(2)}, u32[]{:S(2)}) async-start(bf16[8,152,256]{2,1,0:T(8,128)(2,1)} %broadcast_in_dim.14), calls=%async_computation | async-start | bytes 1245184 | tf_op jit(solution)/shard_map/all_to_all | solution.py:53
  12.7 4.0 %copy.55 = bf16[2432,3,128]{0,2,1:T(8,128)(2,1)} copy(bf16[2432,3,128]{2,0,1:T(8,128)(2,1)} %param.12) | data formatting | bytes 3735552 | tf_op args[4]
  17.2 15.6 %all-to-all-done = bf16[8,152,256]{2,1,0:T(8,128)(2,1)S(1)} async-done(((bf16[8,152,256]{2,1,0:T(8,128)(2,1)}), bf16[8,152,256]{2,1,0:T(8,128)(2,1)S(1)}, u32[]{:S(2)}, u32[]{:S(2)}) %all-to-all-start) | async-done | bytes 622624 | tf_op jit(solution)/shard_map/all_to_all | solution.py:53
  32.7 2.4 %collective-permute-start = (bf16[8,152,256]{2,1,0:T(8,128)(2,1)S(1)}, bf16[8,152,256]{2,1,0:T(8,128)(2,1)S(1)}, u32[]{:S(2)}, u32[]{:S(2)}) collective-permute-start(bf16[8,152,256]{2,1,0:T(8,128)(2,1)S(1)} %all-to-all-done), channel_id=1, source_target_pairs={{0,1},{1,0},{2,3},{3,2},{4,5},{5,4},{6,7},{7,6},{8,9},{9,8},{10,11... | collective-permute-start | bytes 1867784 | tf_op jit(solution)/shard_map/ppermute | solution.py:56
  35.4 2.0 %convolution_bitcast_fusion.1 = f32[2432,256]{0,1:T(8,128)} fusion(bf16[28,3,2432]{2,0,1:T(8,128)(2,1)S(1)} %copy-done.4, f32[256]{0:T(256)S(1)} %bitcast.113), kind=kOutput, calls=%fused_computation.5 | convolution fusion | flops 34872320 | bytes 2647040 | tf_op jit(solution)/shard_map/td,rt->dr/dot_general | solution.py:75
  37.6 0.3 fusion.15
  38.0 1.7 %copy.53 = f32[8,2,152,256]{3,2,1,0:T(8,128)} copy(f32[8,2,152,256]{3,2,0,1:T(8,128)S(1)} %maximum_convert_fusion) | data formatting | bytes 4980736 | tf_op jit(solution)/shard_map/convert_element_type | solution.py:74
  39.7 3.2 %copy.54 = f32[2432,256]{0,1:T(8,128)} copy(f32[2432,256]{1,0:T(8,128)} %bitcast.102) | data formatting | bytes 4980736 | tf_op jit(solution)/shard_map/convert_element_type | solution.py:74
  42.9 0.4 multiply_reduce_fusion
  43.3 4.2 %fusion.12 = f32[256,3,2,64]{0,3,2,1:T(8,128)S(1)} fusion(bf16[3,2,64,2432]{3,2,1,0:T(8,128)(2,1)} %bitcast.103, f32[2432,256]{0,1:T(8,128)} %convolution_bitcast_fusion.1, f32[2432,256]{0,1:T(8,128)} %copy.54, f32[256]{0:T(256)S(1)} %add_rsqrt_fusion.2, f32[256]{0:T(256)S(1)} %broadcast_multiply_fusion, bf16[28,3,2432]{2,0,1:T(8,128)(2,1)S(1)} %copy-done.4, ...), kind=kOutput, calls=%fused_computation.30 | convolution fusion | flops 516758528 | bytes 7400448 | tf_op jit(solution)/shard_map/dr,dk->rk/dot_general | solution.py:80
  47.6 1.1 fusion.9
  48.7 9.7 %all-to-all-start.1 = ((bf16[32,16,384]{2,1,0:T(8,128)(2,1)}), bf16[32,16,384]{2,1,0:T(8,128)(2,1)S(1)}, u32[]{:S(2)}, u32[]{:S(2)}) async-start(bf16[32,16,384]{2,1,0:T(8,128)(2,1)} %bitcast.19), calls=%async_computation.1 | async-start | bytes 786432 | tf_op jit(solution)/shard_map/all_to_all | solution.py:88
  58.9 11.7 %all-to-all-done.1 = bf16[32,16,384]{2,1,0:T(8,128)(2,1)S(1)} async-done(((bf16[32,16,384]{2,1,0:T(8,128)(2,1)}), bf16[32,16,384]{2,1,0:T(8,128)(2,1)S(1)}, u32[]{:S(2)}, u32[]{:S(2)}) %all-to-all-start.1) | async-done | bytes 393248 | tf_op jit(solution)/shard_map/all_to_all | solution.py:88
  70.6 0.4 reshape_reshape.6
  71.0 0.5 fusion.49
  72.0 0.4 fusion.51
  72.4 0.5 fusion.5
  72.9 0.5 copy-done.1
  73.7 0.5 fusion.6
  74.4 0.7 convolution_bitcast_fusion.3
  75.1 0.6 copy-done.2
  75.7 0.4 fusion.11
  76.4 16.3 %all_to_all.20 = bf16[32,16,128]{2,1,0:T(8,128)(2,1)S(1)} all-to-all(bf16[32,16,128]{2,1,0:T(8,128)(2,1)S(1)} %reshape_reshape.7), channel_id=1, replica_groups=mesh['dp'=32,'mp'=16] {'dp'}, dimensions={0} | all-to-all | bytes 262144 | tf_op jit(solution)/shard_map/all_to_all | solution.py:91
  92.7 2.2 %convolution_bitcast_fusion = f32[2432,256]{0,1:T(8,128)} fusion(bf16[128,2432]{1,0:T(8,128)(2,1)S(1)} %copy-done, bf16[512,128]{1,0:T(8,128)(2,1)S(1)} %bitcast.105, s32[256]{0:T(256)S(1)} %multiply_add_fusion), kind=kOutput, calls=%fused_computation.4 | convolution fusion | flops 193101824 | bytes 3245056 | tf_op jit(solution)/shard_map/kd,rk->dr/dot_general | solution.py:94
  95.0 2.1 %copy.64 = f32[2432,256]{1,0:T(8,128)S(1)} copy(f32[2432,256]{0,1:T(8,128)} %convolution_bitcast_fusion) | data formatting | bytes 4980736 | tf_op jit(solution)/shard_map/kd,rk->dr/dot_general | solution.py:94
  97.2 4.1 %collective-permute-start.1 = (bf16[8,152,256]{2,1,0:T(8,128)(2,1)S(1)}, bf16[8,152,256]{2,1,0:T(8,128)(2,1)S(1)}, u32[]{:S(2)}, u32[]{:S(2)}) collective-permute-start(bf16[8,152,256]{2,1,0:T(8,128)(2,1)S(1)} %fusion.13), channel_id=1, source_target_pairs={{0,1},{1,0},{2,3},{3,2},{4,5},{5,4},{6,7},{7,6},{8,9},{9,8},{10,11... | collective-permute-start | bytes 1867784 | tf_op jit(solution)/shard_map/ppermute | solution.py:98
  101.3 1.7 %collective-permute-done.1 = bf16[8,152,256]{2,1,0:T(8,128)(2,1)S(1)} collective-permute-done((bf16[8,152,256]{2,1,0:T(8,128)(2,1)S(1)}, bf16[8,152,256]{2,1,0:T(8,128)(2,1)S(1)}, u32[]{:S(2)}, u32[]{:S(2)}) %collective-permute-start.1) | collective-permute-done | bytes 622624 | tf_op jit(solution)/shard_map/ppermute | solution.py:98
  102.9 1.1 fusion.7
  104.0 3.7 %all-to-all-start.3 = ((bf16[8,152,256]{2,1,0:T(8,128)(2,1)}), bf16[8,152,256]{2,1,0:T(8,128)(2,1)S(1)}, u32[]{:S(2)}, u32[]{:S(2)}) async-start(bf16[8,152,256]{2,1,0:T(8,128)(2,1)} %fusion.7), calls=%async_computation.3 | async-start | bytes 1245184 | tf_op jit(solution)/shard_map/all_to_all | solution.py:99
  107.7 20.0 %all-to-all-done.3 = bf16[8,152,256]{2,1,0:T(8,128)(2,1)S(1)} async-done(((bf16[8,152,256]{2,1,0:T(8,128)(2,1)}), bf16[8,152,256]{2,1,0:T(8,128)(2,1)S(1)}, u32[]{:S(2)}, u32[]{:S(2)}) %all-to-all-start.3) | async-done | bytes 622624 | tf_op jit(solution)/shard_map/all_to_all | solution.py:99
  127.8 0.9 fusion.21
  (49 shorter events, 2.9 us)
Async XLA Ops:
  0.0 92.7 %copy-start = (bf16[128,2432]{1,0:T(8,128)(2,1)S(1)}, bf16[128,2432]{1,0:T(8,128)(2,1)}, u32[]{:S(2)}) copy-start(bf16[128,2432]{1,0:T(8,128)(2,1)} %param.15) | copy-start | bytes 1867780
  1.8 30.9 %all-to-all-start = ((bf16[8,152,256]{2,1,0:T(8,128)(2,1)}), bf16[8,152,256]{2,1,0:T(8,128)(2,1)S(1)}, u32[]{:S(2)}, u32[]{:S(2)}) async-start(bf16[8,152,256]{2,1,0:T(8,128)(2,1)} %broadcast_in_dim.14), calls=%async_computation | async-start | bytes 1245184 | tf_op jit(solution)/shard_map/all_to_all | solution.py:53
  12.7 4.1 %copy-start.6 = (s32[256,1]{0,1:T(1,128)S(1)}, s32[256,1]{0,1:T(1,128)}, u32[]{:S(2)}) copy-start(s32[256,1]{0,1:T(1,128)} %param.9) | copy-start | bytes 3076
  12.7 4.5 %copy-start.7 = (f32[2,64]{1,0:T(2,128)S(1)}, f32[2,64]{1,0:T(2,128)}, u32[]{:S(2)}) copy-start(f32[2,64]{1,0:T(2,128)} %param.13) | copy-start | bytes 1540
  12.7 22.5 %copy-start.8 = (s32[32]{0:T(128)S(1)}, s32[32]{0:T(128)}, u32[]{:S(2)}) copy-start(s32[32]{0:T(128)} %param.10) | copy-start | bytes 388
  12.7 22.7 %copy-start.4 = (bf16[28,3,2432]{2,0,1:T(8,128)(2,1)S(1)}, bf16[28,3,2432]{2,0,1:T(8,128)(2,1)}, u32[]{:S(2)}) copy-start(bf16[28,3,2432]{2,0,1:T(8,128)(2,1)} %param.11) | copy-start | bytes 1225732
  32.7 4.6 %collective-permute-start = (bf16[8,152,256]{2,1,0:T(8,128)(2,1)S(1)}, bf16[8,152,256]{2,1,0:T(8,128)(2,1)S(1)}, u32[]{:S(2)}, u32[]{:S(2)}) collective-permute-start(bf16[8,152,256]{2,1,0:T(8,128)(2,1)S(1)} %all-to-all-done), channel_id=1, source_target_pairs={{0,1},{1,0},{2,3},{3,2},{4,5},{5,4},{6,7},{7,6},{8,9},{9,8},{10,11... | collective-permute-start | bytes 1867784 | tf_op jit(solution)/shard_map/ppermute | solution.py:56
  47.4 11.0 %copy-start.3 = (bf16[1,2,333,128]{3,1,2,0:T(2,128)(2,1)S(1)}, bf16[1,2,333,128]{3,1,2,0:T(2,128)(2,1)}, u32[]{:S(2)}) copy-start(bf16[1,2,333,128]{3,1,2,0:T(2,128)(2,1)} %param.14) | copy-start | bytes 511492
  48.7 21.9 %all-to-all-start.1 = ((bf16[32,16,384]{2,1,0:T(8,128)(2,1)}), bf16[32,16,384]{2,1,0:T(8,128)(2,1)S(1)}, u32[]{:S(2)}, u32[]{:S(2)}) async-start(bf16[32,16,384]{2,1,0:T(8,128)(2,1)} %bitcast.19), calls=%async_computation.1 | async-start | bytes 786432 | tf_op jit(solution)/shard_map/all_to_all | solution.py:88
  72.4 1.1 copy-start.1
  74.3 1.3 %copy-start.2 = (f32[2,512,333]{1,2,0:T(8,128)S(1)}, f32[2,512,333]{1,2,0:T(8,128)}, u32[]{:S(2)}) copy-start(f32[2,512,333]{1,2,0:T(8,128)} %copy-done.1) | copy-start | bytes 4091908
  97.2 5.7 %collective-permute-start.1 = (bf16[8,152,256]{2,1,0:T(8,128)(2,1)S(1)}, bf16[8,152,256]{2,1,0:T(8,128)(2,1)S(1)}, u32[]{:S(2)}, u32[]{:S(2)}) collective-permute-start(bf16[8,152,256]{2,1,0:T(8,128)(2,1)S(1)} %fusion.13), channel_id=1, source_target_pairs={{0,1},{1,0},{2,3},{3,2},{4,5},{5,4},{6,7},{7,6},{8,9},{9,8},{10,11... | collective-permute-start | bytes 1867784 | tf_op jit(solution)/shard_map/ppermute | solution.py:98
  104.0 23.8 %slice-start = ((bf16[28,3,2432]{2,0,1:T(8,128)(2,1)}), bf16[28,1,2432]{2,0,1:T(8,128)(2,1)S(1)}, s32[]{:S(2)}) async-start(bf16[28,3,2432]{2,0,1:T(8,128)(2,1)} %param.11), calls=%async_computation.4 | async-start | bytes 311296 | tf_op jit(solution)/shard_map/slice | solution.py:102
  104.0 23.8 %copy-start.5 = (bf16[256,152]{0,1:T(8,128)(2,1)S(1)}, bf16[256,152]{0,1:T(8,128)(2,1)}, u32[]{:S(2)}) copy-start(bf16[256,152]{0,1:T(8,128)(2,1)} %param.8) | copy-start | bytes 233476
  104.0 23.7 %all-to-all-start.3 = ((bf16[8,152,256]{2,1,0:T(8,128)(2,1)}), bf16[8,152,256]{2,1,0:T(8,128)(2,1)S(1)}, u32[]{:S(2)}, u32[]{:S(2)}) async-start(bf16[8,152,256]{2,1,0:T(8,128)(2,1)} %fusion.7), calls=%async_computation.3 | async-start | bytes 1245184 | tf_op jit(solution)/shard_map/all_to_all | solution.py:99

commit v2 on v1

v2 whole, which is shorter than its diff:
```python
import functools

import jax
import jax.numpy as jnp
from jax import lax
from jax.experimental import pallas as pl
from jax.experimental.pallas import tpu as pltpu
from jax.sharding import PartitionSpec as P

HD = 64
TSTEPS = 28
EPS = 1e-06
DEAD = 1e30
MASKED = -1e30
VMEM_LIMIT = 24 * 1024 * 1024
F32, BF16 = jnp.float32, jnp.bfloat16


def dot_nt(a, b):
    return lax.dot_general(a, b, (((1,), (1,)), ((), ())), preferred_element_type=F32)


def project_kernel(core_ref, own_ref, other_ref, scale_ref, shift_ref, w_ref, gain_ref, pos_ref, send_ref, hid_ref):
    chips, width, rows = own_ref.shape
    depth = 2 * chips * width
    slots = send_ref.shape[0]
    inner = w_ref.shape[0] // 3
    is_first = core_ref[0] == 0

    def columns(ref):
        return [ref[z].astype(F32) for z in range(chips)]

    total = sum(jnp.sum(x, axis=0, keepdims=True) for x in columns(own_ref) + columns(other_ref))
    mean = total * (1.0 / depth)
    square = sum(jnp.sum(jnp.square(x - mean), axis=0, keepdims=True) for x in columns(own_ref) + columns(other_ref))
    inverse = lax.rsqrt(square * (1.0 / depth) + EPS)
    for z in range(chips):
        own, other = own_ref[z].astype(F32), other_ref[z].astype(F32)
        pair = jnp.concatenate([jnp.where(is_first, own, other), jnp.where(is_first, other, own)], axis=0)
        span = pl.ds(z * 2 * width, 2 * width)
        scale, shift = scale_ref[span, :].astype(F32), shift_ref[span, :].astype(F32)
        hid_ref[span, :] = ((pair - mean) * inverse * (1.0 + scale) + shift).astype(BF16)
    proj = jnp.dot(w_ref[...], hid_ref[...], preferred_element_type=F32)
    pieces = []
    for start in range(0, 2 * inner, HD):
        head = proj[start : start + HD]
        power = jnp.mean(jnp.square(head), axis=0, keepdims=True)
        pieces.append(head * lax.rsqrt(power + EPS) * gain_ref[pl.ds(start, HD), :])
    pieces.append(proj[2 * inner :])
    packed = jnp.concatenate(pieces, axis=0).astype(BF16)
    hits = lax.broadcasted_iota(jnp.int32, (slots, rows), 0) == pos_ref[...]
    place = jnp.where(hits, 1.0, 0.0)
    filled = jnp.sum(place, axis=1, keepdims=True)
    send = dot_nt(place.astype(BF16), packed)
    send_ref[:, 0:inner] = send[:, 0:inner].astype(BF16)
    send_ref[:, inner : 2 * inner] = jnp.where(filled > 0.5, send[:, inner : 2 * inner], DEAD).astype(BF16)
    send_ref[:, 2 * inner :] = send[:, 2 * inner :].astype(BF16)


def attend_kernel(text_len, slots_ref, ctx_ref, out_ref):
    slots, inner = out_ref.shape
    block = 128
    text_pad = ctx_ref.shape[1]
    queries = slots_ref[:, 0:inner]
    keys = slots_ref[:, inner : 2 * inner].astype(F32)
    values = slots_ref[:, 2 * inner :]
    text_keys, text_values = ctx_ref[0], ctx_ref[1]
    dead = keys > 0.5 * DEAD
    marks = jnp.where(dead, 1.0, 0.0).astype(BF16)
    keys = jnp.where(dead, 0.0, keys).astype(BF16)
    own_bias = dot_nt(jnp.full((8, inner), MASKED, BF16), marks)[0:1]
    text_lane = lax.broadcasted_iota(jnp.int32, (1, text_pad), 1)
    text_bias = jnp.where(text_lane < text_len, 0.0, MASKED)
    lane = lax.broadcasted_iota(jnp.int32, (1, inner), 1)
    one = jnp.ones((), BF16)
    zero = jnp.zeros((), BF16)
    for row in range(0, slots, block):
        parts = []
        for head in range(inner // HD):
            mine = (lane >= head * HD) & (lane < (head + 1) * HD)
            query = jnp.where(mine, queries[row : row + block], zero)
            own = dot_nt(query, keys) + own_bias
            far = dot_nt(query, text_keys) + text_bias
            top = jnp.maximum(jnp.max(own, axis=1, keepdims=True), jnp.max(far, axis=1, keepdims=True))
            own = jnp.exp(own - top).astype(BF16)
            far = jnp.exp(far - top).astype(BF16)
            mixed = jnp.dot(own, jnp.where(mine, values, one), preferred_element_type=F32)
            mixed = mixed + jnp.dot(far, jnp.where(mine, text_values, one), preferred_element_type=F32)
            parts.append((mine, mixed / pltpu.roll(mixed, HD, 1)))
        out_ref[row : row + block, :] = jnp.where(parts[0][0], parts[0][1], parts[1][1]).astype(BF16)


def give_kernel(core_ref, back_ref, pos_ref, w_ref, give_ref, rows_ref):
    slots = back_ref.shape[0]
    rows = rows_ref.shape[0]
    hits = lax.broadcasted_iota(jnp.int32, (rows, slots), 1) == pos_ref[...]
    place = jnp.where(hits, 1.0, 0.0).astype(BF16)
    attn = jnp.dot(place, back_ref[...], preferred_element_type=F32).astype(BF16)
    rows_ref[...] = attn
    other = 1 - core_ref[0]
    for z in range(give_ref.shape[0]):
        give_ref[z] = dot_nt(w_ref[z, other], attn).astype(BF16)


def keep_kernel(core_ref, rows_ref, w_ref, keep_ref):
    core = core_ref[0]
    for z in range(keep_ref.shape[0]):
        keep_ref[z] = dot_nt(w_ref[z, core], rows_ref[...])


def call(kernel, out_shape, smem, vmem, scratch=(), flops=0):
    whole = pl.BlockSpec(memory_space=pltpu.VMEM)
    outs = jax.tree.map(lambda _: whole, out_shape)
    return pl.pallas_call(
        kernel,
        out_shape=out_shape,
        in_specs=[pl.BlockSpec(memory_space=pltpu.SMEM)] * smem + [whole] * vmem,
        out_specs=outs,
        scratch_shapes=list(scratch),
        compiler_params=pltpu.CompilerParams(vmem_limit_bytes=VMEM_LIMIT),
        cost_estimate=pl.CostEstimate(flops=flops, bytes_accessed=1 << 20, transcendentals=0),
    )


def body(tokens, route, tsteps, mod_table, w_qkv, qk_gain, context, w_out):
    rows, width = tokens.shape
    requests = lax.axis_size("dp")
    parts = lax.axis_size("mp")
    chips = parts // 2
    cap = max(2, 2 * rows // requests)
    slots = requests * cap
    depth = w_qkv.shape[0]
    inner = w_qkv.shape[2]
    text_len = context.shape[2]
    text_pad = -(-text_len // 128) * 128
    along_z = [[2 * z + c for z in range(chips)] for c in range(2)]
    sibling = [(i, i ^ 1) for i in range(parts)]
    core = lax.rem(lax.axis_index("mp"), 2).astype(jnp.int32).reshape(1)

    tokens_t = tokens.T
    own_half = lax.all_to_all(
        jnp.broadcast_to(tokens_t, (chips, width, rows)), "mp", 0, 0, axis_index_groups=along_z, tiled=True
    )

    request = route[:, 0]
    same = request[:, None] == request[None, :]
    before = jnp.arange(rows)[None, :] < jnp.arange(rows)[:, None]
    rank = jnp.sum((same & before).astype(jnp.int32), axis=1)
    position = request * cap + rank
    step_of = jnp.dot(
        (request[:, None] == jnp.arange(requests, dtype=jnp.int32)[None, :]).astype(F32), tsteps.astype(F32)
    )
    pick = (step_of[:, None] == jnp.arange(TSTEPS, dtype=F32)[None, :]).astype(BF16)
    shift_t = jnp.einsum("td,rt->dr", mod_table[:, 0], pick, preferred_element_type=F32).astype(BF16)
    scale_t = jnp.einsum("td,rt->dr", mod_table[:, 1], pick, preferred_element_type=F32).astype(BF16)
    gate_table = lax.dynamic_slice_in_dim(mod_table[:, 2, :], lax.axis_index("mp") * width, width, 1)
    gate_t = jnp.einsum("td,rt->dr", gate_table, pick, preferred_element_type=F32)
    w_t = w_qkv.transpose(1, 2, 0).reshape(3 * inner, depth)
    w_out_t = w_out.T.reshape(chips, 2, width, inner)
    gains = jnp.concatenate(
        [jnp.tile(qk_gain[0] * HD ** (-0.5), inner // HD), jnp.tile(qk_gain[1], inner // HD)]
    ).reshape(2 * inner, 1)
    text = jnp.pad(context[0], ((0, 0), (0, text_pad - text_len), (0, 0)))
    own_half, position, shift_t, scale_t, gate_t, w_t, w_out_t, gains, text = lax.optimization_barrier(
        (own_half, position, shift_t, scale_t, gate_t, w_t, w_out_t, gains, text)
    )
    other_half = lax.ppermute(own_half, "mp", sibling)

    send = call(
        project_kernel,
        jax.ShapeDtypeStruct((slots, 3 * inner), BF16),
        1,
        7,
        [pltpu.VMEM((depth, rows), BF16)],
        flops=2 * depth * rows * 3 * inner,
    )(core, own_half, other_half, scale_t, shift_t, w_t, gains, position.reshape(1, rows))
    arrived = lax.all_to_all(send.reshape(requests, cap, 3 * inner), "dp", 0, 0, tiled=True)

    attn = call(
        functools.partial(attend_kernel, text_len),
        jax.ShapeDtypeStruct((slots, inner), BF16),
        0,
        2,
        flops=8 * slots * (slots + text_pad) * inner,
    )(arrived.reshape(slots, 3 * inner), text)
    returned = lax.all_to_all(attn.reshape(requests, cap, inner), "dp", 0, 0, tiled=True).reshape(slots, inner)

    give, attn_rows = call(
        give_kernel,
        (jax.ShapeDtypeStruct((chips, width, rows), BF16), jax.ShapeDtypeStruct((rows, inner), BF16)),
        1,
        3,
        flops=depth * rows * inner,
    )(core, returned, position.reshape(rows, 1), w_out_t)
    given = lax.ppermute(give, "mp", sibling)
    keep = call(
        keep_kernel, jax.ShapeDtypeStruct((chips, width, rows), F32), 1, 2, flops=depth * rows * inner
    )(core, attn_rows, w_out_t)
    paired = (keep + given.astype(F32)).astype(BF16)
    spread_out = lax.all_to_all(paired, "mp", 0, 0, axis_index_groups=along_z, tiled=True)
    out_sum = jnp.sum(spread_out.astype(F32), axis=0)
    return (tokens_t.astype(F32) + gate_t * out_sum).astype(BF16).T


def solution(mesh):
    return jax.shard_map(
        body,
        mesh=mesh,
        in_specs=(
            P("dp", "mp"),
            P("dp", None),
            P(),
            P(),
            P(None, None, "mp"),
            P(),
            P("dp", None, None, "mp"),
            P("mp", None),
        ),
        out_specs=P("dp", "mp"),
        check_vma=False,
    )
```

time: 129 us -> 115 us (0.89)
  waiting for transfers between devices: 48.9 us -> 18.7 us
  blocking collectives: 16.3 us -> 43.9 us
  Pallas kernels: 0 us -> 8.01 us
  local copies, waits for them, and re-layouts: 16.3 us -> 10.7 us
  matrix products: 12.6 us -> 7 us
  starting transfers between devices: 30.7 us -> 25.2 us
  other arithmetic: 3.65 us -> 1.08 us
    all_to_all x1 -> x2, blocking collectives: 16.3 us -> 43.9 us  [the longest x1 22.6 us: body(): lax.all_to_all(paired, 'mp', 0, 0, axis_index_groups=along_z, tiled=True)]
    all_to_all x2 -> x1, waiting for transfers between devices: 31.7 us -> 9.03 us  [body(): lax.all_to_all(attn.reshape(requests, cap, inner), 'dp', 0, 0, tiled=True)]
    all_to_all x1, waiting for transfers between devices: 15.6 us -> 6.74 us  [body(): lax.all_to_all(jnp.broadcast_to(tokens_t, (chips, width, rows)), 'mp', 0,...]
    pallas_call x0 -> x4, Pallas kernels: none -> 8.01 us  [the longest x1 3.67 us: body(): call(functools.partial(attend_kernel, text_len), jax.ShapeDtypeStruct((sl...]
    all_to_all x2 -> x1, starting transfers between devices: 13.3 us -> 7.56 us  [body(): lax.all_to_all(attn.reshape(requests, cap, inner), 'dp', 0, 0, tiled=True)]
    dot_general x9 -> x3, matrix products: 12.4 us -> 6.78 us  [the longest x1 2.55 us: body(): jnp.einsum('td,rt->dr', mod_table[:, 1], pick, preferred_element_type=F32)]
    convert_element_type x3 -> x0, local copies, waits for them, and re-layouts: 5.05 us -> none  [the longest x2 4.89 us: body(): jnp.stack([first, second], axis=1).reshape(depth, rows).astype(jnp.float32)]
    transpose x0 -> x2, local copies, waits for them, and re-layouts: none -> 4.22 us  [the longest x1 2.75 us: body(): w_t = w_qkv.transpose(1, 2, 0).reshape(3 * inner, depth)]
  transfers between devices with their start and end apart: 5 -> 4, of which waited for: 4 -> 4; matrix products, arithmetic and copies ran while one was open for 6% -> 12% of each run, Pallas kernels for 0% -> 0%
where the time goes in v2:
time: 115 us
  blocking collectives  43.9 us (38%)
  starting transfers between devices  25.2 us (22%)
  waiting for transfers between devices  18.7 us (16%)
  local copies, waits for them, and re-layouts  10.7 us (9%)
  Pallas kernels  8.01 us (7%)
  matrix products  7 us (6%)
    all_to_all x1, blocking collectives, body(): lax.all_to_all(paired, 'mp', 0, 0, axis_index_groups=along_z, tiled=True)  22.6 us
    all_to_all x1, blocking collectives, body(): lax.all_to_all(send.reshape(requests, cap, 3 * inner), 'dp', 0, 0, tiled=...  21.3 us
    all_to_all x1, starting transfers between devices, body(): lax.all_to_all(jnp.broadcast_to(tokens_t, (chips, width, rows)), 'mp', 0,...  10.9 us
    all_to_all x1, waiting for transfers between devices, body(): lax.all_to_all(attn.reshape(requests, cap, inner), 'dp', 0, 0, tiled=True)  9.03 us
    all_to_all x1, starting transfers between devices, body(): lax.all_to_all(attn.reshape(requests, cap, inner), 'dp', 0, 0, tiled=True)  7.56 us
    all_to_all x1, waiting for transfers between devices, body(): lax.all_to_all(jnp.broadcast_to(tokens_t, (chips, width, rows)), 'mp', 0,...  6.74 us
    ppermute x1, starting transfers between devices, body(): given = lax.ppermute(give, 'mp', sibling)  4.37 us
    pallas_call x1, Pallas kernels, body(): call(functools.partial(attend_kernel, text_len), jax.ShapeDtypeStruct((sl...  3.67 us
  transfers between devices with their start and end apart: 4, of which 4 were waited for; matrix products, arithmetic and copies ran while one was open for 12% of the time, Pallas kernels for 0%

profile of v2, /device:TPU:1, one launch (start us, length us, event | category | flops | bytes accessed | tf_op | source)
XLA Modules:
  0.0 114.7 jit_solution(3837718455693078771)
XLA Ops:
  0.0 1.8 %broadcast_in_dim.2 = bf16[8,152,256]{2,1,0:T(8,128)(2,1)} broadcast(bf16[152,256]{1,0:T(8,128)(2,1)} %bitcast.52), dimensions={1,2} | broadcast | bytes 700416 | tf_op jit(solution)/shard_map/broadcast_in_dim | solution.py:142
  1.8 10.9 %all-to-all-start = ((bf16[8,152,256]{2,1,0:T(8,128)(2,1)}), bf16[8,152,256]{2,1,0:T(8,128)(2,1)S(1)}, u32[]{:S(2)}, u32[]{:S(2)}) async-start(bf16[8,152,256]{2,1,0:T(8,128)(2,1)} %broadcast_in_dim.2), calls=%async_computation | async-start | bytes 1245184 | tf_op jit(solution)/shard_map/all_to_all | solution.py:141
  12.6 1.6 %slice.17 = bf16[28,1,2432]{2,0,1:T(8,128)(2,1)} slice(bf16[28,3,2432]{2,0,1:T(8,128)(2,1)} %param.11), slice={[0:28], [2:3], [0:2432]} | slice | bytes 272384 | tf_op jit(solution)/shard_map/slice | solution.py:156
  14.2 0.1 tile.23
  14.3 0.1 tile.26
  14.4 2.8 %copy.23 = bf16[3,128,2432]{2,1,0:T(8,128)(2,1)S(1)} copy(bf16[3,128,2432]{1,2,0:T(8,128)(2,1)} %bitcast.49) | data formatting | bytes 3735552 | tf_op jit(solution)/shard_map/transpose | solution.py:158
  17.2 1.5 %copy.24 = bf16[2432,128]{1,0:T(8,128)(2,1)S(1)} copy(bf16[2432,128]{0,1:T(8,128)(2,1)} %bitcast.51) | data formatting | bytes 1245184 | tf_op jit(solution)/shard_map/transpose | solution.py:159
  18.7 0.2 fusion.8
  19.0 0.2 convert_reduce_fusion.1
  19.2 1.7 %fusion.7 = f32[152,256]{1,0:T(8,128)} fusion(f32[256]{0:T(256)S(1)} %bitcast.53, bf16[28,1,2432]{2,0,1:T(8,128)(2,1)} %slice.17, s32[]{:T(128)S(6)} %select_n.3), kind=kOutput, calls=%fused_computation.16 | convolution fusion | flops 2186240 | bytes 173060 | tf_op jit(solution)/shard_map/td,rt->dr/dot_general | solution.py:157
  20.9 2.5 %fusion.shift_ref = bf16[2432,256]{1,0:T(8,128)(2,1)} fusion(bf16[28,3,2432]{2,0,1:T(8,128)(2,1)} %param.11, f32[256]{0:T(256)S(1)} %bitcast.54), kind=kOutput, calls=%fused_computation.2 | convolution fusion | flops 35494912 | bytes 1401856 | tf_op jit(solution)/shard_map/td,rt->dr/dot_general | solution.py:154
  23.4 2.6 %fusion.1.scale_ref = bf16[2432,256]{1,0:T(8,128)(2,1)} fusion(bf16[28,3,2432]{2,0,1:T(8,128)(2,1)} %param.11, f32[256]{0:T(256)S(1)} %bitcast.55), kind=kOutput, calls=%fused_computation.3 | convolution fusion | flops 35494912 | bytes 1401856 | tf_op jit(solution)/shard_map/td,rt->dr/dot_general | solution.py:155
  26.0 6.7 %all-to-all-done.own_ref = bf16[8,152,256]{2,1,0:T(8,128)(2,1)S(1)} async-done(((bf16[8,152,256]{2,1,0:T(8,128)(2,1)}), bf16[8,152,256]{2,1,0:T(8,128)(2,1)S(1)}, u32[]{:S(2)}, u32[]{:S(2)}) %all-to-all-start) | async-done | bytes 622624 | tf_op jit(solution)/shard_map/all_to_all | solution.py:141
  32.7 2.4 %collective-permute-start = (bf16[8,152,256]{2,1,0:T(8,128)(2,1)S(1)}, bf16[8,152,256]{2,1,0:T(8,128)(2,1)}, u32[]{:S(2)}, u32[]{:S(2)}) collective-permute-start(bf16[8,152,256]{2,1,0:T(8,128)(2,1)S(1)} %all-to-all-done.own_ref), channel_id=1, source_target_pairs={{0,1},{1,0},{2,3},{3,2},{4,5},{5,4},{6,7},{7,6},{8,9},{9,8},{10,11... | collective-permute-start | bytes 1867784 | tf_op jit(solution)/shard_map/ppermute | solution.py:167
  35.1 0.1 copy.26.gain_ref
  35.2 1.6 %collective-permute-done.other_ref = bf16[8,152,256]{2,1,0:T(8,128)(2,1)} collective-permute-done((bf16[8,152,256]{2,1,0:T(8,128)(2,1)S(1)}, bf16[8,152,256]{2,1,0:T(8,128)(2,1)}, u32[]{:S(2)}, u32[]{:S(2)}) %collective-permute-start) | collective-permute-done | bytes 622624 | tf_op jit(solution)/shard_map/ppermute | solution.py:167
  36.9 1.3 %copy-done = bf16[2432,256]{1,0:T(8,128)(2,1)S(1)} copy-done((bf16[2432,256]{1,0:T(8,128)(2,1)S(1)}, bf16[2432,256]{1,0:T(8,128)(2,1)}, u32[]{:S(2)}) %copy-start) | copy-done | bytes 1245208
  38.2 1.3 %copy-done.1 = bf16[2432,256]{1,0:T(8,128)(2,1)S(1)} copy-done((bf16[2432,256]{1,0:T(8,128)(2,1)S(1)}, bf16[2432,256]{1,0:T(8,128)(2,1)}, u32[]{:S(2)}) %copy-start.1) | copy-done | bytes 1245208
  39.5 3.4 %shard_map.82 = bf16[512,384]{1,0:T(8,128)(2,1)S(1)} custom-call(s32[1]{0:T(128)} %bitcast.17.core_ref, bf16[8,152,256]{2,1,0:T(8,128)(2,1)S(1)} %all-to-all-done.own_ref, bf16[8,152,256]{2,1,0:T(8,128)(2,1)} %collective-permute-done.other_ref, bf16[2432,256]{1,0:T(8,128)(2,1)S(1)} %copy-done.1, bf16[2432,256]{1,0:T(8,128)(2,1)S(1)} %copy-done, ...), custom_call_target="tpu_custom_call" | custom-call | flops 478150656 | bytes 1048576 | tf_op jit(solution)/shard_map/pallas_call | solution.py:169
  42.9 21.3 %all_to_all.20 = bf16[32,16,384]{2,1,0:T(8,128)(2,1)S(1)} all-to-all(bf16[32,16,384]{2,1,0:T(8,128)(2,1)S(1)} %bitcast.44), channel_id=1, replica_groups=mesh['dp'=32,'mp'=16] {'dp'}, dimensions={0} | all-to-all | bytes 786432 | tf_op jit(solution)/shard_map/all_to_all | solution.py:177
  64.2 3.7 %shard_map.83 = bf16[512,128]{1,0:T(8,128)(2,1)} custom-call(bf16[512,384]{1,0:T(8,128)(2,1)S(1)} %bitcast.46, bf16[2,384,128]{2,1,0:T(8,128)(2,1)S(1)} %pad.4.ctx_ref), custom_call_target="tpu_custom_call" | custom-call | flops 469762048 | bytes 1048576 | tf_op jit(solution)/shard_map/pallas_call | solution.py:179
  67.8 7.6 %all-to-all-start.2 = ((bf16[32,16,128]{2,1,0:T(8,128)(2,1)}), bf16[32,16,128]{2,1,0:T(8,128)(2,1)S(1)}, u32[]{:S(2)}, u32[]{:S(2)}) async-start(bf16[32,16,128]{2,1,0:T(8,128)(2,1)} %bitcast.21), calls=%async_computation.2 | async-start | bytes 262144 | tf_op jit(solution)/shard_map/all_to_all | solution.py:186
  75.4 0.1 copy.27.pos_ref
  75.5 9.0 %all-to-all-done.2 = bf16[32,16,128]{2,1,0:T(8,128)(2,1)S(1)} async-done(((bf16[32,16,128]{2,1,0:T(8,128)(2,1)}), bf16[32,16,128]{2,1,0:T(8,128)(2,1)S(1)}, u32[]{:S(2)}, u32[]{:S(2)}) %all-to-all-start.2) | async-done | bytes 131104 | tf_op jit(solution)/shard_map/all_to_all | solution.py:186
  84.6 0.6 shard_map.84
  85.2 4.4 %collective-permute-start.1 = (bf16[8,152,256]{2,1,0:T(8,128)(2,1)S(1)}, bf16[8,152,256]{2,1,0:T(8,128)(2,1)S(1)}, u32[]{:S(2)}, u32[]{:S(2)}) collective-permute-start(bf16[8,152,256]{2,1,0:T(8,128)(2,1)S(1)} %get-tuple-element.26), channel_id=1, source_target_pairs={{0,1},{1,0},{2,3},{3,2},{4,5},{5,4},{6,7},{7,6},{8,9},{9,8},{10,11... | collective-permute-start | bytes 1867784 | tf_op jit(solution)/shard_map/ppermute | solution.py:195
  89.5 0.3 shard_map.85
  89.9 1.3 %collective-permute-done.1 = bf16[8,152,256]{2,1,0:T(8,128)(2,1)S(1)} collective-permute-done((bf16[8,152,256]{2,1,0:T(8,128)(2,1)S(1)}, bf16[8,152,256]{2,1,0:T(8,128)(2,1)S(1)}, u32[]{:S(2)}, u32[]{:S(2)}) %collective-permute-start.1) | collective-permute-done | bytes 622624 | tf_op jit(solution)/shard_map/ppermute | solution.py:195
  91.2 0.1 add_convert_fusion
  91.4 22.6 %all_to_all.21 = bf16[8,152,256]{2,1,0:T(8,128)(2,1)S(1)} all-to-all(bf16[8,152,256]{2,1,0:T(8,128)(2,1)S(1)} %add_convert_fusion), channel_id=1, replica_groups={{0,2,4,6,8,10,12,14},{1,3,5,7,9,11,13,15},{16,18,20,22,24,26,28,30},{17..., dimensions={0} | all-to-all | bytes 1245184 | tf_op jit(solution)/shard_map/all_to_all | solution.py:200
  113.9 0.1 convert_reduce_fusion
  114.0 0.7 fusion.9
  (21 shorter events, 0.1 us)
Async XLA Ops:
  0.0 14.2 %copy-start.6 = (f32[2,64]{1,0:T(2,128)S(1)}, f32[2,64]{1,0:T(2,128)}, u32[]{:S(2)}) copy-start(f32[2,64]{1,0:T(2,128)} %param.13) | copy-start | bytes 1540
  1.8 30.9 %all-to-all-start = ((bf16[8,152,256]{2,1,0:T(8,128)(2,1)}), bf16[8,152,256]{2,1,0:T(8,128)(2,1)S(1)}, u32[]{:S(2)}, u32[]{:S(2)}) async-start(bf16[8,152,256]{2,1,0:T(8,128)(2,1)} %broadcast_in_dim.2), calls=%async_computation | async-start | bytes 1245184 | tf_op jit(solution)/shard_map/all_to_all | solution.py:141
  17.2 1.5 %copy-start.4 = (bf16[1,2,333,128]{3,1,2,0:T(2,128)(2,1)S(1)}, bf16[1,2,333,128]{3,1,2,0:T(2,128)(2,1)}, u32[]{:S(2)}) copy-start(bf16[1,2,333,128]{3,1,2,0:T(2,128)(2,1)} %param.14) | copy-start | bytes 511492
  17.2 1.5 %copy-start.5 = (s32[256,1]{0,1:T(1,128)S(1)}, s32[256,1]{0,1:T(1,128)}, u32[]{:S(2)}) copy-start(s32[256,1]{0,1:T(1,128)} %param.9) | copy-start | bytes 3076
  17.2 1.5 %copy-start.7 = (s32[32]{0:T(128)S(1)}, s32[32]{0:T(128)}, u32[]{:S(2)}) copy-start(s32[32]{0:T(128)} %param.10) | copy-start | bytes 388
  32.7 4.2 %collective-permute-start = (bf16[8,152,256]{2,1,0:T(8,128)(2,1)S(1)}, bf16[8,152,256]{2,1,0:T(8,128)(2,1)}, u32[]{:S(2)}, u32[]{:S(2)}) collective-permute-start(bf16[8,152,256]{2,1,0:T(8,128)(2,1)S(1)} %all-to-all-done.own_ref), channel_id=1, source_target_pairs={{0,1},{1,0},{2,3},{3,2},{4,5},{5,4},{6,7},{7,6},{8,9},{9,8},{10,11... | collective-permute-start | bytes 1867784 | tf_op jit(solution)/shard_map/ppermute | solution.py:167
  36.9 1.3 %copy-start = (bf16[2432,256]{1,0:T(8,128)(2,1)S(1)}, bf16[2432,256]{1,0:T(8,128)(2,1)}, u32[]{:S(2)}) copy-start(bf16[2432,256]{1,0:T(8,128)(2,1)} %fusion.shift_ref) | copy-start | bytes 3735556
  38.2 1.3 %copy-start.1 = (bf16[2432,256]{1,0:T(8,128)(2,1)S(1)}, bf16[2432,256]{1,0:T(8,128)(2,1)}, u32[]{:S(2)}) copy-start(bf16[2432,256]{1,0:T(8,128)(2,1)} %fusion.1.scale_ref) | copy-start | bytes 3735556
  67.8 16.7 %all-to-all-start.2 = ((bf16[32,16,128]{2,1,0:T(8,128)(2,1)}), bf16[32,16,128]{2,1,0:T(8,128)(2,1)S(1)}, u32[]{:S(2)}, u32[]{:S(2)}) async-start(bf16[32,16,128]{2,1,0:T(8,128)(2,1)} %bitcast.21), calls=%async_computation.2 | async-start | bytes 262144 | tf_op jit(solution)/shard_map/all_to_all | solution.py:186
  85.2 6.0 %collective-permute-start.1 = (bf16[8,152,256]{2,1,0:T(8,128)(2,1)S(1)}, bf16[8,152,256]{2,1,0:T(8,128)(2,1)S(1)}, u32[]{:S(2)}, u32[]{:S(2)}) collective-permute-start(bf16[8,152,256]{2,1,0:T(8,128)(2,1)S(1)} %get-tuple-element.26), channel_id=1, source_target_pairs={{0,1},{1,0},{2,3},{3,2},{4,5},{5,4},{6,7},{7,6},{8,9},{9,8},{10,11... | collective-permute-start | bytes 1867784 | tf_op jit(solution)/shard_map/ppermute | solution.py:195
  91.3 22.7 %copy-start.2 = (f32[152,256]{1,0:T(8,128)S(1)}, f32[152,256]{1,0:T(8,128)}, u32[]{:S(2)}) copy-start(f32[152,256]{1,0:T(8,128)} %fusion.7) | copy-start | bytes 466948
  91.3 22.7 %copy-start.3 = (bf16[256,152]{0,1:T(8,128)(2,1)S(1)}, bf16[256,152]{0,1:T(8,128)(2,1)}, u32[]{:S(2)}) copy-start(bf16[256,152]{0,1:T(8,128)(2,1)} %param.8) | copy-start | bytes 233476

commit v3 on v2

v3 whole, which is shorter than its diff:
```python
import functools

import jax
import jax.numpy as jnp
from jax import lax
from jax.experimental import pallas as pl
from jax.experimental.pallas import tpu as pltpu
from jax.sharding import PartitionSpec as P

HD = 64
EPS = 1e-06
DEAD = 1e30
MASKED = -1e30
VMEM_LIMIT = 24 * 1024 * 1024
F32, BF16, I32 = jnp.float32, jnp.bfloat16, jnp.int32


def dot_nt(a, b):
    return lax.dot_general(a, b, (((1,), (1,)), ((), ())), preferred_element_type=F32)


def dot_tn(a, b):
    return lax.dot_general(a, b, (((0,), (0,)), ((), ())), preferred_element_type=F32)


def iota(shape, axis):
    return lax.broadcasted_iota(I32, shape, axis)


def as_column(row):
    n = row.shape[1]
    return jnp.sum(jnp.where(iota((n, n), 0) == iota((n, n), 1), row, 0.0), axis=1, keepdims=True)


def one_hot(flags):
    return jnp.where(flags, 1.0, 0.0).astype(BF16)


def dealt(rows):
    half = rows // 2
    place = iota((rows, rows), 0)
    return jnp.where(place < half, 2 * place, 2 * (place - half) + 1).astype(F32)


def spread_kernel(tok_ref, req_ref, out_ref, perm_ref, pos_ref):
    width, rows = tok_ref.shape
    half = rows // 2
    req = req_ref[...].astype(F32)
    req_col = as_column(req)
    earlier = (req_col < req) | ((req_col == req) & (iota((rows, rows), 0) < iota((rows, rows), 1)))
    pos = jnp.sum(jnp.where(earlier, 1.0, 0.0), axis=0, keepdims=True)
    pos_ref[...] = pos
    perm = dot_nt(tok_ref[...], one_hot(pos == dealt(rows))).astype(BF16)
    perm_ref[...] = perm
    for m in range(out_ref.shape[0]):
        out_ref[m] = perm[:, (m % 2) * half : (m % 2 + 1) * half]


def prepare_kernel(
    cap, core_ref, req_ref, pos_ref, steps_ref, table_ref, gate_ref,
    scale_ref, shift_ref, gates_ref, place_ref, place_t_ref, mark_ref,
):
    rows = req_ref.shape[1]
    half = rows // 2
    slots = place_ref.shape[0]
    requests = steps_ref.shape[1]
    levels = table_ref.shape[1]
    is_first = core_ref[0] == 0
    req = req_ref[...].astype(F32)
    first = jnp.sum(jnp.where(as_column(req) < req, 1.0, 0.0), axis=0, keepdims=True)
    deal = one_hot(pos_ref[...] == dealt(rows))
    line = iota((8, rows), 0)
    both = jnp.where(line == 0, req, jnp.where(line == 1, first, 0.0)).astype(BF16)
    both = dot_nt(both, deal)
    req_s, first_s = both[0:1], both[1:2]
    index = iota((1, rows), 1)
    odd = jnp.where(index >= half, 1, 0)
    start = jnp.floor((first_s - odd.astype(F32) + 1.0) * 0.5)
    slot = req_s * cap + (index - half * odd).astype(F32) - start
    chosen = one_hot(iota((requests, rows), 0).astype(F32) == req_s)
    steps = jnp.broadcast_to(steps_ref[...].astype(F32), (8, requests)).astype(BF16)
    step = jnp.dot(steps, chosen, preferred_element_type=F32)[0:1]
    pick = one_hot(iota((levels, rows), 0).astype(F32) == step)
    gates_ref[...] = dot_tn(gate_ref[...], pick)
    pick = jnp.where(is_first, pick[:, :half].astype(F32), pick[:, half:].astype(F32)).astype(BF16)
    shift_ref[...] = dot_tn(table_ref[0], pick).astype(BF16)
    scale_ref[...] = dot_tn(table_ref[1], pick).astype(BF16)
    slot = jnp.where(is_first, slot[:, :half], slot[:, half:])
    hits = iota((slots, half), 0).astype(F32) == slot
    place_ref[...] = one_hot(hits)
    filled = jnp.sum(jnp.where(hits, 1.0, 0.0), axis=1, keepdims=True)
    mark_ref[...] = jnp.broadcast_to(jnp.where(filled > 0.5, 0.0, DEAD), mark_ref.shape)
    place_t_ref[...] = one_hot(iota((half, slots), 1).astype(F32) == as_column(slot))


def project_kernel(
    core_ref, tok_ref, scale_ref, shift_ref, own_ref, sib_ref, gain_ref, place_ref, mark_ref, send_ref, hid_ref
):
    parts, width, rows = tok_ref.shape
    depth = parts * width
    inner = own_ref.shape[0] // 3
    total = sum(jnp.sum(tok_ref[m].astype(F32), axis=0, keepdims=True) for m in range(parts))
    mean = total * (1.0 / depth)
    square = sum(jnp.sum(jnp.square(tok_ref[m].astype(F32) - mean), axis=0, keepdims=True) for m in range(parts))
    inverse = lax.rsqrt(square * (1.0 / depth) + EPS)
    for m in range(0, parts, 2):
        pair = jnp.concatenate([tok_ref[m].astype(F32), tok_ref[m + 1].astype(F32)], axis=0)
        span = pl.ds(m * width, 2 * width)
        scale, shift = scale_ref[span, :].astype(F32), shift_ref[span, :].astype(F32)
        hid_ref[span, :] = ((pair - mean) * inverse * (1.0 + scale) + shift).astype(BF16)
    hidden = hid_ref[...]
    for w_ref, target in ((own_ref, core_ref[0]), (sib_ref, 1 - core_ref[0])):
        proj = jnp.dot(w_ref[...], hidden, preferred_element_type=F32)
        pieces = []
        for start in range(0, 2 * inner, HD):
            head = proj[start : start + HD]
            power = jnp.mean(jnp.square(head), axis=0, keepdims=True)
            pieces.append(head * lax.rsqrt(power + EPS) * gain_ref[pl.ds(start, HD), :])
        pieces.append(proj[2 * inner :])
        send = dot_nt(place_ref[...], jnp.concatenate(pieces, axis=0).astype(BF16))
        mark = mark_ref[...]
        send = jnp.concatenate([send[:, :inner], send[:, inner : 2 * inner] + mark, send[:, 2 * inner :]], axis=1)
        send_ref[target] = send.astype(BF16)


def attend_kernel(text_len, slots_ref, ctx_ref, out_ref):
    slots, inner = out_ref.shape
    block = 128
    text_pad = ctx_ref.shape[1]
    queries = slots_ref[:, 0:inner]
    keys = slots_ref[:, inner : 2 * inner].astype(F32)
    values = slots_ref[:, 2 * inner :]
    text_keys, text_values = ctx_ref[0], ctx_ref[1]
    dead = keys > 0.5 * DEAD
    marks = jnp.where(dead, 1.0, 0.0).astype(BF16)
    keys = jnp.where(dead, 0.0, keys).astype(BF16)
    own_bias = dot_nt(jnp.full((8, inner), MASKED, BF16), marks)[0:1]
    text_bias = jnp.where(iota((1, text_pad), 1) < text_len, 0.0, MASKED)
    lane = iota((1, inner), 1)
    one = jnp.ones((), BF16)
    zero = jnp.zeros((), BF16)
    for row in range(0, slots, block):
        parts = []
        for head in range(inner // HD):
            mine = (lane >= head * HD) & (lane < (head + 1) * HD)
            query = jnp.where(mine, queries[row : row + block], zero)
            own = dot_nt(query, keys) + own_bias
            far = dot_nt(query, text_keys) + text_bias
            top = jnp.maximum(jnp.max(own, axis=1, keepdims=True), jnp.max(far, axis=1, keepdims=True))
            own = jnp.exp(own - top).astype(BF16)
            far = jnp.exp(far - top).astype(BF16)
            mixed = jnp.dot(own, jnp.where(mine, values, one), preferred_element_type=F32)
            mixed = mixed + jnp.dot(far, jnp.where(mine, text_values, one), preferred_element_type=F32)
            parts.append((mine, mixed / pltpu.roll(mixed, HD, 1)))
        out_ref[row : row + block, :] = jnp.where(parts[0][0], parts[0][1], parts[1][1]).astype(BF16)


def output_kernel(core_ref, back_ref, place_t_ref, w_ref, part_ref):
    core = core_ref[0]
    place_t = place_t_ref[...]
    own = jnp.dot(place_t, back_ref[core], preferred_element_type=F32).astype(BF16)
    sib = jnp.dot(place_t, back_ref[1 - core], preferred_element_type=F32).astype(BF16)
    attn = jnp.concatenate([own, sib], axis=1)
    for m in range(part_ref.shape[0]):
        part_ref[m] = dot_nt(w_ref[m], attn).astype(BF16)


def finish_kernel(sums_ref, perm_ref, gates_ref, pos_ref, out_ref):
    parts = sums_ref.shape[0]
    halves = [sum(sums_ref[m].astype(F32) for m in range(c, parts, 2)) for c in range(2)]
    total = jnp.concatenate(halves, axis=1)
    mixed = (perm_ref[...].astype(F32) + gates_ref[...] * total).astype(BF16)
    rows = perm_ref.shape[1]
    deal = one_hot(pos_ref[...] == dealt(rows))
    out_ref[...] = jnp.dot(mixed, deal, preferred_element_type=F32).astype(BF16)


def call(kernel, out_shape, smem, vmem, scratch=(), flops=0):
    whole = pl.BlockSpec(memory_space=pltpu.VMEM)
    outs = jax.tree.map(lambda _: whole, out_shape)
    return pl.pallas_call(
        kernel,
        out_shape=out_shape,
        in_specs=[pl.BlockSpec(memory_space=pltpu.SMEM)] * smem + [whole] * vmem,
        out_specs=outs,
        scratch_shapes=list(scratch),
        compiler_params=pltpu.CompilerParams(vmem_limit_bytes=VMEM_LIMIT),
        cost_estimate=pl.CostEstimate(flops=flops, bytes_accessed=1 << 20, transcendentals=0),
    )


def body(tokens, route, tsteps, mod_table, w_qkv, qk_gain, context, w_out):
    rows, width = tokens.shape
    half = rows // 2
    requests = lax.axis_size("dp")
    parts = lax.axis_size("mp")
    chips = parts // 2
    cap = max(2, 2 * rows // requests) // 2
    slots = requests * cap
    depth = w_qkv.shape[0]
    inner = w_qkv.shape[2]
    text_len = context.shape[2]
    text_pad = -(-text_len // 128) * 128
    sibling = [(i, i ^ 1) for i in range(parts)]
    planes = [[dp * parts + 2 * z + c for c in range(2) for dp in range(requests)] for z in range(chips)]
    core = lax.rem(lax.axis_index("mp"), 2).astype(I32).reshape(1)
    shape = jax.ShapeDtypeStruct

    req = route.reshape(1, rows)
    spread, perm, pos = call(
        spread_kernel,
        (shape((parts, width, half), BF16), shape((width, rows), BF16), shape((1, rows), F32)),
        0,
        2,
    )(tokens.T, req)
    whole = lax.all_to_all(spread, "mp", 0, 0, tiled=True)

    w_own = w_qkv.transpose(1, 2, 0).reshape(3 * inner, depth)
    w_sib = lax.ppermute(w_own, "mp", sibling)
    out_own = w_out.T
    out_sib = lax.ppermute(out_own, "mp", sibling)
    w_back = jnp.concatenate([out_own, out_sib], axis=1).reshape(parts, width, 2 * inner)
    gate_table = lax.dynamic_slice_in_dim(mod_table[:, 2, :], lax.axis_index("mp") * width, width, 1)
    scale, shift, gates, place, place_t, mark = call(
        functools.partial(prepare_kernel, cap),
        (
            shape((depth, half), BF16),
            shape((depth, half), BF16),
            shape((width, rows), F32),
            shape((slots, half), BF16),
            shape((half, slots), BF16),
            shape((slots, inner), F32),
        ),
        1,
        5,
    )(core, req, pos, tsteps.reshape(1, requests), mod_table.transpose(1, 0, 2), gate_table)
    gains = jnp.concatenate(
        [jnp.tile(qk_gain[0] * HD ** (-0.5), inner // HD), jnp.tile(qk_gain[1], inner // HD)]
    ).reshape(2 * inner, 1)
    text = jnp.pad(context[0], ((0, 0), (0, text_pad - text_len), (0, 0)))
    whole, w_own, w_sib, w_back, scale, shift, gates, place, place_t, mark, gains, text = lax.optimization_barrier(
        (whole, w_own, w_sib, w_back, scale, shift, gates, place, place_t, mark, gains, text)
    )

    send = call(
        project_kernel,
        shape((2, slots, 3 * inner), BF16),
        1,
        8,
        [pltpu.VMEM((depth, half), BF16)],
        flops=4 * depth * half * 3 * inner,
    )(core, whole, scale, shift, w_own, w_sib, gains, place, mark)
    arrived = lax.all_to_all(
        send.reshape(2 * requests, cap, 3 * inner), ("dp", "mp"), 0, 0, axis_index_groups=planes, tiled=True
    )
    attn = call(
        functools.partial(attend_kernel, text_len),
        shape((2 * slots, inner), BF16),
        0,
        2,
        flops=16 * slots * (2 * slots + text_pad) * inner,
    )(arrived.reshape(2 * slots, 3 * inner), text)
    returned = lax.all_to_all(
        attn.reshape(2 * requests, cap, inner), ("dp", "mp"), 0, 0, axis_index_groups=planes, tiled=True
    )
    partial = call(output_kernel, shape((parts, width, half), BF16), 1, 3, flops=4 * depth * half * inner)(
        core, returned.reshape(2, slots, inner), place_t, w_back
    )
    sums = lax.all_to_all(partial, "mp", 0, 0, tiled=True)
    return call(finish_kernel, shape((width, rows), BF16), 0, 4)(sums, perm, gates, pos).T


def solution(mesh):
    return jax.shard_map(
        body,
        mesh=mesh,
        in_specs=(
            P("dp", "mp"),
            P("dp", None),
            P(),
            P(),
            P(None, None, "mp"),
            P(),
            P("dp", None, None, "mp"),
            P("mp", None),
        ),
        out_specs=P("dp", "mp"),
        check_vma=False,
    )
```

time: 115 us -> 117 us (1.017)
  blocking collectives: 43.9 us -> 65.5 us
  waiting for transfers between devices: 18.7 us -> 7.7 us
  starting transfers between devices: 25.2 us -> 16 us
  matrix products: 7 us -> 0 us
  Pallas kernels: 8.01 us -> 11.2 us
  local copies, waits for them, and re-layouts: 10.7 us -> 13.2 us
  other arithmetic: 1.08 us -> 2.41 us
    all_to_all x2 -> x3, blocking collectives: 43.9 us -> 65.5 us  [the longest x1 26.3 us: body(): lax.all_to_all(send.reshape(2 * requests, cap, 3 * inner), ('dp', 'mp'),...]
    all_to_all x2 -> x1, starting transfers between devices: 18.4 us -> 5.11 us  [body(): whole = lax.all_to_all(spread, 'mp', 0, 0, tiled=True)]
    all_to_all x2 -> x1, waiting for transfers between devices: 15.8 us -> 7.69 us  [body(): whole = lax.all_to_all(spread, 'mp', 0, 0, tiled=True)]
    dot_general x4 -> x0, matrix products: 7 us -> none  [the longest x1 2.55 us: body(): jnp.einsum('td,rt->dr', mod_table[:, 1], pick, preferred_element_type=F32)]
    unnamed x17 -> x37, local copies, waits for them, and re-layouts: 2.64 us -> 8.22 us
    ppermute x2, starting transfers between devices: 6.77 us -> 10.9 us  [the longest x1 8.88 us: body(): w_sib = lax.ppermute(w_own, 'mp', sibling)]
    pallas_call x4 -> x6, Pallas kernels: 8.01 us -> 11.2 us  [the longest x1 4.52 us: body(): call(project_kernel, shape((2, slots, 3 * inner), BF16), 1, 8, [pltpu.VME...]
    ppermute x2, waiting for transfers between devices: 2.96 us -> 0.01 us  [the longest x1 0.01 us: body(): out_sib = lax.ppermute(out_own, 'mp', sibling)]
  transfers between devices with their start and end apart: 4 -> 3, of which waited for: 4 -> 1; matrix products, arithmetic and copies ran while one was open for 12% -> 4% of each run, Pallas kernels for 0% -> 2%
where the time goes in v3:
time: 117 us; the launch traced here: 116 us
  blocking collectives  65.5 us (56%)
  starting transfers between devices  16 us (14%)
  local copies, waits for them, and re-layouts  13.2 us (11%)
  Pallas kernels  11.2 us (10%)
  waiting for transfers between devices  7.7 us (7%)
  other arithmetic  2.41 us (2%)
    all_to_all x1, blocking collectives, body(): lax.all_to_all(send.reshape(2 * requests, cap, 3 * inner), ('dp', 'mp'),...  26.3 us
    all_to_all x1, blocking collectives, body(): sums = lax.all_to_all(partial, 'mp', 0, 0, tiled=True)  23.5 us
    all_to_all x1, blocking collectives, body(): lax.all_to_all(attn.reshape(2 * requests, cap, inner), ('dp', 'mp'), 0, 0...  15.7 us
    ppermute x1, starting transfers between devices, body(): w_sib = lax.ppermute(w_own, 'mp', sibling)  8.88 us
    unnamed x37, local copies, waits for them, and re-layouts  8.22 us
    all_to_all x1, waiting for transfers between devices, body(): whole = lax.all_to_all(spread, 'mp', 0, 0, tiled=True)  7.69 us
    all_to_all x1, starting transfers between devices, body(): whole = lax.all_to_all(spread, 'mp', 0, 0, tiled=True)  5.11 us
    pallas_call x1, Pallas kernels, body(): call(project_kernel, shape((2, slots, 3 * inner), BF16), 1, 8, [pltpu.VME...  4.52 us
  transfers between devices with their start and end apart: 3, of which 1 were waited for; matrix products, arithmetic and copies ran while one was open for 4% of the time, Pallas kernels for 2%

profile of v3, /device:TPU:1, one launch (start us, length us, event | category | flops | bytes accessed | tf_op | source)
XLA Modules:
  0.0 116.2 jit_solution(14795098844741122148)
XLA Ops:
  0.0 2.8 %copy.12 = bf16[3,128,2432]{2,1,0:T(8,128)(2,1)S(1)} copy(bf16[3,128,2432]{1,2,0:T(8,128)(2,1)} %bitcast.36) | data formatting | bytes 3735552 | tf_op jit(solution)/shard_map/transpose | solution.py:218
  2.9 0.0 slice-start
  2.9 0.0 copy-start.15
  2.9 8.9 %collective-permute-start = (bf16[384,2432]{1,0:T(8,128)(2,1)S(1)}, bf16[384,2432]{1,0:T(8,128)(2,1)}, u32[]{:S(2)}, u32[]{:S(2)}) collective-permute-start(bf16[384,2432]{1,0:T(8,128)(2,1)S(1)} %bitcast.24), channel_id=1, source_target_pairs={{0,1},{1,0},{2,3},{3,2},{4,5},{5,4},{6,7},{7,6},{8,9},{9,8},{10,11... | collective-permute-start | bytes 5603336 | tf_op jit(solution)/shard_map/ppermute | solution.py:219
  11.8 1.2 %shard_map.82 = (bf16[16,152,128]{2,1,0:T(8,128)(2,1)}, bf16[152,256]{1,0:T(8,128)(2,1)S(1)}, f32[1,256]{1,0:T(1,128)S(1)}) custom-call(bf16[152,256]{1,0:T(8,128)(2,1)S(1)} %bitcast.32, s32[1,256]{1,0:T(1,128)S(1)} %bitcast.33), custom_call_target="tpu_custom_call" | custom-call | bytes 1048576 | tf_op jit(solution)/shard_map/pallas_call | solution.py:210
  13.0 5.1 %all-to-all-start = ((bf16[16,152,128]{2,1,0:T(8,128)(2,1)}), bf16[16,152,128]{2,1,0:T(8,128)(2,1)}, u32[]{:S(2)}, u32[]{:S(2)}) async-start(bf16[16,152,128]{2,1,0:T(8,128)(2,1)} %get-tuple-element.26), calls=%async_computation | async-start | bytes 1245184 | tf_op jit(solution)/shard_map/all_to_all | solution.py:216
  18.1 2.1 %collective-permute-start.1 = (bf16[2432,128]{0,1:T(8,128)(2,1)}, bf16[2432,128]{0,1:T(8,128)(2,1)}, u32[]{:S(2)}, u32[]{:S(2)}) collective-permute-start(bf16[2432,128]{0,1:T(8,128)(2,1)} %bitcast.5), channel_id=1, source_target_pairs={{0,1},{1,0},{2,3},{3,2},{4,5},{5,4},{6,7},{7,6},{8,9},{9,8},{10,11... | collective-permute-start | bytes 1867784 | tf_op jit(solution)/shard_map/ppermute | solution.py:221
  20.2 0.1 tile.23
  20.3 0.1 tile.26
  20.5 0.1 dynamic-slice_bitcast_fusion.gate_ref
  20.6 0.9 shard_map.83
  21.5 0.8 copy-done.1
  22.3 0.9 copy-done.3
  23.2 0.7 copy-done.5
  23.8 0.7 copy-done.7
  24.5 0.6 copy-done.10
  25.1 0.6 copy-done.12
  25.8 2.4 %pad_maximum_fusion = bf16[2432,256]{0,1:T(8,128)(2,1)} fusion(bf16[2432,128]{0,1:T(8,128)(2,1)} %collective-permute-done.1, bf16[2432,128]{0,1:T(8,128)(2,1)} %bitcast.5), kind=kLoop, calls=%fused_computation | loop fusion | flops 2490368 | bytes 2490368 | tf_op jit(solution)/shard_map/concatenate | solution.py:222
  28.2 1.7 %copy.13 = bf16[2432,256]{1,0:T(8,128)(2,1)S(1)} copy(bf16[2432,256]{0,1:T(8,128)(2,1)} %pad_maximum_fusion) | data formatting | bytes 2490368 | tf_op jit(solution)/shard_map/concatenate | solution.py:222
  29.9 7.7 %all-to-all-done.tok_ref = bf16[16,152,128]{2,1,0:T(8,128)(2,1)} async-done(((bf16[16,152,128]{2,1,0:T(8,128)(2,1)}), bf16[16,152,128]{2,1,0:T(8,128)(2,1)}, u32[]{:S(2)}, u32[]{:S(2)}) %all-to-all-start) | async-done | bytes 622624 | tf_op jit(solution)/shard_map/all_to_all | solution.py:216
  37.6 0.1 copy.15.gain_ref
  37.7 1.1 copy-done.2
  38.8 1.1 copy-done.4
  39.9 0.9 copy-done.8
  40.8 0.8 copy-done.11
  41.6 4.5 %shard_map.84 = bf16[2,256,384]{2,1,0:T(8,128)(2,1)S(1)} custom-call(s32[1]{0:T(128)} %bitcast.core_ref, bf16[16,152,128]{2,1,0:T(8,128)(2,1)} %all-to-all-done.tok_ref, bf16[2432,128]{1,0:T(8,128)(2,1)S(1)} %copy-done.2, bf16[2432,128]{1,0:T(8,128)(2,1)S(1)} %copy-done.4, bf16[384,2432]{1,0:T(8,128)(2,1)S(1)} %bitcast.25, ...), custom_call_target="tpu_custom_call" | custom-call | flops 478150656 | bytes 1048576 | tf_op jit(solution)/shard_map/pallas_call | solution.py:245
  46.2 26.3 %all_to_all.20 = bf16[64,8,384]{2,1,0:T(8,128)(2,1)S(1)} all-to-all(bf16[64,8,384]{2,1,0:T(8,128)(2,1)S(1)} %bitcast.27), channel_id=1, replica_groups={{0,16,32,48,64,80,96,112,128,144,160,176,192,208,224,240,256,272,288,30..., dimensions={0} | all-to-all | bytes 786432 | tf_op jit(solution)/shard_map/all_to_all | solution.py:253
  72.5 3.0 %shard_map.85 = bf16[512,128]{1,0:T(8,128)(2,1)S(1)} custom-call(bf16[512,384]{1,0:T(8,128)(2,1)S(1)} %bitcast.30, bf16[2,384,128]{2,1,0:T(8,128)(2,1)S(1)} %pad.4.ctx_ref), custom_call_target="tpu_custom_call" | custom-call | flops 469762048 | bytes 1048576 | tf_op jit(solution)/shard_map/pallas_call | solution.py:256
  75.5 15.7 %all_to_all.21 = bf16[64,8,128]{2,1,0:T(8,128)(2,1)S(1)} all-to-all(bf16[64,8,128]{2,1,0:T(8,128)(2,1)S(1)} %bitcast.31), channel_id=1, replica_groups={{0,16,32,48,64,80,96,112,128,144,160,176,192,208,224,240,256,272,288,30..., dimensions={0} | all-to-all | bytes 262144 | tf_op jit(solution)/shard_map/all_to_all | solution.py:263
  91.2 0.6 shard_map.86
  91.8 23.5 %all_to_all.22.sums_ref = bf16[16,152,128]{2,1,0:T(8,128)(2,1)S(1)} all-to-all(bf16[16,152,128]{2,1,0:T(8,128)(2,1)S(1)} %shard_map.86), channel_id=1, replica_groups=mesh['dp'=32,'mp'=16] {'mp'}, dimensions={0} | all-to-all | bytes 1245184 | tf_op jit(solution)/shard_map/all_to_all | solution.py:269
  115.3 0.9 shard_map.87
  (34 shorter events, 0.1 us)
Async XLA Ops:
  0.0 11.8 %copy-start.9 = (bf16[256,152]{0,1:T(8,128)(2,1)S(1)}, bf16[256,152]{0,1:T(8,128)(2,1)}, u32[]{:S(2)}) copy-start(bf16[256,152]{0,1:T(8,128)(2,1)} %param.8) | copy-start | bytes 233476
  0.0 11.8 %copy-start.14 = (s32[256,1]{0,1:T(1,128)S(1)}, s32[256,1]{0,1:T(1,128)}, u32[]{:S(2)}) copy-start(s32[256,1]{0,1:T(1,128)} %param.9) | copy-start | bytes 3076
  0.0 20.2 %copy-start.17 = (f32[2,64]{1,0:T(2,128)S(1)}, f32[2,64]{1,0:T(2,128)}, u32[]{:S(2)}) copy-start(f32[2,64]{1,0:T(2,128)} %param.13) | copy-start | bytes 1540
  0.0 20.4 %copy-start.16 = (bf16[1,2,333,128]{3,1,2,0:T(2,128)(2,1)S(1)}, bf16[1,2,333,128]{3,1,2,0:T(2,128)(2,1)}, u32[]{:S(2)}) copy-start(bf16[1,2,333,128]{3,1,2,0:T(2,128)(2,1)} %param.14) | copy-start | bytes 511492
  2.9 17.6 %slice-start = ((bf16[28,3,2432]{2,0,1:T(8,128)(2,1)}), bf16[28,1,2432]{2,0,1:T(8,128)(2,1)S(1)}, s32[]{:S(2)}) async-start(bf16[28,3,2432]{2,0,1:T(8,128)(2,1)} %param.11), calls=%async_computation.4 | async-start | bytes 311296 | tf_op jit(solution)/shard_map/slice | solution.py:223
  2.9 17.7 %copy-start = (bf16[28,3,2432]{2,0,1:T(8,128)(2,1)S(1)}, bf16[28,3,2432]{2,0,1:T(8,128)(2,1)}, u32[]{:S(2)}) copy-start(bf16[28,3,2432]{2,0,1:T(8,128)(2,1)} %param.11) | copy-start | bytes 1225732
  2.9 17.7 %copy-start.15 = (s32[32]{0:T(128)S(1)}, s32[32]{0:T(128)}, u32[]{:S(2)}) copy-start(s32[32]{0:T(128)} %param.10) | copy-start | bytes 388
  2.9 34.7 %collective-permute-start = (bf16[384,2432]{1,0:T(8,128)(2,1)S(1)}, bf16[384,2432]{1,0:T(8,128)(2,1)}, u32[]{:S(2)}, u32[]{:S(2)}) collective-permute-start(bf16[384,2432]{1,0:T(8,128)(2,1)S(1)} %bitcast.24), channel_id=1, source_target_pairs={{0,1},{1,0},{2,3},{3,2},{4,5},{5,4},{6,7},{7,6},{8,9},{9,8},{10,11... | collective-permute-start | bytes 5603336 | tf_op jit(solution)/shard_map/ppermute | solution.py:219
  13.0 24.6 %all-to-all-start = ((bf16[16,152,128]{2,1,0:T(8,128)(2,1)}), bf16[16,152,128]{2,1,0:T(8,128)(2,1)}, u32[]{:S(2)}, u32[]{:S(2)}) async-start(bf16[16,152,128]{2,1,0:T(8,128)(2,1)} %get-tuple-element.26), calls=%async_computation | async-start | bytes 1245184 | tf_op jit(solution)/shard_map/all_to_all | solution.py:216
  18.1 7.6 %collective-permute-start.1 = (bf16[2432,128]{0,1:T(8,128)(2,1)}, bf16[2432,128]{0,1:T(8,128)(2,1)}, u32[]{:S(2)}, u32[]{:S(2)}) collective-permute-start(bf16[2432,128]{0,1:T(8,128)(2,1)} %bitcast.5), channel_id=1, source_target_pairs={{0,1},{1,0},{2,3},{3,2},{4,5},{5,4},{6,7},{7,6},{8,9},{9,8},{10,11... | collective-permute-start | bytes 1867784 | tf_op jit(solution)/shard_map/ppermute | solution.py:221
  21.5 0.8 copy-start.1
  22.3 0.9 copy-start.3
  23.2 0.7 copy-start.5
  23.8 0.7 copy-start.7
  24.5 0.6 copy-start.10
  25.1 0.6 copy-start.12
  37.7 1.1 copy-start.2
  38.8 1.1 copy-start.4
  39.9 0.9 copy-start.8
  40.8 0.8 copy-start.11
  46.2 45.0 %copy-start.13 = (bf16[128,256]{1,0:T(8,128)(2,1)S(1)}, bf16[128,256]{1,0:T(8,128)(2,1)}, u32[]{:S(2)}) copy-start(bf16[128,256]{1,0:T(8,128)(2,1)} %copy-done.12) | copy-start | bytes 196612
  75.5 39.8 %copy-start.6 = (f32[152,256]{1,0:T(8,128)S(1)}, f32[152,256]{1,0:T(8,128)}, u32[]{:S(2)}) copy-start(f32[152,256]{1,0:T(8,128)} %copy-done.5) | copy-start | bytes 466948

commit v4 on v3

--- a/solution.py
+++ b/solution.py
@@ -13,6 +13,13 @@
 MASKED = -1e30
 VMEM_LIMIT = 24 * 1024 * 1024
 F32, BF16, I32 = jnp.float32, jnp.bfloat16, jnp.int32
+
+
+PLACES = {
+    "s": pl.BlockSpec(memory_space=pltpu.SMEM),
+    "v": pl.BlockSpec(memory_space=pltpu.VMEM),
+    "a": pl.BlockSpec(memory_space=pl.ANY),
+}
 
 
 def dot_nt(a, b):
@@ -57,12 +64,10 @@
 
 
 def prepare_kernel(
-    cap, core_ref, req_ref, pos_ref, steps_ref, table_ref, gate_ref,
-    scale_ref, shift_ref, gates_ref, place_ref, place_t_ref, mark_ref,
+    cap, core_ref, req_ref, pos_ref, steps_ref, table_ref, gate_ref, mod_hbm, gates_ref, slot_ref, mod_ref, sem
 ):
     rows = req_ref.shape[1]
     half = rows // 2
-    slots = place_ref.shape[0]
     requests = steps_ref.shape[1]
     levels = table_ref.shape[1]
     is_first = core_ref[0] == 0
@@ -77,49 +82,73 @@
     odd = jnp.where(index >= half, 1, 0)
     start = jnp.floor((first_s - odd.astype(F32) + 1.0) * 0.5)
     slot = req_s * cap + (index - half * odd).astype(F32) - start
+    slot_ref[...] = jnp.where(is_first, slot[:, :half], slot[:, half:])
     chosen = one_hot(iota((requests, rows), 0).astype(F32) == req_s)
     steps = jnp.broadcast_to(steps_ref[...].astype(F32), (8, requests)).astype(BF16)
     step = jnp.dot(steps, chosen, preferred_element_type=F32)[0:1]
     pick = one_hot(iota((levels, rows), 0).astype(F32) == step)
-    gates_ref[...] = dot_tn(gate_ref[...], pick)
+    gates_ref[...] = dot_tn(gate_ref[...], pick).astype(BF16)
     pick = jnp.where(is_first, pick[:, :half].astype(F32), pick[:, half:].astype(F32)).astype(BF16)
-    shift_ref[...] = dot_tn(table_ref[0], pick).astype(BF16)
-    scale_ref[...] = dot_tn(table_ref[1], pick).astype(BF16)
-    slot = jnp.where(is_first, slot[:, :half], slot[:, half:])
-    hits = iota((slots, half), 0).astype(F32) == slot
-    place_ref[...] = one_hot(hits)
-    filled = jnp.sum(jnp.where(hits, 1.0, 0.0), axis=1, keepdims=True)
-    mark_ref[...] = jnp.broadcast_to(jnp.where(filled > 0.5, 0.0, DEAD), mark_ref.shape)
-    place_t_ref[...] = one_hot(iota((half, slots), 1).astype(F32) == as_column(slot))
+    mod_ref[0] = dot_tn(table_ref[0], pick).astype(BF16)
+    mod_ref[1] = dot_tn(table_ref[1], pick).astype(BF16)
+    copy = pltpu.make_async_copy(mod_ref, mod_hbm, sem)
+    copy.start()
+    copy.wait()
+
+
+def flip_kernel(own_ref, sib_ref, out_ref):
+    inner, depth = own_ref.shape
+    for start in range(0, depth, 128):
+        for side, ref in enumerate((own_ref, sib_ref)):
+            block = ref[:, start : start + 128].astype(F32).T
+            out_ref[start : start + 128, side * inner : (side + 1) * inner] = block.astype(BF16)
 
 
 def project_kernel(
-    core_ref, tok_ref, scale_ref, shift_ref, own_ref, sib_ref, gain_ref, place_ref, mark_ref, send_ref, hid_ref
+    core_ref, tok_hbm, mod_hbm, own_hbm, sib_hbm, gain_ref, slot_ref, send_ref, tok_ref, mod_ref, w_ref, hid_ref, sems
 ):
     parts, width, rows = tok_ref.shape
     depth = parts * width
-    inner = own_ref.shape[0] // 3
+    kinds, _, inner = own_hbm.shape
+    span = kinds * inner
+    copies = [pltpu.make_async_copy(tok_hbm, tok_ref, sems.at[0]), pltpu.make_async_copy(mod_hbm, mod_ref, sems.at[1])]
+    for side, hbm in enumerate((own_hbm, sib_hbm)):
+        for kind in range(kinds):
+            lanes = pl.ds(side * span + kind * inner, inner)
+            copies.append(pltpu.make_async_copy(hbm.at[kind], w_ref.at[:, lanes], sems.at[2 + side * kinds + kind]))
+    for copy in copies:
+        copy.start()
+    hits = iota((send_ref.shape[1], rows), 0).astype(F32) == slot_ref[...]
+    filled = jnp.sum(jnp.where(hits, 1.0, 0.0), axis=1, keepdims=True)
+    mark = jnp.where(filled > 0.5, 0.0, DEAD)
+    place = one_hot(hits)
+    copies[0].wait()
     total = sum(jnp.sum(tok_ref[m].astype(F32), axis=0, keepdims=True) for m in range(parts))
     mean = total * (1.0 / depth)
     square = sum(jnp.sum(jnp.square(tok_ref[m].astype(F32) - mean), axis=0, keepdims=True) for m in range(parts))
     inverse = lax.rsqrt(square * (1.0 / depth) + EPS)
+    copies[1].wait()
     for m in range(0, parts, 2):
         pair = jnp.concatenate([tok_ref[m].astype(F32), tok_ref[m + 1].astype(F32)], axis=0)
-        span = pl.ds(m * width, 2 * width)
-        scale, shift = scale_ref[span, :].astype(F32), shift_ref[span, :].astype(F32)
-        hid_ref[span, :] = ((pair - mean) * inverse * (1.0 + scale) + shift).astype(BF16)
-    hidden = hid_ref[...]
-    for w_ref, target in ((own_ref, core_ref[0]), (sib_ref, 1 - core_ref[0])):
-        proj = jnp.dot(w_ref[...], hidden, preferred_element_type=F32)
-        pieces = []
-        for start in range(0, 2 * inner, HD):
-            head = proj[start : start + HD]
-            power = jnp.mean(jnp.square(head), axis=0, keepdims=True)
-            pieces.append(head * lax.rsqrt(power + EPS) * gain_ref[pl.ds(start, HD), :])
-        pieces.append(proj[2 * inner :])
-        send = dot_nt(place_ref[...], jnp.concatenate(pieces, axis=0).astype(BF16))
-        mark = mark_ref[...]
-        send = jnp.concatenate([send[:, :inner], send[:, inner : 2 * inner] + mark, send[:, 2 * inner :]], axis=1)
+        lines = pl.ds(m * width, 2 * width)
+        shift, scale = mod_ref[0, lines, :].astype(F32), mod_ref[1, lines, :].astype(F32)
+        hid_ref[lines, :] = ((pair - mean) * inverse * (1.0 + scale) + shift).astype(BF16)
+    for copy in copies[2:]:
+        copy.wait()
+    proj = dot_tn(hid_ref[...], w_ref[...])
+    normed = 2 * inner
+    heads = one_hot(iota((normed, normed), 0) // HD == iota((normed, normed), 1) // HD)
+    for side, target in enumerate((core_ref[0], 1 - core_ref[0])):
+        mixed = proj[:, side * span : (side + 1) * span]
+        turned = mixed[:, :normed]
+        power = jnp.square(turned)
+        high = power.astype(BF16)
+        low = (power - high.astype(F32)).astype(BF16)
+        power = jnp.dot(high, heads, preferred_element_type=F32) + jnp.dot(low, heads, preferred_element_type=F32)
+        turned = turned * lax.rsqrt(power * (1.0 / HD) + EPS) * gain_ref[...]
+        packed = jnp.concatenate([turned, mixed[:, normed:]], axis=1).astype(BF16)
+        send = jnp.dot(place, packed, preferred_element_type=F32)
+        send = jnp.concatenate([send[:, :inner], send[:, inner:normed] + mark, send[:, normed:]], axis=1)
         send_ref[target] = send.astype(BF16)
 
 
@@ -155,9 +184,10 @@
         out_ref[row : row + block, :] = jnp.where(parts[0][0], parts[0][1], parts[1][1]).astype(BF16)
 
 
-def output_kernel(core_ref, back_ref, place_t_ref, w_ref, part_ref):
+def output_kernel(core_ref, back_ref, slot_ref, w_ref, part_ref):
     core = core_ref[0]
-    place_t = place_t_ref[...]
+    slots, rows = back_ref.shape[1], slot_ref.shape[1]
+    place_t = one_hot(iota((rows, slots), 1).astype(F32) == as_column(slot_ref[...]))
     own = jnp.dot(place_t, back_ref[core], preferred_element_type=F32).astype(BF16)
     sib = jnp.dot(place_t, back_ref[1 - core], preferred_element_type=F32).astype(BF16)
     attn = jnp.concatenate([own, sib], axis=1)
@@ -169,20 +199,18 @@
     parts = sums_ref.shape[0]
     halves = [sum(sums_ref[m].astype(F32) for m in range(c, parts, 2)) for c in range(2)]
     total = jnp.concatenate(halves, axis=1)
-    mixed = (perm_ref[...].astype(F32) + gates_ref[...] * total).astype(BF16)
+    mixed = (perm_ref[...].astype(F32) + gates_ref[...].astype(F32) * total).astype(BF16)
     rows = perm_ref.shape[1]
     deal = one_hot(pos_ref[...] == dealt(rows))
     out_ref[...] = jnp.dot(mixed, deal, preferred_element_type=F32).astype(BF16)
 
 
-def call(kernel, out_shape, smem, vmem, scratch=(), flops=0):
-    whole = pl.BlockSpec(memory_space=pltpu.VMEM)
-    outs = jax.tree.map(lambda _: whole, out_shape)
+def call(kernel, out_shape, specs, out_specs, scratch=(), flops=0):
     return pl.pallas_call(
         kernel,
         out_shape=out_shape,
-        in_specs=[pl.BlockSpec(memory_space=pltpu.SMEM)] * smem + [whole] * vmem,
-        out_specs=outs,
+        in_specs=[PLACES[letter] for letter in specs],
+        out_specs=tuple(PLACES[letter] for letter in out_specs) if len(out_specs) > 1 else PLACES[out_specs],
         scratch_shapes=list(scratch),
         compiler_params=pltpu.CompilerParams(vmem_limit_bytes=VMEM_LIMIT),
         cost_estimate=pl.CostEstimate(flops=flops, bytes_accessed=1 << 20, transcendentals=0),
@@ -197,8 +225,7 @@
     chips = parts // 2
     cap = max(2, 2 * rows // requests) // 2
     slots = requests * cap
-    depth = w_qkv.shape[0]
-    inner = w_qkv.shape[2]
+    depth, kinds, inner = w_qkv.shape
     text_len = context.shape[2]
     text_pad = -(-text_len // 128) * 128
     sibling = [(i, i ^ 1) for i in range(parts)]
@@ -210,64 +237,64 @@
     spread, perm, pos = call(
         spread_kernel,
         (shape((parts, width, half), BF16), shape((width, rows), BF16), shape((1, rows), F32)),
-        0,
-        2,
+        "vv",
+        "vvv",
     )(tokens.T, req)
+    spread, w_qkv, w_out = lax.optimization_barrier((spread, w_qkv, w_out))
     whole = lax.all_to_all(spread, "mp", 0, 0, tiled=True)
 
-    w_own = w_qkv.transpose(1, 2, 0).reshape(3 * inner, depth)
+    w_own = w_qkv.transpose(1, 0, 2)
     w_sib = lax.ppermute(w_own, "mp", sibling)
-    out_own = w_out.T
-    out_sib = lax.ppermute(out_own, "mp", sibling)
-    w_back = jnp.concatenate([out_own, out_sib], axis=1).reshape(parts, width, 2 * inner)
+    out_sib = lax.ppermute(w_out, "mp", sibling)
     gate_table = lax.dynamic_slice_in_dim(mod_table[:, 2, :], lax.axis_index("mp") * width, width, 1)
-    scale, shift, gates, place, place_t, mark = call(
+    mod, gates, slot = call(
         functools.partial(prepare_kernel, cap),
-        (
-            shape((depth, half), BF16),
-            shape((depth, half), BF16),
-            shape((width, rows), F32),
-            shape((slots, half), BF16),
-            shape((half, slots), BF16),
-            shape((slots, inner), F32),
-        ),
-        1,
-        5,
+        (shape((2, depth, half), BF16), shape((width, rows), BF16), shape((1, half), F32)),
+        "svvvvv",
+        "avv",
+        [pltpu.VMEM((2, depth, half), BF16), pltpu.SemaphoreType.DMA],
     )(core, req, pos, tsteps.reshape(1, requests), mod_table.transpose(1, 0, 2), gate_table)
+    w_back = call(flip_kernel, shape((depth, 2 * inner), BF16), "vv", "v")(w_out, out_sib)
     gains = jnp.concatenate(
         [jnp.tile(qk_gain[0] * HD ** (-0.5), inner // HD), jnp.tile(qk_gain[1], inner // HD)]
-    ).reshape(2 * inner, 1)
+    ).reshape(1, 2 * inner)
     text = jnp.pad(context[0], ((0, 0), (0, text_pad - text_len), (0, 0)))
-    whole, w_own, w_sib, w_back, scale, shift, gates, place, place_t, mark, gains, text = lax.optimization_barrier(
-        (whole, w_own, w_sib, w_back, scale, shift, gates, place, place_t, mark, gains, text)
+    whole, w_sib, w_back, mod, gates, slot, gains, text = lax.optimization_barrier(
+        (whole, w_sib, w_back, mod, gates, slot, gains, text)
     )
 
     send = call(
         project_kernel,
-        shape((2, slots, 3 * inner), BF16),
-        1,
-        8,
-        [pltpu.VMEM((depth, half), BF16)],
-        flops=4 * depth * half * 3 * inner,
-    )(core, whole, scale, shift, w_own, w_sib, gains, place, mark)
+        shape((2, slots, kinds * inner), BF16),
+        "saaaavv",
+        "v",
+        [
+            pltpu.VMEM((parts, width, half), BF16),
+            pltpu.VMEM((2, depth, half), BF16),
+            pltpu.VMEM((depth, 2 * kinds * inner), BF16),
+            pltpu.VMEM((depth, half), BF16),
+            pltpu.SemaphoreType.DMA((2 + 2 * kinds,)),
+        ],
+        flops=4 * depth * half * kinds * inner,
+    )(core, whole, mod, w_own, w_sib, gains, slot)
     arrived = lax.all_to_all(
-        send.reshape(2 * requests, cap, 3 * inner), ("dp", "mp"), 0, 0, axis_index_groups=planes, tiled=True
+        send.reshape(2 * requests, cap, kinds * inner), ("dp", "mp"), 0, 0, axis_index_groups=planes, tiled=True
     )
     attn = call(
         functools.partial(attend_kernel, text_len),
         shape((2 * slots, inner), BF16),
-        0,
-        2,
+        "vv",
+        "v",
         flops=16 * slots * (2 * slots + text_pad) * inner,
-    )(arrived.reshape(2 * slots, 3 * inner), text)
+    )(arrived.reshape(2 * slots, kinds * inner), text)
     returned = lax.all_to_all(
         attn.reshape(2 * requests, cap, inner), ("dp", "mp"), 0, 0, axis_index_groups=planes, tiled=True
     )
-    partial = call(output_kernel, shape((parts, width, half), BF16), 1, 3, flops=4 * depth * half * inner)(
-        core, returned.reshape(2, slots, inner), place_t, w_back
-    )
+    partial = call(
+        output_kernel, shape((parts, width, half), BF16), "svvv", "v", flops=4 * depth * half * inner
+    )(core, returned.reshape(2, slots, inner), slot, w_back.reshape(parts, width, 2 * inner))
     sums = lax.all_to_all(partial, "mp", 0, 0, tiled=True)
-    return call(finish_kernel, shape((width, rows), BF16), 0, 4)(sums, perm, gates, pos).T
+    return call(finish_kernel, shape((width, rows), BF16), "vvvv", "v")(sums, perm, gates, pos).T
 
 
 def solution(mesh):

time: 117 us -> 112 us (0.957)
  local copies, waits for them, and re-layouts: 13.2 us -> 7.36 us
  waiting for transfers between devices: 7.7 us -> 10.7 us
  other arithmetic: 2.41 us -> 0.77 us
    all_to_all x1, waiting for transfers between devices: 7.69 us -> 10.7 us  [body(): whole = lax.all_to_all(spread, 'mp', 0, 0, tiled=True)]
    transpose x1 -> x0, local copies, waits for them, and re-layouts: 2.82 us -> none  [body(): w_own = w_qkv.transpose(1, 2, 0).reshape(3 * inner, depth)]
    concatenate x1 -> x0, other arithmetic: 2.4 us -> none  [body(): jnp.concatenate([out_own, out_sib], axis=1).reshape(parts, width, 2 * inner)]
    concatenate x1 -> x0, local copies, waits for them, and re-layouts: 1.74 us -> none  [body(): jnp.concatenate([out_own, out_sib], axis=1).reshape(parts, width, 2 * inner)]
    unnamed x37 -> x19, local copies, waits for them, and re-layouts: 8.22 us -> 7.08 us
    pallas_call x4 -> x5, Pallas kernels: 6.94 us -> 6.82 us  [the longest x1 3.59 us: body(): call(project_kernel, shape((2, slots, kinds * inner), BF16), 'saaaavv', '...]
  transfers between devices with their start and end apart: 3 -> 3, of which waited for: 1 -> 1; matrix products, arithmetic and copies ran while one was open for 4% -> 2% of each run, Pallas kernels for 2% -> 1%
where the time goes in v4:
time: 112 us; the launch traced here: 111 us
  blocking collectives  65.2 us (58%)
  starting transfers between devices  15.9 us (14%)
  Pallas kernels  11.1 us (10%)
  waiting for transfers between devices  10.7 us (10%)
  local copies, waits for them, and re-layouts  7.36 us (7%)
    all_to_all x1, blocking collectives, body(): lax.all_to_all(send.reshape(2 * requests, cap, kinds * inner), ('dp', 'mp...  26.2 us
    all_to_all x1, blocking collectives, body(): sums = lax.all_to_all(partial, 'mp', 0, 0, tiled=True)  23.5 us
    all_to_all x1, blocking collectives, body(): lax.all_to_all(attn.reshape(2 * requests, cap, inner), ('dp', 'mp'), 0, 0...  15.5 us
    all_to_all x1, waiting for transfers between devices, body(): whole = lax.all_to_all(spread, 'mp', 0, 0, tiled=True)  10.7 us
    ppermute x1, starting transfers between devices, body(): w_sib = lax.ppermute(w_own, 'mp', sibling)  8.78 us
    unnamed x19, local copies, waits for them, and re-layouts  7.08 us
    all_to_all x1, starting transfers between devices, body(): whole = lax.all_to_all(spread, 'mp', 0, 0, tiled=True)  5.08 us
    pallas_call x1, Pallas kernels, body(): call(project_kernel, shape((2, slots, kinds * inner), BF16), 'saaaavv', '...  3.59 us
  transfers between devices with their start and end apart: 3, of which 1 were waited for; matrix products, arithmetic and copies ran while one was open for 2% of the time, Pallas kernels for 1%

profile of v4, /device:TPU:1, one launch (start us, length us, event | category | flops | bytes accessed | tf_op | source)
XLA Modules:
  0.0 111.0 jit_solution(5149492957318927979)
XLA Ops:
  0.0 0.9 copy-done.5
  1.0 0.7 copy-done.6
  1.6 1.2 %shard_map.82 = (bf16[16,152,128]{2,1,0:T(8,128)(2,1)}, bf16[152,256]{1,0:T(8,128)(2,1)S(1)}, f32[1,256]{1,0:T(1,128)S(1)}) custom-call(bf16[152,256]{1,0:T(8,128)(2,1)S(1)} %bitcast.30, s32[1,256]{1,0:T(1,128)S(1)} %bitcast.31), custom_call_target="tpu_custom_call" | custom-call | bytes 1048576 | tf_op jit(solution)/shard_map/pallas_call | solution.py:237
  2.8 8.8 %collective-permute-start = (bf16[3,2432,128]{2,1,0:T(8,128)(2,1)}, bf16[3,2432,128]{2,1,0:T(8,128)(2,1)}, u32[]{:S(2)}, u32[]{:S(2)}) collective-permute-start(bf16[3,2432,128]{2,1,0:T(8,128)(2,1)} %bitcast.23), channel_id=1, source_target_pairs={{0,1},{1,0},{2,3},{3,2},{4,5},{5,4},{6,7},{7,6},{8,9},{9,8},{10,11... | collective-permute-start | bytes 5603336 | tf_op jit(solution)/shard_map/ppermute | solution.py:247
  11.6 5.1 %all-to-all-start = ((bf16[16,152,128]{2,1,0:T(8,128)(2,1)}), bf16[16,152,128]{2,1,0:T(8,128)(2,1)S(1)}, u32[]{:S(2)}, u32[]{:S(2)}) async-start(bf16[16,152,128]{2,1,0:T(8,128)(2,1)} %get-tuple-element.23), calls=%async_computation | async-start | bytes 1245184 | tf_op jit(solution)/shard_map/all_to_all | solution.py:244
  16.7 2.0 %collective-permute-start.1 = (bf16[128,2432]{1,0:T(8,128)(2,1)}, bf16[128,2432]{1,0:T(8,128)(2,1)S(1)}, u32[]{:S(2)}, u32[]{:S(2)}) collective-permute-start(bf16[128,2432]{1,0:T(8,128)(2,1)} %own_ref), channel_id=1, source_target_pairs={{0,1},{1,0},{2,3},{3,2},{4,5},{5,4},{6,7},{7,6},{8,9},{9,8},{10,11... | collective-permute-start | bytes 1867784 | tf_op jit(solution)/shard_map/ppermute | solution.py:248
  18.7 0.8 multiply_bitcast_fusion
  19.5 0.1 tile.23
  19.6 0.1 tile.26
  19.7 0.9 copy.11
  20.6 0.0 slice-done
  20.6 0.1 dynamic-slice_bitcast_fusion.gate_ref
  20.7 0.0 copy-done.1
  20.7 0.0 copy-done.7
  20.7 0.0 copy-done.8
  20.8 1.2 %shard_map.84 = (bf16[2,2432,128]{2,1,0:T(8,128)(2,1)S(1)}, bf16[152,256]{1,0:T(8,128)(2,1)S(1)}, f32[1,128]{1,0:T(1,128)S(1)}) custom-call(s32[1]{0:T(128)} %bitcast.core_ref, s32[1,256]{1,0:T(1,128)S(1)} %bitcast.32, f32[1,256]{1,0:T(1,128)S(1)} %get-tuple-element.26.pos_ref, s32[1,32]{1,0:T(1,128)S(1)} %bitcast.34, bf16[3,28,2432]{2,1,0:T(8,128)(2,1)S(1)} %bitcast.26, ...), custom_call_target="tpu_custom_call" | custom-call | bytes 1048576 | tf_op jit(solution)/shard_map/pallas_call | solution.py:250
  22.0 0.0 collective-permute-done.1.sib_ref
  22.0 0.0 copy-start.3
  22.0 0.8 copy-done.3
  22.9 1.1 copy-done.2
  23.9 1.1 copy-done.4
  25.0 0.4 shard_map.83
  25.4 10.7 %all-to-all-done.tok_hbm = bf16[16,152,128]{2,1,0:T(8,128)(2,1)S(1)} async-done(((bf16[16,152,128]{2,1,0:T(8,128)(2,1)}), bf16[16,152,128]{2,1,0:T(8,128)(2,1)S(1)}, u32[]{:S(2)}, u32[]{:S(2)}) %all-to-all-start) | async-done | bytes 622624 | tf_op jit(solution)/shard_map/all_to_all | solution.py:244
  36.1 0.0 collective-permute-done.sib_hbm
  36.1 1.5 %copy-done = bf16[2432,3,128]{2,0,1:T(8,128)(2,1)S(1)} copy-done((bf16[2432,3,128]{2,0,1:T(8,128)(2,1)S(1)}, bf16[2432,3,128]{2,0,1:T(8,128)(2,1)}, u32[]{:S(2)}) %copy-start) | copy-done | bytes 1867800
  37.6 3.6 %shard_map.85 = bf16[2,256,384]{2,1,0:T(8,128)(2,1)S(1)} custom-call(s32[1]{0:T(128)} %bitcast.core_ref, bf16[16,152,128]{2,1,0:T(8,128)(2,1)S(1)} %all-to-all-done.tok_hbm, bf16[2,2432,128]{2,1,0:T(8,128)(2,1)S(1)} %get-tuple-element.31.mod_hbm, bf16[3,2432,128]{2,1,0:T(8,128)(2,1)S(1)} %bitcast.24, bf16[3,2432,128]{2,1,0:T(8,128)(2,1)} %collective-permute-done.sib_hbm, ...), custom_call_target="tpu_custom_call" | custom-call | flops 478150656 | bytes 1048576 | tf_op jit(solution)/shard_map/pallas_call | solution.py:266
  41.2 26.2 %all_to_all.20 = bf16[64,8,384]{2,1,0:T(8,128)(2,1)S(1)} all-to-all(bf16[64,8,384]{2,1,0:T(8,128)(2,1)S(1)} %bitcast.25), channel_id=1, replica_groups={{0,16,32,48,64,80,96,112,128,144,160,176,192,208,224,240,256,272,288,30..., dimensions={0} | all-to-all | bytes 786432 | tf_op jit(solution)/shard_map/all_to_all | solution.py:280
  67.3 3.0 %shard_map.86 = bf16[512,128]{1,0:T(8,128)(2,1)S(1)} custom-call(bf16[512,384]{1,0:T(8,128)(2,1)S(1)} %bitcast.28, bf16[2,384,128]{2,1,0:T(8,128)(2,1)S(1)} %pad.4.ctx_ref), custom_call_target="tpu_custom_call" | custom-call | flops 469762048 | bytes 1048576 | tf_op jit(solution)/shard_map/pallas_call | solution.py:283
  70.4 15.5 %all_to_all.21 = bf16[64,8,128]{2,1,0:T(8,128)(2,1)S(1)} all-to-all(bf16[64,8,128]{2,1,0:T(8,128)(2,1)S(1)} %bitcast.29), channel_id=1, replica_groups={{0,16,32,48,64,80,96,112,128,144,160,176,192,208,224,240,256,272,288,30..., dimensions={0} | all-to-all | bytes 262144 | tf_op jit(solution)/shard_map/all_to_all | solution.py:290
  85.9 0.7 shard_map.87
  86.6 23.5 %all_to_all.22.sums_ref = bf16[16,152,128]{2,1,0:T(8,128)(2,1)S(1)} all-to-all(bf16[16,152,128]{2,1,0:T(8,128)(2,1)S(1)} %shard_map.87), channel_id=1, replica_groups=mesh['dp'=32,'mp'=16] {'mp'}, dimensions={0} | all-to-all | bytes 1245184 | tf_op jit(solution)/shard_map/all_to_all | solution.py:296
  110.1 0.9 shard_map.88
  (13 shorter events, 0.0 us)
Async XLA Ops:
  0.0 20.6 %slice-start = ((bf16[28,3,2432]{2,0,1:T(8,128)(2,1)}), bf16[28,1,2432]{2,0,1:T(8,128)(2,1)S(1)}, s32[]{:S(2)}) async-start(bf16[28,3,2432]{2,0,1:T(8,128)(2,1)} %param.11), calls=%async_computation.4 | async-start | bytes 311296 | tf_op jit(solution)/shard_map/slice | solution.py:249
  0.0 20.7 %copy-start.1 = (bf16[28,3,2432]{2,0,1:T(8,128)(2,1)S(1)}, bf16[28,3,2432]{2,0,1:T(8,128)(2,1)}, u32[]{:S(2)}) copy-start(bf16[28,3,2432]{2,0,1:T(8,128)(2,1)} %param.11) | copy-start | bytes 1225732
  0.0 0.9 copy-start.5
  1.0 0.7 copy-start.6
  1.6 19.1 %copy-start.7 = (s32[256,1]{0,1:T(1,128)S(1)}, s32[256,1]{0,1:T(1,128)}, u32[]{:S(2)}) copy-start(s32[256,1]{0,1:T(1,128)} %param.9) | copy-start | bytes 3076
  1.6 19.1 %copy-start.8 = (s32[32]{0:T(128)S(1)}, s32[32]{0:T(128)}, u32[]{:S(2)}) copy-start(s32[32]{0:T(128)} %param.10) | copy-start | bytes 388
  2.8 33.2 %collective-permute-start = (bf16[3,2432,128]{2,1,0:T(8,128)(2,1)}, bf16[3,2432,128]{2,1,0:T(8,128)(2,1)}, u32[]{:S(2)}, u32[]{:S(2)}) collective-permute-start(bf16[3,2432,128]{2,1,0:T(8,128)(2,1)} %bitcast.23), channel_id=1, source_target_pairs={{0,1},{1,0},{2,3},{3,2},{4,5},{5,4},{6,7},{7,6},{8,9},{9,8},{10,11... | collective-permute-start | bytes 5603336 | tf_op jit(solution)/shard_map/ppermute | solution.py:247
  11.6 24.4 %all-to-all-start = ((bf16[16,152,128]{2,1,0:T(8,128)(2,1)}), bf16[16,152,128]{2,1,0:T(8,128)(2,1)S(1)}, u32[]{:S(2)}, u32[]{:S(2)}) async-start(bf16[16,152,128]{2,1,0:T(8,128)(2,1)} %get-tuple-element.23), calls=%async_computation | async-start | bytes 1245184 | tf_op jit(solution)/shard_map/all_to_all | solution.py:244
  16.7 5.3 %collective-permute-start.1 = (bf16[128,2432]{1,0:T(8,128)(2,1)}, bf16[128,2432]{1,0:T(8,128)(2,1)S(1)}, u32[]{:S(2)}, u32[]{:S(2)}) collective-permute-start(bf16[128,2432]{1,0:T(8,128)(2,1)} %own_ref), channel_id=1, source_target_pairs={{0,1},{1,0},{2,3},{3,2},{4,5},{5,4},{6,7},{7,6},{8,9},{9,8},{10,11... | collective-permute-start | bytes 1867784 | tf_op jit(solution)/shard_map/ppermute | solution.py:248
  22.0 0.8 copy-start.3
  22.9 1.1 copy-start.2
  23.9 1.1 copy-start.4
  36.1 1.5 %copy-start = (bf16[2432,3,128]{2,0,1:T(8,128)(2,1)S(1)}, bf16[2432,3,128]{2,0,1:T(8,128)(2,1)}, u32[]{:S(2)}) copy-start(bf16[2432,3,128]{2,0,1:T(8,128)(2,1)} %param.12) | copy-start | bytes 5603332

commit v5 on v4

--- a/solution.py
+++ b/solution.py
@@ -12,6 +12,7 @@
 DEAD = 1e30
 MASKED = -1e30
 VMEM_LIMIT = 24 * 1024 * 1024
+CHUNKS = 2
 F32, BF16, I32 = jnp.float32, jnp.bfloat16, jnp.int32
 
 
@@ -49,18 +50,30 @@
     return jnp.where(place < half, 2 * place, 2 * (place - half) + 1).astype(F32)
 
 
-def spread_kernel(tok_ref, req_ref, out_ref, perm_ref, pos_ref):
+def spread_kernel(tok_hbm, req_hbm, out_hbm, perm_ref, pos_ref, tok_ref, req_ref, halves_ref, sems):
     width, rows = tok_ref.shape
     half = rows // 2
+    parts = out_hbm.shape[0]
+    reads = [pltpu.make_async_copy(req_hbm, req_ref, sems.at[0]), pltpu.make_async_copy(tok_hbm, tok_ref, sems.at[1])]
+    for copy in reads:
+        copy.start()
+    reads[0].wait()
     req = req_ref[...].astype(F32)
     req_col = as_column(req)
     earlier = (req_col < req) | ((req_col == req) & (iota((rows, rows), 0) < iota((rows, rows), 1)))
     pos = jnp.sum(jnp.where(earlier, 1.0, 0.0), axis=0, keepdims=True)
+    deal = one_hot(pos == dealt(rows))
     pos_ref[...] = pos
-    perm = dot_nt(tok_ref[...], one_hot(pos == dealt(rows))).astype(BF16)
+    reads[1].wait()
+    perm = dot_nt(tok_ref[...], deal).astype(BF16)
+    halves_ref[0] = perm[:, :half]
+    halves_ref[1] = perm[:, half:]
+    writes = [pltpu.make_async_copy(halves_ref.at[m % 2], out_hbm.at[m], sems.at[2 + m]) for m in range(parts)]
+    for copy in writes:
+        copy.start()
     perm_ref[...] = perm
-    for m in range(out_ref.shape[0]):
-        out_ref[m] = perm[:, (m % 2) * half : (m % 2 + 1) * half]
+    for copy in writes:
+        copy.wait()
 
 
 def prepare_kernel(
@@ -105,37 +118,51 @@
 
 
 def project_kernel(
-    core_ref, tok_hbm, mod_hbm, own_hbm, sib_hbm, gain_ref, slot_ref, send_ref, tok_ref, mod_ref, w_ref, hid_ref, sems
+    core_ref, tok_ref, mod_hbm, own_hbm, sib0_hbm, sib1_hbm, sib2_hbm, gain_ref, slot_ref,
+    send_ref, mod_ref, w_ref, hid_ref, sems,
 ):
     parts, width, rows = tok_ref.shape
     depth = parts * width
     kinds, _, inner = own_hbm.shape
     span = kinds * inner
-    copies = [pltpu.make_async_copy(tok_hbm, tok_ref, sems.at[0]), pltpu.make_async_copy(mod_hbm, mod_ref, sems.at[1])]
-    for side, hbm in enumerate((own_hbm, sib_hbm)):
-        for kind in range(kinds):
-            lanes = pl.ds(side * span + kind * inner, inner)
-            copies.append(pltpu.make_async_copy(hbm.at[kind], w_ref.at[:, lanes], sems.at[2 + side * kinds + kind]))
-    for copy in copies:
-        copy.start()
+    chunk = depth // CHUNKS
+    modulation = pltpu.make_async_copy(mod_hbm, mod_ref, sems.at[0])
+    modulation.start()
+    sources = [own_hbm.at[kind] for kind in range(kinds)] + [sib0_hbm, sib1_hbm, sib2_hbm]
+    weights = []
+    for step in range(CHUNKS):
+        lines = pl.ds(step * chunk, chunk)
+        weights.append(
+            [
+                pltpu.make_async_copy(
+                    source.at[lines], w_ref.at[lines, pl.ds(i * inner, inner)], sems.at[1 + step * len(sources) + i]
+                )
+                for i, source in enumerate(sources)
+            ]
+        )
+        for copy in weights[-1]:
+            copy.start()
     hits = iota((send_ref.shape[1], rows), 0).astype(F32) == slot_ref[...]
     filled = jnp.sum(jnp.where(hits, 1.0, 0.0), axis=1, keepdims=True)
     mark = jnp.where(filled > 0.5, 0.0, DEAD)
     place = one_hot(hits)
-    copies[0].wait()
     total = sum(jnp.sum(tok_ref[m].astype(F32), axis=0, keepdims=True) for m in range(parts))
     mean = total * (1.0 / depth)
     square = sum(jnp.sum(jnp.square(tok_ref[m].astype(F32) - mean), axis=0, keepdims=True) for m in range(parts))
     inverse = lax.rsqrt(square * (1.0 / depth) + EPS)
-    copies[1].wait()
+    modulation.wait()
     for m in range(0, parts, 2):
         pair = jnp.concatenate([tok_ref[m].astype(F32), tok_ref[m + 1].astype(F32)], axis=0)
         lines = pl.ds(m * width, 2 * width)
         shift, scale = mod_ref[0, lines, :].astype(F32), mod_ref[1, lines, :].astype(F32)
         hid_ref[lines, :] = ((pair - mean) * inverse * (1.0 + scale) + shift).astype(BF16)
-    for copy in copies[2:]:
-        copy.wait()
-    proj = dot_tn(hid_ref[...], w_ref[...])
+    proj = None
+    for step in range(CHUNKS):
+        for copy in weights[step]:
+            copy.wait()
+        lines = pl.ds(step * chunk, chunk)
+        part = dot_tn(hid_ref[lines, :], w_ref[lines, :])
+        proj = part if proj is None else proj + part
     normed = 2 * inner
     heads = one_hot(iota((normed, normed), 0) // HD == iota((normed, normed), 1) // HD)
     for side, target in enumerate((core_ref[0], 1 - core_ref[0])):
@@ -154,34 +181,28 @@
 
 def attend_kernel(text_len, slots_ref, ctx_ref, out_ref):
     slots, inner = out_ref.shape
-    block = 128
+    block = 256
     text_pad = ctx_ref.shape[1]
     queries = slots_ref[:, 0:inner]
     keys = slots_ref[:, inner : 2 * inner].astype(F32)
-    values = slots_ref[:, 2 * inner :]
-    text_keys, text_values = ctx_ref[0], ctx_ref[1]
     dead = keys > 0.5 * DEAD
     marks = jnp.where(dead, 1.0, 0.0).astype(BF16)
-    keys = jnp.where(dead, 0.0, keys).astype(BF16)
+    keys = jnp.concatenate([jnp.where(dead, 0.0, keys).astype(BF16), ctx_ref[0]], axis=0)
     own_bias = dot_nt(jnp.full((8, inner), MASKED, BF16), marks)[0:1]
     text_bias = jnp.where(iota((1, text_pad), 1) < text_len, 0.0, MASKED)
-    lane = iota((1, inner), 1)
-    one = jnp.ones((), BF16)
+    bias = jnp.concatenate([own_bias, text_bias], axis=1)
+    values = jnp.concatenate([slots_ref[:, 2 * inner :], ctx_ref[1]], axis=0)
+    values = jnp.concatenate([values, jnp.ones(values.shape, BF16)], axis=1)
+    first = iota((1, inner), 1) < HD
     zero = jnp.zeros((), BF16)
     for row in range(0, slots, block):
-        parts = []
-        for head in range(inner // HD):
-            mine = (lane >= head * HD) & (lane < (head + 1) * HD)
-            query = jnp.where(mine, queries[row : row + block], zero)
-            own = dot_nt(query, keys) + own_bias
-            far = dot_nt(query, text_keys) + text_bias
-            top = jnp.maximum(jnp.max(own, axis=1, keepdims=True), jnp.max(far, axis=1, keepdims=True))
-            own = jnp.exp(own - top).astype(BF16)
-            far = jnp.exp(far - top).astype(BF16)
-            mixed = jnp.dot(own, jnp.where(mine, values, one), preferred_element_type=F32)
-            mixed = mixed + jnp.dot(far, jnp.where(mine, text_values, one), preferred_element_type=F32)
-            parts.append((mine, mixed / pltpu.roll(mixed, HD, 1)))
-        out_ref[row : row + block, :] = jnp.where(parts[0][0], parts[0][1], parts[1][1]).astype(BF16)
+        query = queries[row : row + block]
+        query = jnp.concatenate([jnp.where(first, query, zero), jnp.where(first, zero, query)], axis=0)
+        scores = dot_nt(query, keys) + bias
+        weights = jnp.exp(scores - jnp.max(scores, axis=1, keepdims=True)).astype(BF16)
+        mixed = jnp.dot(weights, values, preferred_element_type=F32)
+        mixed = mixed[:, :inner] / mixed[:, inner:]
+        out_ref[row : row + block, :] = jnp.where(first, mixed[:block], mixed[block:]).astype(BF16)
 
 
 def output_kernel(core_ref, back_ref, slot_ref, w_ref, part_ref):
@@ -234,22 +255,31 @@
     shape = jax.ShapeDtypeStruct
 
     req = route.reshape(1, rows)
+    def in_hbm(x):
+        return pltpu.with_memory_space_constraint(x, pltpu.HBM)
+
     spread, perm, pos = call(
         spread_kernel,
-        (shape((parts, width, half), BF16), shape((width, rows), BF16), shape((1, rows), F32)),
-        "vv",
-        "vvv",
-    )(tokens.T, req)
+        (pltpu.HBM((parts, width, half), BF16), shape((width, rows), BF16), shape((1, rows), F32)),
+        "aa",
+        "avv",
+        [
+            pltpu.VMEM((width, rows), BF16),
+            pltpu.VMEM((1, rows), I32),
+            pltpu.VMEM((2, width, half), BF16),
+            pltpu.SemaphoreType.DMA((2 + parts,)),
+        ],
+    )(in_hbm(tokens.T), in_hbm(req))
     spread, w_qkv, w_out = lax.optimization_barrier((spread, w_qkv, w_out))
     whole = lax.all_to_all(spread, "mp", 0, 0, tiled=True)
 
     w_own = w_qkv.transpose(1, 0, 2)
-    w_sib = lax.ppermute(w_own, "mp", sibling)
+    w_sib = [lax.ppermute(w_own[kind], "mp", sibling) for kind in range(kinds)]
     out_sib = lax.ppermute(w_out, "mp", sibling)
     gate_table = lax.dynamic_slice_in_dim(mod_table[:, 2, :], lax.axis_index("mp") * width, width, 1)
     mod, gates, slot = call(
         functools.partial(prepare_kernel, cap),
-        (shape((2, depth, half), BF16), shape((width, rows), BF16), shape((1, half), F32)),
+        (pltpu.HBM((2, depth, half), BF16), shape((width, rows), BF16), shape((1, half), F32)),
         "svvvvv",
         "avv",
         [pltpu.VMEM((2, depth, half), BF16), pltpu.SemaphoreType.DMA],
@@ -266,17 +296,16 @@
     send = call(
         project_kernel,
         shape((2, slots, kinds * inner), BF16),
-        "saaaavv",
+        "svaaaaavv",
         "v",
         [
-            pltpu.VMEM((parts, width, half), BF16),
             pltpu.VMEM((2, depth, half), BF16),
             pltpu.VMEM((depth, 2 * kinds * inner), BF16),
             pltpu.VMEM((depth, half), BF16),
-            pltpu.SemaphoreType.DMA((2 + 2 * kinds,)),
+            pltpu.SemaphoreType.DMA((1 + 2 * kinds * CHUNKS,)),
         ],
         flops=4 * depth * half * kinds * inner,
-    )(core, whole, mod, w_own, w_sib, gains, slot)
+    )(core, whole, in_hbm(mod), in_hbm(w_own), *[in_hbm(w) for w in w_sib], gains, slot)
     arrived = lax.all_to_all(
         send.reshape(2 * requests, cap, kinds * inner), ("dp", "mp"), 0, 0, axis_index_groups=planes, tiled=True
     )

time: 112 us -> 106 us (0.946)
  waiting for transfers between devices: 10.7 us -> 4.96 us
  starting transfers between devices: 15.9 us -> 20.5 us
  local copies, waits for them, and re-layouts: 7.36 us -> 3.18 us
    unnamed x19 -> x13, local copies, waits for them, and re-layouts: 7.08 us -> 0.06 us
    all_to_all x1, starting transfers between devices: 5.08 us -> 11.8 us  [body(): whole = lax.all_to_all(spread, 'mp', 0, 0, tiled=True)]
    all_to_all x1, waiting for transfers between devices: 10.7 us -> 4.95 us  [body(): whole = lax.all_to_all(spread, 'mp', 0, 0, tiled=True)]
    squeeze x0 -> x1, local copies, waits for them, and re-layouts: none -> 2.84 us  [body(): w_sib = [lax.ppermute(w_own[kind], 'mp', sibling) for kind in range(kinds)]]
    ppermute x1 -> x3, starting transfers between devices: 8.78 us -> 6.33 us  [body(): w_sib = [lax.ppermute(w_own[kind], 'mp', sibling) for kind in range(kinds)]]
    pallas_call x3, Pallas kernels: 6.03 us -> 7.91 us  [the longest x1 3.87 us: body(): call(project_kernel, shape((2, slots, kinds * inner), BF16), 'svaaaaavv',...]
    pallas_call x1, Pallas kernels: 3.03 us -> 1.73 us  [body(): call(functools.partial(attend_kernel, text_len), shape((2 * slots, inner)...]
  transfers between devices with their start and end apart: 3 -> 5, of which waited for: 1 -> 1; matrix products, arithmetic and copies ran while one was open for 2% -> 3% of each run, Pallas kernels for 1% -> 2%
where the time goes in v5:
time: 106 us
  blocking collectives  65.2 us (62%)
  starting transfers between devices  20.5 us (19%)
  Pallas kernels  11.6 us (11%)
  waiting for transfers between devices  4.96 us (5%)
  local copies, waits for them, and re-layouts  3.18 us (3%)
    all_to_all x1, blocking collectives, body(): lax.all_to_all(send.reshape(2 * requests, cap, kinds * inner), ('dp', 'mp...  26.2 us
    all_to_all x1, blocking collectives, body(): sums = lax.all_to_all(partial, 'mp', 0, 0, tiled=True)  23.5 us
    all_to_all x1, blocking collectives, body(): lax.all_to_all(attn.reshape(2 * requests, cap, inner), ('dp', 'mp'), 0, 0...  15.5 us
    all_to_all x1, starting transfers between devices, body(): whole = lax.all_to_all(spread, 'mp', 0, 0, tiled=True)  11.8 us
    ppermute x3, starting transfers between devices, body(): w_sib = [lax.ppermute(w_own[kind], 'mp', sibling) for kind in range(kinds)]  6.33 us
    all_to_all x1, waiting for transfers between devices, body(): whole = lax.all_to_all(spread, 'mp', 0, 0, tiled=True)  4.95 us
    pallas_call x1, Pallas kernels, body(): call(project_kernel, shape((2, slots, kinds * inner), BF16), 'svaaaaavv',...  3.87 us
    squeeze x1, local copies, waits for them, and re-layouts, body(): w_sib = [lax.ppermute(w_own[kind], 'mp', sibling) for kind in range(kinds)]  2.84 us
  transfers between devices with their start and end apart: 5, of which 1 were waited for; matrix products, arithmetic and copies ran while one was open for 3% of the time, Pallas kernels for 2%

profile of v5, /device:TPU:1, one launch (start us, length us, event | category | flops | bytes accessed | tf_op | source)
XLA Modules:
  0.0 105.7 jit_solution(6947666998594098902)
XLA Ops:
  0.0 2.1 %shard_map.82 = (bf16[16,152,128]{2,1,0:T(8,128)(2,1)}, bf16[152,256]{1,0:T(8,128)(2,1)S(1)}, f32[1,256]{1,0:T(1,128)S(1)}) custom-call(bf16[152,256]{1,0:T(8,128)(2,1)} %bitcast.41, s32[1,256]{1,0:T(1,128)} %bitcast.34), custom_call_target="tpu_custom_call" | custom-call | bytes 1048576 | tf_op jit(solution)/shard_map/pallas_call | solution.py:261
  2.1 11.8 %all-to-all-start = ((bf16[16,152,128]{2,1,0:T(8,128)(2,1)}), bf16[16,152,128]{2,1,0:T(8,128)(2,1)S(1)}, u32[]{:S(2)}, u32[]{:S(2)}) async-start(bf16[16,152,128]{2,1,0:T(8,128)(2,1)} %get-tuple-element.25), calls=%async_computation | async-start | bytes 1245184 | tf_op jit(solution)/shard_map/all_to_all | solution.py:274
  13.9 0.0 copy-start.5
  14.0 0.0 copy-start.4
  14.0 0.0 slice-start
  14.0 0.0 copy-start.2
  14.0 0.0 copy-start.3
  14.0 2.8 %slice_bitcast_fusion = (bf16[2432,128]{1,0:T(8,128)(2,1)}, bf16[2432,128]{1,0:T(8,128)(2,1)}, bf16[2432,128]{1,0:T(8,128)(2,1)}) fusion(bf16[3,2432,128]{2,1,0:T(8,128)(2,1)} %bitcast.38), kind=kLoop, calls=%fused_computation | loop fusion | bytes 3735552 | tf_op jit(solution)/shard_map/squeeze | solution.py:277
  16.9 2.0 %collective-permute-start = (bf16[2432,128]{1,0:T(8,128)(2,1)}, bf16[2432,128]{1,0:T(8,128)(2,1)}, u32[]{:S(2)}, u32[]{:S(2)}) collective-permute-start(bf16[2432,128]{1,0:T(8,128)(2,1)} %get-tuple-element.45), channel_id=1, source_target_pairs={{0,1},{1,0},{2,3},{3,2},{4,5},{5,4},{6,7},{7,6},{8,9},{9,8},{10,11... | collective-permute-start | bytes 1867784 | tf_op jit(solution)/shard_map/ppermute | solution.py:277
  18.9 2.3 %collective-permute-start.3 = (bf16[128,2432]{1,0:T(8,128)(2,1)S(1)}, bf16[128,2432]{1,0:T(8,128)(2,1)S(1)}, u32[]{:S(2)}, u32[]{:S(2)}) collective-permute-start(bf16[128,2432]{1,0:T(8,128)(2,1)S(1)} %copy-done.1), channel_id=1, source_target_pairs={{0,1},{1,0},{2,3},{3,2},{4,5},{5,4},{6,7},{7,6},{8,9},{9,8},{10,11... | collective-permute-start | bytes 1867784 | tf_op jit(solution)/shard_map/ppermute | solution.py:278
  21.2 2.0 %collective-permute-start.1 = (bf16[2432,128]{1,0:T(8,128)(2,1)}, bf16[2432,128]{1,0:T(8,128)(2,1)}, u32[]{:S(2)}, u32[]{:S(2)}) collective-permute-start(bf16[2432,128]{1,0:T(8,128)(2,1)} %get-tuple-element.44), channel_id=1, source_target_pairs={{0,1},{1,0},{2,3},{3,2},{4,5},{5,4},{6,7},{7,6},{8,9},{9,8},{10,11... | collective-permute-start | bytes 1867784 | tf_op jit(solution)/shard_map/ppermute | solution.py:277
  23.2 2.3 %collective-permute-start.2 = (bf16[2432,128]{1,0:T(8,128)(2,1)}, bf16[2432,128]{1,0:T(8,128)(2,1)}, u32[]{:S(2)}, u32[]{:S(2)}) collective-permute-start(bf16[2432,128]{1,0:T(8,128)(2,1)} %get-tuple-element.43), channel_id=1, source_target_pairs={{0,1},{1,0},{2,3},{3,2},{4,5},{5,4},{6,7},{7,6},{8,9},{9,8},{10,11... | collective-permute-start | bytes 1867784 | tf_op jit(solution)/shard_map/ppermute | solution.py:277
  25.6 0.1 tile.26
  25.7 0.1 tile.23
  25.7 0.0 copy-done.4
  25.8 0.0 slice-done
  25.8 0.1 dynamic-slice_bitcast_fusion.gate_ref
  25.9 0.0 copy-done.2
  25.9 2.0 %shard_map.84 = (bf16[2,2432,128]{2,1,0:T(8,128)(2,1)}, bf16[152,256]{1,0:T(8,128)(2,1)S(1)}, f32[1,128]{1,0:T(1,128)S(1)}) custom-call(s32[1]{0:T(128)} %bitcast.core_ref, s32[1,256]{1,0:T(1,128)S(1)} %bitcast.35, f32[1,256]{1,0:T(1,128)S(1)} %get-tuple-element.28.pos_ref, s32[1,32]{1,0:T(1,128)S(1)} %bitcast.37, bf16[3,28,2432]{2,1,0:T(8,128)(2,1)S(1)} %bitcast.30, ...), custom_call_target="tpu_custom_call" | custom-call | bytes 1048576 | tf_op jit(solution)/shard_map/pallas_call | solution.py:280
  27.9 0.0 collective-permute-done.3.sib_ref
  27.9 0.4 shard_map.83
  28.3 0.0 collective-permute-done.sib0_hbm
  28.3 0.0 collective-permute-done.1.sib1_hbm
  28.3 0.0 collective-permute-done.2.sib2_hbm
  28.4 4.9 %all-to-all-done.tok_ref = bf16[16,152,128]{2,1,0:T(8,128)(2,1)S(1)} async-done(((bf16[16,152,128]{2,1,0:T(8,128)(2,1)}), bf16[16,152,128]{2,1,0:T(8,128)(2,1)S(1)}, u32[]{:S(2)}, u32[]{:S(2)}) %all-to-all-start) | async-done | bytes 622624 | tf_op jit(solution)/shard_map/all_to_all | solution.py:274
  33.3 3.9 %shard_map.85 = bf16[2,256,384]{2,1,0:T(8,128)(2,1)S(1)} custom-call(s32[1]{0:T(128)} %bitcast.core_ref, bf16[16,152,128]{2,1,0:T(8,128)(2,1)S(1)} %all-to-all-done.tok_ref, bf16[2,2432,128]{2,1,0:T(8,128)(2,1)} %get-tuple-element.33.mod_hbm, bf16[3,2432,128]{2,1,0:T(8,128)(2,1)} %bitcast.39, bf16[2432,128]{1,0:T(8,128)(2,1)} %collective-permute-done.sib0_hbm, ...), custom_call_target="tpu_custom_call" | custom-call | flops 478150656 | bytes 1048576 | tf_op jit(solution)/shard_map/pallas_call | solution.py:296
  37.2 26.2 %all_to_all.20 = bf16[64,8,384]{2,1,0:T(8,128)(2,1)S(1)} all-to-all(bf16[64,8,384]{2,1,0:T(8,128)(2,1)S(1)} %bitcast.29), channel_id=1, replica_groups={{0,16,32,48,64,80,96,112,128,144,160,176,192,208,224,240,256,272,288,30..., dimensions={0} | all-to-all | bytes 786432 | tf_op jit(solution)/shard_map/all_to_all | solution.py:309
  63.3 1.7 %shard_map.86 = bf16[512,128]{1,0:T(8,128)(2,1)S(1)} custom-call(bf16[512,384]{1,0:T(8,128)(2,1)S(1)} %bitcast.32, bf16[2,384,128]{2,1,0:T(8,128)(2,1)S(1)} %pad.4.ctx_ref), custom_call_target="tpu_custom_call" | custom-call | flops 469762048 | bytes 1048576 | tf_op jit(solution)/shard_map/pallas_call | solution.py:312
  65.1 15.5 %all_to_all.21 = bf16[64,8,128]{2,1,0:T(8,128)(2,1)S(1)} all-to-all(bf16[64,8,128]{2,1,0:T(8,128)(2,1)S(1)} %bitcast.33), channel_id=1, replica_groups={{0,16,32,48,64,80,96,112,128,144,160,176,192,208,224,240,256,272,288,30..., dimensions={0} | all-to-all | bytes 262144 | tf_op jit(solution)/shard_map/all_to_all | solution.py:319
  80.6 0.7 shard_map.87
  81.3 23.5 %all_to_all.22.sums_ref = bf16[16,152,128]{2,1,0:T(8,128)(2,1)S(1)} all-to-all(bf16[16,152,128]{2,1,0:T(8,128)(2,1)S(1)} %shard_map.87), channel_id=1, replica_groups=mesh['dp'=32,'mp'=16] {'mp'}, dimensions={0} | all-to-all | bytes 1245184 | tf_op jit(solution)/shard_map/all_to_all | solution.py:325
  104.8 0.9 shard_map.88
  (12 shorter events, 0.1 us)
Async XLA Ops:
  2.1 31.2 %all-to-all-start = ((bf16[16,152,128]{2,1,0:T(8,128)(2,1)}), bf16[16,152,128]{2,1,0:T(8,128)(2,1)S(1)}, u32[]{:S(2)}, u32[]{:S(2)}) async-start(bf16[16,152,128]{2,1,0:T(8,128)(2,1)} %get-tuple-element.25), calls=%async_computation | async-start | bytes 1245184 | tf_op jit(solution)/shard_map/all_to_all | solution.py:274
  13.9 4.9 %copy-start.1 = (bf16[128,2432]{1,0:T(8,128)(2,1)S(1)}, bf16[128,2432]{1,0:T(8,128)(2,1)}, u32[]{:S(2)}) copy-start(bf16[128,2432]{1,0:T(8,128)(2,1)} %own_ref) | copy-start | bytes 1867780
  13.9 11.6 %copy-start.5 = (f32[2,64]{1,0:T(2,128)S(1)}, f32[2,64]{1,0:T(2,128)}, u32[]{:S(2)}) copy-start(f32[2,64]{1,0:T(2,128)} %param.13) | copy-start | bytes 1540
  14.0 11.8 %copy-start.4 = (bf16[1,2,333,128]{3,1,2,0:T(2,128)(2,1)S(1)}, bf16[1,2,333,128]{3,1,2,0:T(2,128)(2,1)}, u32[]{:S(2)}) copy-start(bf16[1,2,333,128]{3,1,2,0:T(2,128)(2,1)} %param.14) | copy-start | bytes 511492
  14.0 11.8 %slice-start = ((bf16[28,3,2432]{2,0,1:T(8,128)(2,1)}), bf16[28,1,2432]{2,0,1:T(8,128)(2,1)S(1)}, s32[]{:S(2)}) async-start(bf16[28,3,2432]{2,0,1:T(8,128)(2,1)} %param.11), calls=%async_computation.4 | async-start | bytes 311296 | tf_op jit(solution)/shard_map/slice | solution.py:279
  14.0 11.9 %copy-start = (bf16[28,3,2432]{2,0,1:T(8,128)(2,1)S(1)}, bf16[28,3,2432]{2,0,1:T(8,128)(2,1)}, u32[]{:S(2)}) copy-start(bf16[28,3,2432]{2,0,1:T(8,128)(2,1)} %param.11) | copy-start | bytes 1225732
  14.0 11.9 %copy-start.2 = (s32[256,1]{0,1:T(1,128)S(1)}, s32[256,1]{0,1:T(1,128)}, u32[]{:S(2)}) copy-start(s32[256,1]{0,1:T(1,128)} %param.9) | copy-start | bytes 3076
  14.0 11.9 %copy-start.3 = (s32[32]{0:T(128)S(1)}, s32[32]{0:T(128)}, u32[]{:S(2)}) copy-start(s32[32]{0:T(128)} %param.10) | copy-start | bytes 388
  16.9 11.5 %collective-permute-start = (bf16[2432,128]{1,0:T(8,128)(2,1)}, bf16[2432,128]{1,0:T(8,128)(2,1)}, u32[]{:S(2)}, u32[]{:S(2)}) collective-permute-start(bf16[2432,128]{1,0:T(8,128)(2,1)} %get-tuple-element.45), channel_id=1, source_target_pairs={{0,1},{1,0},{2,3},{3,2},{4,5},{5,4},{6,7},{7,6},{8,9},{9,8},{10,11... | collective-permute-start | bytes 1867784 | tf_op jit(solution)/shard_map/ppermute | solution.py:277
  18.9 9.0 %collective-permute-start.3 = (bf16[128,2432]{1,0:T(8,128)(2,1)S(1)}, bf16[128,2432]{1,0:T(8,128)(2,1)S(1)}, u32[]{:S(2)}, u32[]{:S(2)}) collective-permute-start(bf16[128,2432]{1,0:T(8,128)(2,1)S(1)} %copy-done.1), channel_id=1, source_target_pairs={{0,1},{1,0},{2,3},{3,2},{4,5},{5,4},{6,7},{7,6},{8,9},{9,8},{10,11... | collective-permute-start | bytes 1867784 | tf_op jit(solution)/shard_map/ppermute | solution.py:278
  21.2 7.1 %collective-permute-start.1 = (bf16[2432,128]{1,0:T(8,128)(2,1)}, bf16[2432,128]{1,0:T(8,128)(2,1)}, u32[]{:S(2)}, u32[]{:S(2)}) collective-permute-start(bf16[2432,128]{1,0:T(8,128)(2,1)} %get-tuple-element.44), channel_id=1, source_target_pairs={{0,1},{1,0},{2,3},{3,2},{4,5},{5,4},{6,7},{7,6},{8,9},{9,8},{10,11... | collective-permute-start | bytes 1867784 | tf_op jit(solution)/shard_map/ppermute | solution.py:277
  23.2 5.1 %collective-permute-start.2 = (bf16[2432,128]{1,0:T(8,128)(2,1)}, bf16[2432,128]{1,0:T(8,128)(2,1)}, u32[]{:S(2)}, u32[]{:S(2)}) collective-permute-start(bf16[2432,128]{1,0:T(8,128)(2,1)} %get-tuple-element.43), channel_id=1, source_target_pairs={{0,1},{1,0},{2,3},{3,2},{4,5},{5,4},{6,7},{7,6},{8,9},{9,8},{10,11... | collective-permute-start | bytes 1867784 | tf_op jit(solution)/shard_map/ppermute | solution.py:277

commit v6 on v5

--- a/solution.py
+++ b/solution.py
@@ -12,7 +12,6 @@
 DEAD = 1e30
 MASKED = -1e30
 VMEM_LIMIT = 24 * 1024 * 1024
-CHUNKS = 2
 F32, BF16, I32 = jnp.float32, jnp.bfloat16, jnp.int32
 
 
@@ -77,7 +76,7 @@
 
 
 def prepare_kernel(
-    cap, core_ref, req_ref, pos_ref, steps_ref, table_ref, gate_ref, mod_hbm, gates_ref, slot_ref, mod_ref, sem
+    cap, core_ref, req_ref, pos_ref, steps_ref, table_ref, gate_ref, mod_ref, gates_ref, slot_ref
 ):
     rows = req_ref.shape[1]
     half = rows // 2
@@ -104,44 +103,34 @@
     pick = jnp.where(is_first, pick[:, :half].astype(F32), pick[:, half:].astype(F32)).astype(BF16)
     mod_ref[0] = dot_tn(table_ref[0], pick).astype(BF16)
     mod_ref[1] = dot_tn(table_ref[1], pick).astype(BF16)
-    copy = pltpu.make_async_copy(mod_ref, mod_hbm, sem)
-    copy.start()
-    copy.wait()
-
-
-def flip_kernel(own_ref, sib_ref, out_ref):
+
+
+def flip_kernel(own_ref, sib_ref, out_hbm, out_ref, sem):
     inner, depth = own_ref.shape
     for start in range(0, depth, 128):
         for side, ref in enumerate((own_ref, sib_ref)):
             block = ref[:, start : start + 128].astype(F32).T
             out_ref[start : start + 128, side * inner : (side + 1) * inner] = block.astype(BF16)
+    copy = pltpu.make_async_copy(out_ref, out_hbm, sem)
+    copy.start()
+    copy.wait()
 
 
 def project_kernel(
-    core_ref, tok_ref, mod_hbm, own_hbm, sib0_hbm, sib1_hbm, sib2_hbm, gain_ref, slot_ref,
-    send_ref, mod_ref, w_ref, hid_ref, sems,
+    core_ref, tok_ref, mod_ref, own0_ref, own1_ref, own2_hbm, sib0_hbm, sib1_hbm, sib2_hbm, gain_ref, slot_ref,
+    send_ref, w_ref, hid_ref, sems,
 ):
     parts, width, rows = tok_ref.shape
     depth = parts * width
-    kinds, _, inner = own_hbm.shape
+    inner = own0_ref.shape[1]
+    kinds = 3
     span = kinds * inner
-    chunk = depth // CHUNKS
-    modulation = pltpu.make_async_copy(mod_hbm, mod_ref, sems.at[0])
-    modulation.start()
-    sources = [own_hbm.at[kind] for kind in range(kinds)] + [sib0_hbm, sib1_hbm, sib2_hbm]
-    weights = []
-    for step in range(CHUNKS):
-        lines = pl.ds(step * chunk, chunk)
-        weights.append(
-            [
-                pltpu.make_async_copy(
-                    source.at[lines], w_ref.at[lines, pl.ds(i * inner, inner)], sems.at[1 + step * len(sources) + i]
-                )
-                for i, source in enumerate(sources)
-            ]
-        )
-        for copy in weights[-1]:
-            copy.start()
+    weights = [
+        pltpu.make_async_copy(source, w_ref.at[:, pl.ds(i * inner, inner)], sems.at[i])
+        for i, source in enumerate((own2_hbm, sib0_hbm, sib1_hbm, sib2_hbm))
+    ]
+    for copy in weights:
+        copy.start()
     hits = iota((send_ref.shape[1], rows), 0).astype(F32) == slot_ref[...]
     filled = jnp.sum(jnp.where(hits, 1.0, 0.0), axis=1, keepdims=True)
     mark = jnp.where(filled > 0.5, 0.0, DEAD)
@@ -150,19 +139,16 @@
     mean = total * (1.0 / depth)
     square = sum(jnp.sum(jnp.square(tok_ref[m].astype(F32) - mean), axis=0, keepdims=True) for m in range(parts))
     inverse = lax.rsqrt(square * (1.0 / depth) + EPS)
-    modulation.wait()
     for m in range(0, parts, 2):
         pair = jnp.concatenate([tok_ref[m].astype(F32), tok_ref[m + 1].astype(F32)], axis=0)
         lines = pl.ds(m * width, 2 * width)
         shift, scale = mod_ref[0, lines, :].astype(F32), mod_ref[1, lines, :].astype(F32)
         hid_ref[lines, :] = ((pair - mean) * inverse * (1.0 + scale) + shift).astype(BF16)
-    proj = None
-    for step in range(CHUNKS):
-        for copy in weights[step]:
-            copy.wait()
-        lines = pl.ds(step * chunk, chunk)
-        part = dot_tn(hid_ref[lines, :], w_ref[lines, :])
-        proj = part if proj is None else proj + part
+    hidden = hid_ref[...]
+    start = dot_tn(hidden, jnp.concatenate([own0_ref[...], own1_ref[...]], axis=1))
+    for copy in weights:
+        copy.wait()
+    proj = jnp.concatenate([start, dot_tn(hidden, w_ref[...])], axis=1)
     normed = 2 * inner
     heads = one_hot(iota((normed, normed), 0) // HD == iota((normed, normed), 1) // HD)
     for side, target in enumerate((core_ref[0], 1 - core_ref[0])):
@@ -258,6 +244,9 @@
     def in_hbm(x):
         return pltpu.with_memory_space_constraint(x, pltpu.HBM)
 
+    def in_vmem(x):
+        return pltpu.with_memory_space_constraint(x, pltpu.VMEM)
+
     spread, perm, pos = call(
         spread_kernel,
         (pltpu.HBM((parts, width, half), BF16), shape((width, rows), BF16), shape((1, rows), F32)),
@@ -273,39 +262,43 @@
     spread, w_qkv, w_out = lax.optimization_barrier((spread, w_qkv, w_out))
     whole = lax.all_to_all(spread, "mp", 0, 0, tiled=True)
 
-    w_own = w_qkv.transpose(1, 0, 2)
-    w_sib = [lax.ppermute(w_own[kind], "mp", sibling) for kind in range(kinds)]
+    w_own = [w_qkv[:, kind] for kind in range(kinds)]
+    w_sib = [lax.ppermute(block, "mp", sibling) for block in w_own]
     out_sib = lax.ppermute(w_out, "mp", sibling)
     gate_table = lax.dynamic_slice_in_dim(mod_table[:, 2, :], lax.axis_index("mp") * width, width, 1)
     mod, gates, slot = call(
         functools.partial(prepare_kernel, cap),
-        (pltpu.HBM((2, depth, half), BF16), shape((width, rows), BF16), shape((1, half), F32)),
+        (pltpu.VMEM((2, depth, half), BF16), shape((width, rows), BF16), shape((1, half), F32)),
         "svvvvv",
-        "avv",
-        [pltpu.VMEM((2, depth, half), BF16), pltpu.SemaphoreType.DMA],
+        "vvv",
     )(core, req, pos, tsteps.reshape(1, requests), mod_table.transpose(1, 0, 2), gate_table)
-    w_back = call(flip_kernel, shape((depth, 2 * inner), BF16), "vv", "v")(w_out, out_sib)
+    w_back = call(
+        flip_kernel,
+        pltpu.HBM((depth, 2 * inner), BF16),
+        "vv",
+        "a",
+        [pltpu.VMEM((depth, 2 * inner), BF16), pltpu.SemaphoreType.DMA],
+    )(w_out, out_sib)
     gains = jnp.concatenate(
         [jnp.tile(qk_gain[0] * HD ** (-0.5), inner // HD), jnp.tile(qk_gain[1], inner // HD)]
     ).reshape(1, 2 * inner)
     text = jnp.pad(context[0], ((0, 0), (0, text_pad - text_len), (0, 0)))
-    whole, w_sib, w_back, mod, gates, slot, gains, text = lax.optimization_barrier(
-        (whole, w_sib, w_back, mod, gates, slot, gains, text)
+    whole, w_own, w_sib, w_back, mod, gates, slot, gains, text = lax.optimization_barrier(
+        (whole, w_own, w_sib, w_back, mod, gates, slot, gains, text)
     )
 
     send = call(
         project_kernel,
         shape((2, slots, kinds * inner), BF16),
-        "svaaaaavv",
+        "svvvvaaaavv",
         "v",
         [
-            pltpu.VMEM((2, depth, half), BF16),
-            pltpu.VMEM((depth, 2 * kinds * inner), BF16),
+            pltpu.VMEM((depth, 4 * inner), BF16),
             pltpu.VMEM((depth, half), BF16),
-            pltpu.SemaphoreType.DMA((1 + 2 * kinds * CHUNKS,)),
+            pltpu.SemaphoreType.DMA((4,)),
         ],
         flops=4 * depth * half * kinds * inner,
-    )(core, whole, in_hbm(mod), in_hbm(w_own), *[in_hbm(w) for w in w_sib], gains, slot)
+    )(core, whole, in_vmem(mod), *[in_vmem(w) for w in w_own[:2]], *[in_hbm(w) for w in w_own[2:] + w_sib], gains, slot)
     arrived = lax.all_to_all(
         send.reshape(2 * requests, cap, kinds * inner), ("dp", "mp"), 0, 0, axis_index_groups=planes, tiled=True
     )

time: 106 us -> 110 us (1.038)
  waiting for transfers between devices: 4.96 us -> 0.28 us
  blocking collectives: 65.2 us -> 69.3 us
  local copies, waits for them, and re-layouts: 3.18 us -> 6.01 us
    all_to_all x1, waiting for transfers between devices: 4.95 us -> 0.27 us  [body(): whole = lax.all_to_all(spread, 'mp', 0, 0, tiled=True)]
    all_to_all x1, blocking collectives: 23.5 us -> 27.5 us  [body(): sums = lax.all_to_all(partial, 'mp', 0, 0, tiled=True)]
    unnamed x13 -> x15, local copies, waits for them, and re-layouts: 0.06 us -> 2.14 us
  transfers between devices with their start and end apart: 5 -> 5, of which waited for: 1 -> 1; matrix products, arithmetic and copies ran while one was open for 3% -> 4% of each run, Pallas kernels for 2% -> 3%
where the time goes in v6:
time: 110 us
  blocking collectives  69.3 us (63%)
  starting transfers between devices  20.6 us (19%)
  Pallas kernels  12.4 us (11%)
  local copies, waits for them, and re-layouts  6.01 us (5%)
    all_to_all x1, blocking collectives, body(): sums = lax.all_to_all(partial, 'mp', 0, 0, tiled=True)  27.5 us
    all_to_all x1, blocking collectives, body(): lax.all_to_all(send.reshape(2 * requests, cap, kinds * inner), ('dp', 'mp...  26.3 us
    all_to_all x1, blocking collectives, body(): lax.all_to_all(attn.reshape(2 * requests, cap, inner), ('dp', 'mp'), 0, 0...  15.5 us
    all_to_all x1, starting transfers between devices, body(): whole = lax.all_to_all(spread, 'mp', 0, 0, tiled=True)  11.8 us
    ppermute x3, starting transfers between devices, body(): w_sib = [lax.ppermute(block, 'mp', sibling) for block in w_own]  6.63 us
    pallas_call x1, Pallas kernels, body(): call(project_kernel, shape((2, slots, kinds * inner), BF16), 'svvvvaaaavv...  3.63 us
    pallas_call x1, Pallas kernels, body(): call(flip_kernel, pltpu.HBM((depth, 2 * inner), BF16), 'vv', 'a', [pltpu....  2.55 us
    squeeze x1, local copies, waits for them, and re-layouts, body(): w_own = [w_qkv[:, kind] for kind in range(kinds)]  2.41 us
  transfers between devices with their start and end apart: 5, of which 1 were waited for; matrix products, arithmetic and copies ran while one was open for 4% of the time, Pallas kernels for 3%

profile of v6, /device:TPU:1, one launch (start us, length us, event | category | flops | bytes accessed | tf_op | source)
XLA Modules:
  0.0 109.6 jit_solution(3739211897052523559)
XLA Ops:
  0.0 2.1 %shard_map.82 = (bf16[16,152,128]{2,1,0:T(8,128)(2,1)}, bf16[152,256]{1,0:T(8,128)(2,1)S(1)}, f32[1,256]{1,0:T(1,128)S(1)}) custom-call(bf16[152,256]{1,0:T(8,128)(2,1)} %bitcast.38, s32[1,256]{1,0:T(1,128)} %bitcast.33), custom_call_target="tpu_custom_call" | custom-call | bytes 1048576 | tf_op jit(solution)/shard_map/pallas_call | solution.py:250
  2.1 11.8 %all-to-all-start = ((bf16[16,152,128]{2,1,0:T(8,128)(2,1)}), bf16[16,152,128]{2,1,0:T(8,128)(2,1)S(1)}, u32[]{:S(2)}, u32[]{:S(2)}) async-start(bf16[16,152,128]{2,1,0:T(8,128)(2,1)} %get-tuple-element.28), calls=%async_computation | async-start | bytes 1245184 | tf_op jit(solution)/shard_map/all_to_all | solution.py:263
  13.9 0.0 copy-start.5
  14.0 0.0 slice-start
  14.0 0.0 copy-start.3
  14.0 0.0 copy-start.4
  14.0 2.1 %collective-permute-start.3 = (bf16[128,2432]{1,0:T(8,128)(2,1)}, bf16[128,2432]{1,0:T(8,128)(2,1)}, u32[]{:S(2)}, u32[]{:S(2)}) collective-permute-start(bf16[128,2432]{1,0:T(8,128)(2,1)} %own_ref), channel_id=1, source_target_pairs={{0,1},{1,0},{2,3},{3,2},{4,5},{5,4},{6,7},{7,6},{8,9},{9,8},{10,11... | collective-permute-start | bytes 1867784 | tf_op jit(solution)/shard_map/ppermute | solution.py:267
  16.1 2.4 %slice_bitcast_fusion = (bf16[2432,128]{1,0:T(8,128)(2,1)}, bf16[2432,128]{1,0:T(8,128)(2,1)S(1)}, bf16[2432,128]{1,0:T(8,128)(2,1)S(1)}) fusion(bf16[2432,3,128]{2,0,1:T(8,128)(2,1)} %param.12), kind=kLoop, calls=%fused_computation | loop fusion | bytes 3735552 | tf_op jit(solution)/shard_map/squeeze | solution.py:265
  18.6 2.3 %collective-permute-start.2 = (bf16[2432,128]{1,0:T(8,128)(2,1)}, bf16[2432,128]{1,0:T(8,128)(2,1)}, u32[]{:S(2)}, u32[]{:S(2)}) collective-permute-start(bf16[2432,128]{1,0:T(8,128)(2,1)} %get-tuple-element.39.own2_hbm), channel_id=1, source_target_pairs={{0,1},{1,0},{2,3},{3,2},{4,5},{5,4},{6,7},{7,6},{8,9},{9,8},{10,11... | collective-permute-start | bytes 1867784 | tf_op jit(solution)/shard_map/ppermute | solution.py:266
  20.9 2.0 %collective-permute-start.1 = (bf16[2432,128]{1,0:T(8,128)(2,1)S(1)}, bf16[2432,128]{1,0:T(8,128)(2,1)}, u32[]{:S(2)}, u32[]{:S(2)}) collective-permute-start(bf16[2432,128]{1,0:T(8,128)(2,1)S(1)} %get-tuple-element.38.own1_ref), channel_id=1, source_target_pairs={{0,1},{1,0},{2,3},{3,2},{4,5},{5,4},{6,7},{7,6},{8,9},{9,8},{10,11... | collective-permute-start | bytes 1867784 | tf_op jit(solution)/shard_map/ppermute | solution.py:266
  22.9 2.3 %collective-permute-start = (bf16[2432,128]{1,0:T(8,128)(2,1)S(1)}, bf16[2432,128]{1,0:T(8,128)(2,1)}, u32[]{:S(2)}, u32[]{:S(2)}) collective-permute-start(bf16[2432,128]{1,0:T(8,128)(2,1)S(1)} %get-tuple-element.37.own0_ref), channel_id=1, source_target_pairs={{0,1},{1,0},{2,3},{3,2},{4,5},{5,4},{6,7},{7,6},{8,9},{9,8},{10,11... | collective-permute-start | bytes 1867784 | tf_op jit(solution)/shard_map/ppermute | solution.py:266
  25.3 0.7 tile.23
  25.9 0.7 tile.26
  26.7 0.1 dynamic-slice_bitcast_fusion.gate_ref
  26.8 0.0 copy-start.1
  26.8 1.0 copy-done.1
  27.8 0.9 shard_map.84
  28.7 0.7 pad_maximum_fusion
  29.4 0.0 collective-permute-done.3.sib_ref
  29.4 0.0 copy-start.2
  29.4 1.1 copy-done.2
  30.4 2.5 %shard_map.83 = bf16[2432,256]{1,0:T(8,128)(2,1)} custom-call(bf16[128,2432]{1,0:T(8,128)(2,1)S(1)} %copy-done.2, bf16[128,2432]{1,0:T(8,128)(2,1)} %collective-permute-done.3.sib_ref), custom_call_target="tpu_custom_call" | custom-call | bytes 1048576 | tf_op jit(solution)/shard_map/pallas_call | solution.py:275
  33.0 0.0 collective-permute-done.2.sib2_hbm
  33.0 0.0 collective-permute-done.sib0_hbm
  33.0 0.3 all-to-all-done.tok_ref
  33.3 3.6 %shard_map.85 = bf16[2,256,384]{2,1,0:T(8,128)(2,1)S(1)} custom-call(s32[1]{0:T(128)} %bitcast.core_ref, bf16[16,152,128]{2,1,0:T(8,128)(2,1)S(1)} %all-to-all-done.tok_ref, bf16[2,2432,128]{2,1,0:T(8,128)(2,1)S(1)} %get-tuple-element.36.mod_ref, bf16[2432,128]{1,0:T(8,128)(2,1)S(1)} %get-tuple-element.37.own0_ref, ...), custom_call_target="tpu_custom_call" | custom-call | flops 478150656 | bytes 1048576 | tf_op jit(solution)/shard_map/pallas_call | solution.py:290
  36.9 26.3 %all_to_all.20 = bf16[64,8,384]{2,1,0:T(8,128)(2,1)S(1)} all-to-all(bf16[64,8,384]{2,1,0:T(8,128)(2,1)S(1)} %bitcast.28), channel_id=1, replica_groups={{0,16,32,48,64,80,96,112,128,144,160,176,192,208,224,240,256,272,288,30..., dimensions={0} | all-to-all | bytes 786432 | tf_op jit(solution)/shard_map/all_to_all | solution.py:302
  63.2 1.7 %shard_map.86 = bf16[512,128]{1,0:T(8,128)(2,1)S(1)} custom-call(bf16[512,384]{1,0:T(8,128)(2,1)S(1)} %bitcast.31, bf16[2,384,128]{2,1,0:T(8,128)(2,1)S(1)} %pad.4.ctx_ref), custom_call_target="tpu_custom_call" | custom-call | flops 469762048 | bytes 1048576 | tf_op jit(solution)/shard_map/pallas_call | solution.py:305
  65.0 15.5 %all_to_all.21 = bf16[64,8,128]{2,1,0:T(8,128)(2,1)S(1)} all-to-all(bf16[64,8,128]{2,1,0:T(8,128)(2,1)S(1)} %bitcast.32), channel_id=1, replica_groups={{0,16,32,48,64,80,96,112,128,144,160,176,192,208,224,240,256,272,288,30..., dimensions={0} | all-to-all | bytes 262144 | tf_op jit(solution)/shard_map/all_to_all | solution.py:312
  80.5 0.7 shard_map.87
  81.2 27.5 %all_to_all.22.sums_ref = bf16[16,152,128]{2,1,0:T(8,128)(2,1)S(1)} all-to-all(bf16[16,152,128]{2,1,0:T(8,128)(2,1)S(1)} %shard_map.87), channel_id=1, replica_groups=mesh['dp'=32,'mp'=16] {'mp'}, dimensions={0} | all-to-all | bytes 1245184 | tf_op jit(solution)/shard_map/all_to_all | solution.py:318
  108.7 0.9 shard_map.88
  (14 shorter events, 0.1 us)
Async XLA Ops:
  2.1 31.2 %all-to-all-start = ((bf16[16,152,128]{2,1,0:T(8,128)(2,1)}), bf16[16,152,128]{2,1,0:T(8,128)(2,1)S(1)}, u32[]{:S(2)}, u32[]{:S(2)}) async-start(bf16[16,152,128]{2,1,0:T(8,128)(2,1)} %get-tuple-element.28), calls=%async_computation | async-start | bytes 1245184 | tf_op jit(solution)/shard_map/all_to_all | solution.py:263
  13.9 11.3 %copy-start.6 = (f32[2,64]{1,0:T(2,128)S(1)}, f32[2,64]{1,0:T(2,128)}, u32[]{:S(2)}) copy-start(f32[2,64]{1,0:T(2,128)} %param.13) | copy-start | bytes 1540
  13.9 12.7 %copy-start.5 = (bf16[1,2,333,128]{3,1,2,0:T(2,128)(2,1)S(1)}, bf16[1,2,333,128]{3,1,2,0:T(2,128)(2,1)}, u32[]{:S(2)}) copy-start(bf16[1,2,333,128]{3,1,2,0:T(2,128)(2,1)} %param.14) | copy-start | bytes 511492
  14.0 12.7 %slice-start = ((bf16[28,3,2432]{2,0,1:T(8,128)(2,1)}), bf16[28,1,2432]{2,0,1:T(8,128)(2,1)S(1)}, s32[]{:S(2)}) async-start(bf16[28,3,2432]{2,0,1:T(8,128)(2,1)} %param.11), calls=%async_computation.4 | async-start | bytes 311296 | tf_op jit(solution)/shard_map/slice | solution.py:268
  14.0 12.8 %copy-start.3 = (s32[256,1]{0,1:T(1,128)S(1)}, s32[256,1]{0,1:T(1,128)}, u32[]{:S(2)}) copy-start(s32[256,1]{0,1:T(1,128)} %param.9) | copy-start | bytes 3076
  14.0 12.8 %copy-start.4 = (s32[32]{0:T(128)S(1)}, s32[32]{0:T(128)}, u32[]{:S(2)}) copy-start(s32[32]{0:T(128)} %param.10) | copy-start | bytes 388
  14.0 15.4 %collective-permute-start.3 = (bf16[128,2432]{1,0:T(8,128)(2,1)}, bf16[128,2432]{1,0:T(8,128)(2,1)}, u32[]{:S(2)}, u32[]{:S(2)}) collective-permute-start(bf16[128,2432]{1,0:T(8,128)(2,1)} %own_ref), channel_id=1, source_target_pairs={{0,1},{1,0},{2,3},{3,2},{4,5},{5,4},{6,7},{7,6},{8,9},{9,8},{10,11... | collective-permute-start | bytes 1867784 | tf_op jit(solution)/shard_map/ppermute | solution.py:267
  18.6 14.4 %collective-permute-start.2 = (bf16[2432,128]{1,0:T(8,128)(2,1)}, bf16[2432,128]{1,0:T(8,128)(2,1)}, u32[]{:S(2)}, u32[]{:S(2)}) collective-permute-start(bf16[2432,128]{1,0:T(8,128)(2,1)} %get-tuple-element.39.own2_hbm), channel_id=1, source_target_pairs={{0,1},{1,0},{2,3},{3,2},{4,5},{5,4},{6,7},{7,6},{8,9},{9,8},{10,11... | collective-permute-start | bytes 1867784 | tf_op jit(solution)/shard_map/ppermute | solution.py:266
  20.9 12.1 %collective-permute-start.1 = (bf16[2432,128]{1,0:T(8,128)(2,1)S(1)}, bf16[2432,128]{1,0:T(8,128)(2,1)}, u32[]{:S(2)}, u32[]{:S(2)}) collective-permute-start(bf16[2432,128]{1,0:T(8,128)(2,1)S(1)} %get-tuple-element.38.own1_ref), channel_id=1, source_target_pairs={{0,1},{1,0},{2,3},{3,2},{4,5},{5,4},{6,7},{7,6},{8,9},{9,8},{10,11... | collective-permute-start | bytes 1867784 | tf_op jit(solution)/shard_map/ppermute | solution.py:266
  22.9 10.1 %collective-permute-start = (bf16[2432,128]{1,0:T(8,128)(2,1)S(1)}, bf16[2432,128]{1,0:T(8,128)(2,1)}, u32[]{:S(2)}, u32[]{:S(2)}) collective-permute-start(bf16[2432,128]{1,0:T(8,128)(2,1)S(1)} %get-tuple-element.37.own0_ref), channel_id=1, source_target_pairs={{0,1},{1,0},{2,3},{3,2},{4,5},{5,4},{6,7},{7,6},{8,9},{9,8},{10,11... | collective-permute-start | bytes 1867784 | tf_op jit(solution)/shard_map/ppermute | solution.py:266
  26.8 1.0 copy-start.1
  29.4 1.1 copy-start.2
  36.9 43.6 %copy-start = (bf16[2432,256]{1,0:T(8,128)(2,1)S(1)}, bf16[2432,256]{1,0:T(8,128)(2,1)}, u32[]{:S(2)}) copy-start(bf16[2432,256]{1,0:T(8,128)(2,1)} %shard_map.83) | copy-start | bytes 3735556

commit v7 on v5

--- a/solution.py
+++ b/solution.py
@@ -12,7 +12,6 @@
 DEAD = 1e30
 MASKED = -1e30
 VMEM_LIMIT = 24 * 1024 * 1024
-CHUNKS = 2
 F32, BF16, I32 = jnp.float32, jnp.bfloat16, jnp.int32
 
 
@@ -124,24 +123,15 @@
     parts, width, rows = tok_ref.shape
     depth = parts * width
     kinds, _, inner = own_hbm.shape
-    span = kinds * inner
-    chunk = depth // CHUNKS
     modulation = pltpu.make_async_copy(mod_hbm, mod_ref, sems.at[0])
     modulation.start()
     sources = [own_hbm.at[kind] for kind in range(kinds)] + [sib0_hbm, sib1_hbm, sib2_hbm]
-    weights = []
-    for step in range(CHUNKS):
-        lines = pl.ds(step * chunk, chunk)
-        weights.append(
-            [
-                pltpu.make_async_copy(
-                    source.at[lines], w_ref.at[lines, pl.ds(i * inner, inner)], sems.at[1 + step * len(sources) + i]
-                )
-                for i, source in enumerate(sources)
-            ]
-        )
-        for copy in weights[-1]:
-            copy.start()
+    weights = [
+        pltpu.make_async_copy(source, w_ref.at[i // kinds, :, pl.ds(i % kinds * inner, inner)], sems.at[1 + i])
+        for i, source in enumerate(sources)
+    ]
+    for copy in weights:
+        copy.start()
     hits = iota((send_ref.shape[1], rows), 0).astype(F32) == slot_ref[...]
     filled = jnp.sum(jnp.where(hits, 1.0, 0.0), axis=1, keepdims=True)
     mark = jnp.where(filled > 0.5, 0.0, DEAD)
@@ -156,17 +146,15 @@
         lines = pl.ds(m * width, 2 * width)
         shift, scale = mod_ref[0, lines, :].astype(F32), mod_ref[1, lines, :].astype(F32)
         hid_ref[lines, :] = ((pair - mean) * inverse * (1.0 + scale) + shift).astype(BF16)
-    proj = None
-    for step in range(CHUNKS):
-        for copy in weights[step]:
-            copy.wait()
-        lines = pl.ds(step * chunk, chunk)
-        part = dot_tn(hid_ref[lines, :], w_ref[lines, :])
-        proj = part if proj is None else proj + part
+    hidden = hid_ref[...].astype(F32).T.astype(BF16)
     normed = 2 * inner
     heads = one_hot(iota((normed, normed), 0) // HD == iota((normed, normed), 1) // HD)
-    for side, target in enumerate((core_ref[0], 1 - core_ref[0])):
-        mixed = proj[:, side * span : (side + 1) * span]
+    projected = []
+    for side in range(2):
+        for copy in weights[side * kinds : (side + 1) * kinds]:
+            copy.wait()
+        projected.append(jnp.dot(hidden, w_ref[side], preferred_element_type=F32))
+    for mixed, target in zip(projected, (core_ref[0], 1 - core_ref[0])):
         turned = mixed[:, :normed]
         power = jnp.square(turned)
         high = power.astype(BF16)
@@ -300,9 +288,9 @@
         "v",
         [
             pltpu.VMEM((2, depth, half), BF16),
-            pltpu.VMEM((depth, 2 * kinds * inner), BF16),
+            pltpu.VMEM((2, depth, kinds * inner), BF16),
             pltpu.VMEM((depth, half), BF16),
-            pltpu.SemaphoreType.DMA((1 + 2 * kinds * CHUNKS,)),
+            pltpu.SemaphoreType.DMA((1 + 2 * kinds,)),
         ],
         flops=4 * depth * half * kinds * inner,
     )(core, whole, in_hbm(mod), in_hbm(w_own), *[in_hbm(w) for w in w_sib], gains, slot)

time: 106 us -> 106 us (level)
  no operation moved by 1% of the time
where the time goes in v7:
time: 106 us; the launch traced here: 105 us
  blocking collectives  65.2 us (62%)
  starting transfers between devices  20.5 us (19%)
  Pallas kernels  11.1 us (10%)
  waiting for transfers between devices  4.96 us (5%)
  local copies, waits for them, and re-layouts  3.18 us (3%)
    all_to_all x1, blocking collectives, body(): lax.all_to_all(send.reshape(2 * requests, cap, kinds * inner), ('dp', 'mp...  26.2 us
    all_to_all x1, blocking collectives, body(): sums = lax.all_to_all(partial, 'mp', 0, 0, tiled=True)  23.5 us
    all_to_all x1, blocking collectives, body(): lax.all_to_all(attn.reshape(2 * requests, cap, inner), ('dp', 'mp'), 0, 0...  15.5 us
    all_to_all x1, starting transfers between devices, body(): whole = lax.all_to_all(spread, 'mp', 0, 0, tiled=True)  11.8 us
    ppermute x3, starting transfers between devices, body(): w_sib = [lax.ppermute(w_own[kind], 'mp', sibling) for kind in range(kinds)]  6.33 us
    all_to_all x1, waiting for transfers between devices, body(): whole = lax.all_to_all(spread, 'mp', 0, 0, tiled=True)  4.95 us
    pallas_call x1, Pallas kernels, body(): call(project_kernel, shape((2, slots, kinds * inner), BF16), 'svaaaaavv',...  3.32 us
    squeeze x1, local copies, waits for them, and re-layouts, body(): w_sib = [lax.ppermute(w_own[kind], 'mp', sibling) for kind in range(kinds)]  2.84 us
  transfers between devices with their start and end apart: 5, of which 1 were waited for; matrix products, arithmetic and copies ran while one was open for 3% of the time, Pallas kernels for 2%

profile of v7, /device:TPU:1, one launch (start us, length us, event | category | flops | bytes accessed | tf_op | source)
XLA Modules:
  0.0 105.1 jit_solution(12776687345001321647)
XLA Ops:
  0.0 2.1 %shard_map.82 = (bf16[16,152,128]{2,1,0:T(8,128)(2,1)}, bf16[152,256]{1,0:T(8,128)(2,1)S(1)}, f32[1,256]{1,0:T(1,128)S(1)}) custom-call(bf16[152,256]{1,0:T(8,128)(2,1)} %bitcast.41, s32[1,256]{1,0:T(1,128)} %bitcast.34), custom_call_target="tpu_custom_call" | custom-call | bytes 1048576 | tf_op jit(solution)/shard_map/pallas_call | solution.py:249
  2.1 11.8 %all-to-all-start = ((bf16[16,152,128]{2,1,0:T(8,128)(2,1)}), bf16[16,152,128]{2,1,0:T(8,128)(2,1)S(1)}, u32[]{:S(2)}, u32[]{:S(2)}) async-start(bf16[16,152,128]{2,1,0:T(8,128)(2,1)} %get-tuple-element.25), calls=%async_computation | async-start | bytes 1245184 | tf_op jit(solution)/shard_map/all_to_all | solution.py:262
  13.9 0.0 copy-start.5
  14.0 0.0 copy-start.4
  14.0 0.0 slice-start
  14.0 0.0 copy-start.2
  14.0 0.0 copy-start.3
  14.0 2.8 %slice_bitcast_fusion = (bf16[2432,128]{1,0:T(8,128)(2,1)}, bf16[2432,128]{1,0:T(8,128)(2,1)}, bf16[2432,128]{1,0:T(8,128)(2,1)}) fusion(bf16[3,2432,128]{2,1,0:T(8,128)(2,1)} %bitcast.38), kind=kLoop, calls=%fused_computation | loop fusion | bytes 3735552 | tf_op jit(solution)/shard_map/squeeze | solution.py:265
  16.9 2.0 %collective-permute-start = (bf16[2432,128]{1,0:T(8,128)(2,1)}, bf16[2432,128]{1,0:T(8,128)(2,1)}, u32[]{:S(2)}, u32[]{:S(2)}) collective-permute-start(bf16[2432,128]{1,0:T(8,128)(2,1)} %get-tuple-element.45), channel_id=1, source_target_pairs={{0,1},{1,0},{2,3},{3,2},{4,5},{5,4},{6,7},{7,6},{8,9},{9,8},{10,11... | collective-permute-start | bytes 1867784 | tf_op jit(solution)/shard_map/ppermute | solution.py:265
  18.9 2.3 %collective-permute-start.3 = (bf16[128,2432]{1,0:T(8,128)(2,1)S(1)}, bf16[128,2432]{1,0:T(8,128)(2,1)S(1)}, u32[]{:S(2)}, u32[]{:S(2)}) collective-permute-start(bf16[128,2432]{1,0:T(8,128)(2,1)S(1)} %copy-done.1), channel_id=1, source_target_pairs={{0,1},{1,0},{2,3},{3,2},{4,5},{5,4},{6,7},{7,6},{8,9},{9,8},{10,11... | collective-permute-start | bytes 1867784 | tf_op jit(solution)/shard_map/ppermute | solution.py:266
  21.2 2.0 %collective-permute-start.1 = (bf16[2432,128]{1,0:T(8,128)(2,1)}, bf16[2432,128]{1,0:T(8,128)(2,1)}, u32[]{:S(2)}, u32[]{:S(2)}) collective-permute-start(bf16[2432,128]{1,0:T(8,128)(2,1)} %get-tuple-element.44), channel_id=1, source_target_pairs={{0,1},{1,0},{2,3},{3,2},{4,5},{5,4},{6,7},{7,6},{8,9},{9,8},{10,11... | collective-permute-start | bytes 1867784 | tf_op jit(solution)/shard_map/ppermute | solution.py:265
  23.2 2.3 %collective-permute-start.2 = (bf16[2432,128]{1,0:T(8,128)(2,1)}, bf16[2432,128]{1,0:T(8,128)(2,1)}, u32[]{:S(2)}, u32[]{:S(2)}) collective-permute-start(bf16[2432,128]{1,0:T(8,128)(2,1)} %get-tuple-element.43), channel_id=1, source_target_pairs={{0,1},{1,0},{2,3},{3,2},{4,5},{5,4},{6,7},{7,6},{8,9},{9,8},{10,11... | collective-permute-start | bytes 1867784 | tf_op jit(solution)/shard_map/ppermute | solution.py:265
  25.6 0.1 tile.26
  25.7 0.1 tile.23
  25.7 0.0 copy-done.4
  25.8 0.0 slice-done
  25.8 0.1 dynamic-slice_bitcast_fusion.gate_ref
  25.9 0.0 copy-done.2
  25.9 2.0 %shard_map.84 = (bf16[2,2432,128]{2,1,0:T(8,128)(2,1)}, bf16[152,256]{1,0:T(8,128)(2,1)S(1)}, f32[1,128]{1,0:T(1,128)S(1)}) custom-call(s32[1]{0:T(128)} %bitcast.core_ref, s32[1,256]{1,0:T(1,128)S(1)} %bitcast.35, f32[1,256]{1,0:T(1,128)S(1)} %get-tuple-element.28.pos_ref, s32[1,32]{1,0:T(1,128)S(1)} %bitcast.37, bf16[3,28,2432]{2,1,0:T(8,128)(2,1)S(1)} %bitcast.30, ...), custom_call_target="tpu_custom_call" | custom-call | bytes 1048576 | tf_op jit(solution)/shard_map/pallas_call | solution.py:268
  27.9 0.0 collective-permute-done.3.sib_ref
  27.9 0.4 shard_map.83
  28.3 0.0 collective-permute-done.sib0_hbm
  28.3 0.0 collective-permute-done.1.sib1_hbm
  28.3 0.0 collective-permute-done.2.sib2_hbm
  28.4 4.9 %all-to-all-done.tok_ref = bf16[16,152,128]{2,1,0:T(8,128)(2,1)S(1)} async-done(((bf16[16,152,128]{2,1,0:T(8,128)(2,1)}), bf16[16,152,128]{2,1,0:T(8,128)(2,1)S(1)}, u32[]{:S(2)}, u32[]{:S(2)}) %all-to-all-start) | async-done | bytes 622624 | tf_op jit(solution)/shard_map/all_to_all | solution.py:262
  33.3 3.3 %shard_map.85 = bf16[2,256,384]{2,1,0:T(8,128)(2,1)S(1)} custom-call(s32[1]{0:T(128)} %bitcast.core_ref, bf16[16,152,128]{2,1,0:T(8,128)(2,1)S(1)} %all-to-all-done.tok_ref, bf16[2,2432,128]{2,1,0:T(8,128)(2,1)} %get-tuple-element.33.mod_hbm, bf16[3,2432,128]{2,1,0:T(8,128)(2,1)} %bitcast.39, bf16[2432,128]{1,0:T(8,128)(2,1)} %collective-permute-done.sib0_hbm, ...), custom_call_target="tpu_custom_call" | custom-call | flops 478150656 | bytes 1048576 | tf_op jit(solution)/shard_map/pallas_call | solution.py:284
  36.6 26.2 %all_to_all.20 = bf16[64,8,384]{2,1,0:T(8,128)(2,1)S(1)} all-to-all(bf16[64,8,384]{2,1,0:T(8,128)(2,1)S(1)} %bitcast.29), channel_id=1, replica_groups={{0,16,32,48,64,80,96,112,128,144,160,176,192,208,224,240,256,272,288,30..., dimensions={0} | all-to-all | bytes 786432 | tf_op jit(solution)/shard_map/all_to_all | solution.py:297
  62.8 1.7 %shard_map.86 = bf16[512,128]{1,0:T(8,128)(2,1)S(1)} custom-call(bf16[512,384]{1,0:T(8,128)(2,1)S(1)} %bitcast.32, bf16[2,384,128]{2,1,0:T(8,128)(2,1)S(1)} %pad.4.ctx_ref), custom_call_target="tpu_custom_call" | custom-call | flops 469762048 | bytes 1048576 | tf_op jit(solution)/shard_map/pallas_call | solution.py:300
  64.5 15.5 %all_to_all.21 = bf16[64,8,128]{2,1,0:T(8,128)(2,1)S(1)} all-to-all(bf16[64,8,128]{2,1,0:T(8,128)(2,1)S(1)} %bitcast.33), channel_id=1, replica_groups={{0,16,32,48,64,80,96,112,128,144,160,176,192,208,224,240,256,272,288,30..., dimensions={0} | all-to-all | bytes 262144 | tf_op jit(solution)/shard_map/all_to_all | solution.py:307
  80.1 0.7 shard_map.87
  80.8 23.5 %all_to_all.22.sums_ref = bf16[16,152,128]{2,1,0:T(8,128)(2,1)S(1)} all-to-all(bf16[16,152,128]{2,1,0:T(8,128)(2,1)S(1)} %shard_map.87), channel_id=1, replica_groups=mesh['dp'=32,'mp'=16] {'mp'}, dimensions={0} | all-to-all | bytes 1245184 | tf_op jit(solution)/shard_map/all_to_all | solution.py:313
  104.3 0.9 shard_map.88
  (12 shorter events, 0.1 us)
Async XLA Ops:
  2.1 31.2 %all-to-all-start = ((bf16[16,152,128]{2,1,0:T(8,128)(2,1)}), bf16[16,152,128]{2,1,0:T(8,128)(2,1)S(1)}, u32[]{:S(2)}, u32[]{:S(2)}) async-start(bf16[16,152,128]{2,1,0:T(8,128)(2,1)} %get-tuple-element.25), calls=%async_computation | async-start | bytes 1245184 | tf_op jit(solution)/shard_map/all_to_all | solution.py:262
  13.9 4.9 %copy-start.1 = (bf16[128,2432]{1,0:T(8,128)(2,1)S(1)}, bf16[128,2432]{1,0:T(8,128)(2,1)}, u32[]{:S(2)}) copy-start(bf16[128,2432]{1,0:T(8,128)(2,1)} %own_ref) | copy-start | bytes 1867780
  13.9 11.6 %copy-start.5 = (f32[2,64]{1,0:T(2,128)S(1)}, f32[2,64]{1,0:T(2,128)}, u32[]{:S(2)}) copy-start(f32[2,64]{1,0:T(2,128)} %param.13) | copy-start | bytes 1540
  14.0 11.8 %copy-start.4 = (bf16[1,2,333,128]{3,1,2,0:T(2,128)(2,1)S(1)}, bf16[1,2,333,128]{3,1,2,0:T(2,128)(2,1)}, u32[]{:S(2)}) copy-start(bf16[1,2,333,128]{3,1,2,0:T(2,128)(2,1)} %param.14) | copy-start | bytes 511492
  14.0 11.8 %slice-start = ((bf16[28,3,2432]{2,0,1:T(8,128)(2,1)}), bf16[28,1,2432]{2,0,1:T(8,128)(2,1)S(1)}, s32[]{:S(2)}) async-start(bf16[28,3,2432]{2,0,1:T(8,128)(2,1)} %param.11), calls=%async_computation.4 | async-start | bytes 311296 | tf_op jit(solution)/shard_map/slice | solution.py:267
  14.0 11.9 %copy-start = (bf16[28,3,2432]{2,0,1:T(8,128)(2,1)S(1)}, bf16[28,3,2432]{2,0,1:T(8,128)(2,1)}, u32[]{:S(2)}) copy-start(bf16[28,3,2432]{2,0,1:T(8,128)(2,1)} %param.11) | copy-start | bytes 1225732
  14.0 11.9 %copy-start.2 = (s32[256,1]{0,1:T(1,128)S(1)}, s32[256,1]{0,1:T(1,128)}, u32[]{:S(2)}) copy-start(s32[256,1]{0,1:T(1,128)} %param.9) | copy-start | bytes 3076
  14.0 11.9 %copy-start.3 = (s32[32]{0:T(128)S(1)}, s32[32]{0:T(128)}, u32[]{:S(2)}) copy-start(s32[32]{0:T(128)} %param.10) | copy-start | bytes 388
  16.9 11.5 %collective-permute-start = (bf16[2432,128]{1,0:T(8,128)(2,1)}, bf16[2432,128]{1,0:T(8,128)(2,1)}, u32[]{:S(2)}, u32[]{:S(2)}) collective-permute-start(bf16[2432,128]{1,0:T(8,128)(2,1)} %get-tuple-element.45), channel_id=1, source_target_pairs={{0,1},{1,0},{2,3},{3,2},{4,5},{5,4},{6,7},{7,6},{8,9},{9,8},{10,11... | collective-permute-start | bytes 1867784 | tf_op jit(solution)/shard_map/ppermute | solution.py:265
  18.9 9.0 %collective-permute-start.3 = (bf16[128,2432]{1,0:T(8,128)(2,1)S(1)}, bf16[128,2432]{1,0:T(8,128)(2,1)S(1)}, u32[]{:S(2)}, u32[]{:S(2)}) collective-permute-start(bf16[128,2432]{1,0:T(8,128)(2,1)S(1)} %copy-done.1), channel_id=1, source_target_pairs={{0,1},{1,0},{2,3},{3,2},{4,5},{5,4},{6,7},{7,6},{8,9},{9,8},{10,11... | collective-permute-start | bytes 1867784 | tf_op jit(solution)/shard_map/ppermute | solution.py:266
  21.2 7.1 %collective-permute-start.1 = (bf16[2432,128]{1,0:T(8,128)(2,1)}, bf16[2432,128]{1,0:T(8,128)(2,1)}, u32[]{:S(2)}, u32[]{:S(2)}) collective-permute-start(bf16[2432,128]{1,0:T(8,128)(2,1)} %get-tuple-element.44), channel_id=1, source_target_pairs={{0,1},{1,0},{2,3},{3,2},{4,5},{5,4},{6,7},{7,6},{8,9},{9,8},{10,11... | collective-permute-start | bytes 1867784 | tf_op jit(solution)/shard_map/ppermute | solution.py:265
  23.2 5.1 %collective-permute-start.2 = (bf16[2432,128]{1,0:T(8,128)(2,1)}, bf16[2432,128]{1,0:T(8,128)(2,1)}, u32[]{:S(2)}, u32[]{:S(2)}) collective-permute-start(bf16[2432,128]{1,0:T(8,128)(2,1)} %get-tuple-element.43), channel_id=1, source_target_pairs={{0,1},{1,0},{2,3},{3,2},{4,5},{5,4},{6,7},{7,6},{8,9},{9,8},{10,11... | collective-permute-start | bytes 1867784 | tf_op jit(solution)/shard_map/ppermute | solution.py:265

commit v8 on v7

--- a/solution.py
+++ b/solution.py
@@ -44,9 +44,12 @@
 
 
 def dealt(rows):
-    half = rows // 2
+    half, quarter = rows // 2, rows // 4
     place = iota((rows, rows), 0)
-    return jnp.where(place < half, 2 * place, 2 * (place - half) + 1).astype(F32)
+    core = jnp.where(place >= half, 1, 0)
+    place = place - half * core
+    parity = jnp.where(place >= quarter, 1, 0)
+    return (4 * (place - quarter * parity) + 2 * parity + core).astype(F32)
 
 
 def spread_kernel(tok_hbm, req_hbm, out_hbm, perm_ref, pos_ref, tok_ref, req_ref, halves_ref, sems):
@@ -91,9 +94,12 @@
     both = dot_nt(both, deal)
     req_s, first_s = both[0:1], both[1:2]
     index = iota((1, rows), 1)
-    odd = jnp.where(index >= half, 1, 0)
-    start = jnp.floor((first_s - odd.astype(F32) + 1.0) * 0.5)
-    slot = req_s * cap + (index - half * odd).astype(F32) - start
+    side = jnp.where(index >= half, 1, 0)
+    index = index - half * side
+    parity = jnp.where(index >= half // 2, 1, 0)
+    index = (index - half // 2 * parity).astype(F32)
+    start = jnp.floor((first_s - (2 * parity + side).astype(F32) + 3.0) * 0.25)
+    slot = req_s * cap + (parity * (cap // 2)).astype(F32) + index - start
     slot_ref[...] = jnp.where(is_first, slot[:, :half], slot[:, half:])
     chosen = one_hot(iota((requests, rows), 0).astype(F32) == req_s)
     steps = jnp.broadcast_to(steps_ref[...].astype(F32), (8, requests)).astype(BF16)
@@ -108,12 +114,21 @@
     copy.wait()
 
 
-def flip_kernel(own_ref, sib_ref, out_ref):
-    inner, depth = own_ref.shape
-    for start in range(0, depth, 128):
-        for side, ref in enumerate((own_ref, sib_ref)):
-            block = ref[:, start : start + 128].astype(F32).T
-            out_ref[start : start + 128, side * inner : (side + 1) * inner] = block.astype(BF16)
+def flip_kernel(*refs):
+    sources, (out_ref, *held, sems) = refs[:4], refs[4:]
+    inner, depth = held[0].shape
+    parts, padded, _ = out_ref.shape
+    width = depth // parts
+    reads = [pltpu.make_async_copy(source, ref, sems.at[i]) for i, (source, ref) in enumerate(zip(sources, held))]
+    for copy in reads:
+        copy.start()
+    for m in range(parts):
+        out_ref[m, width:, :] = jnp.zeros((padded - width, out_ref.shape[2]), BF16)
+    for i, ref in enumerate(held):
+        reads[i].wait()
+        turned = ref[...].astype(F32).T
+        for m in range(parts):
+            out_ref[m, :width, i * inner : (i + 1) * inner] = turned[m * width : (m + 1) * width].astype(BF16)
 
 
 def project_kernel(
@@ -193,23 +208,38 @@
         out_ref[row : row + block, :] = jnp.where(first, mixed[:block], mixed[block:]).astype(BF16)
 
 
-def output_kernel(core_ref, back_ref, slot_ref, w_ref, part_ref):
-    core = core_ref[0]
-    slots, rows = back_ref.shape[1], slot_ref.shape[1]
-    place_t = one_hot(iota((rows, slots), 1).astype(F32) == as_column(slot_ref[...]))
-    own = jnp.dot(place_t, back_ref[core], preferred_element_type=F32).astype(BF16)
-    sib = jnp.dot(place_t, back_ref[1 - core], preferred_element_type=F32).astype(BF16)
-    attn = jnp.concatenate([own, sib], axis=1)
+def output_kernel(sub_slots, core_ref, parity_ref, back_ref, slot_ref, w_ref, part_ref):
+    core, parity = core_ref[0], parity_ref[0]
+    slots, inner = back_ref.shape[1:]
+    quarter = slot_ref.shape[1] // 2
+    upper = part_ref.shape[1]
+    slot = slot_ref[...]
+    slot = as_column(jnp.where(parity == 0, slot[:, :quarter], slot[:, quarter:]))
+    shift = (sub_slots * (1 - 2 * parity)).astype(F32)
+    attn = []
+    for moved in (slot, slot + shift):
+        place_t = one_hot(iota((quarter, slots), 1).astype(F32) == moved)
+        for side in (core, 1 - core):
+            attn.append(jnp.dot(place_t, back_ref[side], preferred_element_type=F32).astype(BF16))
+    attn = jnp.concatenate(attn, axis=1)
+    empty = jnp.zeros(attn.shape, BF16)
+    left, right = jnp.concatenate([attn, empty], axis=0), jnp.concatenate([empty, attn], axis=0)
     for m in range(part_ref.shape[0]):
-        part_ref[m] = dot_nt(w_ref[m], attn).astype(BF16)
+        part_ref[m] = (dot_nt(w_ref[m, :upper], left) + dot_nt(w_ref[m, upper:], right)).astype(BF16)
 
 
 def finish_kernel(sums_ref, perm_ref, gates_ref, pos_ref, out_ref):
-    parts = sums_ref.shape[0]
-    halves = [sum(sums_ref[m].astype(F32) for m in range(c, parts, 2)) for c in range(2)]
+    parts, upper, lanes = sums_ref.shape
+    width, rows = perm_ref.shape
+    halves = []
+    first = iota((1, lanes), 1) < lanes // 2
+    for core in range(2):
+        even, odd = [sum(sums_ref[m].astype(F32) for m in range(2 * p + core, parts, 4)) for p in range(2)]
+        above = jnp.where(first, even, pltpu.roll(odd, lanes // 2, 1))
+        below = jnp.where(first, pltpu.roll(even, lanes // 2, 1), odd)
+        halves.append(jnp.concatenate([above, below[: width - upper]], axis=0))
     total = jnp.concatenate(halves, axis=1)
     mixed = (perm_ref[...].astype(F32) + gates_ref[...].astype(F32) * total).astype(BF16)
-    rows = perm_ref.shape[1]
     deal = one_hot(pos_ref[...] == dealt(rows))
     out_ref[...] = jnp.dot(mixed, deal, preferred_element_type=F32).astype(BF16)
 
@@ -239,7 +269,14 @@
     text_pad = -(-text_len // 128) * 128
     sibling = [(i, i ^ 1) for i in range(parts)]
     planes = [[dp * parts + 2 * z + c for c in range(2) for dp in range(requests)] for z in range(chips)]
-    core = lax.rem(lax.axis_index("mp"), 2).astype(I32).reshape(1)
+    pairs = [
+        [dp * parts + 2 * z + c for c in range(2) for dp in range(requests) for z in (even, even + 1)]
+        for even in range(0, chips, 2)
+    ]
+    upper = -(-width // 32) * 16
+    place = lax.axis_index("mp").astype(I32)
+    core = lax.rem(place, 2).reshape(1)
+    parity = lax.rem(lax.div(place, 2), 2).reshape(1)
     shape = jax.ShapeDtypeStruct
 
     req = route.reshape(1, rows)
@@ -258,12 +295,11 @@
             pltpu.SemaphoreType.DMA((2 + parts,)),
         ],
     )(in_hbm(tokens.T), in_hbm(req))
-    spread, w_qkv, w_out = lax.optimization_barrier((spread, w_qkv, w_out))
+    spread, w_qkv = lax.optimization_barrier((spread, w_qkv))
     whole = lax.all_to_all(spread, "mp", 0, 0, tiled=True)
 
     w_own = w_qkv.transpose(1, 0, 2)
     w_sib = [lax.ppermute(w_own[kind], "mp", sibling) for kind in range(kinds)]
-    out_sib = lax.ppermute(w_out, "mp", sibling)
     gate_table = lax.dynamic_slice_in_dim(mod_table[:, 2, :], lax.axis_index("mp") * width, width, 1)
     mod, gates, slot = call(
         functools.partial(prepare_kernel, cap),
@@ -272,13 +308,12 @@
         "avv",
         [pltpu.VMEM((2, depth, half), BF16), pltpu.SemaphoreType.DMA],
     )(core, req, pos, tsteps.reshape(1, requests), mod_table.transpose(1, 0, 2), gate_table)
-    w_back = call(flip_kernel, shape((depth, 2 * inner), BF16), "vv", "v")(w_out, out_sib)
     gains = jnp.concatenate(
         [jnp.tile(qk_gain[0] * HD ** (-0.5), inner // HD), jnp.tile(qk_gain[1], inner // HD)]
     ).reshape(1, 2 * inner)
     text = jnp.pad(context[0], ((0, 0), (0, text_pad - text_len), (0, 0)))
-    whole, w_sib, w_back, mod, gates, slot, gains, text = lax.optimization_barrier(
-        (whole, w_sib, w_back, mod, gates, slot, gains, text)
+    whole, w_sib, mod, gates, slot, gains, text = lax.optimization_barrier(
+        (whole, w_sib, mod, gates, slot, gains, text)
     )
 
     send = call(
@@ -294,9 +329,11 @@
         ],
         flops=4 * depth * half * kinds * inner,
     )(core, whole, in_hbm(mod), in_hbm(w_own), *[in_hbm(w) for w in w_sib], gains, slot)
+    send, w_out = lax.optimization_barrier((send, w_out))
     arrived = lax.all_to_all(
         send.reshape(2 * requests, cap, kinds * inner), ("dp", "mp"), 0, 0, axis_index_groups=planes, tiled=True
     )
+    w_outs = [lax.ppermute(w_out, "mp", [(i, i ^ step) for i in range(parts)]) for step in (1, 2, 3)]
     attn = call(
         functools.partial(attend_kernel, text_len),
         shape((2 * slots, inner), BF16),
@@ -305,11 +342,23 @@
         flops=16 * slots * (2 * slots + text_pad) * inner,
     )(arrived.reshape(2 * slots, kinds * inner), text)
     returned = lax.all_to_all(
-        attn.reshape(2 * requests, cap, inner), ("dp", "mp"), 0, 0, axis_index_groups=planes, tiled=True
-    )
+        attn.reshape(4 * requests, cap // 2, inner), ("dp", "mp"), 0, 0, axis_index_groups=pairs, tiled=True
+    )
+    _, w_out, w_outs = lax.optimization_barrier((attn, w_out, w_outs))
+    w_back = call(
+        flip_kernel,
+        shape((parts, 2 * upper, 4 * inner), BF16),
+        "aaaa",
+        "v",
+        [pltpu.VMEM((inner, depth), BF16)] * 4 + [pltpu.SemaphoreType.DMA((4,))],
+    )(*[in_hbm(w) for w in (w_out, *w_outs)])
     partial = call(
-        output_kernel, shape((parts, width, half), BF16), "svvv", "v", flops=4 * depth * half * inner
-    )(core, returned.reshape(2, slots, inner), slot, w_back.reshape(parts, width, 2 * inner))
+        functools.partial(output_kernel, cap // 2),
+        shape((parts, upper, half), BF16),
+        "ssvvv",
+        "v",
+        flops=8 * depth * half * inner,
+    )(core, parity, returned.reshape(2, slots, inner), slot, w_back)
     sums = lax.all_to_all(partial, "mp", 0, 0, tiled=True)
     return call(finish_kernel, shape((width, rows), BF16), "vvvv", "v")(sums, perm, gates, pos).T
 

time: 106 us -> 103 us (0.972)
  blocking collectives: 65.2 us -> 16.3 us
  starting transfers between devices: 20.5 us -> 43.3 us
  waiting for transfers between devices: 4.96 us -> 23.8 us
  Pallas kernels: 11.1 us -> 14.9 us
    all_to_all x2 -> x0, blocking collectives: 41.7 us -> none  [the longest x1 26.2 us: body(): lax.all_to_all(send.reshape(2 * requests, cap, kinds * inner), ('dp', 'mp...]
    all_to_all x0 -> x2, starting transfers between devices: none -> 17.3 us  [the longest x1 10.3 us: body(): lax.all_to_all(send.reshape(2 * requests, cap, kinds * inner), ('dp', 'mp...]
    all_to_all x0 -> x2, waiting for transfers between devices: none -> 8.93 us  [the longest x1 8.12 us: body(): lax.all_to_all(send.reshape(2 * requests, cap, kinds * inner), ('dp', 'mp...]
    all_to_all x1, blocking collectives: 23.5 us -> 16.3 us  [body(): sums = lax.all_to_all(partial, 'mp', 0, 0, tiled=True)]
    ppermute x1 -> x3, waiting for transfers between devices: 0.01 us -> 6.82 us  [body(): lax.ppermute(w_out, 'mp', [(i, i ^ step) for i in range(parts)])]
    ppermute x1 -> x3, starting transfers between devices: 2.31 us -> 7.87 us  [body(): lax.ppermute(w_out, 'mp', [(i, i ^ step) for i in range(parts)])]
    all_to_all x1, waiting for transfers between devices: 4.95 us -> 8.05 us  [body(): whole = lax.all_to_all(spread, 'mp', 0, 0, tiled=True)]
    pallas_call x2, Pallas kernels: 1.11 us -> 3.47 us  [the longest x1 2.07 us: body(): call(flip_kernel, shape((parts, 2 * upper, 4 * inner), BF16), 'aaaa', 'v'...]
  transfers between devices with their start and end apart: 5 -> 9, of which waited for: 1 -> 4; matrix products, arithmetic and copies ran while one was open for 3% -> 3% of each run, Pallas kernels for 2% -> 6%
where the time goes in v8:
time: 103 us; the launch traced here: 102 us
  starting transfers between devices  43.3 us (42%)
  waiting for transfers between devices  23.8 us (23%)
  blocking collectives  16.3 us (16%)
  Pallas kernels  14.9 us (14%)
  local copies, waits for them, and re-layouts  3.68 us (4%)
    all_to_all x1, blocking collectives, body(): sums = lax.all_to_all(partial, 'mp', 0, 0, tiled=True)  16.3 us
    all_to_all x1, starting transfers between devices, body(): whole = lax.all_to_all(spread, 'mp', 0, 0, tiled=True)  11.8 us
    all_to_all x1, starting transfers between devices, body(): lax.all_to_all(send.reshape(2 * requests, cap, kinds * inner), ('dp', 'mp...  10.3 us
    all_to_all x1, waiting for transfers between devices, body(): lax.all_to_all(send.reshape(2 * requests, cap, kinds * inner), ('dp', 'mp...  8.12 us
    all_to_all x1, waiting for transfers between devices, body(): whole = lax.all_to_all(spread, 'mp', 0, 0, tiled=True)  8.05 us
    ppermute x3, starting transfers between devices, body(): lax.ppermute(w_out, 'mp', [(i, i ^ step) for i in range(parts)])  7.87 us
    all_to_all x1, starting transfers between devices, body(): lax.all_to_all(attn.reshape(4 * requests, cap // 2, inner), ('dp', 'mp'),...  6.95 us
    ppermute x3, waiting for transfers between devices, body(): lax.ppermute(w_out, 'mp', [(i, i ^ step) for i in range(parts)])  6.82 us
  transfers between devices with their start and end apart: 9, of which 4 were waited for; matrix products, arithmetic and copies ran while one was open for 3% of the time, Pallas kernels for 6%

profile of v8, /device:TPU:1, one launch (start us, length us, event | category | flops | bytes accessed | tf_op | source)
XLA Modules:
  0.0 102.3 jit_solution(8234105175171810072)
XLA Ops:
  0.0 2.1 %shard_map.82 = (bf16[16,152,128]{2,1,0:T(8,128)(2,1)}, bf16[152,256]{1,0:T(8,128)(2,1)S(1)}, f32[1,256]{1,0:T(1,128)S(1)}) custom-call(bf16[152,256]{1,0:T(8,128)(2,1)} %bitcast.38, s32[1,256]{1,0:T(1,128)} %bitcast.31), custom_call_target="tpu_custom_call" | custom-call | bytes 1048576 | tf_op jit(solution)/shard_map/pallas_call | solution.py:286
  2.1 11.8 %all-to-all-start = ((bf16[16,152,128]{2,1,0:T(8,128)(2,1)}), bf16[16,152,128]{2,1,0:T(8,128)(2,1)S(1)}, u32[]{:S(2)}, u32[]{:S(2)}) async-start(bf16[16,152,128]{2,1,0:T(8,128)(2,1)} %get-tuple-element.29), calls=%async_computation | async-start | bytes 1245184 | tf_op jit(solution)/shard_map/all_to_all | solution.py:299
  13.9 0.0 copy-start.6
  14.0 0.0 slice-start
  14.0 0.0 copy-start.1
  14.0 0.0 copy-start.2
  14.0 2.5 %slice_bitcast_fusion = (bf16[2432,128]{1,0:T(8,128)(2,1)}, bf16[2432,128]{1,0:T(8,128)(2,1)S(1)}, bf16[2432,128]{1,0:T(8,128)(2,1)S(1)}) fusion(bf16[3,2432,128]{2,1,0:T(8,128)(2,1)} %bitcast.35), kind=kLoop, calls=%fused_computation | loop fusion | bytes 3735552 | tf_op jit(solution)/shard_map/squeeze | solution.py:302
  16.5 2.0 %collective-permute-start.2 = (bf16[2432,128]{1,0:T(8,128)(2,1)}, bf16[2432,128]{1,0:T(8,128)(2,1)}, u32[]{:S(2)}, u32[]{:S(2)}) collective-permute-start(bf16[2432,128]{1,0:T(8,128)(2,1)} %get-tuple-element.51), channel_id=1, source_target_pairs={{0,1},{1,0},{2,3},{3,2},{4,5},{5,4},{6,7},{7,6},{8,9},{9,8},{10,11... | collective-permute-start | bytes 1867784 | tf_op jit(solution)/shard_map/ppermute | solution.py:302
  18.5 2.3 %collective-permute-start.1 = (bf16[2432,128]{1,0:T(8,128)(2,1)S(1)}, bf16[2432,128]{1,0:T(8,128)(2,1)}, u32[]{:S(2)}, u32[]{:S(2)}) collective-permute-start(bf16[2432,128]{1,0:T(8,128)(2,1)S(1)} %get-tuple-element.52), channel_id=1, source_target_pairs={{0,1},{1,0},{2,3},{3,2},{4,5},{5,4},{6,7},{7,6},{8,9},{9,8},{10,11... | collective-permute-start | bytes 1867784 | tf_op jit(solution)/shard_map/ppermute | solution.py:302
  20.8 2.0 %collective-permute-start = (bf16[2432,128]{1,0:T(8,128)(2,1)S(1)}, bf16[2432,128]{1,0:T(8,128)(2,1)}, u32[]{:S(2)}, u32[]{:S(2)}) collective-permute-start(bf16[2432,128]{1,0:T(8,128)(2,1)S(1)} %get-tuple-element.53), channel_id=1, source_target_pairs={{0,1},{1,0},{2,3},{3,2},{4,5},{5,4},{6,7},{7,6},{8,9},{9,8},{10,11... | collective-permute-start | bytes 1867784 | tf_op jit(solution)/shard_map/ppermute | solution.py:302
  22.9 0.1 tile.23
  23.0 0.1 tile.26
  23.1 0.1 dynamic-slice_bitcast_fusion.gate_ref
  23.2 2.0 %shard_map.83 = (bf16[2,2432,128]{2,1,0:T(8,128)(2,1)}, bf16[152,256]{1,0:T(8,128)(2,1)S(1)}, f32[1,128]{1,0:T(1,128)S(1)}) custom-call(s32[1]{0:T(128)} %bitcast.core_ref, s32[1,256]{1,0:T(1,128)S(1)} %bitcast.32, f32[1,256]{1,0:T(1,128)S(1)} %get-tuple-element.31.pos_ref, s32[1,32]{1,0:T(1,128)S(1)} %bitcast.34, bf16[3,28,2432]{2,1,0:T(8,128)(2,1)S(1)} %bitcast.28, ...), custom_call_target="tpu_custom_call" | custom-call | bytes 1048576 | tf_op jit(solution)/shard_map/pallas_call | solution.py:304
  25.2 0.0 collective-permute-done.sib0_hbm
  25.3 8.1 %all-to-all-done.tok_ref = bf16[16,152,128]{2,1,0:T(8,128)(2,1)S(1)} async-done(((bf16[16,152,128]{2,1,0:T(8,128)(2,1)}), bf16[16,152,128]{2,1,0:T(8,128)(2,1)S(1)}, u32[]{:S(2)}, u32[]{:S(2)}) %all-to-all-start) | async-done | bytes 622624 | tf_op jit(solution)/shard_map/all_to_all | solution.py:299
  33.3 4.1 %shard_map.84 = bf16[2,256,384]{2,1,0:T(8,128)(2,1)} custom-call(s32[1]{0:T(128)} %bitcast.core_ref, bf16[16,152,128]{2,1,0:T(8,128)(2,1)S(1)} %all-to-all-done.tok_ref, bf16[2,2432,128]{2,1,0:T(8,128)(2,1)} %get-tuple-element.36.mod_hbm, bf16[3,2432,128]{2,1,0:T(8,128)(2,1)} %bitcast.36, bf16[2432,128]{1,0:T(8,128)(2,1)} %collective-permute-done.sib0_hbm, ...), custom_call_target="tpu_custom_call" | custom-call | flops 478150656 | bytes 1048576 | tf_op jit(solution)/shard_map/pallas_call | solution.py:319
  37.4 10.3 %all-to-all-start.1 = ((bf16[64,8,384]{2,1,0:T(8,128)(2,1)}), bf16[64,8,384]{2,1,0:T(8,128)(2,1)S(1)}, u32[]{:S(2)}, u32[]{:S(2)}) async-start(bf16[64,8,384]{2,1,0:T(8,128)(2,1)} %bitcast.15), calls=%async_computation.1 | async-start | bytes 786432 | tf_op jit(solution)/shard_map/all_to_all | solution.py:333
  47.8 1.9 %collective-permute-start.5 = (bf16[128,2432]{1,0:T(8,128)(2,1)S(1)}, bf16[128,2432]{1,0:T(8,128)(2,1)S(1)}, u32[]{:S(2)}, u32[]{:S(2)}) collective-permute-start(bf16[128,2432]{1,0:T(8,128)(2,1)S(1)} %copy-done.3), channel_id=1, source_target_pairs={{0,3},{1,2},{2,1},{3,0},{4,7},{5,6},{6,5},{7,4},{8,11},{9,10},{10,... | collective-permute-start | bytes 1867784 | tf_op jit(solution)/shard_map/ppermute | solution.py:336
  49.7 3.6 %collective-permute-start.4 = (bf16[128,2432]{1,0:T(8,128)(2,1)S(1)}, bf16[128,2432]{1,0:T(8,128)(2,1)S(1)}, u32[]{:S(2)}, u32[]{:S(2)}) collective-permute-start(bf16[128,2432]{1,0:T(8,128)(2,1)S(1)} %copy-done.3), channel_id=1, source_target_pairs={{0,2},{1,3},{2,0},{3,1},{4,6},{5,7},{6,4},{7,5},{8,10},{9,11},{10,... | collective-permute-start | bytes 1867784 | tf_op jit(solution)/shard_map/ppermute | solution.py:336
  53.3 2.3 %collective-permute-start.3 = (bf16[128,2432]{1,0:T(8,128)(2,1)S(1)}, bf16[128,2432]{1,0:T(8,128)(2,1)}, u32[]{:S(2)}, u32[]{:S(2)}) collective-permute-start(bf16[128,2432]{1,0:T(8,128)(2,1)S(1)} %copy-done.3), channel_id=1, source_target_pairs={{0,1},{1,0},{2,3},{3,2},{4,5},{5,4},{6,7},{7,6},{8,9},{9,8},{10,11... | collective-permute-start | bytes 1867784 | tf_op jit(solution)/shard_map/ppermute | solution.py:336
  55.7 8.1 %all-to-all-done.1 = bf16[64,8,384]{2,1,0:T(8,128)(2,1)S(1)} async-done(((bf16[64,8,384]{2,1,0:T(8,128)(2,1)}), bf16[64,8,384]{2,1,0:T(8,128)(2,1)S(1)}, u32[]{:S(2)}, u32[]{:S(2)}) %all-to-all-start.1) | async-done | bytes 393248 | tf_op jit(solution)/shard_map/all_to_all | solution.py:333
  63.8 2.4 %shard_map.85 = bf16[512,128]{1,0:T(8,128)(2,1)} custom-call(bf16[512,384]{1,0:T(8,128)(2,1)S(1)} %bitcast.30, bf16[2,384,128]{2,1,0:T(8,128)(2,1)S(1)} %pad.4.ctx_ref), custom_call_target="tpu_custom_call" | custom-call | flops 469762048 | bytes 1048576 | tf_op jit(solution)/shard_map/pallas_call | solution.py:337
  66.2 6.9 %all-to-all-start.2 = ((bf16[128,4,128]{2,1,0:T(4,128)(2,1)}), bf16[128,4,128]{2,1,0:T(4,128)(2,1)S(1)}, u32[]{:S(2)}, u32[]{:S(2)}) async-start(bf16[128,4,128]{2,1,0:T(4,128)(2,1)} %bitcast.17), calls=%async_computation.2 | async-start | bytes 262144 | tf_op jit(solution)/shard_map/all_to_all | solution.py:344
  73.2 6.8 %collective-permute-done.4.refs_2_ = bf16[128,2432]{1,0:T(8,128)(2,1)S(1)} collective-permute-done((bf16[128,2432]{1,0:T(8,128)(2,1)S(1)}, bf16[128,2432]{1,0:T(8,128)(2,1)S(1)}, u32[]{:S(2)}, u32[]{:S(2)}) %collective-permute-start.4) | collective-permute-done | bytes 622624 | tf_op jit(solution)/shard_map/ppermute | solution.py:336
  80.0 0.8 copy-done.5
  80.8 0.0 collective-permute-done.3.refs_1_
  80.8 2.1 %shard_map.86.w_ref = bf16[16,160,512]{2,1,0:T(8,128)(2,1)S(1)} custom-call(bf16[128,2432]{1,0:T(8,128)(2,1)} %refs_0_, bf16[128,2432]{1,0:T(8,128)(2,1)} %collective-permute-done.3.refs_1_, bf16[128,2432]{1,0:T(8,128)(2,1)} %copy-done.5, bf16[128,2432]{1,0:T(8,128)(2,1)} %copy-done.4), custom_call_target="tpu_custom_call" | custom-call | bytes 1048576 | tf_op jit(solution)/shard_map/pallas_call | solution.py:348
  82.9 0.8 all-to-all-done.2
  83.7 1.4 %shard_map.87 = bf16[16,80,128]{2,1,0:T(8,128)(2,1)S(1)} custom-call(s32[1]{0:T(128)} %bitcast.core_ref, s32[1]{0:T(128)} %bitcast.1.parity_ref, bf16[2,256,128]{2,1,0:T(8,128)(2,1)S(1)} %bitcast.29, f32[1,128]{1,0:T(1,128)S(1)} %get-tuple-element.41.slot_ref, bf16[16,160,512]{2,1,0:T(8,128)(2,1)S(1)} %shard_map.86.w_ref), custom_call_target="tpu_custom_call" | custom-call | flops 318767104 | bytes 1048576 | tf_op jit(solution)/shard_map/pallas_call | solution.py:355
  85.1 16.3 %all_to_all.20.sums_ref = bf16[16,80,128]{2,1,0:T(8,128)(2,1)S(1)} all-to-all(bf16[16,80,128]{2,1,0:T(8,128)(2,1)S(1)} %shard_map.87), channel_id=1, replica_groups=mesh['dp'=32,'mp'=16] {'mp'}, dimensions={0} | all-to-all | bytes 655360 | tf_op jit(solution)/shard_map/all_to_all | solution.py:362
  101.5 0.9 shard_map.88
  (22 shorter events, 0.1 us)
Async XLA Ops:
  2.1 31.2 %all-to-all-start = ((bf16[16,152,128]{2,1,0:T(8,128)(2,1)}), bf16[16,152,128]{2,1,0:T(8,128)(2,1)S(1)}, u32[]{:S(2)}, u32[]{:S(2)}) async-start(bf16[16,152,128]{2,1,0:T(8,128)(2,1)} %get-tuple-element.29), calls=%async_computation | async-start | bytes 1245184 | tf_op jit(solution)/shard_map/all_to_all | solution.py:299
  13.9 8.9 %copy-start.7 = (f32[2,64]{1,0:T(2,128)S(1)}, f32[2,64]{1,0:T(2,128)}, u32[]{:S(2)}) copy-start(f32[2,64]{1,0:T(2,128)} %param.13) | copy-start | bytes 1540
  13.9 9.1 %copy-start.6 = (bf16[1,2,333,128]{3,1,2,0:T(2,128)(2,1)S(1)}, bf16[1,2,333,128]{3,1,2,0:T(2,128)(2,1)}, u32[]{:S(2)}) copy-start(bf16[1,2,333,128]{3,1,2,0:T(2,128)(2,1)} %param.14) | copy-start | bytes 511492
  14.0 9.2 %slice-start = ((bf16[28,3,2432]{2,0,1:T(8,128)(2,1)}), bf16[28,1,2432]{2,0,1:T(8,128)(2,1)S(1)}, s32[]{:S(2)}) async-start(bf16[28,3,2432]{2,0,1:T(8,128)(2,1)} %param.11), calls=%async_computation.4 | async-start | bytes 311296 | tf_op jit(solution)/shard_map/slice | solution.py:303
  14.0 9.3 %copy-start = (bf16[28,3,2432]{2,0,1:T(8,128)(2,1)S(1)}, bf16[28,3,2432]{2,0,1:T(8,128)(2,1)}, u32[]{:S(2)}) copy-start(bf16[28,3,2432]{2,0,1:T(8,128)(2,1)} %param.11) | copy-start | bytes 1225732
  14.0 9.2 %copy-start.1 = (s32[256,1]{0,1:T(1,128)S(1)}, s32[256,1]{0,1:T(1,128)}, u32[]{:S(2)}) copy-start(s32[256,1]{0,1:T(1,128)} %param.9) | copy-start | bytes 3076
  14.0 9.2 %copy-start.2 = (s32[32]{0:T(128)S(1)}, s32[32]{0:T(128)}, u32[]{:S(2)}) copy-start(s32[32]{0:T(128)} %param.10) | copy-start | bytes 388
  16.5 8.7 %collective-permute-start.2 = (bf16[2432,128]{1,0:T(8,128)(2,1)}, bf16[2432,128]{1,0:T(8,128)(2,1)}, u32[]{:S(2)}, u32[]{:S(2)}) collective-permute-start(bf16[2432,128]{1,0:T(8,128)(2,1)} %get-tuple-element.51), channel_id=1, source_target_pairs={{0,1},{1,0},{2,3},{3,2},{4,5},{5,4},{6,7},{7,6},{8,9},{9,8},{10,11... | collective-permute-start | bytes 1867784 | tf_op jit(solution)/shard_map/ppermute | solution.py:302
  18.5 6.7 %collective-permute-start.1 = (bf16[2432,128]{1,0:T(8,128)(2,1)S(1)}, bf16[2432,128]{1,0:T(8,128)(2,1)}, u32[]{:S(2)}, u32[]{:S(2)}) collective-permute-start(bf16[2432,128]{1,0:T(8,128)(2,1)S(1)} %get-tuple-element.52), channel_id=1, source_target_pairs={{0,1},{1,0},{2,3},{3,2},{4,5},{5,4},{6,7},{7,6},{8,9},{9,8},{10,11... | collective-permute-start | bytes 1867784 | tf_op jit(solution)/shard_map/ppermute | solution.py:302
  20.8 4.4 %collective-permute-start = (bf16[2432,128]{1,0:T(8,128)(2,1)S(1)}, bf16[2432,128]{1,0:T(8,128)(2,1)}, u32[]{:S(2)}, u32[]{:S(2)}) collective-permute-start(bf16[2432,128]{1,0:T(8,128)(2,1)S(1)} %get-tuple-element.53), channel_id=1, source_target_pairs={{0,1},{1,0},{2,3},{3,2},{4,5},{5,4},{6,7},{7,6},{8,9},{9,8},{10,11... | collective-permute-start | bytes 1867784 | tf_op jit(solution)/shard_map/ppermute | solution.py:302
  33.3 14.5 %copy-start.3 = (bf16[128,2432]{1,0:T(8,128)(2,1)S(1)}, bf16[128,2432]{1,0:T(8,128)(2,1)}, u32[]{:S(2)}) copy-start(bf16[128,2432]{1,0:T(8,128)(2,1)} %refs_0_) | copy-start | bytes 1867780
  37.4 26.4 %all-to-all-start.1 = ((bf16[64,8,384]{2,1,0:T(8,128)(2,1)}), bf16[64,8,384]{2,1,0:T(8,128)(2,1)S(1)}, u32[]{:S(2)}, u32[]{:S(2)}) async-start(bf16[64,8,384]{2,1,0:T(8,128)(2,1)} %bitcast.15), calls=%async_computation.1 | async-start | bytes 786432 | tf_op jit(solution)/shard_map/all_to_all | solution.py:333
  47.8 25.4 %collective-permute-start.5 = (bf16[128,2432]{1,0:T(8,128)(2,1)S(1)}, bf16[128,2432]{1,0:T(8,128)(2,1)S(1)}, u32[]{:S(2)}, u32[]{:S(2)}) collective-permute-start(bf16[128,2432]{1,0:T(8,128)(2,1)S(1)} %copy-done.3), channel_id=1, source_target_pairs={{0,3},{1,2},{2,1},{3,0},{4,7},{5,6},{6,5},{7,4},{8,11},{9,10},{10,... | collective-permute-start | bytes 1867784 | tf_op jit(solution)/shard_map/ppermute | solution.py:336
  49.7 30.3 %collective-permute-start.4 = (bf16[128,2432]{1,0:T(8,128)(2,1)S(1)}, bf16[128,2432]{1,0:T(8,128)(2,1)S(1)}, u32[]{:S(2)}, u32[]{:S(2)}) collective-permute-start(bf16[128,2432]{1,0:T(8,128)(2,1)S(1)} %copy-done.3), channel_id=1, source_target_pairs={{0,2},{1,3},{2,0},{3,1},{4,6},{5,7},{6,4},{7,5},{8,10},{9,11},{10,... | collective-permute-start | bytes 1867784 | tf_op jit(solution)/shard_map/ppermute | solution.py:336
  53.3 27.5 %collective-permute-start.3 = (bf16[128,2432]{1,0:T(8,128)(2,1)S(1)}, bf16[128,2432]{1,0:T(8,128)(2,1)}, u32[]{:S(2)}, u32[]{:S(2)}) collective-permute-start(bf16[128,2432]{1,0:T(8,128)(2,1)S(1)} %copy-done.3), channel_id=1, source_target_pairs={{0,1},{1,0},{2,3},{3,2},{4,5},{5,4},{6,7},{7,6},{8,9},{9,8},{10,11... | collective-permute-start | bytes 1867784 | tf_op jit(solution)/shard_map/ppermute | solution.py:336
  66.2 17.5 %all-to-all-start.2 = ((bf16[128,4,128]{2,1,0:T(4,128)(2,1)}), bf16[128,4,128]{2,1,0:T(4,128)(2,1)S(1)}, u32[]{:S(2)}, u32[]{:S(2)}) async-start(bf16[128,4,128]{2,1,0:T(4,128)(2,1)} %bitcast.17), calls=%async_computation.2 | async-start | bytes 262144 | tf_op jit(solution)/shard_map/all_to_all | solution.py:344
  73.2 6.8 %copy-start.4 = (bf16[128,2432]{1,0:T(8,128)(2,1)}, bf16[128,2432]{1,0:T(8,128)(2,1)S(1)}, u32[]{:S(2)}) copy-start(bf16[128,2432]{1,0:T(8,128)(2,1)S(1)} %collective-permute-done.5.refs_3_) | copy-start | bytes 1867780
  80.0 0.8 copy-start.5

commit v9 on v8

--- a/solution.py
+++ b/solution.py
@@ -114,26 +114,9 @@
     copy.wait()
 
 
-def flip_kernel(*refs):
-    sources, (out_ref, *held, sems) = refs[:4], refs[4:]
-    inner, depth = held[0].shape
-    parts, padded, _ = out_ref.shape
-    width = depth // parts
-    reads = [pltpu.make_async_copy(source, ref, sems.at[i]) for i, (source, ref) in enumerate(zip(sources, held))]
-    for copy in reads:
-        copy.start()
-    for m in range(parts):
-        out_ref[m, width:, :] = jnp.zeros((padded - width, out_ref.shape[2]), BF16)
-    for i, ref in enumerate(held):
-        reads[i].wait()
-        turned = ref[...].astype(F32).T
-        for m in range(parts):
-            out_ref[m, :width, i * inner : (i + 1) * inner] = turned[m * width : (m + 1) * width].astype(BF16)
-
-
 def project_kernel(
     core_ref, tok_ref, mod_hbm, own_hbm, sib0_hbm, sib1_hbm, sib2_hbm, gain_ref, slot_ref,
-    send_ref, mod_ref, w_ref, hid_ref, sems,
+    send_hbm, mod_ref, w_ref, hid_ref, send_ref, sems,
 ):
     parts, width, rows = tok_ref.shape
     depth = parts * width
@@ -147,7 +130,7 @@
     ]
     for copy in weights:
         copy.start()
-    hits = iota((send_ref.shape[1], rows), 0).astype(F32) == slot_ref[...]
+    hits = iota((send_hbm.shape[1], rows), 0).astype(F32) == slot_ref[...]
     filled = jnp.sum(jnp.where(hits, 1.0, 0.0), axis=1, keepdims=True)
     mark = jnp.where(filled > 0.5, 0.0, DEAD)
     place = one_hot(hits)
@@ -164,12 +147,11 @@
     hidden = hid_ref[...].astype(F32).T.astype(BF16)
     normed = 2 * inner
     heads = one_hot(iota((normed, normed), 0) // HD == iota((normed, normed), 1) // HD)
-    projected = []
-    for side in range(2):
+    writes = []
+    for side, target in enumerate((core_ref[0], 1 - core_ref[0])):
         for copy in weights[side * kinds : (side + 1) * kinds]:
             copy.wait()
-        projected.append(jnp.dot(hidden, w_ref[side], preferred_element_type=F32))
-    for mixed, target in zip(projected, (core_ref[0], 1 - core_ref[0])):
+        mixed = jnp.dot(hidden, w_ref[side], preferred_element_type=F32)
         turned = mixed[:, :normed]
         power = jnp.square(turned)
         high = power.astype(BF16)
@@ -179,7 +161,11 @@
         packed = jnp.concatenate([turned, mixed[:, normed:]], axis=1).astype(BF16)
         send = jnp.dot(place, packed, preferred_element_type=F32)
         send = jnp.concatenate([send[:, :inner], send[:, inner:normed] + mark, send[:, normed:]], axis=1)
-        send_ref[target] = send.astype(BF16)
+        send_ref[side] = send.astype(BF16)
+        writes.append(pltpu.make_async_copy(send_ref.at[side], send_hbm.at[target], sems.at[1 + 2 * kinds + side]))
+        writes[-1].start()
+    for copy in writes:
+        copy.wait()
 
 
 def attend_kernel(text_len, slots_ref, ctx_ref, out_ref):
@@ -208,11 +194,13 @@
         out_ref[row : row + block, :] = jnp.where(first, mixed[:block], mixed[block:]).astype(BF16)
 
 
-def output_kernel(sub_slots, core_ref, parity_ref, back_ref, slot_ref, w_ref, part_ref):
+def output_kernel(sub_slots, core_ref, parity_ref, back_ref, slot_ref, own_ref, sib_ref, zn_ref, zs_ref, part_ref):
     core, parity = core_ref[0], parity_ref[0]
     slots, inner = back_ref.shape[1:]
+    parts, upper, lanes = part_ref.shape
+    depth = own_ref.shape[1]
+    width = depth // parts
     quarter = slot_ref.shape[1] // 2
-    upper = part_ref.shape[1]
     slot = slot_ref[...]
     slot = as_column(jnp.where(parity == 0, slot[:, :quarter], slot[:, quarter:]))
     shift = (sub_slots * (1 - 2 * parity)).astype(F32)
@@ -222,10 +210,14 @@
         for side in (core, 1 - core):
             attn.append(jnp.dot(place_t, back_ref[side], preferred_element_type=F32).astype(BF16))
     attn = jnp.concatenate(attn, axis=1)
-    empty = jnp.zeros(attn.shape, BF16)
-    left, right = jnp.concatenate([attn, empty], axis=0), jnp.concatenate([empty, attn], axis=0)
-    for m in range(part_ref.shape[0]):
-        part_ref[m] = (dot_nt(w_ref[m, :upper], left) + dot_nt(w_ref[m, upper:], right)).astype(BF16)
+    weights = jnp.concatenate([ref[...] for ref in (own_ref, sib_ref, zn_ref, zs_ref)], axis=0)
+    total = jnp.dot(attn, weights, preferred_element_type=F32)
+    total = jnp.concatenate([total, jnp.zeros((lanes - quarter, depth), F32)], axis=0).T
+    total = jnp.concatenate([total, jnp.zeros((2 * upper - width, lanes), F32)], axis=0)
+    for m in range(parts):
+        above = total[m * width : m * width + upper]
+        below = total[m * width + upper : m * width + 2 * upper]
+        part_ref[m] = (above + pltpu.roll(below, quarter, 1)).astype(BF16)
 
 
 def finish_kernel(sums_ref, perm_ref, gates_ref, pos_ref, out_ref):
@@ -318,14 +310,15 @@
 
     send = call(
         project_kernel,
-        shape((2, slots, kinds * inner), BF16),
+        pltpu.HBM((2, slots, kinds * inner), BF16),
         "svaaaaavv",
-        "v",
+        "a",
         [
             pltpu.VMEM((2, depth, half), BF16),
             pltpu.VMEM((2, depth, kinds * inner), BF16),
             pltpu.VMEM((depth, half), BF16),
-            pltpu.SemaphoreType.DMA((1 + 2 * kinds,)),
+            pltpu.VMEM((2, slots, kinds * inner), BF16),
+            pltpu.SemaphoreType.DMA((3 + 2 * kinds,)),
         ],
         flops=4 * depth * half * kinds * inner,
     )(core, whole, in_hbm(mod), in_hbm(w_own), *[in_hbm(w) for w in w_sib], gains, slot)
@@ -344,21 +337,13 @@
     returned = lax.all_to_all(
         attn.reshape(4 * requests, cap // 2, inner), ("dp", "mp"), 0, 0, axis_index_groups=pairs, tiled=True
     )
-    _, w_out, w_outs = lax.optimization_barrier((attn, w_out, w_outs))
-    w_back = call(
-        flip_kernel,
-        shape((parts, 2 * upper, 4 * inner), BF16),
-        "aaaa",
-        "v",
-        [pltpu.VMEM((inner, depth), BF16)] * 4 + [pltpu.SemaphoreType.DMA((4,))],
-    )(*[in_hbm(w) for w in (w_out, *w_outs)])
     partial = call(
         functools.partial(output_kernel, cap // 2),
         shape((parts, upper, half), BF16),
-        "ssvvv",
+        "ssvvvvvv",
         "v",
         flops=8 * depth * half * inner,
-    )(core, parity, returned.reshape(2, slots, inner), slot, w_back)
+    )(core, parity, returned.reshape(2, slots, inner), slot, w_out, *w_outs)
     sums = lax.all_to_all(partial, "mp", 0, 0, tiled=True)
     return call(finish_kernel, shape((width, rows), BF16), "vvvv", "v")(sums, perm, gates, pos).T
 

time: 103 us -> 104 us (level)
  waiting for transfers between devices: 23.8 us -> 28 us
  Pallas kernels: 14.9 us -> 13 us
    ppermute x3, waiting for transfers between devices: 6.82 us -> 9.5 us  [body(): lax.ppermute(w_out, 'mp', [(i, i ^ step) for i in range(parts)])]
    pallas_call x2 -> x1, Pallas kernels: 6.21 us -> 4.36 us  [body(): call(project_kernel, pltpu.HBM((2, slots, kinds * inner), BF16), 'svaaaaa...]
    all_to_all x1, waiting for transfers between devices: 0.81 us -> 2.33 us  [body(): lax.all_to_all(attn.reshape(4 * requests, cap // 2, inner), ('dp', 'mp'),...]
  transfers between devices with their start and end apart: 9 -> 9, of which waited for: 4 -> 4; matrix products, arithmetic and copies ran while one was open for 3% -> 3% of each run, Pallas kernels for 6% -> 4%
where the time goes in v9:
time: 104 us
  starting transfers between devices  43.3 us (42%)
  waiting for transfers between devices  28 us (27%)
  blocking collectives  16.3 us (16%)
  Pallas kernels  13 us (12%)
  local copies, waits for them, and re-layouts  2.83 us (3%)
    all_to_all x1, blocking collectives, body(): sums = lax.all_to_all(partial, 'mp', 0, 0, tiled=True)  16.3 us
    all_to_all x1, starting transfers between devices, body(): whole = lax.all_to_all(spread, 'mp', 0, 0, tiled=True)  11.8 us
    all_to_all x1, starting transfers between devices, body(): lax.all_to_all(send.reshape(2 * requests, cap, kinds * inner), ('dp', 'mp...  10.3 us
    ppermute x3, waiting for transfers between devices, body(): lax.ppermute(w_out, 'mp', [(i, i ^ step) for i in range(parts)])  9.5 us
    all_to_all x1, waiting for transfers between devices, body(): lax.all_to_all(send.reshape(2 * requests, cap, kinds * inner), ('dp', 'mp...  8.12 us
    all_to_all x1, waiting for transfers between devices, body(): whole = lax.all_to_all(spread, 'mp', 0, 0, tiled=True)  8.06 us
    ppermute x3, starting transfers between devices, body(): lax.ppermute(w_out, 'mp', [(i, i ^ step) for i in range(parts)])  7.87 us
    all_to_all x1, starting transfers between devices, body(): lax.all_to_all(attn.reshape(4 * requests, cap // 2, inner), ('dp', 'mp'),...  6.94 us
  transfers between devices with their start and end apart: 9, of which 4 were waited for; matrix products, arithmetic and copies ran while one was open for 3% of the time, Pallas kernels for 4%

profile of v9, /device:TPU:1, one launch (start us, length us, event | category | flops | bytes accessed | tf_op | source)
XLA Modules:
  0.0 103.8 jit_solution(12286705620703354459)
XLA Ops:
  0.0 2.1 %shard_map.82 = (bf16[16,152,128]{2,1,0:T(8,128)(2,1)}, bf16[152,256]{1,0:T(8,128)(2,1)S(1)}, f32[1,256]{1,0:T(1,128)S(1)}) custom-call(bf16[152,256]{1,0:T(8,128)(2,1)} %bitcast.39, s32[1,256]{1,0:T(1,128)} %bitcast.31), custom_call_target="tpu_custom_call" | custom-call | bytes 1048576 | tf_op jit(solution)/shard_map/pallas_call | solution.py:278
  2.1 11.8 %all-to-all-start = ((bf16[16,152,128]{2,1,0:T(8,128)(2,1)}), bf16[16,152,128]{2,1,0:T(8,128)(2,1)S(1)}, u32[]{:S(2)}, u32[]{:S(2)}) async-start(bf16[16,152,128]{2,1,0:T(8,128)(2,1)} %get-tuple-element.25), calls=%async_computation | async-start | bytes 1245184 | tf_op jit(solution)/shard_map/all_to_all | solution.py:291
  13.9 0.0 copy-start.4
  14.0 0.0 slice-start
  14.0 0.0 copy-start.2
  14.0 0.0 copy-start.3
  14.0 2.5 %slice_bitcast_fusion = (bf16[2432,128]{1,0:T(8,128)(2,1)S(1)}, bf16[2432,128]{1,0:T(8,128)(2,1)S(1)}, bf16[2432,128]{1,0:T(8,128)(2,1)}) fusion(bf16[3,2432,128]{2,1,0:T(8,128)(2,1)} %bitcast.35), kind=kLoop, calls=%fused_computation | loop fusion | bytes 3735552 | tf_op jit(solution)/shard_map/squeeze | solution.py:294
  16.5 2.0 %collective-permute-start = (bf16[2432,128]{1,0:T(8,128)(2,1)}, bf16[2432,128]{1,0:T(8,128)(2,1)}, u32[]{:S(2)}, u32[]{:S(2)}) collective-permute-start(bf16[2432,128]{1,0:T(8,128)(2,1)} %get-tuple-element.45), channel_id=1, source_target_pairs={{0,1},{1,0},{2,3},{3,2},{4,5},{5,4},{6,7},{7,6},{8,9},{9,8},{10,11... | collective-permute-start | bytes 1867784 | tf_op jit(solution)/shard_map/ppermute | solution.py:294
  18.5 2.3 %collective-permute-start.1 = (bf16[2432,128]{1,0:T(8,128)(2,1)S(1)}, bf16[2432,128]{1,0:T(8,128)(2,1)}, u32[]{:S(2)}, u32[]{:S(2)}) collective-permute-start(bf16[2432,128]{1,0:T(8,128)(2,1)S(1)} %get-tuple-element.44), channel_id=1, source_target_pairs={{0,1},{1,0},{2,3},{3,2},{4,5},{5,4},{6,7},{7,6},{8,9},{9,8},{10,11... | collective-permute-start | bytes 1867784 | tf_op jit(solution)/shard_map/ppermute | solution.py:294
  20.8 2.0 %collective-permute-start.2 = (bf16[2432,128]{1,0:T(8,128)(2,1)S(1)}, bf16[2432,128]{1,0:T(8,128)(2,1)}, u32[]{:S(2)}, u32[]{:S(2)}) collective-permute-start(bf16[2432,128]{1,0:T(8,128)(2,1)S(1)} %get-tuple-element.43), channel_id=1, source_target_pairs={{0,1},{1,0},{2,3},{3,2},{4,5},{5,4},{6,7},{7,6},{8,9},{9,8},{10,11... | collective-permute-start | bytes 1867784 | tf_op jit(solution)/shard_map/ppermute | solution.py:294
  22.9 0.1 tile.26
  23.0 0.1 tile.23
  23.1 0.1 dynamic-slice_bitcast_fusion.gate_ref
  23.2 2.0 %shard_map.83 = (bf16[2,2432,128]{2,1,0:T(8,128)(2,1)}, bf16[152,256]{1,0:T(8,128)(2,1)S(1)}, f32[1,128]{1,0:T(1,128)S(1)}) custom-call(s32[1]{0:T(128)} %bitcast.core_ref, s32[1,256]{1,0:T(1,128)S(1)} %bitcast.32, f32[1,256]{1,0:T(1,128)S(1)} %get-tuple-element.27.pos_ref, s32[1,32]{1,0:T(1,128)S(1)} %bitcast.34, bf16[3,28,2432]{2,1,0:T(8,128)(2,1)S(1)} %bitcast.28, ...), custom_call_target="tpu_custom_call" | custom-call | bytes 1048576 | tf_op jit(solution)/shard_map/pallas_call | solution.py:296
  25.2 0.0 collective-permute-done.sib0_hbm
  25.2 0.0 collective-permute-done.1.sib1_hbm
  25.2 8.1 %all-to-all-done.tok_ref = bf16[16,152,128]{2,1,0:T(8,128)(2,1)S(1)} async-done(((bf16[16,152,128]{2,1,0:T(8,128)(2,1)}), bf16[16,152,128]{2,1,0:T(8,128)(2,1)S(1)}, u32[]{:S(2)}, u32[]{:S(2)}) %all-to-all-start) | async-done | bytes 622624 | tf_op jit(solution)/shard_map/all_to_all | solution.py:291
  33.3 4.4 %shard_map.84 = bf16[2,256,384]{2,1,0:T(8,128)(2,1)} custom-call(s32[1]{0:T(128)} %bitcast.core_ref, bf16[16,152,128]{2,1,0:T(8,128)(2,1)S(1)} %all-to-all-done.tok_ref, bf16[2,2432,128]{2,1,0:T(8,128)(2,1)} %get-tuple-element.32.mod_hbm, bf16[3,2432,128]{2,1,0:T(8,128)(2,1)} %bitcast.36, bf16[2432,128]{1,0:T(8,128)(2,1)} %collective-permute-done.sib0_hbm, ...), custom_call_target="tpu_custom_call" | custom-call | flops 478150656 | bytes 1048576 | tf_op jit(solution)/shard_map/pallas_call | solution.py:311
  37.7 10.3 %all-to-all-start.1 = ((bf16[64,8,384]{2,1,0:T(8,128)(2,1)}), bf16[64,8,384]{2,1,0:T(8,128)(2,1)S(1)}, u32[]{:S(2)}, u32[]{:S(2)}) async-start(bf16[64,8,384]{2,1,0:T(8,128)(2,1)} %bitcast.37), calls=%async_computation.1 | async-start | bytes 786432 | tf_op jit(solution)/shard_map/all_to_all | solution.py:326
  48.0 2.3 %collective-permute-start.3 = (bf16[128,2432]{1,0:T(8,128)(2,1)S(1)}, bf16[128,2432]{1,0:T(8,128)(2,1)S(1)}, u32[]{:S(2)}, u32[]{:S(2)}) collective-permute-start(bf16[128,2432]{1,0:T(8,128)(2,1)S(1)} %copy-done.1), channel_id=1, source_target_pairs={{0,1},{1,0},{2,3},{3,2},{4,5},{5,4},{6,7},{7,6},{8,9},{9,8},{10,11... | collective-permute-start | bytes 1867784 | tf_op jit(solution)/shard_map/ppermute | solution.py:329
  50.3 1.9 %collective-permute-start.4 = (bf16[128,2432]{1,0:T(8,128)(2,1)S(1)}, bf16[128,2432]{1,0:T(8,128)(2,1)S(1)}, u32[]{:S(2)}, u32[]{:S(2)}) collective-permute-start(bf16[128,2432]{1,0:T(8,128)(2,1)S(1)} %copy-done.1), channel_id=1, source_target_pairs={{0,2},{1,3},{2,0},{3,1},{4,6},{5,7},{6,4},{7,5},{8,10},{9,11},{10,... | collective-permute-start | bytes 1867784 | tf_op jit(solution)/shard_map/ppermute | solution.py:329
  52.2 3.7 %collective-permute-start.5 = (bf16[128,2432]{1,0:T(8,128)(2,1)S(1)}, bf16[128,2432]{1,0:T(8,128)(2,1)S(1)}, u32[]{:S(2)}, u32[]{:S(2)}) collective-permute-start(bf16[128,2432]{1,0:T(8,128)(2,1)S(1)} %copy-done.1), channel_id=1, source_target_pairs={{0,3},{1,2},{2,1},{3,0},{4,7},{5,6},{6,5},{7,4},{8,11},{9,10},{10,... | collective-permute-start | bytes 1867784 | tf_op jit(solution)/shard_map/ppermute | solution.py:329
  55.9 8.1 %all-to-all-done.1 = bf16[64,8,384]{2,1,0:T(8,128)(2,1)S(1)} async-done(((bf16[64,8,384]{2,1,0:T(8,128)(2,1)}), bf16[64,8,384]{2,1,0:T(8,128)(2,1)S(1)}, u32[]{:S(2)}, u32[]{:S(2)}) %all-to-all-start.1) | async-done | bytes 393248 | tf_op jit(solution)/shard_map/all_to_all | solution.py:326
  64.0 2.4 %shard_map.85 = bf16[512,128]{1,0:T(8,128)(2,1)} custom-call(bf16[512,384]{1,0:T(8,128)(2,1)S(1)} %bitcast.30, bf16[2,384,128]{2,1,0:T(8,128)(2,1)S(1)} %pad.4.ctx_ref), custom_call_target="tpu_custom_call" | custom-call | flops 469762048 | bytes 1048576 | tf_op jit(solution)/shard_map/pallas_call | solution.py:330
  66.4 6.9 %all-to-all-start.2 = ((bf16[128,4,128]{2,1,0:T(4,128)(2,1)}), bf16[128,4,128]{2,1,0:T(4,128)(2,1)S(1)}, u32[]{:S(2)}, u32[]{:S(2)}) async-start(bf16[128,4,128]{2,1,0:T(4,128)(2,1)} %bitcast.17), calls=%async_computation.2 | async-start | bytes 262144 | tf_op jit(solution)/shard_map/all_to_all | solution.py:337
  73.4 0.0 collective-permute-done.3.sib_ref
  73.4 0.0 collective-permute-done.4.zn_ref
  73.4 9.5 %collective-permute-done.5.zs_ref = bf16[128,2432]{1,0:T(8,128)(2,1)S(1)} collective-permute-done((bf16[128,2432]{1,0:T(8,128)(2,1)S(1)}, bf16[128,2432]{1,0:T(8,128)(2,1)S(1)}, u32[]{:S(2)}, u32[]{:S(2)}) %collective-permute-start.5) | collective-permute-done | bytes 622624 | tf_op jit(solution)/shard_map/ppermute | solution.py:329
  82.9 2.3 %all-to-all-done.2 = bf16[128,4,128]{2,1,0:T(4,128)(2,1)S(1)} async-done(((bf16[128,4,128]{2,1,0:T(4,128)(2,1)}), bf16[128,4,128]{2,1,0:T(4,128)(2,1)S(1)}, u32[]{:S(2)}, u32[]{:S(2)}) %all-to-all-start.2) | async-done | bytes 131104 | tf_op jit(solution)/shard_map/all_to_all | solution.py:337
  85.2 1.3 %shard_map.86 = bf16[16,80,128]{2,1,0:T(8,128)(2,1)S(1)} custom-call(s32[1]{0:T(128)} %bitcast.core_ref, s32[1]{0:T(128)} %bitcast.1.parity_ref, bf16[2,256,128]{2,1,0:T(8,128)(2,1)S(1)} %bitcast.29, f32[1,128]{1,0:T(1,128)S(1)} %get-tuple-element.37.slot_ref, bf16[128,2432]{1,0:T(8,128)(2,1)S(1)} %copy-done.1, ...), custom_call_target="tpu_custom_call" | custom-call | flops 318767104 | bytes 1048576 | tf_op jit(solution)/shard_map/pallas_call | solution.py:340
  86.6 16.3 %all_to_all.20.sums_ref = bf16[16,80,128]{2,1,0:T(8,128)(2,1)S(1)} all-to-all(bf16[16,80,128]{2,1,0:T(8,128)(2,1)S(1)} %shard_map.86), channel_id=1, replica_groups=mesh['dp'=32,'mp'=16] {'mp'}, dimensions={0} | all-to-all | bytes 655360 | tf_op jit(solution)/shard_map/all_to_all | solution.py:347
  102.9 0.9 shard_map.87
  (17 shorter events, 0.1 us)
Async XLA Ops:
  2.1 31.2 %all-to-all-start = ((bf16[16,152,128]{2,1,0:T(8,128)(2,1)}), bf16[16,152,128]{2,1,0:T(8,128)(2,1)S(1)}, u32[]{:S(2)}, u32[]{:S(2)}) async-start(bf16[16,152,128]{2,1,0:T(8,128)(2,1)} %get-tuple-element.25), calls=%async_computation | async-start | bytes 1245184 | tf_op jit(solution)/shard_map/all_to_all | solution.py:291
  13.9 8.9 %copy-start.5 = (f32[2,64]{1,0:T(2,128)S(1)}, f32[2,64]{1,0:T(2,128)}, u32[]{:S(2)}) copy-start(f32[2,64]{1,0:T(2,128)} %param.13) | copy-start | bytes 1540
  13.9 9.1 %copy-start.4 = (bf16[1,2,333,128]{3,1,2,0:T(2,128)(2,1)S(1)}, bf16[1,2,333,128]{3,1,2,0:T(2,128)(2,1)}, u32[]{:S(2)}) copy-start(bf16[1,2,333,128]{3,1,2,0:T(2,128)(2,1)} %param.14) | copy-start | bytes 511492
  14.0 9.2 %slice-start = ((bf16[28,3,2432]{2,0,1:T(8,128)(2,1)}), bf16[28,1,2432]{2,0,1:T(8,128)(2,1)S(1)}, s32[]{:S(2)}) async-start(bf16[28,3,2432]{2,0,1:T(8,128)(2,1)} %param.11), calls=%async_computation.4 | async-start | bytes 311296 | tf_op jit(solution)/shard_map/slice | solution.py:295
  14.0 9.2 %copy-start = (bf16[28,3,2432]{2,0,1:T(8,128)(2,1)S(1)}, bf16[28,3,2432]{2,0,1:T(8,128)(2,1)}, u32[]{:S(2)}) copy-start(bf16[28,3,2432]{2,0,1:T(8,128)(2,1)} %param.11) | copy-start | bytes 1225732
  14.0 9.2 %copy-start.2 = (s32[256,1]{0,1:T(1,128)S(1)}, s32[256,1]{0,1:T(1,128)}, u32[]{:S(2)}) copy-start(s32[256,1]{0,1:T(1,128)} %param.9) | copy-start | bytes 3076
  14.0 9.2 %copy-start.3 = (s32[32]{0:T(128)S(1)}, s32[32]{0:T(128)}, u32[]{:S(2)}) copy-start(s32[32]{0:T(128)} %param.10) | copy-start | bytes 388
  16.5 8.7 %collective-permute-start = (bf16[2432,128]{1,0:T(8,128)(2,1)}, bf16[2432,128]{1,0:T(8,128)(2,1)}, u32[]{:S(2)}, u32[]{:S(2)}) collective-permute-start(bf16[2432,128]{1,0:T(8,128)(2,1)} %get-tuple-element.45), channel_id=1, source_target_pairs={{0,1},{1,0},{2,3},{3,2},{4,5},{5,4},{6,7},{7,6},{8,9},{9,8},{10,11... | collective-permute-start | bytes 1867784 | tf_op jit(solution)/shard_map/ppermute | solution.py:294
  18.5 6.7 %collective-permute-start.1 = (bf16[2432,128]{1,0:T(8,128)(2,1)S(1)}, bf16[2432,128]{1,0:T(8,128)(2,1)}, u32[]{:S(2)}, u32[]{:S(2)}) collective-permute-start(bf16[2432,128]{1,0:T(8,128)(2,1)S(1)} %get-tuple-element.44), channel_id=1, source_target_pairs={{0,1},{1,0},{2,3},{3,2},{4,5},{5,4},{6,7},{7,6},{8,9},{9,8},{10,11... | collective-permute-start | bytes 1867784 | tf_op jit(solution)/shard_map/ppermute | solution.py:294
  20.8 4.4 %collective-permute-start.2 = (bf16[2432,128]{1,0:T(8,128)(2,1)S(1)}, bf16[2432,128]{1,0:T(8,128)(2,1)}, u32[]{:S(2)}, u32[]{:S(2)}) collective-permute-start(bf16[2432,128]{1,0:T(8,128)(2,1)S(1)} %get-tuple-element.43), channel_id=1, source_target_pairs={{0,1},{1,0},{2,3},{3,2},{4,5},{5,4},{6,7},{7,6},{8,9},{9,8},{10,11... | collective-permute-start | bytes 1867784 | tf_op jit(solution)/shard_map/ppermute | solution.py:294
  33.3 14.7 %copy-start.1 = (bf16[128,2432]{1,0:T(8,128)(2,1)S(1)}, bf16[128,2432]{1,0:T(8,128)(2,1)}, u32[]{:S(2)}) copy-start(bf16[128,2432]{1,0:T(8,128)(2,1)} %own_ref) | copy-start | bytes 1867780
  37.7 26.4 %all-to-all-start.1 = ((bf16[64,8,384]{2,1,0:T(8,128)(2,1)}), bf16[64,8,384]{2,1,0:T(8,128)(2,1)S(1)}, u32[]{:S(2)}, u32[]{:S(2)}) async-start(bf16[64,8,384]{2,1,0:T(8,128)(2,1)} %bitcast.37), calls=%async_computation.1 | async-start | bytes 786432 | tf_op jit(solution)/shard_map/all_to_all | solution.py:326
  48.0 25.4 %collective-permute-start.3 = (bf16[128,2432]{1,0:T(8,128)(2,1)S(1)}, bf16[128,2432]{1,0:T(8,128)(2,1)S(1)}, u32[]{:S(2)}, u32[]{:S(2)}) collective-permute-start(bf16[128,2432]{1,0:T(8,128)(2,1)S(1)} %copy-done.1), channel_id=1, source_target_pairs={{0,1},{1,0},{2,3},{3,2},{4,5},{5,4},{6,7},{7,6},{8,9},{9,8},{10,11... | collective-permute-start | bytes 1867784 | tf_op jit(solution)/shard_map/ppermute | solution.py:329
  50.3 23.1 %collective-permute-start.4 = (bf16[128,2432]{1,0:T(8,128)(2,1)S(1)}, bf16[128,2432]{1,0:T(8,128)(2,1)S(1)}, u32[]{:S(2)}, u32[]{:S(2)}) collective-permute-start(bf16[128,2432]{1,0:T(8,128)(2,1)S(1)} %copy-done.1), channel_id=1, source_target_pairs={{0,2},{1,3},{2,0},{3,1},{4,6},{5,7},{6,4},{7,5},{8,10},{9,11},{10,... | collective-permute-start | bytes 1867784 | tf_op jit(solution)/shard_map/ppermute | solution.py:329
  52.2 30.7 %collective-permute-start.5 = (bf16[128,2432]{1,0:T(8,128)(2,1)S(1)}, bf16[128,2432]{1,0:T(8,128)(2,1)S(1)}, u32[]{:S(2)}, u32[]{:S(2)}) collective-permute-start(bf16[128,2432]{1,0:T(8,128)(2,1)S(1)} %copy-done.1), channel_id=1, source_target_pairs={{0,3},{1,2},{2,1},{3,0},{4,7},{5,6},{6,5},{7,4},{8,11},{9,10},{10,... | collective-permute-start | bytes 1867784 | tf_op jit(solution)/shard_map/ppermute | solution.py:329
  66.4 18.8 %all-to-all-start.2 = ((bf16[128,4,128]{2,1,0:T(4,128)(2,1)}), bf16[128,4,128]{2,1,0:T(4,128)(2,1)S(1)}, u32[]{:S(2)}, u32[]{:S(2)}) async-start(bf16[128,4,128]{2,1,0:T(4,128)(2,1)} %bitcast.17), calls=%async_computation.2 | async-start | bytes 262144 | tf_op jit(solution)/shard_map/all_to_all | solution.py:337

commit v10 on v9

--- a/solution.py
+++ b/solution.py
@@ -116,7 +116,7 @@
 
 def project_kernel(
     core_ref, tok_ref, mod_hbm, own_hbm, sib0_hbm, sib1_hbm, sib2_hbm, gain_ref, slot_ref,
-    send_hbm, mod_ref, w_ref, hid_ref, send_ref, sems,
+    send_ref, mod_ref, w_ref, hid_ref, sems,
 ):
     parts, width, rows = tok_ref.shape
     depth = parts * width
@@ -130,7 +130,7 @@
     ]
     for copy in weights:
         copy.start()
-    hits = iota((send_hbm.shape[1], rows), 0).astype(F32) == slot_ref[...]
+    hits = iota((send_ref.shape[1], rows), 0).astype(F32) == slot_ref[...]
     filled = jnp.sum(jnp.where(hits, 1.0, 0.0), axis=1, keepdims=True)
     mark = jnp.where(filled > 0.5, 0.0, DEAD)
     place = one_hot(hits)
@@ -147,11 +147,12 @@
     hidden = hid_ref[...].astype(F32).T.astype(BF16)
     normed = 2 * inner
     heads = one_hot(iota((normed, normed), 0) // HD == iota((normed, normed), 1) // HD)
-    writes = []
-    for side, target in enumerate((core_ref[0], 1 - core_ref[0])):
+    projected = []
+    for side in range(2):
         for copy in weights[side * kinds : (side + 1) * kinds]:
             copy.wait()
-        mixed = jnp.dot(hidden, w_ref[side], preferred_element_type=F32)
+        projected.append(jnp.dot(hidden, w_ref[side], preferred_element_type=F32))
+    for mixed, target in zip(projected, (core_ref[0], 1 - core_ref[0])):
         turned = mixed[:, :normed]
         power = jnp.square(turned)
         high = power.astype(BF16)
@@ -161,11 +162,7 @@
         packed = jnp.concatenate([turned, mixed[:, normed:]], axis=1).astype(BF16)
         send = jnp.dot(place, packed, preferred_element_type=F32)
         send = jnp.concatenate([send[:, :inner], send[:, inner:normed] + mark, send[:, normed:]], axis=1)
-        send_ref[side] = send.astype(BF16)
-        writes.append(pltpu.make_async_copy(send_ref.at[side], send_hbm.at[target], sems.at[1 + 2 * kinds + side]))
-        writes[-1].start()
-    for copy in writes:
-        copy.wait()
+        send_ref[target] = send.astype(BF16)
 
 
 def attend_kernel(text_len, slots_ref, ctx_ref, out_ref):
@@ -194,11 +191,12 @@
         out_ref[row : row + block, :] = jnp.where(first, mixed[:block], mixed[block:]).astype(BF16)
 
 
-def output_kernel(sub_slots, core_ref, parity_ref, back_ref, slot_ref, own_ref, sib_ref, zn_ref, zs_ref, part_ref):
+def output_kernel(sub_slots, core_ref, parity_ref, back_ref, slot_ref, *refs):
     core, parity = core_ref[0], parity_ref[0]
     slots, inner = back_ref.shape[1:]
+    *w_refs, part_ref = refs
     parts, upper, lanes = part_ref.shape
-    depth = own_ref.shape[1]
+    depth = w_refs[0].shape[1]
     width = depth // parts
     quarter = slot_ref.shape[1] // 2
     slot = slot_ref[...]
@@ -210,7 +208,7 @@
         for side in (core, 1 - core):
             attn.append(jnp.dot(place_t, back_ref[side], preferred_element_type=F32).astype(BF16))
     attn = jnp.concatenate(attn, axis=1)
-    weights = jnp.concatenate([ref[...] for ref in (own_ref, sib_ref, zn_ref, zs_ref)], axis=0)
+    weights = jnp.concatenate([ref[...] for ref in w_refs], axis=0)
     total = jnp.dot(attn, weights, preferred_element_type=F32)
     total = jnp.concatenate([total, jnp.zeros((lanes - quarter, depth), F32)], axis=0).T
     total = jnp.concatenate([total, jnp.zeros((2 * upper - width, lanes), F32)], axis=0)
@@ -287,11 +285,13 @@
             pltpu.SemaphoreType.DMA((2 + parts,)),
         ],
     )(in_hbm(tokens.T), in_hbm(req))
-    spread, w_qkv = lax.optimization_barrier((spread, w_qkv))
+    spread, w_qkv, w_out = lax.optimization_barrier((spread, w_qkv, w_out))
     whole = lax.all_to_all(spread, "mp", 0, 0, tiled=True)
 
     w_own = w_qkv.transpose(1, 0, 2)
     w_sib = [lax.ppermute(w_own[kind], "mp", sibling) for kind in range(kinds)]
+    out_sib = lax.ppermute(w_out, "mp", sibling)
+    first_rows = inner * 3 // 8
     gate_table = lax.dynamic_slice_in_dim(mod_table[:, 2, :], lax.axis_index("mp") * width, width, 1)
     mod, gates, slot = call(
         functools.partial(prepare_kernel, cap),
@@ -304,29 +304,33 @@
         [jnp.tile(qk_gain[0] * HD ** (-0.5), inner // HD), jnp.tile(qk_gain[1], inner // HD)]
     ).reshape(1, 2 * inner)
     text = jnp.pad(context[0], ((0, 0), (0, text_pad - text_len), (0, 0)))
-    whole, w_sib, mod, gates, slot, gains, text = lax.optimization_barrier(
-        (whole, w_sib, mod, gates, slot, gains, text)
+    whole, w_sib, out_sib, mod, gates, slot, gains, text = lax.optimization_barrier(
+        (whole, w_sib, out_sib, mod, gates, slot, gains, text)
     )
 
     send = call(
         project_kernel,
-        pltpu.HBM((2, slots, kinds * inner), BF16),
+        shape((2, slots, kinds * inner), BF16),
         "svaaaaavv",
-        "a",
+        "v",
         [
             pltpu.VMEM((2, depth, half), BF16),
             pltpu.VMEM((2, depth, kinds * inner), BF16),
             pltpu.VMEM((depth, half), BF16),
-            pltpu.VMEM((2, slots, kinds * inner), BF16),
-            pltpu.SemaphoreType.DMA((3 + 2 * kinds,)),
+            pltpu.SemaphoreType.DMA((1 + 2 * kinds,)),
         ],
         flops=4 * depth * half * kinds * inner,
     )(core, whole, in_hbm(mod), in_hbm(w_own), *[in_hbm(w) for w in w_sib], gains, slot)
-    send, w_out = lax.optimization_barrier((send, w_out))
+    send, early, late = lax.optimization_barrier((send, w_out[:first_rows], w_out[first_rows:]))
     arrived = lax.all_to_all(
         send.reshape(2 * requests, cap, kinds * inner), ("dp", "mp"), 0, 0, axis_index_groups=planes, tiled=True
     )
-    w_outs = [lax.ppermute(w_out, "mp", [(i, i ^ step) for i in range(parts)]) for step in (1, 2, 3)]
+    next_level = [(i, i ^ 2) for i in range(parts)]
+    next_early = lax.ppermute(early, "mp", next_level)
+    next_late = lax.ppermute(late, "mp", next_level)
+    far_late = lax.ppermute(late, "mp", [(i, i ^ 3) for i in range(parts)])
+    far_early = lax.ppermute(next_early, "mp", sibling)
+    blocks = (w_out, out_sib, next_early, next_late, far_early, far_late)
     attn = call(
         functools.partial(attend_kernel, text_len),
         shape((2 * slots, inner), BF16),
@@ -340,10 +344,10 @@
     partial = call(
         functools.partial(output_kernel, cap // 2),
         shape((parts, upper, half), BF16),
-        "ssvvvvvv",
+        "ssvvvvvvvv",
         "v",
         flops=8 * depth * half * inner,
-    )(core, parity, returned.reshape(2, slots, inner), slot, w_out, *w_outs)
+    )(core, parity, returned.reshape(2, slots, inner), slot, *blocks)
     sums = lax.all_to_all(partial, "mp", 0, 0, tiled=True)
     return call(finish_kernel, shape((width, rows), BF16), "vvvv", "v")(sums, perm, gates, pos).T
 

time: 104 us -> 103 us (level)
  waiting for transfers between devices: 28 us -> 20.9 us
  starting transfers between devices: 43.3 us -> 48.1 us
  local copies, waits for them, and re-layouts: 2.83 us -> 3.91 us
    ppermute x3 -> x5, waiting for transfers between devices: 9.5 us -> 1.08 us  [the longest x1 1.07 us: body(): far_early = lax.ppermute(next_early, 'mp', sibling)]
    all_to_all x1, waiting for transfers between devices: 2.33 us -> 7.03 us  [body(): lax.all_to_all(attn.reshape(4 * requests, cap // 2, inner), ('dp', 'mp'),...]
    ppermute x3 -> x5, starting transfers between devices: 7.87 us -> 12.5 us  [the longest x1 3.36 us: body(): next_late = lax.ppermute(late, 'mp', next_level)]
    all_to_all x1, waiting for transfers between devices: 8.06 us -> 4.51 us  [body(): whole = lax.all_to_all(spread, 'mp', 0, 0, tiled=True)]
  transfers between devices with their start and end apart: 9 -> 11, of which waited for: 4 -> 4; matrix products, arithmetic and copies ran while one was open for 3% -> 4% of each run, Pallas kernels for 4% -> 4%
where the time goes in v10:
time: 103 us; the launch traced here: 102 us
  starting transfers between devices  48.1 us (47%)
  waiting for transfers between devices  20.9 us (20%)
  blocking collectives  16.5 us (16%)
  Pallas kernels  12.7 us (12%)
  local copies, waits for them, and re-layouts  3.91 us (4%)
    all_to_all x1, blocking collectives, body(): sums = lax.all_to_all(partial, 'mp', 0, 0, tiled=True)  16.5 us
    all_to_all x1, starting transfers between devices, body(): whole = lax.all_to_all(spread, 'mp', 0, 0, tiled=True)  11.8 us
    all_to_all x1, starting transfers between devices, body(): lax.all_to_all(send.reshape(2 * requests, cap, kinds * inner), ('dp', 'mp...  10.3 us
    all_to_all x1, waiting for transfers between devices, body(): lax.all_to_all(send.reshape(2 * requests, cap, kinds * inner), ('dp', 'mp...  8.27 us
    all_to_all x1, waiting for transfers between devices, body(): lax.all_to_all(attn.reshape(4 * requests, cap // 2, inner), ('dp', 'mp'),...  7.03 us
    all_to_all x1, starting transfers between devices, body(): lax.all_to_all(attn.reshape(4 * requests, cap // 2, inner), ('dp', 'mp'),...  6.95 us
    ppermute x3, starting transfers between devices, body(): w_sib = [lax.ppermute(w_own[kind], 'mp', sibling) for kind in range(kinds)]  6.47 us
    all_to_all x1, waiting for transfers between devices, body(): whole = lax.all_to_all(spread, 'mp', 0, 0, tiled=True)  4.51 us
  transfers between devices with their start and end apart: 11, of which 4 were waited for; matrix products, arithmetic and copies ran while one was open for 4% of the time, Pallas kernels for 4%

profile of v10, /device:TPU:1, one launch (start us, length us, event | category | flops | bytes accessed | tf_op | source)
XLA Modules:
  0.0 102.4 jit_solution(17361457513841131931)
XLA Ops:
  0.0 2.1 %shard_map.82 = (bf16[16,152,128]{2,1,0:T(8,128)(2,1)}, bf16[152,256]{1,0:T(8,128)(2,1)S(1)}, f32[1,256]{1,0:T(1,128)S(1)}) custom-call(bf16[152,256]{1,0:T(8,128)(2,1)} %bitcast.38, s32[1,256]{1,0:T(1,128)} %bitcast.31), custom_call_target="tpu_custom_call" | custom-call | bytes 1048576 | tf_op jit(solution)/shard_map/pallas_call | solution.py:276
  2.1 11.8 %all-to-all-start = ((bf16[16,152,128]{2,1,0:T(8,128)(2,1)}), bf16[16,152,128]{2,1,0:T(8,128)(2,1)S(1)}, u32[]{:S(2)}, u32[]{:S(2)}) async-start(bf16[16,152,128]{2,1,0:T(8,128)(2,1)} %get-tuple-element.28), calls=%async_computation | async-start | bytes 1245184 | tf_op jit(solution)/shard_map/all_to_all | solution.py:289
  13.9 0.0 copy-start.5
  14.0 0.0 copy-start.4
  14.0 2.8 %slice_bitcast_fusion = (bf16[2432,128]{1,0:T(8,128)(2,1)}, bf16[2432,128]{1,0:T(8,128)(2,1)}, bf16[2432,128]{1,0:T(8,128)(2,1)}) fusion(bf16[3,2432,128]{2,1,0:T(8,128)(2,1)} %bitcast.35), kind=kLoop, calls=%fused_computation | loop fusion | bytes 3735552 | tf_op jit(solution)/shard_map/squeeze | solution.py:292
  16.8 2.1 %collective-permute-start = (bf16[2432,128]{1,0:T(8,128)(2,1)}, bf16[2432,128]{1,0:T(8,128)(2,1)}, u32[]{:S(2)}, u32[]{:S(2)}) collective-permute-start(bf16[2432,128]{1,0:T(8,128)(2,1)} %get-tuple-element.51), channel_id=1, source_target_pairs={{0,1},{1,0},{2,3},{3,2},{4,5},{5,4},{6,7},{7,6},{8,9},{9,8},{10,11... | collective-permute-start | bytes 1867784 | tf_op jit(solution)/shard_map/ppermute | solution.py:292
  19.0 2.3 %collective-permute-start.1 = (bf16[2432,128]{1,0:T(8,128)(2,1)}, bf16[2432,128]{1,0:T(8,128)(2,1)}, u32[]{:S(2)}, u32[]{:S(2)}) collective-permute-start(bf16[2432,128]{1,0:T(8,128)(2,1)} %get-tuple-element.50), channel_id=1, source_target_pairs={{0,1},{1,0},{2,3},{3,2},{4,5},{5,4},{6,7},{7,6},{8,9},{9,8},{10,11... | collective-permute-start | bytes 1867784 | tf_op jit(solution)/shard_map/ppermute | solution.py:292
  21.3 2.0 %collective-permute-start.2 = (bf16[2432,128]{1,0:T(8,128)(2,1)}, bf16[2432,128]{1,0:T(8,128)(2,1)}, u32[]{:S(2)}, u32[]{:S(2)}) collective-permute-start(bf16[2432,128]{1,0:T(8,128)(2,1)} %get-tuple-element.49), channel_id=1, source_target_pairs={{0,1},{1,0},{2,3},{3,2},{4,5},{5,4},{6,7},{7,6},{8,9},{9,8},{10,11... | collective-permute-start | bytes 1867784 | tf_op jit(solution)/shard_map/ppermute | solution.py:292
  23.3 2.3 %collective-permute-start.3 = (bf16[128,2432]{1,0:T(8,128)(2,1)S(1)}, bf16[128,2432]{1,0:T(8,128)(2,1)S(1)}, u32[]{:S(2)}, u32[]{:S(2)}) collective-permute-start(bf16[128,2432]{1,0:T(8,128)(2,1)S(1)} %copy-done), channel_id=1, source_target_pairs={{0,1},{1,0},{2,3},{3,2},{4,5},{5,4},{6,7},{7,6},{8,9},{9,8},{10,11... | collective-permute-start | bytes 1867784 | tf_op jit(solution)/shard_map/ppermute | solution.py:293
  25.6 0.7 slice.30
  26.4 0.1 tile.26
  26.5 0.1 tile.23
  26.7 0.1 dynamic-slice_bitcast_fusion.gate_ref
  26.8 2.0 %shard_map.83 = (bf16[2,2432,128]{2,1,0:T(8,128)(2,1)}, bf16[152,256]{1,0:T(8,128)(2,1)S(1)}, f32[1,128]{1,0:T(1,128)S(1)}) custom-call(s32[1]{0:T(128)} %bitcast.core_ref, s32[1,256]{1,0:T(1,128)S(1)} %bitcast.32, f32[1,256]{1,0:T(1,128)S(1)} %get-tuple-element.31.pos_ref, s32[1,32]{1,0:T(1,128)S(1)} %bitcast.34, bf16[3,28,2432]{2,1,0:T(8,128)(2,1)S(1)} %bitcast.28, ...), custom_call_target="tpu_custom_call" | custom-call | bytes 1048576 | tf_op jit(solution)/shard_map/pallas_call | solution.py:296
  28.8 0.0 collective-permute-done.sib0_hbm
  28.8 0.0 collective-permute-done.1.sib1_hbm
  28.8 0.0 collective-permute-done.3.refs_1_
  28.8 4.5 %all-to-all-done.tok_ref = bf16[16,152,128]{2,1,0:T(8,128)(2,1)S(1)} async-done(((bf16[16,152,128]{2,1,0:T(8,128)(2,1)}), bf16[16,152,128]{2,1,0:T(8,128)(2,1)S(1)}, u32[]{:S(2)}, u32[]{:S(2)}) %all-to-all-start) | async-done | bytes 622624 | tf_op jit(solution)/shard_map/all_to_all | solution.py:289
  33.3 4.1 %shard_map.84 = bf16[2,256,384]{2,1,0:T(8,128)(2,1)} custom-call(s32[1]{0:T(128)} %bitcast.core_ref, bf16[16,152,128]{2,1,0:T(8,128)(2,1)S(1)} %all-to-all-done.tok_ref, bf16[2,2432,128]{2,1,0:T(8,128)(2,1)} %get-tuple-element.36.mod_hbm, bf16[3,2432,128]{2,1,0:T(8,128)(2,1)} %bitcast.36, bf16[2432,128]{1,0:T(8,128)(2,1)} %collective-permute-done.sib0_hbm, ...), custom_call_target="tpu_custom_call" | custom-call | flops 478150656 | bytes 1048576 | tf_op jit(solution)/shard_map/pallas_call | solution.py:311
  37.4 10.3 %all-to-all-start.1 = ((bf16[64,8,384]{2,1,0:T(8,128)(2,1)}), bf16[64,8,384]{2,1,0:T(8,128)(2,1)S(1)}, u32[]{:S(2)}, u32[]{:S(2)}) async-start(bf16[64,8,384]{2,1,0:T(8,128)(2,1)} %bitcast.15), calls=%async_computation.1 | async-start | bytes 786432 | tf_op jit(solution)/shard_map/all_to_all | solution.py:325
  47.7 1.9 %collective-permute-start.4 = (bf16[48,2432]{1,0:T(8,128)(2,1)}, bf16[48,2432]{1,0:T(8,128)(2,1)S(1)}, u32[]{:S(2)}, u32[]{:S(2)}) collective-permute-start(bf16[48,2432]{1,0:T(8,128)(2,1)} %slice.30), channel_id=1, source_target_pairs={{0,2},{1,3},{2,0},{3,1},{4,6},{5,7},{6,4},{7,5},{8,10},{9,11},{10,... | collective-permute-start | bytes 700424 | tf_op jit(solution)/shard_map/ppermute | solution.py:329
  49.7 3.4 %collective-permute-start.5 = (bf16[80,2432]{1,0:T(8,128)(2,1)S(1)}, bf16[80,2432]{1,0:T(8,128)(2,1)S(1)}, u32[]{:S(2)}, u32[]{:S(2)}) collective-permute-start(bf16[80,2432]{1,0:T(8,128)(2,1)S(1)} %slice.31), channel_id=1, source_target_pairs={{0,2},{1,3},{2,0},{3,1},{4,6},{5,7},{6,4},{7,5},{8,10},{9,11},{10,... | collective-permute-start | bytes 1167368 | tf_op jit(solution)/shard_map/ppermute | solution.py:330
  53.0 2.4 %collective-permute-start.7 = (bf16[80,2432]{1,0:T(8,128)(2,1)S(1)}, bf16[80,2432]{1,0:T(8,128)(2,1)S(1)}, u32[]{:S(2)}, u32[]{:S(2)}) collective-permute-start(bf16[80,2432]{1,0:T(8,128)(2,1)S(1)} %slice.31), channel_id=1, source_target_pairs={{0,3},{1,2},{2,1},{3,0},{4,7},{5,6},{6,5},{7,4},{8,11},{9,10},{10,... | collective-permute-start | bytes 1167368 | tf_op jit(solution)/shard_map/ppermute | solution.py:331
  55.5 8.3 %all-to-all-done.1 = bf16[64,8,384]{2,1,0:T(8,128)(2,1)S(1)} async-done(((bf16[64,8,384]{2,1,0:T(8,128)(2,1)}), bf16[64,8,384]{2,1,0:T(8,128)(2,1)S(1)}, u32[]{:S(2)}, u32[]{:S(2)}) %all-to-all-start.1) | async-done | bytes 393248 | tf_op jit(solution)/shard_map/all_to_all | solution.py:325
  63.8 2.4 %shard_map.85 = bf16[512,128]{1,0:T(8,128)(2,1)} custom-call(bf16[512,384]{1,0:T(8,128)(2,1)S(1)} %bitcast.30, bf16[2,384,128]{2,1,0:T(8,128)(2,1)S(1)} %pad.4.ctx_ref), custom_call_target="tpu_custom_call" | custom-call | flops 469762048 | bytes 1048576 | tf_op jit(solution)/shard_map/pallas_call | solution.py:334
  66.1 7.0 %all-to-all-start.2 = ((bf16[128,4,128]{2,1,0:T(4,128)(2,1)}), bf16[128,4,128]{2,1,0:T(4,128)(2,1)S(1)}, u32[]{:S(2)}, u32[]{:S(2)}) async-start(bf16[128,4,128]{2,1,0:T(4,128)(2,1)} %bitcast.17), calls=%async_computation.2 | async-start | bytes 262144 | tf_op jit(solution)/shard_map/all_to_all | solution.py:341
  73.1 2.5 %collective-permute-start.6 = (bf16[48,2432]{1,0:T(8,128)(2,1)S(1)}, bf16[48,2432]{1,0:T(8,128)(2,1)S(1)}, u32[]{:S(2)}, u32[]{:S(2)}) collective-permute-start(bf16[48,2432]{1,0:T(8,128)(2,1)S(1)} %collective-permute-done.4.refs_2_), channel_id=1, source_target_pairs={{0,1},{1,0},{2,3},{3,2},{4,5},{5,4},{6,7},{7,6},{8,9},{9,8},{10,11... | collective-permute-start | bytes 700424 | tf_op jit(solution)/shard_map/ppermute | solution.py:332
  75.6 1.1 %collective-permute-done.6.refs_4_ = bf16[48,2432]{1,0:T(8,128)(2,1)S(1)} collective-permute-done((bf16[48,2432]{1,0:T(8,128)(2,1)S(1)}, bf16[48,2432]{1,0:T(8,128)(2,1)S(1)}, u32[]{:S(2)}, u32[]{:S(2)}) %collective-permute-start.6) | collective-permute-done | bytes 233504 | tf_op jit(solution)/shard_map/ppermute | solution.py:332
  76.7 7.0 %all-to-all-done.2 = bf16[128,4,128]{2,1,0:T(4,128)(2,1)S(1)} async-done(((bf16[128,4,128]{2,1,0:T(4,128)(2,1)}), bf16[128,4,128]{2,1,0:T(4,128)(2,1)S(1)}, u32[]{:S(2)}, u32[]{:S(2)}) %all-to-all-start.2) | async-done | bytes 131104 | tf_op jit(solution)/shard_map/all_to_all | solution.py:341
  83.7 1.3 %shard_map.86 = bf16[16,80,128]{2,1,0:T(8,128)(2,1)S(1)} custom-call(s32[1]{0:T(128)} %bitcast.core_ref, s32[1]{0:T(128)} %bitcast.1.parity_ref, bf16[2,256,128]{2,1,0:T(8,128)(2,1)S(1)} %bitcast.29, f32[1,128]{1,0:T(1,128)S(1)} %get-tuple-element.41.slot_ref, bf16[128,2432]{1,0:T(8,128)(2,1)S(1)} %copy-done, ...), custom_call_target="tpu_custom_call" | custom-call | flops 318767104 | bytes 1048576 | tf_op jit(solution)/shard_map/pallas_call | solution.py:344
  85.1 16.5 %all_to_all.20.sums_ref = bf16[16,80,128]{2,1,0:T(8,128)(2,1)S(1)} all-to-all(bf16[16,80,128]{2,1,0:T(8,128)(2,1)S(1)} %shard_map.86), channel_id=1, replica_groups=mesh['dp'=32,'mp'=16] {'mp'}, dimensions={0} | all-to-all | bytes 655360 | tf_op jit(solution)/shard_map/all_to_all | solution.py:351
  101.5 0.9 shard_map.87
  (23 shorter events, 0.1 us)
Async XLA Ops:
  2.1 31.2 %all-to-all-start = ((bf16[16,152,128]{2,1,0:T(8,128)(2,1)}), bf16[16,152,128]{2,1,0:T(8,128)(2,1)S(1)}, u32[]{:S(2)}, u32[]{:S(2)}) async-start(bf16[16,152,128]{2,1,0:T(8,128)(2,1)} %get-tuple-element.28), calls=%async_computation | async-start | bytes 1245184 | tf_op jit(solution)/shard_map/all_to_all | solution.py:289
  13.9 9.4 %copy-start = (bf16[128,2432]{1,0:T(8,128)(2,1)S(1)}, bf16[128,2432]{1,0:T(8,128)(2,1)}, u32[]{:S(2)}) copy-start(bf16[128,2432]{1,0:T(8,128)(2,1)} %refs_0_) | copy-start | bytes 1867780
  13.9 12.5 %copy-start.5 = (f32[2,64]{1,0:T(2,128)S(1)}, f32[2,64]{1,0:T(2,128)}, u32[]{:S(2)}) copy-start(f32[2,64]{1,0:T(2,128)} %param.13) | copy-start | bytes 1540
  14.0 12.7 %copy-start.4 = (bf16[1,2,333,128]{3,1,2,0:T(2,128)(2,1)S(1)}, bf16[1,2,333,128]{3,1,2,0:T(2,128)(2,1)}, u32[]{:S(2)}) copy-start(bf16[1,2,333,128]{3,1,2,0:T(2,128)(2,1)} %param.14) | copy-start | bytes 511492
  16.8 9.9 %slice-start = ((bf16[28,3,2432]{2,0,1:T(8,128)(2,1)}), bf16[28,1,2432]{2,0,1:T(8,128)(2,1)S(1)}, s32[]{:S(2)}) async-start(bf16[28,3,2432]{2,0,1:T(8,128)(2,1)} %param.11), calls=%async_computation.4 | async-start | bytes 311296 | tf_op jit(solution)/shard_map/slice | solution.py:295
  16.8 10.0 %copy-start.1 = (bf16[28,3,2432]{2,0,1:T(8,128)(2,1)S(1)}, bf16[28,3,2432]{2,0,1:T(8,128)(2,1)}, u32[]{:S(2)}) copy-start(bf16[28,3,2432]{2,0,1:T(8,128)(2,1)} %param.11) | copy-start | bytes 1225732
  16.8 10.0 %copy-start.2 = (s32[256,1]{0,1:T(1,128)S(1)}, s32[256,1]{0,1:T(1,128)}, u32[]{:S(2)}) copy-start(s32[256,1]{0,1:T(1,128)} %param.9) | copy-start | bytes 3076
  16.8 10.0 %copy-start.3 = (s32[32]{0:T(128)S(1)}, s32[32]{0:T(128)}, u32[]{:S(2)}) copy-start(s32[32]{0:T(128)} %param.10) | copy-start | bytes 388
  16.8 12.0 %collective-permute-start = (bf16[2432,128]{1,0:T(8,128)(2,1)}, bf16[2432,128]{1,0:T(8,128)(2,1)}, u32[]{:S(2)}, u32[]{:S(2)}) collective-permute-start(bf16[2432,128]{1,0:T(8,128)(2,1)} %get-tuple-element.51), channel_id=1, source_target_pairs={{0,1},{1,0},{2,3},{3,2},{4,5},{5,4},{6,7},{7,6},{8,9},{9,8},{10,11... | collective-permute-start | bytes 1867784 | tf_op jit(solution)/shard_map/ppermute | solution.py:292
  19.0 9.8 %collective-permute-start.1 = (bf16[2432,128]{1,0:T(8,128)(2,1)}, bf16[2432,128]{1,0:T(8,128)(2,1)}, u32[]{:S(2)}, u32[]{:S(2)}) collective-permute-start(bf16[2432,128]{1,0:T(8,128)(2,1)} %get-tuple-element.50), channel_id=1, source_target_pairs={{0,1},{1,0},{2,3},{3,2},{4,5},{5,4},{6,7},{7,6},{8,9},{9,8},{10,11... | collective-permute-start | bytes 1867784 | tf_op jit(solution)/shard_map/ppermute | solution.py:292
  21.3 7.5 %collective-permute-start.2 = (bf16[2432,128]{1,0:T(8,128)(2,1)}, bf16[2432,128]{1,0:T(8,128)(2,1)}, u32[]{:S(2)}, u32[]{:S(2)}) collective-permute-start(bf16[2432,128]{1,0:T(8,128)(2,1)} %get-tuple-element.49), channel_id=1, source_target_pairs={{0,1},{1,0},{2,3},{3,2},{4,5},{5,4},{6,7},{7,6},{8,9},{9,8},{10,11... | collective-permute-start | bytes 1867784 | tf_op jit(solution)/shard_map/ppermute | solution.py:292
  23.3 5.5 %collective-permute-start.3 = (bf16[128,2432]{1,0:T(8,128)(2,1)S(1)}, bf16[128,2432]{1,0:T(8,128)(2,1)S(1)}, u32[]{:S(2)}, u32[]{:S(2)}) collective-permute-start(bf16[128,2432]{1,0:T(8,128)(2,1)S(1)} %copy-done), channel_id=1, source_target_pairs={{0,1},{1,0},{2,3},{3,2},{4,5},{5,4},{6,7},{7,6},{8,9},{9,8},{10,11... | collective-permute-start | bytes 1867784 | tf_op jit(solution)/shard_map/ppermute | solution.py:293
  37.4 26.4 %all-to-all-start.1 = ((bf16[64,8,384]{2,1,0:T(8,128)(2,1)}), bf16[64,8,384]{2,1,0:T(8,128)(2,1)S(1)}, u32[]{:S(2)}, u32[]{:S(2)}) async-start(bf16[64,8,384]{2,1,0:T(8,128)(2,1)} %bitcast.15), calls=%async_computation.1 | async-start | bytes 786432 | tf_op jit(solution)/shard_map/all_to_all | solution.py:325
  47.7 25.4 %collective-permute-start.4 = (bf16[48,2432]{1,0:T(8,128)(2,1)}, bf16[48,2432]{1,0:T(8,128)(2,1)S(1)}, u32[]{:S(2)}, u32[]{:S(2)}) collective-permute-start(bf16[48,2432]{1,0:T(8,128)(2,1)} %slice.30), channel_id=1, source_target_pairs={{0,2},{1,3},{2,0},{3,1},{4,6},{5,7},{6,4},{7,5},{8,10},{9,11},{10,... | collective-permute-start | bytes 700424 | tf_op jit(solution)/shard_map/ppermute | solution.py:329
  49.7 25.9 %collective-permute-start.5 = (bf16[80,2432]{1,0:T(8,128)(2,1)S(1)}, bf16[80,2432]{1,0:T(8,128)(2,1)S(1)}, u32[]{:S(2)}, u32[]{:S(2)}) collective-permute-start(bf16[80,2432]{1,0:T(8,128)(2,1)S(1)} %slice.31), channel_id=1, source_target_pairs={{0,2},{1,3},{2,0},{3,1},{4,6},{5,7},{6,4},{7,5},{8,10},{9,11},{10,... | collective-permute-start | bytes 1167368 | tf_op jit(solution)/shard_map/ppermute | solution.py:330
  53.0 22.6 %collective-permute-start.7 = (bf16[80,2432]{1,0:T(8,128)(2,1)S(1)}, bf16[80,2432]{1,0:T(8,128)(2,1)S(1)}, u32[]{:S(2)}, u32[]{:S(2)}) collective-permute-start(bf16[80,2432]{1,0:T(8,128)(2,1)S(1)} %slice.31), channel_id=1, source_target_pairs={{0,3},{1,2},{2,1},{3,0},{4,7},{5,6},{6,5},{7,4},{8,11},{9,10},{10,... | collective-permute-start | bytes 1167368 | tf_op jit(solution)/shard_map/ppermute | solution.py:331
  66.1 17.6 %all-to-all-start.2 = ((bf16[128,4,128]{2,1,0:T(4,128)(2,1)}), bf16[128,4,128]{2,1,0:T(4,128)(2,1)S(1)}, u32[]{:S(2)}, u32[]{:S(2)}) async-start(bf16[128,4,128]{2,1,0:T(4,128)(2,1)} %bitcast.17), calls=%async_computation.2 | async-start | bytes 262144 | tf_op jit(solution)/shard_map/all_to_all | solution.py:341
  73.1 3.6 %collective-permute-start.6 = (bf16[48,2432]{1,0:T(8,128)(2,1)S(1)}, bf16[48,2432]{1,0:T(8,128)(2,1)S(1)}, u32[]{:S(2)}, u32[]{:S(2)}) collective-permute-start(bf16[48,2432]{1,0:T(8,128)(2,1)S(1)} %collective-permute-done.4.refs_2_), channel_id=1, source_target_pairs={{0,1},{1,0},{2,3},{3,2},{4,5},{5,4},{6,7},{7,6},{8,9},{9,8},{10,11... | collective-permute-start | bytes 700424 | tf_op jit(solution)/shard_map/ppermute | solution.py:332

commit v11 on v10

--- a/solution.py
+++ b/solution.py
@@ -79,12 +79,15 @@
 
 
 def prepare_kernel(
-    cap, core_ref, req_ref, pos_ref, steps_ref, table_ref, gate_ref, mod_hbm, gates_ref, slot_ref, mod_ref, sem
+    cap, core_ref, req_ref, pos_ref, steps_ref, table_hbm, gate_ref,
+    mod_hbm, gates_ref, slot_ref, mod_ref, table_ref, sems,
 ):
+    read = pltpu.make_async_copy(table_hbm.at[pl.ds(0, 2)], table_ref, sems.at[2])
+    read.start()
     rows = req_ref.shape[1]
     half = rows // 2
     requests = steps_ref.shape[1]
-    levels = table_ref.shape[1]
+    levels = gate_ref.shape[0]
     is_first = core_ref[0] == 0
     req = req_ref[...].astype(F32)
     first = jnp.sum(jnp.where(as_column(req) < req, 1.0, 0.0), axis=0, keepdims=True)
@@ -107,26 +110,28 @@
     pick = one_hot(iota((levels, rows), 0).astype(F32) == step)
     gates_ref[...] = dot_tn(gate_ref[...], pick).astype(BF16)
     pick = jnp.where(is_first, pick[:, :half].astype(F32), pick[:, half:].astype(F32)).astype(BF16)
-    mod_ref[0] = dot_tn(table_ref[0], pick).astype(BF16)
-    mod_ref[1] = dot_tn(table_ref[1], pick).astype(BF16)
-    copy = pltpu.make_async_copy(mod_ref, mod_hbm, sem)
-    copy.start()
-    copy.wait()
+    read.wait()
+    writes = []
+    for part in range(2):
+        mod_ref[part] = dot_tn(table_ref[part], pick).astype(BF16)
+        writes.append(pltpu.make_async_copy(mod_ref.at[part], mod_hbm.at[part], sems.at[part]))
+        writes[-1].start()
+    for copy in writes:
+        copy.wait()
 
 
 def project_kernel(
-    core_ref, tok_ref, mod_hbm, own_hbm, sib0_hbm, sib1_hbm, sib2_hbm, gain_ref, slot_ref,
+    core_ref, tok_ref, mod_hbm, own0_ref, own1_ref, own2_ref, sib0_hbm, sib1_hbm, sib2_hbm, gain_ref, slot_ref,
     send_ref, mod_ref, w_ref, hid_ref, sems,
 ):
     parts, width, rows = tok_ref.shape
     depth = parts * width
-    kinds, _, inner = own_hbm.shape
+    inner = own0_ref.shape[1]
     modulation = pltpu.make_async_copy(mod_hbm, mod_ref, sems.at[0])
     modulation.start()
-    sources = [own_hbm.at[kind] for kind in range(kinds)] + [sib0_hbm, sib1_hbm, sib2_hbm]
     weights = [
-        pltpu.make_async_copy(source, w_ref.at[i // kinds, :, pl.ds(i % kinds * inner, inner)], sems.at[1 + i])
-        for i, source in enumerate(sources)
+        pltpu.make_async_copy(source, w_ref.at[:, pl.ds(i * inner, inner)], sems.at[1 + i])
+        for i, source in enumerate((sib0_hbm, sib1_hbm, sib2_hbm))
     ]
     for copy in weights:
         copy.start()
@@ -147,18 +152,20 @@
     hidden = hid_ref[...].astype(F32).T.astype(BF16)
     normed = 2 * inner
     heads = one_hot(iota((normed, normed), 0) // HD == iota((normed, normed), 1) // HD)
-    projected = []
-    for side in range(2):
-        for copy in weights[side * kinds : (side + 1) * kinds]:
-            copy.wait()
-        projected.append(jnp.dot(hidden, w_ref[side], preferred_element_type=F32))
+    gain = [gain_ref[0:1, :] * HD ** (-0.5)] * (inner // HD) + [gain_ref[1:2, :]] * (inner // HD)
+    gain = jnp.concatenate(gain, axis=1)
+    own = jnp.concatenate([own0_ref[...], own1_ref[...], own2_ref[...]], axis=1)
+    projected = [jnp.dot(hidden, own, preferred_element_type=F32)]
+    for copy in weights:
+        copy.wait()
+    projected.append(jnp.dot(hidden, w_ref[...], preferred_element_type=F32))
     for mixed, target in zip(projected, (core_ref[0], 1 - core_ref[0])):
         turned = mixed[:, :normed]
         power = jnp.square(turned)
         high = power.astype(BF16)
         low = (power - high.astype(F32)).astype(BF16)
         power = jnp.dot(high, heads, preferred_element_type=F32) + jnp.dot(low, heads, preferred_element_type=F32)
-        turned = turned * lax.rsqrt(power * (1.0 / HD) + EPS) * gain_ref[...]
+        turned = turned * lax.rsqrt(power * (1.0 / HD) + EPS) * gain
         packed = jnp.concatenate([turned, mixed[:, normed:]], axis=1).astype(BF16)
         send = jnp.dot(place, packed, preferred_element_type=F32)
         send = jnp.concatenate([send[:, :inner], send[:, inner:normed] + mark, send[:, normed:]], axis=1)
@@ -273,6 +280,9 @@
     def in_hbm(x):
         return pltpu.with_memory_space_constraint(x, pltpu.HBM)
 
+    def in_vmem(x):
+        return pltpu.with_memory_space_constraint(x, pltpu.VMEM)
+
     spread, perm, pos = call(
         spread_kernel,
         (pltpu.HBM((parts, width, half), BF16), shape((width, rows), BF16), shape((1, rows), F32)),
@@ -288,40 +298,43 @@
     spread, w_qkv, w_out = lax.optimization_barrier((spread, w_qkv, w_out))
     whole = lax.all_to_all(spread, "mp", 0, 0, tiled=True)
 
-    w_own = w_qkv.transpose(1, 0, 2)
-    w_sib = [lax.ppermute(w_own[kind], "mp", sibling) for kind in range(kinds)]
+    w_own = [w_qkv[:, kind] for kind in range(kinds)]
+    w_sib = [lax.ppermute(block, "mp", sibling) for block in w_own]
     out_sib = lax.ppermute(w_out, "mp", sibling)
     first_rows = inner * 3 // 8
     gate_table = lax.dynamic_slice_in_dim(mod_table[:, 2, :], lax.axis_index("mp") * width, width, 1)
     mod, gates, slot = call(
         functools.partial(prepare_kernel, cap),
         (pltpu.HBM((2, depth, half), BF16), shape((width, rows), BF16), shape((1, half), F32)),
-        "svvvvv",
+        "svvvav",
         "avv",
-        [pltpu.VMEM((2, depth, half), BF16), pltpu.SemaphoreType.DMA],
-    )(core, req, pos, tsteps.reshape(1, requests), mod_table.transpose(1, 0, 2), gate_table)
-    gains = jnp.concatenate(
-        [jnp.tile(qk_gain[0] * HD ** (-0.5), inner // HD), jnp.tile(qk_gain[1], inner // HD)]
-    ).reshape(1, 2 * inner)
-    text = jnp.pad(context[0], ((0, 0), (0, text_pad - text_len), (0, 0)))
-    whole, w_sib, out_sib, mod, gates, slot, gains, text = lax.optimization_barrier(
-        (whole, w_sib, out_sib, mod, gates, slot, gains, text)
+        [
+            pltpu.VMEM((2, depth, half), BF16),
+            pltpu.VMEM((2, gate_table.shape[0], depth), BF16),
+            pltpu.SemaphoreType.DMA((3,)),
+        ],
+    )(core, req, pos, tsteps.reshape(1, requests), in_hbm(mod_table.transpose(1, 0, 2)), gate_table)
+    whole, w_own, w_sib, out_sib, mod, gates, slot = lax.optimization_barrier(
+        (whole, w_own, w_sib, out_sib, mod, gates, slot)
     )
 
     send = call(
         project_kernel,
         shape((2, slots, kinds * inner), BF16),
-        "svaaaaavv",
+        "svavvvaaavv",
         "v",
         [
             pltpu.VMEM((2, depth, half), BF16),
-            pltpu.VMEM((2, depth, kinds * inner), BF16),
+            pltpu.VMEM((depth, kinds * inner), BF16),
             pltpu.VMEM((depth, half), BF16),
-            pltpu.SemaphoreType.DMA((1 + 2 * kinds,)),
+            pltpu.SemaphoreType.DMA((1 + kinds,)),
         ],
         flops=4 * depth * half * kinds * inner,
-    )(core, whole, in_hbm(mod), in_hbm(w_own), *[in_hbm(w) for w in w_sib], gains, slot)
-    send, early, late = lax.optimization_barrier((send, w_out[:first_rows], w_out[first_rows:]))
+    )(core, whole, in_hbm(mod), *[in_vmem(w) for w in w_own], *[in_hbm(w) for w in w_sib], qk_gain, slot)
+    send, early, late, context = lax.optimization_barrier(
+        (send, w_out[:first_rows], w_out[first_rows:], context)
+    )
+    text = jnp.pad(context[0], ((0, 0), (0, text_pad - text_len), (0, 0)))
     arrived = lax.all_to_all(
         send.reshape(2 * requests, cap, kinds * inner), ("dp", "mp"), 0, 0, axis_index_groups=planes, tiled=True
     )

time: 103 us -> 104 us (level)
  Pallas kernels: 12.7 us -> 14.3 us
    squeeze x1, local copies, waits for them, and re-layouts: 2.82 us -> 1.64 us  [body(): w_own = [w_qkv[:, kind] for kind in range(kinds)]]
    pallas_call x1, Pallas kernels: 1.34 us -> 2.41 us  [body(): call(functools.partial(output_kernel, cap // 2), shape((parts, upper, hal...]
  transfers between devices with their start and end apart: 11 -> 11, of which waited for: 4 -> 4; matrix products, arithmetic and copies ran while one was open for 4% -> 4% of each run, Pallas kernels for 4% -> 5%
where the time goes in v11:
time: 104 us; the launch traced here: 103 us
  starting transfers between devices  48 us (46%)
  waiting for transfers between devices  19.9 us (19%)
  blocking collectives  16.4 us (16%)
  Pallas kernels  14.3 us (14%)
  local copies, waits for them, and re-layouts  4.2 us (4%)
    all_to_all x1, blocking collectives, body(): sums = lax.all_to_all(partial, 'mp', 0, 0, tiled=True)  16.4 us
    all_to_all x1, starting transfers between devices, body(): whole = lax.all_to_all(spread, 'mp', 0, 0, tiled=True)  11.8 us
    all_to_all x1, starting transfers between devices, body(): lax.all_to_all(send.reshape(2 * requests, cap, kinds * inner), ('dp', 'mp...  10.3 us
    all_to_all x1, waiting for transfers between devices, body(): lax.all_to_all(send.reshape(2 * requests, cap, kinds * inner), ('dp', 'mp...  7.29 us
    all_to_all x1, waiting for transfers between devices, body(): lax.all_to_all(attn.reshape(4 * requests, cap // 2, inner), ('dp', 'mp'),...  7.03 us
    all_to_all x1, starting transfers between devices, body(): lax.all_to_all(attn.reshape(4 * requests, cap // 2, inner), ('dp', 'mp'),...  6.95 us
    ppermute x3, starting transfers between devices, body(): w_sib = [lax.ppermute(block, 'mp', sibling) for block in w_own]  6.34 us
    all_to_all x1, waiting for transfers between devices, body(): whole = lax.all_to_all(spread, 'mp', 0, 0, tiled=True)  4.5 us
  transfers between devices with their start and end apart: 11, of which 4 were waited for; matrix products, arithmetic and copies ran while one was open for 4% of the time, Pallas kernels for 5%

profile of v11, /device:TPU:1, one launch (start us, length us, event | category | flops | bytes accessed | tf_op | source)
XLA Modules:
  0.0 103.1 jit_solution(6491461357973361736)
XLA Ops:
  0.0 2.1 %shard_map.82 = (bf16[16,152,128]{2,1,0:T(8,128)(2,1)}, bf16[152,256]{1,0:T(8,128)(2,1)S(1)}, f32[1,256]{1,0:T(1,128)S(1)}) custom-call(bf16[152,256]{1,0:T(8,128)(2,1)} %bitcast.29, s32[1,256]{1,0:T(1,128)} %bitcast.24), custom_call_target="tpu_custom_call" | custom-call | bytes 1048576 | tf_op jit(solution)/shard_map/pallas_call | solution.py:286
  2.1 11.8 %all-to-all-start = ((bf16[16,152,128]{2,1,0:T(8,128)(2,1)}), bf16[16,152,128]{2,1,0:T(8,128)(2,1)S(1)}, u32[]{:S(2)}, u32[]{:S(2)}) async-start(bf16[16,152,128]{2,1,0:T(8,128)(2,1)} %get-tuple-element.30), calls=%async_computation | async-start | bytes 1245184 | tf_op jit(solution)/shard_map/all_to_all | solution.py:299
  13.9 0.0 slice-start
  14.0 0.0 copy-start.1
  14.0 0.0 copy-start.3
  14.0 1.6 %slice_bitcast_fusion = (bf16[2432,128]{1,0:T(8,128)(2,1)S(1)}, bf16[2432,128]{1,0:T(8,128)(2,1)S(1)}, bf16[2432,128]{1,0:T(8,128)(2,1)S(1)}) fusion(bf16[2432,3,128]{2,0,1:T(8,128)(2,1)} %param.12), kind=kLoop, calls=%fused_computation | loop fusion | bytes 3735552 | tf_op jit(solution)/shard_map/squeeze | solution.py:301
  15.6 0.0 copy-start.2
  15.6 2.0 %collective-permute-start = (bf16[2432,128]{1,0:T(8,128)(2,1)S(1)}, bf16[2432,128]{1,0:T(8,128)(2,1)}, u32[]{:S(2)}, u32[]{:S(2)}) collective-permute-start(bf16[2432,128]{1,0:T(8,128)(2,1)S(1)} %get-tuple-element.39.own0_ref), channel_id=1, source_target_pairs={{0,1},{1,0},{2,3},{3,2},{4,5},{5,4},{6,7},{7,6},{8,9},{9,8},{10,11... | collective-permute-start | bytes 1867784 | tf_op jit(solution)/shard_map/ppermute | solution.py:302
  17.7 2.3 %collective-permute-start.1 = (bf16[2432,128]{1,0:T(8,128)(2,1)S(1)}, bf16[2432,128]{1,0:T(8,128)(2,1)}, u32[]{:S(2)}, u32[]{:S(2)}) collective-permute-start(bf16[2432,128]{1,0:T(8,128)(2,1)S(1)} %get-tuple-element.40.own1_ref), channel_id=1, source_target_pairs={{0,1},{1,0},{2,3},{3,2},{4,5},{5,4},{6,7},{7,6},{8,9},{9,8},{10,11... | collective-permute-start | bytes 1867784 | tf_op jit(solution)/shard_map/ppermute | solution.py:302
  20.0 2.0 %collective-permute-start.2 = (bf16[2432,128]{1,0:T(8,128)(2,1)S(1)}, bf16[2432,128]{1,0:T(8,128)(2,1)}, u32[]{:S(2)}, u32[]{:S(2)}) collective-permute-start(bf16[2432,128]{1,0:T(8,128)(2,1)S(1)} %get-tuple-element.41.own2_ref), channel_id=1, source_target_pairs={{0,1},{1,0},{2,3},{3,2},{4,5},{5,4},{6,7},{7,6},{8,9},{9,8},{10,11... | collective-permute-start | bytes 1867784 | tf_op jit(solution)/shard_map/ppermute | solution.py:302
  22.0 2.3 %collective-permute-start.3 = (bf16[128,2432]{1,0:T(8,128)(2,1)S(1)}, bf16[128,2432]{1,0:T(8,128)(2,1)}, u32[]{:S(2)}, u32[]{:S(2)}) collective-permute-start(bf16[128,2432]{1,0:T(8,128)(2,1)S(1)} %copy-done), channel_id=1, source_target_pairs={{0,1},{1,0},{2,3},{3,2},{4,5},{5,4},{6,7},{7,6},{8,9},{9,8},{10,11... | collective-permute-start | bytes 1867784 | tf_op jit(solution)/shard_map/ppermute | solution.py:303
  24.3 0.7 slice.22
  25.0 0.8 slice.23
  25.8 0.1 dynamic-slice_bitcast_fusion.gate_ref
  25.9 2.8 %shard_map.83 = (bf16[2,2432,128]{2,1,0:T(8,128)(2,1)}, bf16[152,256]{1,0:T(8,128)(2,1)S(1)}, f32[1,128]{1,0:T(1,128)S(1)}) custom-call(s32[1]{0:T(128)} %bitcast.core_ref, s32[1,256]{1,0:T(1,128)S(1)} %bitcast.25, f32[1,256]{1,0:T(1,128)S(1)} %get-tuple-element.33.pos_ref, s32[1,32]{1,0:T(1,128)S(1)} %bitcast.26, bf16[3,28,2432]{2,1,0:T(8,128)(2,1)} %bitcast.27, ...), custom_call_target="tpu_custom_call" | custom-call | bytes 1048576 | tf_op jit(solution)/shard_map/pallas_call | solution.py:306
  28.8 0.0 collective-permute-done.sib0_hbm
  28.8 4.5 %all-to-all-done.tok_ref = bf16[16,152,128]{2,1,0:T(8,128)(2,1)S(1)} async-done(((bf16[16,152,128]{2,1,0:T(8,128)(2,1)}), bf16[16,152,128]{2,1,0:T(8,128)(2,1)S(1)}, u32[]{:S(2)}, u32[]{:S(2)}) %all-to-all-start) | async-done | bytes 622624 | tf_op jit(solution)/shard_map/all_to_all | solution.py:299
  33.3 3.8 %shard_map.84 = bf16[2,256,384]{2,1,0:T(8,128)(2,1)} custom-call(s32[1]{0:T(128)} %bitcast.core_ref, bf16[16,152,128]{2,1,0:T(8,128)(2,1)S(1)} %all-to-all-done.tok_ref, bf16[2,2432,128]{2,1,0:T(8,128)(2,1)} %get-tuple-element.38.mod_hbm, bf16[2432,128]{1,0:T(8,128)(2,1)S(1)} %get-tuple-element.39.own0_ref, ...), custom_call_target="tpu_custom_call" | custom-call | flops 478150656 | bytes 1048576 | tf_op jit(solution)/shard_map/pallas_call | solution.py:321
  37.1 10.3 %all-to-all-start.1 = ((bf16[64,8,384]{2,1,0:T(8,128)(2,1)}), bf16[64,8,384]{2,1,0:T(8,128)(2,1)S(1)}, u32[]{:S(2)}, u32[]{:S(2)}) async-start(bf16[64,8,384]{2,1,0:T(8,128)(2,1)} %bitcast.10), calls=%async_computation.1 | async-start | bytes 786432 | tf_op jit(solution)/shard_map/all_to_all | solution.py:338
  47.4 1.9 %collective-permute-start.4 = (bf16[48,2432]{1,0:T(8,128)(2,1)S(1)}, bf16[48,2432]{1,0:T(8,128)(2,1)S(1)}, u32[]{:S(2)}, u32[]{:S(2)}) collective-permute-start(bf16[48,2432]{1,0:T(8,128)(2,1)S(1)} %copy-done.4), channel_id=1, source_target_pairs={{0,2},{1,3},{2,0},{3,1},{4,6},{5,7},{6,4},{7,5},{8,10},{9,11},{10,... | collective-permute-start | bytes 700424 | tf_op jit(solution)/shard_map/ppermute | solution.py:342
  49.3 3.4 %collective-permute-start.5 = (bf16[80,2432]{1,0:T(8,128)(2,1)}, bf16[80,2432]{1,0:T(8,128)(2,1)S(1)}, u32[]{:S(2)}, u32[]{:S(2)}) collective-permute-start(bf16[80,2432]{1,0:T(8,128)(2,1)} %slice.23), channel_id=1, source_target_pairs={{0,2},{1,3},{2,0},{3,1},{4,6},{5,7},{6,4},{7,5},{8,10},{9,11},{10,... | collective-permute-start | bytes 1167368 | tf_op jit(solution)/shard_map/ppermute | solution.py:343
  52.7 2.4 %collective-permute-start.7 = (bf16[80,2432]{1,0:T(8,128)(2,1)}, bf16[80,2432]{1,0:T(8,128)(2,1)S(1)}, u32[]{:S(2)}, u32[]{:S(2)}) collective-permute-start(bf16[80,2432]{1,0:T(8,128)(2,1)} %slice.23), channel_id=1, source_target_pairs={{0,3},{1,2},{2,1},{3,0},{4,7},{5,6},{6,5},{7,4},{8,11},{9,10},{10,... | collective-permute-start | bytes 1167368 | tf_op jit(solution)/shard_map/ppermute | solution.py:344
  55.1 0.9 copy.11
  56.1 7.3 %all-to-all-done.1 = bf16[64,8,384]{2,1,0:T(8,128)(2,1)S(1)} async-done(((bf16[64,8,384]{2,1,0:T(8,128)(2,1)}), bf16[64,8,384]{2,1,0:T(8,128)(2,1)S(1)}, u32[]{:S(2)}, u32[]{:S(2)}) %all-to-all-start.1) | async-done | bytes 393248 | tf_op jit(solution)/shard_map/all_to_all | solution.py:338
  63.4 2.4 %shard_map.85 = bf16[512,128]{1,0:T(8,128)(2,1)} custom-call(bf16[512,384]{1,0:T(8,128)(2,1)S(1)} %bitcast.23, bf16[2,384,128]{2,1,0:T(8,128)(2,1)S(1)} %pad.4.ctx_ref), custom_call_target="tpu_custom_call" | custom-call | flops 469762048 | bytes 1048576 | tf_op jit(solution)/shard_map/pallas_call | solution.py:347
  65.8 7.0 %all-to-all-start.2 = ((bf16[128,4,128]{2,1,0:T(4,128)(2,1)}), bf16[128,4,128]{2,1,0:T(4,128)(2,1)S(1)}, u32[]{:S(2)}, u32[]{:S(2)}) async-start(bf16[128,4,128]{2,1,0:T(4,128)(2,1)} %bitcast.13), calls=%async_computation.2 | async-start | bytes 262144 | tf_op jit(solution)/shard_map/all_to_all | solution.py:354
  72.8 2.5 %collective-permute-start.6 = (bf16[48,2432]{1,0:T(8,128)(2,1)S(1)}, bf16[48,2432]{1,0:T(8,128)(2,1)S(1)}, u32[]{:S(2)}, u32[]{:S(2)}) collective-permute-start(bf16[48,2432]{1,0:T(8,128)(2,1)S(1)} %collective-permute-done.4.refs_2_), channel_id=1, source_target_pairs={{0,1},{1,0},{2,3},{3,2},{4,5},{5,4},{6,7},{7,6},{8,9},{9,8},{10,11... | collective-permute-start | bytes 700424 | tf_op jit(solution)/shard_map/ppermute | solution.py:345
  75.3 1.1 %collective-permute-done.6.refs_4_ = bf16[48,2432]{1,0:T(8,128)(2,1)S(1)} collective-permute-done((bf16[48,2432]{1,0:T(8,128)(2,1)S(1)}, bf16[48,2432]{1,0:T(8,128)(2,1)S(1)}, u32[]{:S(2)}, u32[]{:S(2)}) %collective-permute-start.6) | collective-permute-done | bytes 233504 | tf_op jit(solution)/shard_map/ppermute | solution.py:345
  76.4 7.0 %all-to-all-done.2 = bf16[128,4,128]{2,1,0:T(4,128)(2,1)S(1)} async-done(((bf16[128,4,128]{2,1,0:T(4,128)(2,1)}), bf16[128,4,128]{2,1,0:T(4,128)(2,1)S(1)}, u32[]{:S(2)}, u32[]{:S(2)}) %all-to-all-start.2) | async-done | bytes 131104 | tf_op jit(solution)/shard_map/all_to_all | solution.py:354
  83.4 2.4 %shard_map.86 = bf16[16,80,128]{2,1,0:T(8,128)(2,1)S(1)} custom-call(s32[1]{0:T(128)} %bitcast.core_ref, s32[1]{0:T(128)} %bitcast.1.parity_ref, bf16[2,256,128]{2,1,0:T(8,128)(2,1)S(1)} %bitcast.22, f32[1,128]{1,0:T(1,128)S(1)} %get-tuple-element.45.slot_ref, bf16[128,2432]{1,0:T(8,128)(2,1)S(1)} %copy-done, ...), custom_call_target="tpu_custom_call" | custom-call | flops 318767104 | bytes 1048576 | tf_op jit(solution)/shard_map/pallas_call | solution.py:357
  85.8 16.4 %all_to_all.20.sums_ref = bf16[16,80,128]{2,1,0:T(8,128)(2,1)S(1)} all-to-all(bf16[16,80,128]{2,1,0:T(8,128)(2,1)S(1)} %shard_map.86), channel_id=1, replica_groups=mesh['dp'=32,'mp'=16] {'mp'}, dimensions={0} | all-to-all | bytes 655360 | tf_op jit(solution)/shard_map/all_to_all | solution.py:364
  102.2 0.9 shard_map.87
  (15 shorter events, 0.0 us)
Async XLA Ops:
  2.1 31.2 %all-to-all-start = ((bf16[16,152,128]{2,1,0:T(8,128)(2,1)}), bf16[16,152,128]{2,1,0:T(8,128)(2,1)S(1)}, u32[]{:S(2)}, u32[]{:S(2)}) async-start(bf16[16,152,128]{2,1,0:T(8,128)(2,1)} %get-tuple-element.30), calls=%async_computation | async-start | bytes 1245184 | tf_op jit(solution)/shard_map/all_to_all | solution.py:299
  13.9 8.1 %copy-start = (bf16[128,2432]{1,0:T(8,128)(2,1)S(1)}, bf16[128,2432]{1,0:T(8,128)(2,1)}, u32[]{:S(2)}) copy-start(bf16[128,2432]{1,0:T(8,128)(2,1)} %refs_0_) | copy-start | bytes 1867780
  13.9 11.9 %slice-start = ((bf16[28,3,2432]{2,0,1:T(8,128)(2,1)}), bf16[28,1,2432]{2,0,1:T(8,128)(2,1)S(1)}, s32[]{:S(2)}) async-start(bf16[28,3,2432]{2,0,1:T(8,128)(2,1)} %param.11), calls=%async_computation.4 | async-start | bytes 311296 | tf_op jit(solution)/shard_map/slice | solution.py:305
  14.0 12.0 %copy-start.1 = (s32[256,1]{0,1:T(1,128)S(1)}, s32[256,1]{0,1:T(1,128)}, u32[]{:S(2)}) copy-start(s32[256,1]{0,1:T(1,128)} %param.9) | copy-start | bytes 3076
  14.0 11.9 %copy-start.3 = (s32[32]{0:T(128)S(1)}, s32[32]{0:T(128)}, u32[]{:S(2)}) copy-start(s32[32]{0:T(128)} %param.10) | copy-start | bytes 388
  15.6 17.7 %copy-start.2 = (f32[2,64]{1,0:T(2,128)S(1)}, f32[2,64]{1,0:T(2,128)}, u32[]{:S(2)}) copy-start(f32[2,64]{1,0:T(2,128)} %gain_ref.1) | copy-start | bytes 1540
  15.6 13.1 %collective-permute-start = (bf16[2432,128]{1,0:T(8,128)(2,1)S(1)}, bf16[2432,128]{1,0:T(8,128)(2,1)}, u32[]{:S(2)}, u32[]{:S(2)}) collective-permute-start(bf16[2432,128]{1,0:T(8,128)(2,1)S(1)} %get-tuple-element.39.own0_ref), channel_id=1, source_target_pairs={{0,1},{1,0},{2,3},{3,2},{4,5},{5,4},{6,7},{7,6},{8,9},{9,8},{10,11... | collective-permute-start | bytes 1867784 | tf_op jit(solution)/shard_map/ppermute | solution.py:302
  17.7 11.1 %collective-permute-start.1 = (bf16[2432,128]{1,0:T(8,128)(2,1)S(1)}, bf16[2432,128]{1,0:T(8,128)(2,1)}, u32[]{:S(2)}, u32[]{:S(2)}) collective-permute-start(bf16[2432,128]{1,0:T(8,128)(2,1)S(1)} %get-tuple-element.40.own1_ref), channel_id=1, source_target_pairs={{0,1},{1,0},{2,3},{3,2},{4,5},{5,4},{6,7},{7,6},{8,9},{9,8},{10,11... | collective-permute-start | bytes 1867784 | tf_op jit(solution)/shard_map/ppermute | solution.py:302
  20.0 8.8 %collective-permute-start.2 = (bf16[2432,128]{1,0:T(8,128)(2,1)S(1)}, bf16[2432,128]{1,0:T(8,128)(2,1)}, u32[]{:S(2)}, u32[]{:S(2)}) collective-permute-start(bf16[2432,128]{1,0:T(8,128)(2,1)S(1)} %get-tuple-element.41.own2_ref), channel_id=1, source_target_pairs={{0,1},{1,0},{2,3},{3,2},{4,5},{5,4},{6,7},{7,6},{8,9},{9,8},{10,11... | collective-permute-start | bytes 1867784 | tf_op jit(solution)/shard_map/ppermute | solution.py:302
  22.0 6.8 %collective-permute-start.3 = (bf16[128,2432]{1,0:T(8,128)(2,1)S(1)}, bf16[128,2432]{1,0:T(8,128)(2,1)}, u32[]{:S(2)}, u32[]{:S(2)}) collective-permute-start(bf16[128,2432]{1,0:T(8,128)(2,1)S(1)} %copy-done), channel_id=1, source_target_pairs={{0,1},{1,0},{2,3},{3,2},{4,5},{5,4},{6,7},{7,6},{8,9},{9,8},{10,11... | collective-permute-start | bytes 1867784 | tf_op jit(solution)/shard_map/ppermute | solution.py:303
  33.3 14.1 %copy-start.4 = (bf16[48,2432]{1,0:T(8,128)(2,1)S(1)}, bf16[48,2432]{1,0:T(8,128)(2,1)}, u32[]{:S(2)}) copy-start(bf16[48,2432]{1,0:T(8,128)(2,1)} %slice.22) | copy-start | bytes 700420
  37.1 26.3 %all-to-all-start.1 = ((bf16[64,8,384]{2,1,0:T(8,128)(2,1)}), bf16[64,8,384]{2,1,0:T(8,128)(2,1)S(1)}, u32[]{:S(2)}, u32[]{:S(2)}) async-start(bf16[64,8,384]{2,1,0:T(8,128)(2,1)} %bitcast.10), calls=%async_computation.1 | async-start | bytes 786432 | tf_op jit(solution)/shard_map/all_to_all | solution.py:338
  47.4 25.4 %collective-permute-start.4 = (bf16[48,2432]{1,0:T(8,128)(2,1)S(1)}, bf16[48,2432]{1,0:T(8,128)(2,1)S(1)}, u32[]{:S(2)}, u32[]{:S(2)}) collective-permute-start(bf16[48,2432]{1,0:T(8,128)(2,1)S(1)} %copy-done.4), channel_id=1, source_target_pairs={{0,2},{1,3},{2,0},{3,1},{4,6},{5,7},{6,4},{7,5},{8,10},{9,11},{10,... | collective-permute-start | bytes 700424 | tf_op jit(solution)/shard_map/ppermute | solution.py:342
  49.3 26.0 %collective-permute-start.5 = (bf16[80,2432]{1,0:T(8,128)(2,1)}, bf16[80,2432]{1,0:T(8,128)(2,1)S(1)}, u32[]{:S(2)}, u32[]{:S(2)}) collective-permute-start(bf16[80,2432]{1,0:T(8,128)(2,1)} %slice.23), channel_id=1, source_target_pairs={{0,2},{1,3},{2,0},{3,1},{4,6},{5,7},{6,4},{7,5},{8,10},{9,11},{10,... | collective-permute-start | bytes 1167368 | tf_op jit(solution)/shard_map/ppermute | solution.py:343
  52.7 22.6 %collective-permute-start.7 = (bf16[80,2432]{1,0:T(8,128)(2,1)}, bf16[80,2432]{1,0:T(8,128)(2,1)S(1)}, u32[]{:S(2)}, u32[]{:S(2)}) collective-permute-start(bf16[80,2432]{1,0:T(8,128)(2,1)} %slice.23), channel_id=1, source_target_pairs={{0,3},{1,2},{2,1},{3,0},{4,7},{5,6},{6,5},{7,4},{8,11},{9,10},{10,... | collective-permute-start | bytes 1167368 | tf_op jit(solution)/shard_map/ppermute | solution.py:344
  65.8 17.6 %all-to-all-start.2 = ((bf16[128,4,128]{2,1,0:T(4,128)(2,1)}), bf16[128,4,128]{2,1,0:T(4,128)(2,1)S(1)}, u32[]{:S(2)}, u32[]{:S(2)}) async-start(bf16[128,4,128]{2,1,0:T(4,128)(2,1)} %bitcast.13), calls=%async_computation.2 | async-start | bytes 262144 | tf_op jit(solution)/shard_map/all_to_all | solution.py:354
  72.8 3.6 %collective-permute-start.6 = (bf16[48,2432]{1,0:T(8,128)(2,1)S(1)}, bf16[48,2432]{1,0:T(8,128)(2,1)S(1)}, u32[]{:S(2)}, u32[]{:S(2)}) collective-permute-start(bf16[48,2432]{1,0:T(8,128)(2,1)S(1)} %collective-permute-done.4.refs_2_), channel_id=1, source_target_pairs={{0,1},{1,0},{2,3},{3,2},{4,5},{5,4},{6,7},{7,6},{8,9},{9,8},{10,11... | collective-permute-start | bytes 700424 | tf_op jit(solution)/shard_map/ppermute | solution.py:345

commit v12 on v11

--- a/solution.py
+++ b/solution.py
@@ -225,6 +225,12 @@
         part_ref[m] = (above + pltpu.roll(below, quarter, 1)).astype(BF16)
 
 
+def stage_kernel(hbm, out_ref, sem):
+    copy = pltpu.make_async_copy(hbm, out_ref, sem)
+    copy.start()
+    copy.wait()
+
+
 def finish_kernel(sums_ref, perm_ref, gates_ref, pos_ref, out_ref):
     parts, upper, lanes = sums_ref.shape
     width, rows = perm_ref.shape
@@ -343,7 +349,6 @@
     next_late = lax.ppermute(late, "mp", next_level)
     far_late = lax.ppermute(late, "mp", [(i, i ^ 3) for i in range(parts)])
     far_early = lax.ppermute(next_early, "mp", sibling)
-    blocks = (w_out, out_sib, next_early, next_late, far_early, far_late)
     attn = call(
         functools.partial(attend_kernel, text_len),
         shape((2 * slots, inner), BF16),
@@ -354,6 +359,9 @@
     returned = lax.all_to_all(
         attn.reshape(4 * requests, cap // 2, inner), ("dp", "mp"), 0, 0, axis_index_groups=pairs, tiled=True
     )
+    _, out_sib = lax.optimization_barrier((attn, out_sib))
+    out_sib = call(stage_kernel, shape((inner, depth), BF16), "a", "v", [pltpu.SemaphoreType.DMA])(in_hbm(out_sib))
+    blocks = (w_out, out_sib, next_early, next_late, far_early, far_late)
     partial = call(
         functools.partial(output_kernel, cap // 2),
         shape((parts, upper, half), BF16),

time: 104 us -> 103 us (level)
  waiting for transfers between devices: 19.9 us -> 18.8 us
    pallas_call x0 -> x1, Pallas kernels: none -> 1.09 us  [body(): call(stage_kernel, shape((inner, depth), BF16), 'a', 'v', [pltpu.Semaphor...]
    pallas_call x1, Pallas kernels: 2.41 us -> 1.34 us  [body(): call(functools.partial(output_kernel, cap // 2), shape((parts, upper, hal...]
    ppermute x1, waiting for transfers between devices: 1.07 us -> 0.01 us  [body(): far_early = lax.ppermute(next_early, 'mp', sibling)]
  transfers between devices with their start and end apart: 11 -> 11, of which waited for: 4 -> 3; matrix products, arithmetic and copies ran while one was open for 4% -> 4% of each run, Pallas kernels for 5% -> 6%
where the time goes in v12:
time: 103 us; the launch traced here: 102 us
  starting transfers between devices  48 us (47%)
  waiting for transfers between devices  18.8 us (18%)
  blocking collectives  16.4 us (16%)
  Pallas kernels  14.3 us (14%)
  local copies, waits for them, and re-layouts  4.2 us (4%)
    all_to_all x1, blocking collectives, body(): sums = lax.all_to_all(partial, 'mp', 0, 0, tiled=True)  16.4 us
    all_to_all x1, starting transfers between devices, body(): whole = lax.all_to_all(spread, 'mp', 0, 0, tiled=True)  11.8 us
    all_to_all x1, starting transfers between devices, body(): lax.all_to_all(send.reshape(2 * requests, cap, kinds * inner), ('dp', 'mp...  10.3 us
    all_to_all x1, waiting for transfers between devices, body(): lax.all_to_all(send.reshape(2 * requests, cap, kinds * inner), ('dp', 'mp...  7.29 us
    all_to_all x1, waiting for transfers between devices, body(): lax.all_to_all(attn.reshape(4 * requests, cap // 2, inner), ('dp', 'mp'),...  6.99 us
    all_to_all x1, starting transfers between devices, body(): lax.all_to_all(attn.reshape(4 * requests, cap // 2, inner), ('dp', 'mp'),...  6.95 us
    ppermute x3, starting transfers between devices, body(): w_sib = [lax.ppermute(block, 'mp', sibling) for block in w_own]  6.34 us
    all_to_all x1, waiting for transfers between devices, body(): whole = lax.all_to_all(spread, 'mp', 0, 0, tiled=True)  4.5 us
  transfers between devices with their start and end apart: 11, of which 3 were waited for; matrix products, arithmetic and copies ran while one was open for 4% of the time, Pallas kernels for 6%

profile of v12, /device:TPU:1, one launch (start us, length us, event | category | flops | bytes accessed | tf_op | source)
XLA Modules:
  0.0 102.1 jit_solution(13225966662538763159)
XLA Ops:
  0.0 2.1 %shard_map.82 = (bf16[16,152,128]{2,1,0:T(8,128)(2,1)}, bf16[152,256]{1,0:T(8,128)(2,1)S(1)}, f32[1,256]{1,0:T(1,128)S(1)}) custom-call(bf16[152,256]{1,0:T(8,128)(2,1)} %bitcast.29, s32[1,256]{1,0:T(1,128)} %bitcast.24), custom_call_target="tpu_custom_call" | custom-call | bytes 1048576 | tf_op jit(solution)/shard_map/pallas_call | solution.py:292
  2.1 11.8 %all-to-all-start = ((bf16[16,152,128]{2,1,0:T(8,128)(2,1)}), bf16[16,152,128]{2,1,0:T(8,128)(2,1)S(1)}, u32[]{:S(2)}, u32[]{:S(2)}) async-start(bf16[16,152,128]{2,1,0:T(8,128)(2,1)} %get-tuple-element.31), calls=%async_computation | async-start | bytes 1245184 | tf_op jit(solution)/shard_map/all_to_all | solution.py:305
  13.9 0.0 slice-start
  14.0 0.0 copy-start.1
  14.0 0.0 copy-start.3
  14.0 1.6 %slice_bitcast_fusion = (bf16[2432,128]{1,0:T(8,128)(2,1)S(1)}, bf16[2432,128]{1,0:T(8,128)(2,1)S(1)}, bf16[2432,128]{1,0:T(8,128)(2,1)S(1)}) fusion(bf16[2432,3,128]{2,0,1:T(8,128)(2,1)} %param.12), kind=kLoop, calls=%fused_computation | loop fusion | bytes 3735552 | tf_op jit(solution)/shard_map/squeeze | solution.py:307
  15.6 0.0 copy-start.2
  15.6 2.0 %collective-permute-start = (bf16[2432,128]{1,0:T(8,128)(2,1)S(1)}, bf16[2432,128]{1,0:T(8,128)(2,1)}, u32[]{:S(2)}, u32[]{:S(2)}) collective-permute-start(bf16[2432,128]{1,0:T(8,128)(2,1)S(1)} %get-tuple-element.40.own0_ref), channel_id=1, source_target_pairs={{0,1},{1,0},{2,3},{3,2},{4,5},{5,4},{6,7},{7,6},{8,9},{9,8},{10,11... | collective-permute-start | bytes 1867784 | tf_op jit(solution)/shard_map/ppermute | solution.py:308
  17.7 2.3 %collective-permute-start.1 = (bf16[2432,128]{1,0:T(8,128)(2,1)S(1)}, bf16[2432,128]{1,0:T(8,128)(2,1)}, u32[]{:S(2)}, u32[]{:S(2)}) collective-permute-start(bf16[2432,128]{1,0:T(8,128)(2,1)S(1)} %get-tuple-element.41.own1_ref), channel_id=1, source_target_pairs={{0,1},{1,0},{2,3},{3,2},{4,5},{5,4},{6,7},{7,6},{8,9},{9,8},{10,11... | collective-permute-start | bytes 1867784 | tf_op jit(solution)/shard_map/ppermute | solution.py:308
  20.0 2.0 %collective-permute-start.2 = (bf16[2432,128]{1,0:T(8,128)(2,1)S(1)}, bf16[2432,128]{1,0:T(8,128)(2,1)}, u32[]{:S(2)}, u32[]{:S(2)}) collective-permute-start(bf16[2432,128]{1,0:T(8,128)(2,1)S(1)} %get-tuple-element.42.own2_ref), channel_id=1, source_target_pairs={{0,1},{1,0},{2,3},{3,2},{4,5},{5,4},{6,7},{7,6},{8,9},{9,8},{10,11... | collective-permute-start | bytes 1867784 | tf_op jit(solution)/shard_map/ppermute | solution.py:308
  22.0 2.3 %collective-permute-start.3 = (bf16[128,2432]{1,0:T(8,128)(2,1)S(1)}, bf16[128,2432]{1,0:T(8,128)(2,1)}, u32[]{:S(2)}, u32[]{:S(2)}) collective-permute-start(bf16[128,2432]{1,0:T(8,128)(2,1)S(1)} %copy-done), channel_id=1, source_target_pairs={{0,1},{1,0},{2,3},{3,2},{4,5},{5,4},{6,7},{7,6},{8,9},{9,8},{10,11... | collective-permute-start | bytes 1867784 | tf_op jit(solution)/shard_map/ppermute | solution.py:309
  24.3 0.7 slice.22
  25.0 0.8 slice.23
  25.8 0.1 dynamic-slice_bitcast_fusion.gate_ref
  25.9 2.8 %shard_map.83 = (bf16[2,2432,128]{2,1,0:T(8,128)(2,1)}, bf16[152,256]{1,0:T(8,128)(2,1)S(1)}, f32[1,128]{1,0:T(1,128)S(1)}) custom-call(s32[1]{0:T(128)} %bitcast.core_ref, s32[1,256]{1,0:T(1,128)S(1)} %bitcast.25, f32[1,256]{1,0:T(1,128)S(1)} %get-tuple-element.34.pos_ref, s32[1,32]{1,0:T(1,128)S(1)} %bitcast.26, bf16[3,28,2432]{2,1,0:T(8,128)(2,1)} %bitcast.27, ...), custom_call_target="tpu_custom_call" | custom-call | bytes 1048576 | tf_op jit(solution)/shard_map/pallas_call | solution.py:312
  28.8 0.0 collective-permute-done.sib0_hbm
  28.8 4.5 %all-to-all-done.tok_ref = bf16[16,152,128]{2,1,0:T(8,128)(2,1)S(1)} async-done(((bf16[16,152,128]{2,1,0:T(8,128)(2,1)}), bf16[16,152,128]{2,1,0:T(8,128)(2,1)S(1)}, u32[]{:S(2)}, u32[]{:S(2)}) %all-to-all-start) | async-done | bytes 622624 | tf_op jit(solution)/shard_map/all_to_all | solution.py:305
  33.3 3.8 %shard_map.84 = bf16[2,256,384]{2,1,0:T(8,128)(2,1)} custom-call(s32[1]{0:T(128)} %bitcast.core_ref, bf16[16,152,128]{2,1,0:T(8,128)(2,1)S(1)} %all-to-all-done.tok_ref, bf16[2,2432,128]{2,1,0:T(8,128)(2,1)} %get-tuple-element.39.mod_hbm, bf16[2432,128]{1,0:T(8,128)(2,1)S(1)} %get-tuple-element.40.own0_ref, ...), custom_call_target="tpu_custom_call" | custom-call | flops 478150656 | bytes 1048576 | tf_op jit(solution)/shard_map/pallas_call | solution.py:327
  37.1 10.3 %all-to-all-start.1 = ((bf16[64,8,384]{2,1,0:T(8,128)(2,1)}), bf16[64,8,384]{2,1,0:T(8,128)(2,1)S(1)}, u32[]{:S(2)}, u32[]{:S(2)}) async-start(bf16[64,8,384]{2,1,0:T(8,128)(2,1)} %bitcast.10), calls=%async_computation.1 | async-start | bytes 786432 | tf_op jit(solution)/shard_map/all_to_all | solution.py:344
  47.4 1.9 %collective-permute-start.4 = (bf16[48,2432]{1,0:T(8,128)(2,1)S(1)}, bf16[48,2432]{1,0:T(8,128)(2,1)S(1)}, u32[]{:S(2)}, u32[]{:S(2)}) collective-permute-start(bf16[48,2432]{1,0:T(8,128)(2,1)S(1)} %copy-done.4), channel_id=1, source_target_pairs={{0,2},{1,3},{2,0},{3,1},{4,6},{5,7},{6,4},{7,5},{8,10},{9,11},{10,... | collective-permute-start | bytes 700424 | tf_op jit(solution)/shard_map/ppermute | solution.py:348
  49.3 3.4 %collective-permute-start.5 = (bf16[80,2432]{1,0:T(8,128)(2,1)}, bf16[80,2432]{1,0:T(8,128)(2,1)S(1)}, u32[]{:S(2)}, u32[]{:S(2)}) collective-permute-start(bf16[80,2432]{1,0:T(8,128)(2,1)} %slice.23), channel_id=1, source_target_pairs={{0,2},{1,3},{2,0},{3,1},{4,6},{5,7},{6,4},{7,5},{8,10},{9,11},{10,... | collective-permute-start | bytes 1167368 | tf_op jit(solution)/shard_map/ppermute | solution.py:349
  52.7 2.4 %collective-permute-start.7 = (bf16[80,2432]{1,0:T(8,128)(2,1)}, bf16[80,2432]{1,0:T(8,128)(2,1)S(1)}, u32[]{:S(2)}, u32[]{:S(2)}) collective-permute-start(bf16[80,2432]{1,0:T(8,128)(2,1)} %slice.23), channel_id=1, source_target_pairs={{0,3},{1,2},{2,1},{3,0},{4,7},{5,6},{6,5},{7,4},{8,11},{9,10},{10,... | collective-permute-start | bytes 1167368 | tf_op jit(solution)/shard_map/ppermute | solution.py:350
  55.2 0.9 copy.11
  56.1 7.3 %all-to-all-done.1 = bf16[64,8,384]{2,1,0:T(8,128)(2,1)S(1)} async-done(((bf16[64,8,384]{2,1,0:T(8,128)(2,1)}), bf16[64,8,384]{2,1,0:T(8,128)(2,1)S(1)}, u32[]{:S(2)}, u32[]{:S(2)}) %all-to-all-start.1) | async-done | bytes 393248 | tf_op jit(solution)/shard_map/all_to_all | solution.py:344
  63.4 2.4 %shard_map.85 = bf16[512,128]{1,0:T(8,128)(2,1)} custom-call(bf16[512,384]{1,0:T(8,128)(2,1)S(1)} %bitcast.23, bf16[2,384,128]{2,1,0:T(8,128)(2,1)S(1)} %pad.4.ctx_ref), custom_call_target="tpu_custom_call" | custom-call | flops 469762048 | bytes 1048576 | tf_op jit(solution)/shard_map/pallas_call | solution.py:352
  65.8 6.9 %all-to-all-start.2 = ((bf16[128,4,128]{2,1,0:T(4,128)(2,1)}), bf16[128,4,128]{2,1,0:T(4,128)(2,1)S(1)}, u32[]{:S(2)}, u32[]{:S(2)}) async-start(bf16[128,4,128]{2,1,0:T(4,128)(2,1)} %bitcast.13), calls=%async_computation.2 | async-start | bytes 262144 | tf_op jit(solution)/shard_map/all_to_all | solution.py:359
  72.8 2.5 %collective-permute-start.6 = (bf16[48,2432]{1,0:T(8,128)(2,1)S(1)}, bf16[48,2432]{1,0:T(8,128)(2,1)S(1)}, u32[]{:S(2)}, u32[]{:S(2)}) collective-permute-start(bf16[48,2432]{1,0:T(8,128)(2,1)S(1)} %collective-permute-done.4.refs_2_), channel_id=1, source_target_pairs={{0,1},{1,0},{2,3},{3,2},{4,5},{5,4},{6,7},{7,6},{8,9},{9,8},{10,11... | collective-permute-start | bytes 700424 | tf_op jit(solution)/shard_map/ppermute | solution.py:351
  75.3 1.1 %shard_map.86.refs_1_ = bf16[128,2432]{1,0:T(8,128)(2,1)S(1)} custom-call(bf16[128,2432]{1,0:T(8,128)(2,1)} %collective-permute-done.3.hbm), custom_call_target="tpu_custom_call" | custom-call | bytes 1048576 | tf_op jit(solution)/shard_map/pallas_call | solution.py:363
  76.4 7.0 %all-to-all-done.2 = bf16[128,4,128]{2,1,0:T(4,128)(2,1)S(1)} async-done(((bf16[128,4,128]{2,1,0:T(4,128)(2,1)}), bf16[128,4,128]{2,1,0:T(4,128)(2,1)S(1)}, u32[]{:S(2)}, u32[]{:S(2)}) %all-to-all-start.2) | async-done | bytes 131104 | tf_op jit(solution)/shard_map/all_to_all | solution.py:359
  83.4 1.3 %shard_map.87 = bf16[16,80,128]{2,1,0:T(8,128)(2,1)S(1)} custom-call(s32[1]{0:T(128)} %bitcast.core_ref, s32[1]{0:T(128)} %bitcast.1.parity_ref, bf16[2,256,128]{2,1,0:T(8,128)(2,1)S(1)} %bitcast.22, f32[1,128]{1,0:T(1,128)S(1)} %get-tuple-element.46.slot_ref, bf16[128,2432]{1,0:T(8,128)(2,1)S(1)} %copy-done, bf16[128,2432]{1,0:T(8,128)(2,1)S(1)} %shard_map.86.refs_1_, ...), custom_call_target="tpu_custom_call" | custom-call | flops 318767104 | bytes 1048576 | tf_op jit(solution)/shard_map/pallas_call | solution.py:365
  84.7 16.4 %all_to_all.20.sums_ref = bf16[16,80,128]{2,1,0:T(8,128)(2,1)S(1)} all-to-all(bf16[16,80,128]{2,1,0:T(8,128)(2,1)S(1)} %shard_map.87), channel_id=1, replica_groups=mesh['dp'=32,'mp'=16] {'mp'}, dimensions={0} | all-to-all | bytes 655360 | tf_op jit(solution)/shard_map/all_to_all | solution.py:372
  101.2 0.9 shard_map.88
  (16 shorter events, 0.1 us)
Async XLA Ops:
  2.1 31.2 %all-to-all-start = ((bf16[16,152,128]{2,1,0:T(8,128)(2,1)}), bf16[16,152,128]{2,1,0:T(8,128)(2,1)S(1)}, u32[]{:S(2)}, u32[]{:S(2)}) async-start(bf16[16,152,128]{2,1,0:T(8,128)(2,1)} %get-tuple-element.31), calls=%async_computation | async-start | bytes 1245184 | tf_op jit(solution)/shard_map/all_to_all | solution.py:305
  13.9 8.1 %copy-start = (bf16[128,2432]{1,0:T(8,128)(2,1)S(1)}, bf16[128,2432]{1,0:T(8,128)(2,1)}, u32[]{:S(2)}) copy-start(bf16[128,2432]{1,0:T(8,128)(2,1)} %refs_0_) | copy-start | bytes 1867780
  13.9 11.9 %slice-start = ((bf16[28,3,2432]{2,0,1:T(8,128)(2,1)}), bf16[28,1,2432]{2,0,1:T(8,128)(2,1)S(1)}, s32[]{:S(2)}) async-start(bf16[28,3,2432]{2,0,1:T(8,128)(2,1)} %param.11), calls=%async_computation.4 | async-start | bytes 311296 | tf_op jit(solution)/shard_map/slice | solution.py:311
  14.0 12.0 %copy-start.1 = (s32[256,1]{0,1:T(1,128)S(1)}, s32[256,1]{0,1:T(1,128)}, u32[]{:S(2)}) copy-start(s32[256,1]{0,1:T(1,128)} %param.9) | copy-start | bytes 3076
  14.0 11.9 %copy-start.3 = (s32[32]{0:T(128)S(1)}, s32[32]{0:T(128)}, u32[]{:S(2)}) copy-start(s32[32]{0:T(128)} %param.10) | copy-start | bytes 388
  15.6 17.7 %copy-start.2 = (f32[2,64]{1,0:T(2,128)S(1)}, f32[2,64]{1,0:T(2,128)}, u32[]{:S(2)}) copy-start(f32[2,64]{1,0:T(2,128)} %gain_ref.1) | copy-start | bytes 1540
  15.6 13.1 %collective-permute-start = (bf16[2432,128]{1,0:T(8,128)(2,1)S(1)}, bf16[2432,128]{1,0:T(8,128)(2,1)}, u32[]{:S(2)}, u32[]{:S(2)}) collective-permute-start(bf16[2432,128]{1,0:T(8,128)(2,1)S(1)} %get-tuple-element.40.own0_ref), channel_id=1, source_target_pairs={{0,1},{1,0},{2,3},{3,2},{4,5},{5,4},{6,7},{7,6},{8,9},{9,8},{10,11... | collective-permute-start | bytes 1867784 | tf_op jit(solution)/shard_map/ppermute | solution.py:308
  17.7 11.1 %collective-permute-start.1 = (bf16[2432,128]{1,0:T(8,128)(2,1)S(1)}, bf16[2432,128]{1,0:T(8,128)(2,1)}, u32[]{:S(2)}, u32[]{:S(2)}) collective-permute-start(bf16[2432,128]{1,0:T(8,128)(2,1)S(1)} %get-tuple-element.41.own1_ref), channel_id=1, source_target_pairs={{0,1},{1,0},{2,3},{3,2},{4,5},{5,4},{6,7},{7,6},{8,9},{9,8},{10,11... | collective-permute-start | bytes 1867784 | tf_op jit(solution)/shard_map/ppermute | solution.py:308
  20.0 8.8 %collective-permute-start.2 = (bf16[2432,128]{1,0:T(8,128)(2,1)S(1)}, bf16[2432,128]{1,0:T(8,128)(2,1)}, u32[]{:S(2)}, u32[]{:S(2)}) collective-permute-start(bf16[2432,128]{1,0:T(8,128)(2,1)S(1)} %get-tuple-element.42.own2_ref), channel_id=1, source_target_pairs={{0,1},{1,0},{2,3},{3,2},{4,5},{5,4},{6,7},{7,6},{8,9},{9,8},{10,11... | collective-permute-start | bytes 1867784 | tf_op jit(solution)/shard_map/ppermute | solution.py:308
  22.0 6.8 %collective-permute-start.3 = (bf16[128,2432]{1,0:T(8,128)(2,1)S(1)}, bf16[128,2432]{1,0:T(8,128)(2,1)}, u32[]{:S(2)}, u32[]{:S(2)}) collective-permute-start(bf16[128,2432]{1,0:T(8,128)(2,1)S(1)} %copy-done), channel_id=1, source_target_pairs={{0,1},{1,0},{2,3},{3,2},{4,5},{5,4},{6,7},{7,6},{8,9},{9,8},{10,11... | collective-permute-start | bytes 1867784 | tf_op jit(solution)/shard_map/ppermute | solution.py:309
  33.3 14.1 %copy-start.4 = (bf16[48,2432]{1,0:T(8,128)(2,1)S(1)}, bf16[48,2432]{1,0:T(8,128)(2,1)}, u32[]{:S(2)}) copy-start(bf16[48,2432]{1,0:T(8,128)(2,1)} %slice.22) | copy-start | bytes 700420
  37.1 26.4 %all-to-all-start.1 = ((bf16[64,8,384]{2,1,0:T(8,128)(2,1)}), bf16[64,8,384]{2,1,0:T(8,128)(2,1)S(1)}, u32[]{:S(2)}, u32[]{:S(2)}) async-start(bf16[64,8,384]{2,1,0:T(8,128)(2,1)} %bitcast.10), calls=%async_computation.1 | async-start | bytes 786432 | tf_op jit(solution)/shard_map/all_to_all | solution.py:344
  47.4 25.4 %collective-permute-start.4 = (bf16[48,2432]{1,0:T(8,128)(2,1)S(1)}, bf16[48,2432]{1,0:T(8,128)(2,1)S(1)}, u32[]{:S(2)}, u32[]{:S(2)}) collective-permute-start(bf16[48,2432]{1,0:T(8,128)(2,1)S(1)} %copy-done.4), channel_id=1, source_target_pairs={{0,2},{1,3},{2,0},{3,1},{4,6},{5,7},{6,4},{7,5},{8,10},{9,11},{10,... | collective-permute-start | bytes 700424 | tf_op jit(solution)/shard_map/ppermute | solution.py:348
  49.3 27.0 %collective-permute-start.5 = (bf16[80,2432]{1,0:T(8,128)(2,1)}, bf16[80,2432]{1,0:T(8,128)(2,1)S(1)}, u32[]{:S(2)}, u32[]{:S(2)}) collective-permute-start(bf16[80,2432]{1,0:T(8,128)(2,1)} %slice.23), channel_id=1, source_target_pairs={{0,2},{1,3},{2,0},{3,1},{4,6},{5,7},{6,4},{7,5},{8,10},{9,11},{10,... | collective-permute-start | bytes 1167368 | tf_op jit(solution)/shard_map/ppermute | solution.py:349
  52.7 23.7 %collective-permute-start.7 = (bf16[80,2432]{1,0:T(8,128)(2,1)}, bf16[80,2432]{1,0:T(8,128)(2,1)S(1)}, u32[]{:S(2)}, u32[]{:S(2)}) collective-permute-start(bf16[80,2432]{1,0:T(8,128)(2,1)} %slice.23), channel_id=1, source_target_pairs={{0,3},{1,2},{2,1},{3,0},{4,7},{5,6},{6,5},{7,4},{8,11},{9,10},{10,... | collective-permute-start | bytes 1167368 | tf_op jit(solution)/shard_map/ppermute | solution.py:350
  65.8 17.6 %all-to-all-start.2 = ((bf16[128,4,128]{2,1,0:T(4,128)(2,1)}), bf16[128,4,128]{2,1,0:T(4,128)(2,1)S(1)}, u32[]{:S(2)}, u32[]{:S(2)}) async-start(bf16[128,4,128]{2,1,0:T(4,128)(2,1)} %bitcast.13), calls=%async_computation.2 | async-start | bytes 262144 | tf_op jit(solution)/shard_map/all_to_all | solution.py:359
  72.8 3.6 %collective-permute-start.6 = (bf16[48,2432]{1,0:T(8,128)(2,1)S(1)}, bf16[48,2432]{1,0:T(8,128)(2,1)S(1)}, u32[]{:S(2)}, u32[]{:S(2)}) collective-permute-start(bf16[48,2432]{1,0:T(8,128)(2,1)S(1)} %collective-permute-done.4.refs_2_), channel_id=1, source_target_pairs={{0,1},{1,0},{2,3},{3,2},{4,5},{5,4},{6,7},{7,6},{8,9},{9,8},{10,11... | collective-permute-start | bytes 700424 | tf_op jit(solution)/shard_map/ppermute | solution.py:351

commit v13 on v12

--- a/solution.py
+++ b/solution.py
@@ -337,18 +337,15 @@
         ],
         flops=4 * depth * half * kinds * inner,
     )(core, whole, in_hbm(mod), *[in_vmem(w) for w in w_own], *[in_hbm(w) for w in w_sib], qk_gain, slot)
-    send, early, late, context = lax.optimization_barrier(
-        (send, w_out[:first_rows], w_out[first_rows:], context)
-    )
+    send, late, w_out, context = lax.optimization_barrier((send, w_out[first_rows:], w_out, context))
     text = jnp.pad(context[0], ((0, 0), (0, text_pad - text_len), (0, 0)))
     arrived = lax.all_to_all(
         send.reshape(2 * requests, cap, kinds * inner), ("dp", "mp"), 0, 0, axis_index_groups=planes, tiled=True
     )
     next_level = [(i, i ^ 2) for i in range(parts)]
-    next_early = lax.ppermute(early, "mp", next_level)
-    next_late = lax.ppermute(late, "mp", next_level)
+    out_next = lax.ppermute(w_out, "mp", next_level)
     far_late = lax.ppermute(late, "mp", [(i, i ^ 3) for i in range(parts)])
-    far_early = lax.ppermute(next_early, "mp", sibling)
+    far_early = lax.ppermute(out_next[:first_rows], "mp", sibling)
     attn = call(
         functools.partial(attend_kernel, text_len),
         shape((2 * slots, inner), BF16),
@@ -361,11 +358,11 @@
     )
     _, out_sib = lax.optimization_barrier((attn, out_sib))
     out_sib = call(stage_kernel, shape((inner, depth), BF16), "a", "v", [pltpu.SemaphoreType.DMA])(in_hbm(out_sib))
-    blocks = (w_out, out_sib, next_early, next_late, far_early, far_late)
+    blocks = (w_out, out_sib, out_next, far_early, far_late)
     partial = call(
         functools.partial(output_kernel, cap // 2),
         shape((parts, upper, half), BF16),
-        "ssvvvvvvvv",
+        "ssvvvvvvv",
         "v",
         flops=8 * depth * half * inner,
     )(core, parity, returned.reshape(2, slots, inner), slot, *blocks)

time: 103 us -> 103 us (level)
  waiting for transfers between devices: 18.8 us -> 22.3 us
  starting transfers between devices: 48 us -> 46 us
  local copies, waits for them, and re-layouts: 4.2 us -> 2.6 us
    ppermute x3 -> x2, starting transfers between devices: 7.76 us -> 4.4 us  [the longest x1 2.48 us: body(): far_early = lax.ppermute(out_next[:first_rows], 'mp', sibling)]
    all_to_all x1, waiting for transfers between devices: 7.29 us -> 10.1 us  [body(): lax.all_to_all(send.reshape(2 * requests, cap, kinds * inner), ('dp', 'mp...]
    ppermute x1, starting transfers between devices: 2.44 us -> 3.88 us  [body(): far_late = lax.ppermute(late, 'mp', [(i, i ^ 3) for i in range(parts)])]
  transfers between devices with their start and end apart: 11 -> 10, of which waited for: 3 -> 3; matrix products, arithmetic and copies ran while one was open for 4% -> 3% of each run, Pallas kernels for 6% -> 6%
where the time goes in v13:
time: 103 us; the launch traced here: 102 us
  starting transfers between devices  46 us (45%)
  waiting for transfers between devices  22.3 us (22%)
  blocking collectives  16.4 us (16%)
  Pallas kernels  14.3 us (14%)
  local copies, waits for them, and re-layouts  2.6 us (3%)
    all_to_all x1, blocking collectives, body(): sums = lax.all_to_all(partial, 'mp', 0, 0, tiled=True)  16.4 us
    all_to_all x1, starting transfers between devices, body(): whole = lax.all_to_all(spread, 'mp', 0, 0, tiled=True)  11.8 us
    all_to_all x1, starting transfers between devices, body(): lax.all_to_all(send.reshape(2 * requests, cap, kinds * inner), ('dp', 'mp...  10.3 us
    all_to_all x1, waiting for transfers between devices, body(): lax.all_to_all(send.reshape(2 * requests, cap, kinds * inner), ('dp', 'mp...  10.1 us
    all_to_all x1, waiting for transfers between devices, body(): lax.all_to_all(attn.reshape(4 * requests, cap // 2, inner), ('dp', 'mp'),...  6.98 us
    all_to_all x1, starting transfers between devices, body(): lax.all_to_all(attn.reshape(4 * requests, cap // 2, inner), ('dp', 'mp'),...  6.91 us
    ppermute x3, starting transfers between devices, body(): w_sib = [lax.ppermute(block, 'mp', sibling) for block in w_own]  6.34 us
    all_to_all x1, waiting for transfers between devices, body(): whole = lax.all_to_all(spread, 'mp', 0, 0, tiled=True)  5.2 us
  transfers between devices with their start and end apart: 10, of which 3 were waited for; matrix products, arithmetic and copies ran while one was open for 3% of the time, Pallas kernels for 6%

profile of v13, /device:TPU:1, one launch (start us, length us, event | category | flops | bytes accessed | tf_op | source)
XLA Modules:
  0.0 102.0 jit_solution(12035161802618895971)
XLA Ops:
  0.0 2.1 %shard_map.82 = (bf16[16,152,128]{2,1,0:T(8,128)(2,1)}, bf16[152,256]{1,0:T(8,128)(2,1)S(1)}, f32[1,256]{1,0:T(1,128)S(1)}) custom-call(bf16[152,256]{1,0:T(8,128)(2,1)} %bitcast.29, s32[1,256]{1,0:T(1,128)} %bitcast.24), custom_call_target="tpu_custom_call" | custom-call | bytes 1048576 | tf_op jit(solution)/shard_map/pallas_call | solution.py:292
  2.1 11.8 %all-to-all-start = ((bf16[16,152,128]{2,1,0:T(8,128)(2,1)}), bf16[16,152,128]{2,1,0:T(8,128)(2,1)S(1)}, u32[]{:S(2)}, u32[]{:S(2)}) async-start(bf16[16,152,128]{2,1,0:T(8,128)(2,1)} %get-tuple-element.31), calls=%async_computation | async-start | bytes 1245184 | tf_op jit(solution)/shard_map/all_to_all | solution.py:305
  13.9 0.0 slice-start
  13.9 0.0 copy-start.1
  14.0 0.0 copy-start.3
  14.0 0.0 copy-start.2
  14.0 1.6 %slice_bitcast_fusion = (bf16[2432,128]{1,0:T(8,128)(2,1)S(1)}, bf16[2432,128]{1,0:T(8,128)(2,1)S(1)}, bf16[2432,128]{1,0:T(8,128)(2,1)S(1)}) fusion(bf16[2432,3,128]{2,0,1:T(8,128)(2,1)} %param.12), kind=kLoop, calls=%fused_computation | loop fusion | bytes 3735552 | tf_op jit(solution)/shard_map/squeeze | solution.py:307
  15.6 2.0 %collective-permute-start = (bf16[2432,128]{1,0:T(8,128)(2,1)S(1)}, bf16[2432,128]{1,0:T(8,128)(2,1)}, u32[]{:S(2)}, u32[]{:S(2)}) collective-permute-start(bf16[2432,128]{1,0:T(8,128)(2,1)S(1)} %get-tuple-element.40.own0_ref), channel_id=1, source_target_pairs={{0,1},{1,0},{2,3},{3,2},{4,5},{5,4},{6,7},{7,6},{8,9},{9,8},{10,11... | collective-permute-start | bytes 1867784 | tf_op jit(solution)/shard_map/ppermute | solution.py:308
  17.6 2.3 %collective-permute-start.1 = (bf16[2432,128]{1,0:T(8,128)(2,1)S(1)}, bf16[2432,128]{1,0:T(8,128)(2,1)}, u32[]{:S(2)}, u32[]{:S(2)}) collective-permute-start(bf16[2432,128]{1,0:T(8,128)(2,1)S(1)} %get-tuple-element.41.own1_ref), channel_id=1, source_target_pairs={{0,1},{1,0},{2,3},{3,2},{4,5},{5,4},{6,7},{7,6},{8,9},{9,8},{10,11... | collective-permute-start | bytes 1867784 | tf_op jit(solution)/shard_map/ppermute | solution.py:308
  20.0 2.0 %collective-permute-start.2 = (bf16[2432,128]{1,0:T(8,128)(2,1)S(1)}, bf16[2432,128]{1,0:T(8,128)(2,1)}, u32[]{:S(2)}, u32[]{:S(2)}) collective-permute-start(bf16[2432,128]{1,0:T(8,128)(2,1)S(1)} %get-tuple-element.42.own2_ref), channel_id=1, source_target_pairs={{0,1},{1,0},{2,3},{3,2},{4,5},{5,4},{6,7},{7,6},{8,9},{9,8},{10,11... | collective-permute-start | bytes 1867784 | tf_op jit(solution)/shard_map/ppermute | solution.py:308
  22.0 2.3 %collective-permute-start.3 = (bf16[128,2432]{1,0:T(8,128)(2,1)S(1)}, bf16[128,2432]{1,0:T(8,128)(2,1)}, u32[]{:S(2)}, u32[]{:S(2)}) collective-permute-start(bf16[128,2432]{1,0:T(8,128)(2,1)S(1)} %copy-done), channel_id=1, source_target_pairs={{0,1},{1,0},{2,3},{3,2},{4,5},{5,4},{6,7},{7,6},{8,9},{9,8},{10,11... | collective-permute-start | bytes 1867784 | tf_op jit(solution)/shard_map/ppermute | solution.py:309
  24.3 0.8 slice.22
  25.1 0.1 dynamic-slice_bitcast_fusion.gate_ref
  25.2 2.8 %shard_map.83 = (bf16[2,2432,128]{2,1,0:T(8,128)(2,1)}, bf16[152,256]{1,0:T(8,128)(2,1)S(1)}, f32[1,128]{1,0:T(1,128)S(1)}) custom-call(s32[1]{0:T(128)} %bitcast.core_ref, s32[1,256]{1,0:T(1,128)S(1)} %bitcast.25, f32[1,256]{1,0:T(1,128)S(1)} %get-tuple-element.34.pos_ref, s32[1,32]{1,0:T(1,128)S(1)} %bitcast.26, bf16[3,28,2432]{2,1,0:T(8,128)(2,1)} %bitcast.27, ...), custom_call_target="tpu_custom_call" | custom-call | bytes 1048576 | tf_op jit(solution)/shard_map/pallas_call | solution.py:312
  28.1 0.0 collective-permute-done.sib0_hbm
  28.1 0.0 collective-permute-done.2.sib2_hbm
  28.1 0.0 collective-permute-done.3.hbm
  28.1 5.2 %all-to-all-done.tok_ref = bf16[16,152,128]{2,1,0:T(8,128)(2,1)S(1)} async-done(((bf16[16,152,128]{2,1,0:T(8,128)(2,1)}), bf16[16,152,128]{2,1,0:T(8,128)(2,1)S(1)}, u32[]{:S(2)}, u32[]{:S(2)}) %all-to-all-start) | async-done | bytes 622624 | tf_op jit(solution)/shard_map/all_to_all | solution.py:305
  33.3 3.7 %shard_map.84 = bf16[2,256,384]{2,1,0:T(8,128)(2,1)} custom-call(s32[1]{0:T(128)} %bitcast.core_ref, bf16[16,152,128]{2,1,0:T(8,128)(2,1)S(1)} %all-to-all-done.tok_ref, bf16[2,2432,128]{2,1,0:T(8,128)(2,1)} %get-tuple-element.39.mod_hbm, bf16[2432,128]{1,0:T(8,128)(2,1)S(1)} %get-tuple-element.40.own0_ref, ...), custom_call_target="tpu_custom_call" | custom-call | flops 478150656 | bytes 1048576 | tf_op jit(solution)/shard_map/pallas_call | solution.py:327
  37.1 10.3 %all-to-all-start.1 = ((bf16[64,8,384]{2,1,0:T(8,128)(2,1)}), bf16[64,8,384]{2,1,0:T(8,128)(2,1)S(1)}, u32[]{:S(2)}, u32[]{:S(2)}) async-start(bf16[64,8,384]{2,1,0:T(8,128)(2,1)} %bitcast.10), calls=%async_computation.1 | async-start | bytes 786432 | tf_op jit(solution)/shard_map/all_to_all | solution.py:342
  47.4 1.9 %collective-permute-start.4 = (bf16[128,2432]{1,0:T(8,128)(2,1)S(1)}, bf16[128,2432]{1,0:T(8,128)(2,1)S(1)}, u32[]{:S(2)}, u32[]{:S(2)}) collective-permute-start(bf16[128,2432]{1,0:T(8,128)(2,1)S(1)} %copy-done), channel_id=1, source_target_pairs={{0,2},{1,3},{2,0},{3,1},{4,6},{5,7},{6,4},{7,5},{8,10},{9,11},{10,... | collective-permute-start | bytes 1867784 | tf_op jit(solution)/shard_map/ppermute | solution.py:346
  49.3 3.9 %collective-permute-start.6 = (bf16[80,2432]{1,0:T(8,128)(2,1)}, bf16[80,2432]{1,0:T(8,128)(2,1)S(1)}, u32[]{:S(2)}, u32[]{:S(2)}) collective-permute-start(bf16[80,2432]{1,0:T(8,128)(2,1)} %slice.22), channel_id=1, source_target_pairs={{0,3},{1,2},{2,1},{3,0},{4,7},{5,6},{6,5},{7,4},{8,11},{9,10},{10,... | collective-permute-start | bytes 1167368 | tf_op jit(solution)/shard_map/ppermute | solution.py:347
  53.3 10.1 %all-to-all-done.1 = bf16[64,8,384]{2,1,0:T(8,128)(2,1)S(1)} async-done(((bf16[64,8,384]{2,1,0:T(8,128)(2,1)}), bf16[64,8,384]{2,1,0:T(8,128)(2,1)S(1)}, u32[]{:S(2)}, u32[]{:S(2)}) %all-to-all-start.1) | async-done | bytes 393248 | tf_op jit(solution)/shard_map/all_to_all | solution.py:342
  63.4 2.4 %shard_map.85 = bf16[512,128]{1,0:T(8,128)(2,1)} custom-call(bf16[512,384]{1,0:T(8,128)(2,1)S(1)} %bitcast.23, bf16[2,384,128]{2,1,0:T(8,128)(2,1)S(1)} %pad.4.ctx_ref), custom_call_target="tpu_custom_call" | custom-call | flops 469762048 | bytes 1048576 | tf_op jit(solution)/shard_map/pallas_call | solution.py:349
  65.8 6.9 %all-to-all-start.2 = ((bf16[128,4,128]{2,1,0:T(4,128)(2,1)}), bf16[128,4,128]{2,1,0:T(4,128)(2,1)S(1)}, u32[]{:S(2)}, u32[]{:S(2)}) async-start(bf16[128,4,128]{2,1,0:T(4,128)(2,1)} %bitcast.13), calls=%async_computation.2 | async-start | bytes 262144 | tf_op jit(solution)/shard_map/all_to_all | solution.py:356
  72.7 0.0 collective-permute-done.4.refs_2_
  72.8 2.5 %collective-permute-start.5 = (bf16[48,2432]{1,0:T(8,128)(2,1)S(1)}, bf16[48,2432]{1,0:T(8,128)(2,1)S(1)}, u32[]{:S(2)}, u32[]{:S(2)}) collective-permute-start(bf16[48,2432]{1,0:T(8,128)(2,1)S(1)} %slice.24), channel_id=1, source_target_pairs={{0,1},{1,0},{2,3},{3,2},{4,5},{5,4},{6,7},{7,6},{8,9},{9,8},{10,11... | collective-permute-start | bytes 700424 | tf_op jit(solution)/shard_map/ppermute | solution.py:348
  75.3 1.1 %shard_map.86.refs_1_ = bf16[128,2432]{1,0:T(8,128)(2,1)S(1)} custom-call(bf16[128,2432]{1,0:T(8,128)(2,1)} %collective-permute-done.3.hbm), custom_call_target="tpu_custom_call" | custom-call | bytes 1048576 | tf_op jit(solution)/shard_map/pallas_call | solution.py:360
  76.4 7.0 %all-to-all-done.2 = bf16[128,4,128]{2,1,0:T(4,128)(2,1)S(1)} async-done(((bf16[128,4,128]{2,1,0:T(4,128)(2,1)}), bf16[128,4,128]{2,1,0:T(4,128)(2,1)S(1)}, u32[]{:S(2)}, u32[]{:S(2)}) %all-to-all-start.2) | async-done | bytes 131104 | tf_op jit(solution)/shard_map/all_to_all | solution.py:356
  83.4 1.3 %shard_map.87 = bf16[16,80,128]{2,1,0:T(8,128)(2,1)S(1)} custom-call(s32[1]{0:T(128)} %bitcast.core_ref, s32[1]{0:T(128)} %bitcast.1.parity_ref, bf16[2,256,128]{2,1,0:T(8,128)(2,1)S(1)} %bitcast.22, f32[1,128]{1,0:T(1,128)S(1)} %get-tuple-element.46.slot_ref, bf16[128,2432]{1,0:T(8,128)(2,1)S(1)} %copy-done, bf16[128,2432]{1,0:T(8,128)(2,1)S(1)} %shard_map.86.refs_1_, ...), custom_call_target="tpu_custom_call" | custom-call | flops 318767104 | bytes 1048576 | tf_op jit(solution)/shard_map/pallas_call | solution.py:362
  84.7 16.4 %all_to_all.20.sums_ref = bf16[16,80,128]{2,1,0:T(8,128)(2,1)S(1)} all-to-all(bf16[16,80,128]{2,1,0:T(8,128)(2,1)S(1)} %shard_map.87), channel_id=1, replica_groups=mesh['dp'=32,'mp'=16] {'mp'}, dimensions={0} | all-to-all | bytes 655360 | tf_op jit(solution)/shard_map/all_to_all | solution.py:369
  101.1 0.9 shard_map.88
  (14 shorter events, 0.1 us)
Async XLA Ops:
  2.1 31.2 %all-to-all-start = ((bf16[16,152,128]{2,1,0:T(8,128)(2,1)}), bf16[16,152,128]{2,1,0:T(8,128)(2,1)S(1)}, u32[]{:S(2)}, u32[]{:S(2)}) async-start(bf16[16,152,128]{2,1,0:T(8,128)(2,1)} %get-tuple-element.31), calls=%async_computation | async-start | bytes 1245184 | tf_op jit(solution)/shard_map/all_to_all | solution.py:305
  13.9 8.1 %copy-start = (bf16[128,2432]{1,0:T(8,128)(2,1)S(1)}, bf16[128,2432]{1,0:T(8,128)(2,1)}, u32[]{:S(2)}) copy-start(bf16[128,2432]{1,0:T(8,128)(2,1)} %refs_0_) | copy-start | bytes 1867780
  13.9 11.2 %slice-start = ((bf16[28,3,2432]{2,0,1:T(8,128)(2,1)}), bf16[28,1,2432]{2,0,1:T(8,128)(2,1)S(1)}, s32[]{:S(2)}) async-start(bf16[28,3,2432]{2,0,1:T(8,128)(2,1)} %param.11), calls=%async_computation.4 | async-start | bytes 311296 | tf_op jit(solution)/shard_map/slice | solution.py:311
  13.9 11.3 %copy-start.1 = (s32[256,1]{0,1:T(1,128)S(1)}, s32[256,1]{0,1:T(1,128)}, u32[]{:S(2)}) copy-start(s32[256,1]{0,1:T(1,128)} %param.9) | copy-start | bytes 3076
  14.0 11.2 %copy-start.3 = (s32[32]{0:T(128)S(1)}, s32[32]{0:T(128)}, u32[]{:S(2)}) copy-start(s32[32]{0:T(128)} %param.10) | copy-start | bytes 388
  14.0 19.3 %copy-start.2 = (f32[2,64]{1,0:T(2,128)S(1)}, f32[2,64]{1,0:T(2,128)}, u32[]{:S(2)}) copy-start(f32[2,64]{1,0:T(2,128)} %gain_ref.1) | copy-start | bytes 1540
  15.6 12.4 %collective-permute-start = (bf16[2432,128]{1,0:T(8,128)(2,1)S(1)}, bf16[2432,128]{1,0:T(8,128)(2,1)}, u32[]{:S(2)}, u32[]{:S(2)}) collective-permute-start(bf16[2432,128]{1,0:T(8,128)(2,1)S(1)} %get-tuple-element.40.own0_ref), channel_id=1, source_target_pairs={{0,1},{1,0},{2,3},{3,2},{4,5},{5,4},{6,7},{7,6},{8,9},{9,8},{10,11... | collective-permute-start | bytes 1867784 | tf_op jit(solution)/shard_map/ppermute | solution.py:308
  17.6 10.4 %collective-permute-start.1 = (bf16[2432,128]{1,0:T(8,128)(2,1)S(1)}, bf16[2432,128]{1,0:T(8,128)(2,1)}, u32[]{:S(2)}, u32[]{:S(2)}) collective-permute-start(bf16[2432,128]{1,0:T(8,128)(2,1)S(1)} %get-tuple-element.41.own1_ref), channel_id=1, source_target_pairs={{0,1},{1,0},{2,3},{3,2},{4,5},{5,4},{6,7},{7,6},{8,9},{9,8},{10,11... | collective-permute-start | bytes 1867784 | tf_op jit(solution)/shard_map/ppermute | solution.py:308
  20.0 8.1 %collective-permute-start.2 = (bf16[2432,128]{1,0:T(8,128)(2,1)S(1)}, bf16[2432,128]{1,0:T(8,128)(2,1)}, u32[]{:S(2)}, u32[]{:S(2)}) collective-permute-start(bf16[2432,128]{1,0:T(8,128)(2,1)S(1)} %get-tuple-element.42.own2_ref), channel_id=1, source_target_pairs={{0,1},{1,0},{2,3},{3,2},{4,5},{5,4},{6,7},{7,6},{8,9},{9,8},{10,11... | collective-permute-start | bytes 1867784 | tf_op jit(solution)/shard_map/ppermute | solution.py:308
  22.0 6.1 %collective-permute-start.3 = (bf16[128,2432]{1,0:T(8,128)(2,1)S(1)}, bf16[128,2432]{1,0:T(8,128)(2,1)}, u32[]{:S(2)}, u32[]{:S(2)}) collective-permute-start(bf16[128,2432]{1,0:T(8,128)(2,1)S(1)} %copy-done), channel_id=1, source_target_pairs={{0,1},{1,0},{2,3},{3,2},{4,5},{5,4},{6,7},{7,6},{8,9},{9,8},{10,11... | collective-permute-start | bytes 1867784 | tf_op jit(solution)/shard_map/ppermute | solution.py:309
  33.3 19.9 %copy-start.4 = (bf16[1,2,333,128]{3,1,2,0:T(2,128)(2,1)S(1)}, bf16[1,2,333,128]{3,1,2,0:T(2,128)(2,1)}, u32[]{:S(2)}) copy-start(bf16[1,2,333,128]{3,1,2,0:T(2,128)(2,1)} %param.14) | copy-start | bytes 511492
  37.1 26.4 %all-to-all-start.1 = ((bf16[64,8,384]{2,1,0:T(8,128)(2,1)}), bf16[64,8,384]{2,1,0:T(8,128)(2,1)S(1)}, u32[]{:S(2)}, u32[]{:S(2)}) async-start(bf16[64,8,384]{2,1,0:T(8,128)(2,1)} %bitcast.10), calls=%async_computation.1 | async-start | bytes 786432 | tf_op jit(solution)/shard_map/all_to_all | solution.py:342
  47.4 25.3 %collective-permute-start.4 = (bf16[128,2432]{1,0:T(8,128)(2,1)S(1)}, bf16[128,2432]{1,0:T(8,128)(2,1)S(1)}, u32[]{:S(2)}, u32[]{:S(2)}) collective-permute-start(bf16[128,2432]{1,0:T(8,128)(2,1)S(1)} %copy-done), channel_id=1, source_target_pairs={{0,2},{1,3},{2,0},{3,1},{4,6},{5,7},{6,4},{7,5},{8,10},{9,11},{10,... | collective-permute-start | bytes 1867784 | tf_op jit(solution)/shard_map/ppermute | solution.py:346
  49.3 27.0 %collective-permute-start.6 = (bf16[80,2432]{1,0:T(8,128)(2,1)}, bf16[80,2432]{1,0:T(8,128)(2,1)S(1)}, u32[]{:S(2)}, u32[]{:S(2)}) collective-permute-start(bf16[80,2432]{1,0:T(8,128)(2,1)} %slice.22), channel_id=1, source_target_pairs={{0,3},{1,2},{2,1},{3,0},{4,7},{5,6},{6,5},{7,4},{8,11},{9,10},{10,... | collective-permute-start | bytes 1167368 | tf_op jit(solution)/shard_map/ppermute | solution.py:347
  65.8 17.5 %all-to-all-start.2 = ((bf16[128,4,128]{2,1,0:T(4,128)(2,1)}), bf16[128,4,128]{2,1,0:T(4,128)(2,1)S(1)}, u32[]{:S(2)}, u32[]{:S(2)}) async-start(bf16[128,4,128]{2,1,0:T(4,128)(2,1)} %bitcast.13), calls=%async_computation.2 | async-start | bytes 262144 | tf_op jit(solution)/shard_map/all_to_all | solution.py:356
  72.8 3.6 %collective-permute-start.5 = (bf16[48,2432]{1,0:T(8,128)(2,1)S(1)}, bf16[48,2432]{1,0:T(8,128)(2,1)S(1)}, u32[]{:S(2)}, u32[]{:S(2)}) collective-permute-start(bf16[48,2432]{1,0:T(8,128)(2,1)S(1)} %slice.24), channel_id=1, source_target_pairs={{0,1},{1,0},{2,3},{3,2},{4,5},{5,4},{6,7},{7,6},{8,9},{9,8},{10,11... | collective-permute-start | bytes 700424 | tf_op jit(solution)/shard_map/ppermute | solution.py:348

commit v14 on v13

--- a/solution.py
+++ b/solution.py
@@ -174,7 +174,7 @@
 
 def attend_kernel(text_len, slots_ref, ctx_ref, out_ref):
     slots, inner = out_ref.shape
-    block = 256
+    block = 512
     text_pad = ctx_ref.shape[1]
     queries = slots_ref[:, 0:inner]
     keys = slots_ref[:, inner : 2 * inner].astype(F32)
@@ -185,17 +185,17 @@
     text_bias = jnp.where(iota((1, text_pad), 1) < text_len, 0.0, MASKED)
     bias = jnp.concatenate([own_bias, text_bias], axis=1)
     values = jnp.concatenate([slots_ref[:, 2 * inner :], ctx_ref[1]], axis=0)
-    values = jnp.concatenate([values, jnp.ones(values.shape, BF16)], axis=1)
     first = iota((1, inner), 1) < HD
-    zero = jnp.zeros((), BF16)
+    zero, one = jnp.zeros((), BF16), jnp.ones((), BF16)
     for row in range(0, slots, block):
         query = queries[row : row + block]
         query = jnp.concatenate([jnp.where(first, query, zero), jnp.where(first, zero, query)], axis=0)
         scores = dot_nt(query, keys) + bias
         weights = jnp.exp(scores - jnp.max(scores, axis=1, keepdims=True)).astype(BF16)
-        mixed = jnp.dot(weights, values, preferred_element_type=F32)
-        mixed = mixed[:, :inner] / mixed[:, inner:]
-        out_ref[row : row + block, :] = jnp.where(first, mixed[:block], mixed[block:]).astype(BF16)
+        upper = jnp.dot(weights[:block], jnp.where(first, values, one), preferred_element_type=F32)
+        lower = jnp.dot(weights[block:], jnp.where(first, one, values), preferred_element_type=F32)
+        sums = pltpu.roll(jnp.where(first, lower, upper), HD, 1)
+        out_ref[row : row + block, :] = (jnp.where(first, upper, lower) / sums).astype(BF16)
 
 
 def output_kernel(sub_slots, core_ref, parity_ref, back_ref, slot_ref, *refs):
@@ -216,13 +216,14 @@
             attn.append(jnp.dot(place_t, back_ref[side], preferred_element_type=F32).astype(BF16))
     attn = jnp.concatenate(attn, axis=1)
     weights = jnp.concatenate([ref[...] for ref in w_refs], axis=0)
-    total = jnp.dot(attn, weights, preferred_element_type=F32)
-    total = jnp.concatenate([total, jnp.zeros((lanes - quarter, depth), F32)], axis=0).T
+    attn = jnp.concatenate([attn] * (lanes // quarter), axis=0)
+    total = jnp.dot(attn, weights, preferred_element_type=F32).T
     total = jnp.concatenate([total, jnp.zeros((2 * upper - width, lanes), F32)], axis=0)
+    first = iota((1, lanes), 1) < quarter
     for m in range(parts):
         above = total[m * width : m * width + upper]
         below = total[m * width + upper : m * width + 2 * upper]
-        part_ref[m] = (above + pltpu.roll(below, quarter, 1)).astype(BF16)
+        part_ref[m] = jnp.where(first, above, below).astype(BF16)
 
 
 def stage_kernel(hbm, out_ref, sem):

time: 103 us -> 102 us (level)
  no operation moved by 1% of the time
where the time goes in v14:
time: 102 us; the launch traced here: 101 us
  starting transfers between devices  46 us (45%)
  waiting for transfers between devices  22.3 us (22%)
  blocking collectives  16.4 us (16%)
  Pallas kernels  13.7 us (13%)
  local copies, waits for them, and re-layouts  2.6 us (3%)
    all_to_all x1, blocking collectives, body(): sums = lax.all_to_all(partial, 'mp', 0, 0, tiled=True)  16.4 us
    all_to_all x1, starting transfers between devices, body(): whole = lax.all_to_all(spread, 'mp', 0, 0, tiled=True)  11.8 us
    all_to_all x1, starting transfers between devices, body(): lax.all_to_all(send.reshape(2 * requests, cap, kinds * inner), ('dp', 'mp...  10.3 us
    all_to_all x1, waiting for transfers between devices, body(): lax.all_to_all(send.reshape(2 * requests, cap, kinds * inner), ('dp', 'mp...  10.1 us
    all_to_all x1, waiting for transfers between devices, body(): lax.all_to_all(attn.reshape(4 * requests, cap // 2, inner), ('dp', 'mp'),...  6.98 us
    all_to_all x1, starting transfers between devices, body(): lax.all_to_all(attn.reshape(4 * requests, cap // 2, inner), ('dp', 'mp'),...  6.91 us
    ppermute x3, starting transfers between devices, body(): w_sib = [lax.ppermute(block, 'mp', sibling) for block in w_own]  6.34 us
    all_to_all x1, waiting for transfers between devices, body(): whole = lax.all_to_all(spread, 'mp', 0, 0, tiled=True)  5.2 us
  transfers between devices with their start and end apart: 10, of which 3 were waited for; matrix products, arithmetic and copies ran while one was open for 3% of the time, Pallas kernels for 6%

profile of v14, /device:TPU:1, one launch (start us, length us, event | category | flops | bytes accessed | tf_op | source)
XLA Modules:
  0.0 101.4 jit_solution(11060239773758503391)
XLA Ops:
  0.0 2.1 %shard_map.82 = (bf16[16,152,128]{2,1,0:T(8,128)(2,1)}, bf16[152,256]{1,0:T(8,128)(2,1)S(1)}, f32[1,256]{1,0:T(1,128)S(1)}) custom-call(bf16[152,256]{1,0:T(8,128)(2,1)} %bitcast.29, s32[1,256]{1,0:T(1,128)} %bitcast.24), custom_call_target="tpu_custom_call" | custom-call | bytes 1048576 | tf_op jit(solution)/shard_map/pallas_call | solution.py:293
  2.1 11.8 %all-to-all-start = ((bf16[16,152,128]{2,1,0:T(8,128)(2,1)}), bf16[16,152,128]{2,1,0:T(8,128)(2,1)S(1)}, u32[]{:S(2)}, u32[]{:S(2)}) async-start(bf16[16,152,128]{2,1,0:T(8,128)(2,1)} %get-tuple-element.31), calls=%async_computation | async-start | bytes 1245184 | tf_op jit(solution)/shard_map/all_to_all | solution.py:306
  13.9 0.0 slice-start
  13.9 0.0 copy-start.1
  14.0 0.0 copy-start.3
  14.0 0.0 copy-start.2
  14.0 1.6 %slice_bitcast_fusion = (bf16[2432,128]{1,0:T(8,128)(2,1)S(1)}, bf16[2432,128]{1,0:T(8,128)(2,1)S(1)}, bf16[2432,128]{1,0:T(8,128)(2,1)S(1)}) fusion(bf16[2432,3,128]{2,0,1:T(8,128)(2,1)} %param.12), kind=kLoop, calls=%fused_computation | loop fusion | bytes 3735552 | tf_op jit(solution)/shard_map/squeeze | solution.py:308
  15.6 2.0 %collective-permute-start = (bf16[2432,128]{1,0:T(8,128)(2,1)S(1)}, bf16[2432,128]{1,0:T(8,128)(2,1)}, u32[]{:S(2)}, u32[]{:S(2)}) collective-permute-start(bf16[2432,128]{1,0:T(8,128)(2,1)S(1)} %get-tuple-element.40.own0_ref), channel_id=1, source_target_pairs={{0,1},{1,0},{2,3},{3,2},{4,5},{5,4},{6,7},{7,6},{8,9},{9,8},{10,11... | collective-permute-start | bytes 1867784 | tf_op jit(solution)/shard_map/ppermute | solution.py:309
  17.6 2.3 %collective-permute-start.1 = (bf16[2432,128]{1,0:T(8,128)(2,1)S(1)}, bf16[2432,128]{1,0:T(8,128)(2,1)}, u32[]{:S(2)}, u32[]{:S(2)}) collective-permute-start(bf16[2432,128]{1,0:T(8,128)(2,1)S(1)} %get-tuple-element.41.own1_ref), channel_id=1, source_target_pairs={{0,1},{1,0},{2,3},{3,2},{4,5},{5,4},{6,7},{7,6},{8,9},{9,8},{10,11... | collective-permute-start | bytes 1867784 | tf_op jit(solution)/shard_map/ppermute | solution.py:309
  20.0 2.0 %collective-permute-start.2 = (bf16[2432,128]{1,0:T(8,128)(2,1)S(1)}, bf16[2432,128]{1,0:T(8,128)(2,1)}, u32[]{:S(2)}, u32[]{:S(2)}) collective-permute-start(bf16[2432,128]{1,0:T(8,128)(2,1)S(1)} %get-tuple-element.42.own2_ref), channel_id=1, source_target_pairs={{0,1},{1,0},{2,3},{3,2},{4,5},{5,4},{6,7},{7,6},{8,9},{9,8},{10,11... | collective-permute-start | bytes 1867784 | tf_op jit(solution)/shard_map/ppermute | solution.py:309
  22.0 2.3 %collective-permute-start.3 = (bf16[128,2432]{1,0:T(8,128)(2,1)S(1)}, bf16[128,2432]{1,0:T(8,128)(2,1)}, u32[]{:S(2)}, u32[]{:S(2)}) collective-permute-start(bf16[128,2432]{1,0:T(8,128)(2,1)S(1)} %copy-done), channel_id=1, source_target_pairs={{0,1},{1,0},{2,3},{3,2},{4,5},{5,4},{6,7},{7,6},{8,9},{9,8},{10,11... | collective-permute-start | bytes 1867784 | tf_op jit(solution)/shard_map/ppermute | solution.py:310
  24.3 0.8 slice.22
  25.1 0.1 dynamic-slice_bitcast_fusion.gate_ref
  25.2 2.8 %shard_map.83 = (bf16[2,2432,128]{2,1,0:T(8,128)(2,1)}, bf16[152,256]{1,0:T(8,128)(2,1)S(1)}, f32[1,128]{1,0:T(1,128)S(1)}) custom-call(s32[1]{0:T(128)} %bitcast.core_ref, s32[1,256]{1,0:T(1,128)S(1)} %bitcast.25, f32[1,256]{1,0:T(1,128)S(1)} %get-tuple-element.34.pos_ref, s32[1,32]{1,0:T(1,128)S(1)} %bitcast.26, bf16[3,28,2432]{2,1,0:T(8,128)(2,1)} %bitcast.27, ...), custom_call_target="tpu_custom_call" | custom-call | bytes 1048576 | tf_op jit(solution)/shard_map/pallas_call | solution.py:313
  28.1 0.0 collective-permute-done.sib0_hbm
  28.1 0.0 collective-permute-done.2.sib2_hbm
  28.1 0.0 collective-permute-done.3.hbm
  28.1 5.2 %all-to-all-done.tok_ref = bf16[16,152,128]{2,1,0:T(8,128)(2,1)S(1)} async-done(((bf16[16,152,128]{2,1,0:T(8,128)(2,1)}), bf16[16,152,128]{2,1,0:T(8,128)(2,1)S(1)}, u32[]{:S(2)}, u32[]{:S(2)}) %all-to-all-start) | async-done | bytes 622624 | tf_op jit(solution)/shard_map/all_to_all | solution.py:306
  33.3 3.7 %shard_map.84 = bf16[2,256,384]{2,1,0:T(8,128)(2,1)} custom-call(s32[1]{0:T(128)} %bitcast.core_ref, bf16[16,152,128]{2,1,0:T(8,128)(2,1)S(1)} %all-to-all-done.tok_ref, bf16[2,2432,128]{2,1,0:T(8,128)(2,1)} %get-tuple-element.39.mod_hbm, bf16[2432,128]{1,0:T(8,128)(2,1)S(1)} %get-tuple-element.40.own0_ref, ...), custom_call_target="tpu_custom_call" | custom-call | flops 478150656 | bytes 1048576 | tf_op jit(solution)/shard_map/pallas_call | solution.py:328
  37.1 10.3 %all-to-all-start.1 = ((bf16[64,8,384]{2,1,0:T(8,128)(2,1)}), bf16[64,8,384]{2,1,0:T(8,128)(2,1)S(1)}, u32[]{:S(2)}, u32[]{:S(2)}) async-start(bf16[64,8,384]{2,1,0:T(8,128)(2,1)} %bitcast.10), calls=%async_computation.1 | async-start | bytes 786432 | tf_op jit(solution)/shard_map/all_to_all | solution.py:343
  47.4 1.9 %collective-permute-start.4 = (bf16[128,2432]{1,0:T(8,128)(2,1)S(1)}, bf16[128,2432]{1,0:T(8,128)(2,1)S(1)}, u32[]{:S(2)}, u32[]{:S(2)}) collective-permute-start(bf16[128,2432]{1,0:T(8,128)(2,1)S(1)} %copy-done), channel_id=1, source_target_pairs={{0,2},{1,3},{2,0},{3,1},{4,6},{5,7},{6,4},{7,5},{8,10},{9,11},{10,... | collective-permute-start | bytes 1867784 | tf_op jit(solution)/shard_map/ppermute | solution.py:347
  49.3 3.9 %collective-permute-start.6 = (bf16[80,2432]{1,0:T(8,128)(2,1)}, bf16[80,2432]{1,0:T(8,128)(2,1)S(1)}, u32[]{:S(2)}, u32[]{:S(2)}) collective-permute-start(bf16[80,2432]{1,0:T(8,128)(2,1)} %slice.22), channel_id=1, source_target_pairs={{0,3},{1,2},{2,1},{3,0},{4,7},{5,6},{6,5},{7,4},{8,11},{9,10},{10,... | collective-permute-start | bytes 1167368 | tf_op jit(solution)/shard_map/ppermute | solution.py:348
  53.3 10.1 %all-to-all-done.1 = bf16[64,8,384]{2,1,0:T(8,128)(2,1)S(1)} async-done(((bf16[64,8,384]{2,1,0:T(8,128)(2,1)}), bf16[64,8,384]{2,1,0:T(8,128)(2,1)S(1)}, u32[]{:S(2)}, u32[]{:S(2)}) %all-to-all-start.1) | async-done | bytes 393248 | tf_op jit(solution)/shard_map/all_to_all | solution.py:343
  63.4 2.3 %shard_map.85 = bf16[512,128]{1,0:T(8,128)(2,1)} custom-call(bf16[512,384]{1,0:T(8,128)(2,1)S(1)} %bitcast.23, bf16[2,384,128]{2,1,0:T(8,128)(2,1)S(1)} %pad.4.ctx_ref), custom_call_target="tpu_custom_call" | custom-call | flops 469762048 | bytes 1048576 | tf_op jit(solution)/shard_map/pallas_call | solution.py:350
  65.7 6.9 %all-to-all-start.2 = ((bf16[128,4,128]{2,1,0:T(4,128)(2,1)}), bf16[128,4,128]{2,1,0:T(4,128)(2,1)S(1)}, u32[]{:S(2)}, u32[]{:S(2)}) async-start(bf16[128,4,128]{2,1,0:T(4,128)(2,1)} %bitcast.13), calls=%async_computation.2 | async-start | bytes 262144 | tf_op jit(solution)/shard_map/all_to_all | solution.py:357
  72.6 0.0 collective-permute-done.4.refs_2_
  72.6 2.5 %collective-permute-start.5 = (bf16[48,2432]{1,0:T(8,128)(2,1)S(1)}, bf16[48,2432]{1,0:T(8,128)(2,1)S(1)}, u32[]{:S(2)}, u32[]{:S(2)}) collective-permute-start(bf16[48,2432]{1,0:T(8,128)(2,1)S(1)} %slice.24), channel_id=1, source_target_pairs={{0,1},{1,0},{2,3},{3,2},{4,5},{5,4},{6,7},{7,6},{8,9},{9,8},{10,11... | collective-permute-start | bytes 700424 | tf_op jit(solution)/shard_map/ppermute | solution.py:349
  75.1 1.1 %shard_map.86.refs_1_ = bf16[128,2432]{1,0:T(8,128)(2,1)S(1)} custom-call(bf16[128,2432]{1,0:T(8,128)(2,1)} %collective-permute-done.3.hbm), custom_call_target="tpu_custom_call" | custom-call | bytes 1048576 | tf_op jit(solution)/shard_map/pallas_call | solution.py:361
  76.2 7.0 %all-to-all-done.2 = bf16[128,4,128]{2,1,0:T(4,128)(2,1)S(1)} async-done(((bf16[128,4,128]{2,1,0:T(4,128)(2,1)}), bf16[128,4,128]{2,1,0:T(4,128)(2,1)S(1)}, u32[]{:S(2)}, u32[]{:S(2)}) %all-to-all-start.2) | async-done | bytes 131104 | tf_op jit(solution)/shard_map/all_to_all | solution.py:357
  83.2 0.8 shard_map.87
  84.1 16.4 %all_to_all.20.sums_ref = bf16[16,80,128]{2,1,0:T(8,128)(2,1)S(1)} all-to-all(bf16[16,80,128]{2,1,0:T(8,128)(2,1)S(1)} %shard_map.87), channel_id=1, replica_groups=mesh['dp'=32,'mp'=16] {'mp'}, dimensions={0} | all-to-all | bytes 655360 | tf_op jit(solution)/shard_map/all_to_all | solution.py:370
  100.5 0.9 shard_map.88
  (14 shorter events, 0.1 us)
Async XLA Ops:
  2.1 31.2 %all-to-all-start = ((bf16[16,152,128]{2,1,0:T(8,128)(2,1)}), bf16[16,152,128]{2,1,0:T(8,128)(2,1)S(1)}, u32[]{:S(2)}, u32[]{:S(2)}) async-start(bf16[16,152,128]{2,1,0:T(8,128)(2,1)} %get-tuple-element.31), calls=%async_computation | async-start | bytes 1245184 | tf_op jit(solution)/shard_map/all_to_all | solution.py:306
  13.9 8.1 %copy-start = (bf16[128,2432]{1,0:T(8,128)(2,1)S(1)}, bf16[128,2432]{1,0:T(8,128)(2,1)}, u32[]{:S(2)}) copy-start(bf16[128,2432]{1,0:T(8,128)(2,1)} %refs_0_) | copy-start | bytes 1867780
  13.9 11.2 %slice-start = ((bf16[28,3,2432]{2,0,1:T(8,128)(2,1)}), bf16[28,1,2432]{2,0,1:T(8,128)(2,1)S(1)}, s32[]{:S(2)}) async-start(bf16[28,3,2432]{2,0,1:T(8,128)(2,1)} %param.11), calls=%async_computation.4 | async-start | bytes 311296 | tf_op jit(solution)/shard_map/slice | solution.py:312
  13.9 11.3 %copy-start.1 = (s32[256,1]{0,1:T(1,128)S(1)}, s32[256,1]{0,1:T(1,128)}, u32[]{:S(2)}) copy-start(s32[256,1]{0,1:T(1,128)} %param.9) | copy-start | bytes 3076
  14.0 11.2 %copy-start.3 = (s32[32]{0:T(128)S(1)}, s32[32]{0:T(128)}, u32[]{:S(2)}) copy-start(s32[32]{0:T(128)} %param.10) | copy-start | bytes 388
  14.0 19.3 %copy-start.2 = (f32[2,64]{1,0:T(2,128)S(1)}, f32[2,64]{1,0:T(2,128)}, u32[]{:S(2)}) copy-start(f32[2,64]{1,0:T(2,128)} %gain_ref.1) | copy-start | bytes 1540
  15.6 12.4 %collective-permute-start = (bf16[2432,128]{1,0:T(8,128)(2,1)S(1)}, bf16[2432,128]{1,0:T(8,128)(2,1)}, u32[]{:S(2)}, u32[]{:S(2)}) collective-permute-start(bf16[2432,128]{1,0:T(8,128)(2,1)S(1)} %get-tuple-element.40.own0_ref), channel_id=1, source_target_pairs={{0,1},{1,0},{2,3},{3,2},{4,5},{5,4},{6,7},{7,6},{8,9},{9,8},{10,11... | collective-permute-start | bytes 1867784 | tf_op jit(solution)/shard_map/ppermute | solution.py:309
  17.6 10.4 %collective-permute-start.1 = (bf16[2432,128]{1,0:T(8,128)(2,1)S(1)}, bf16[2432,128]{1,0:T(8,128)(2,1)}, u32[]{:S(2)}, u32[]{:S(2)}) collective-permute-start(bf16[2432,128]{1,0:T(8,128)(2,1)S(1)} %get-tuple-element.41.own1_ref), channel_id=1, source_target_pairs={{0,1},{1,0},{2,3},{3,2},{4,5},{5,4},{6,7},{7,6},{8,9},{9,8},{10,11... | collective-permute-start | bytes 1867784 | tf_op jit(solution)/shard_map/ppermute | solution.py:309
  20.0 8.1 %collective-permute-start.2 = (bf16[2432,128]{1,0:T(8,128)(2,1)S(1)}, bf16[2432,128]{1,0:T(8,128)(2,1)}, u32[]{:S(2)}, u32[]{:S(2)}) collective-permute-start(bf16[2432,128]{1,0:T(8,128)(2,1)S(1)} %get-tuple-element.42.own2_ref), channel_id=1, source_target_pairs={{0,1},{1,0},{2,3},{3,2},{4,5},{5,4},{6,7},{7,6},{8,9},{9,8},{10,11... | collective-permute-start | bytes 1867784 | tf_op jit(solution)/shard_map/ppermute | solution.py:309
  22.0 6.1 %collective-permute-start.3 = (bf16[128,2432]{1,0:T(8,128)(2,1)S(1)}, bf16[128,2432]{1,0:T(8,128)(2,1)}, u32[]{:S(2)}, u32[]{:S(2)}) collective-permute-start(bf16[128,2432]{1,0:T(8,128)(2,1)S(1)} %copy-done), channel_id=1, source_target_pairs={{0,1},{1,0},{2,3},{3,2},{4,5},{5,4},{6,7},{7,6},{8,9},{9,8},{10,11... | collective-permute-start | bytes 1867784 | tf_op jit(solution)/shard_map/ppermute | solution.py:310
  33.3 19.9 %copy-start.4 = (bf16[1,2,333,128]{3,1,2,0:T(2,128)(2,1)S(1)}, bf16[1,2,333,128]{3,1,2,0:T(2,128)(2,1)}, u32[]{:S(2)}) copy-start(bf16[1,2,333,128]{3,1,2,0:T(2,128)(2,1)} %param.14) | copy-start | bytes 511492
  37.1 26.4 %all-to-all-start.1 = ((bf16[64,8,384]{2,1,0:T(8,128)(2,1)}), bf16[64,8,384]{2,1,0:T(8,128)(2,1)S(1)}, u32[]{:S(2)}, u32[]{:S(2)}) async-start(bf16[64,8,384]{2,1,0:T(8,128)(2,1)} %bitcast.10), calls=%async_computation.1 | async-start | bytes 786432 | tf_op jit(solution)/shard_map/all_to_all | solution.py:343
  47.4 25.2 %collective-permute-start.4 = (bf16[128,2432]{1,0:T(8,128)(2,1)S(1)}, bf16[128,2432]{1,0:T(8,128)(2,1)S(1)}, u32[]{:S(2)}, u32[]{:S(2)}) collective-permute-start(bf16[128,2432]{1,0:T(8,128)(2,1)S(1)} %copy-done), channel_id=1, source_target_pairs={{0,2},{1,3},{2,0},{3,1},{4,6},{5,7},{6,4},{7,5},{8,10},{9,11},{10,... | collective-permute-start | bytes 1867784 | tf_op jit(solution)/shard_map/ppermute | solution.py:347
  49.3 26.9 %collective-permute-start.6 = (bf16[80,2432]{1,0:T(8,128)(2,1)}, bf16[80,2432]{1,0:T(8,128)(2,1)S(1)}, u32[]{:S(2)}, u32[]{:S(2)}) collective-permute-start(bf16[80,2432]{1,0:T(8,128)(2,1)} %slice.22), channel_id=1, source_target_pairs={{0,3},{1,2},{2,1},{3,0},{4,7},{5,6},{6,5},{7,4},{8,11},{9,10},{10,... | collective-permute-start | bytes 1167368 | tf_op jit(solution)/shard_map/ppermute | solution.py:348
  65.7 17.6 %all-to-all-start.2 = ((bf16[128,4,128]{2,1,0:T(4,128)(2,1)}), bf16[128,4,128]{2,1,0:T(4,128)(2,1)S(1)}, u32[]{:S(2)}, u32[]{:S(2)}) async-start(bf16[128,4,128]{2,1,0:T(4,128)(2,1)} %bitcast.13), calls=%async_computation.2 | async-start | bytes 262144 | tf_op jit(solution)/shard_map/all_to_all | solution.py:357
  72.6 3.6 %collective-permute-start.5 = (bf16[48,2432]{1,0:T(8,128)(2,1)S(1)}, bf16[48,2432]{1,0:T(8,128)(2,1)S(1)}, u32[]{:S(2)}, u32[]{:S(2)}) collective-permute-start(bf16[48,2432]{1,0:T(8,128)(2,1)S(1)} %slice.24), channel_id=1, source_target_pairs={{0,1},{1,0},{2,3},{3,2},{4,5},{5,4},{6,7},{7,6},{8,9},{9,8},{10,11... | collective-permute-start | bytes 700424 | tf_op jit(solution)/shard_map/ppermute | solution.py:349

commit v15 on v14

--- a/solution.py
+++ b/solution.py
@@ -12,6 +12,7 @@
 DEAD = 1e30
 MASKED = -1e30
 VMEM_LIMIT = 24 * 1024 * 1024
+VMEM_MOST = 60 * 1024 * 1024
 F32, BF16, I32 = jnp.float32, jnp.bfloat16, jnp.int32
 
 
@@ -52,38 +53,23 @@
     return (4 * (place - quarter * parity) + 2 * parity + core).astype(F32)
 
 
-def spread_kernel(tok_hbm, req_hbm, out_hbm, perm_ref, pos_ref, tok_ref, req_ref, halves_ref, sems):
+def spread_kernel(tok_ref, req_ref, out_ref, perm_ref, pos_ref):
     width, rows = tok_ref.shape
     half = rows // 2
-    parts = out_hbm.shape[0]
-    reads = [pltpu.make_async_copy(req_hbm, req_ref, sems.at[0]), pltpu.make_async_copy(tok_hbm, tok_ref, sems.at[1])]
-    for copy in reads:
-        copy.start()
-    reads[0].wait()
     req = req_ref[...].astype(F32)
     req_col = as_column(req)
     earlier = (req_col < req) | ((req_col == req) & (iota((rows, rows), 0) < iota((rows, rows), 1)))
     pos = jnp.sum(jnp.where(earlier, 1.0, 0.0), axis=0, keepdims=True)
-    deal = one_hot(pos == dealt(rows))
     pos_ref[...] = pos
-    reads[1].wait()
-    perm = dot_nt(tok_ref[...], deal).astype(BF16)
-    halves_ref[0] = perm[:, :half]
-    halves_ref[1] = perm[:, half:]
-    writes = [pltpu.make_async_copy(halves_ref.at[m % 2], out_hbm.at[m], sems.at[2 + m]) for m in range(parts)]
-    for copy in writes:
-        copy.start()
+    perm = dot_nt(tok_ref[...], one_hot(pos == dealt(rows))).astype(BF16)
     perm_ref[...] = perm
-    for copy in writes:
-        copy.wait()
+    for m in range(out_ref.shape[0]):
+        out_ref[m] = perm[:, (m % 2) * half : (m % 2 + 1) * half]
 
 
 def prepare_kernel(
-    cap, core_ref, req_ref, pos_ref, steps_ref, table_hbm, gate_ref,
-    mod_hbm, gates_ref, slot_ref, mod_ref, table_ref, sems,
+    cap, core_ref, req_ref, pos_ref, steps_ref, table_ref, gate_ref, mod_hbm, gates_ref, slot_ref, mod_ref, sems
 ):
-    read = pltpu.make_async_copy(table_hbm.at[pl.ds(0, 2)], table_ref, sems.at[2])
-    read.start()
     rows = req_ref.shape[1]
     half = rows // 2
     requests = steps_ref.shape[1]
@@ -110,7 +96,6 @@
     pick = one_hot(iota((levels, rows), 0).astype(F32) == step)
     gates_ref[...] = dot_tn(gate_ref[...], pick).astype(BF16)
     pick = jnp.where(is_first, pick[:, :half].astype(F32), pick[:, half:].astype(F32)).astype(BF16)
-    read.wait()
     writes = []
     for part in range(2):
         mod_ref[part] = dot_tn(table_ref[part], pick).astype(BF16)
@@ -248,14 +233,14 @@
     out_ref[...] = jnp.dot(mixed, deal, preferred_element_type=F32).astype(BF16)
 
 
-def call(kernel, out_shape, specs, out_specs, scratch=(), flops=0):
+def call(kernel, out_shape, specs, out_specs, scratch=(), flops=0, limit=VMEM_LIMIT):
     return pl.pallas_call(
         kernel,
         out_shape=out_shape,
         in_specs=[PLACES[letter] for letter in specs],
         out_specs=tuple(PLACES[letter] for letter in out_specs) if len(out_specs) > 1 else PLACES[out_specs],
         scratch_shapes=list(scratch),
-        compiler_params=pltpu.CompilerParams(vmem_limit_bytes=VMEM_LIMIT),
+        compiler_params=pltpu.CompilerParams(vmem_limit_bytes=limit),
         cost_estimate=pl.CostEstimate(flops=flops, bytes_accessed=1 << 20, transcendentals=0),
     )
 
@@ -292,16 +277,11 @@
 
     spread, perm, pos = call(
         spread_kernel,
-        (pltpu.HBM((parts, width, half), BF16), shape((width, rows), BF16), shape((1, rows), F32)),
-        "aa",
-        "avv",
-        [
-            pltpu.VMEM((width, rows), BF16),
-            pltpu.VMEM((1, rows), I32),
-            pltpu.VMEM((2, width, half), BF16),
-            pltpu.SemaphoreType.DMA((2 + parts,)),
-        ],
-    )(in_hbm(tokens.T), in_hbm(req))
+        (shape((parts, width, half), BF16), shape((width, rows), BF16), shape((1, rows), F32)),
+        "vv",
+        "vvv",
+        limit=VMEM_MOST,
+    )(tokens.T, req)
     spread, w_qkv, w_out = lax.optimization_barrier((spread, w_qkv, w_out))
     whole = lax.all_to_all(spread, "mp", 0, 0, tiled=True)
 
@@ -313,14 +293,10 @@
     mod, gates, slot = call(
         functools.partial(prepare_kernel, cap),
         (pltpu.HBM((2, depth, half), BF16), shape((width, rows), BF16), shape((1, half), F32)),
-        "svvvav",
+        "svvvvv",
         "avv",
-        [
-            pltpu.VMEM((2, depth, half), BF16),
-            pltpu.VMEM((2, gate_table.shape[0], depth), BF16),
-            pltpu.SemaphoreType.DMA((3,)),
-        ],
-    )(core, req, pos, tsteps.reshape(1, requests), in_hbm(mod_table.transpose(1, 0, 2)), gate_table)
+        [pltpu.VMEM((2, depth, half), BF16), pltpu.SemaphoreType.DMA((2,))],
+    )(core, req, pos, tsteps.reshape(1, requests), mod_table.transpose(1, 0, 2), gate_table)
     whole, w_own, w_sib, out_sib, mod, gates, slot = lax.optimization_barrier(
         (whole, w_own, w_sib, out_sib, mod, gates, slot)
     )

time: 102 us -> 102 us (level)
  local copies, waits for them, and re-layouts: 2.6 us -> 3.63 us
    unnamed x10 -> x16, local copies, waits for them, and re-layouts: 0.03 us -> 1.05 us
  transfers between devices with their start and end apart: 10 -> 10, of which waited for: 3 -> 3; matrix products, arithmetic and copies ran while one was open for 3% -> 3% of each run, Pallas kernels for 6% -> 5%
where the time goes in v15:
time: 102 us; the launch traced here: 101 us
  starting transfers between devices  46.1 us (45%)
  waiting for transfers between devices  22.2 us (22%)
  blocking collectives  16.5 us (16%)
  Pallas kernels  12.8 us (13%)
  local copies, waits for them, and re-layouts  3.63 us (4%)
    all_to_all x1, blocking collectives, body(): sums = lax.all_to_all(partial, 'mp', 0, 0, tiled=True)  16.5 us
    all_to_all x1, starting transfers between devices, body(): whole = lax.all_to_all(spread, 'mp', 0, 0, tiled=True)  11.8 us
    all_to_all x1, starting transfers between devices, body(): lax.all_to_all(send.reshape(2 * requests, cap, kinds * inner), ('dp', 'mp...  10.3 us
    all_to_all x1, waiting for transfers between devices, body(): lax.all_to_all(send.reshape(2 * requests, cap, kinds * inner), ('dp', 'mp...  10.1 us
    all_to_all x1, waiting for transfers between devices, body(): lax.all_to_all(attn.reshape(4 * requests, cap // 2, inner), ('dp', 'mp'),...  6.96 us
    all_to_all x1, starting transfers between devices, body(): lax.all_to_all(attn.reshape(4 * requests, cap // 2, inner), ('dp', 'mp'),...  6.96 us
    ppermute x3, starting transfers between devices, body(): w_sib = [lax.ppermute(block, 'mp', sibling) for block in w_own]  6.34 us
    all_to_all x1, waiting for transfers between devices, body(): whole = lax.all_to_all(spread, 'mp', 0, 0, tiled=True)  5.04 us
  transfers between devices with their start and end apart: 10, of which 3 were waited for; matrix products, arithmetic and copies ran while one was open for 3% of the time, Pallas kernels for 5%

profile of v15, /device:TPU:1, one launch (start us, length us, event | category | flops | bytes accessed | tf_op | source)
XLA Modules:
  0.0 101.4 jit_solution(7143406876109486368)
XLA Ops:
  0.0 2.1 %shard_map.82 = (bf16[16,152,128]{2,1,0:T(8,128)(2,1)}, bf16[152,256]{1,0:T(8,128)(2,1)}, f32[1,256]{1,0:T(1,128)}) custom-call(bf16[152,256]{1,0:T(8,128)(2,1)} %bitcast.29, s32[1,256]{1,0:T(1,128)} %bitcast.25), custom_call_target="tpu_custom_call" | custom-call | bytes 1048576 | tf_op jit(solution)/shard_map/pallas_call | solution.py:278
  2.1 11.8 %all-to-all-start = ((bf16[16,152,128]{2,1,0:T(8,128)(2,1)}), bf16[16,152,128]{2,1,0:T(8,128)(2,1)S(1)}, u32[]{:S(2)}, u32[]{:S(2)}) async-start(bf16[16,152,128]{2,1,0:T(8,128)(2,1)} %get-tuple-element.31), calls=%async_computation | async-start | bytes 1245184 | tf_op jit(solution)/shard_map/all_to_all | solution.py:286
  14.0 0.0 slice-start
  14.0 0.0 copy-start.3
  14.0 0.0 copy-start.6
  14.0 0.0 copy-start.5
  14.0 1.6 %slice_bitcast_fusion = (bf16[2432,128]{1,0:T(8,128)(2,1)S(1)}, bf16[2432,128]{1,0:T(8,128)(2,1)S(1)}, bf16[2432,128]{1,0:T(8,128)(2,1)S(1)}) fusion(bf16[2432,3,128]{2,0,1:T(8,128)(2,1)} %param.12), kind=kLoop, calls=%fused_computation | loop fusion | bytes 3735552 | tf_op jit(solution)/shard_map/squeeze | solution.py:288
  15.7 2.0 %collective-permute-start = (bf16[2432,128]{1,0:T(8,128)(2,1)S(1)}, bf16[2432,128]{1,0:T(8,128)(2,1)}, u32[]{:S(2)}, u32[]{:S(2)}) collective-permute-start(bf16[2432,128]{1,0:T(8,128)(2,1)S(1)} %get-tuple-element.40.own0_ref), channel_id=1, source_target_pairs={{0,1},{1,0},{2,3},{3,2},{4,5},{5,4},{6,7},{7,6},{8,9},{9,8},{10,11... | collective-permute-start | bytes 1867784 | tf_op jit(solution)/shard_map/ppermute | solution.py:289
  17.7 2.3 %collective-permute-start.1 = (bf16[2432,128]{1,0:T(8,128)(2,1)S(1)}, bf16[2432,128]{1,0:T(8,128)(2,1)}, u32[]{:S(2)}, u32[]{:S(2)}) collective-permute-start(bf16[2432,128]{1,0:T(8,128)(2,1)S(1)} %get-tuple-element.41.own1_ref), channel_id=1, source_target_pairs={{0,1},{1,0},{2,3},{3,2},{4,5},{5,4},{6,7},{7,6},{8,9},{9,8},{10,11... | collective-permute-start | bytes 1867784 | tf_op jit(solution)/shard_map/ppermute | solution.py:289
  20.0 2.0 %collective-permute-start.2 = (bf16[2432,128]{1,0:T(8,128)(2,1)S(1)}, bf16[2432,128]{1,0:T(8,128)(2,1)}, u32[]{:S(2)}, u32[]{:S(2)}) collective-permute-start(bf16[2432,128]{1,0:T(8,128)(2,1)S(1)} %get-tuple-element.42.own2_ref), channel_id=1, source_target_pairs={{0,1},{1,0},{2,3},{3,2},{4,5},{5,4},{6,7},{7,6},{8,9},{9,8},{10,11... | collective-permute-start | bytes 1867784 | tf_op jit(solution)/shard_map/ppermute | solution.py:289
  22.0 2.3 %collective-permute-start.3 = (bf16[128,2432]{1,0:T(8,128)(2,1)S(1)}, bf16[128,2432]{1,0:T(8,128)(2,1)}, u32[]{:S(2)}, u32[]{:S(2)}) collective-permute-start(bf16[128,2432]{1,0:T(8,128)(2,1)S(1)} %copy-done), channel_id=1, source_target_pairs={{0,1},{1,0},{2,3},{3,2},{4,5},{5,4},{6,7},{7,6},{8,9},{9,8},{10,11... | collective-permute-start | bytes 1867784 | tf_op jit(solution)/shard_map/ppermute | solution.py:290
  24.4 0.8 slice.22
  25.2 0.1 dynamic-slice_bitcast_fusion.gate_ref
  25.3 0.0 copy-start.1
  25.3 1.0 copy-done.1
  26.3 1.9 %shard_map.83 = (bf16[2,2432,128]{2,1,0:T(8,128)(2,1)}, bf16[152,256]{1,0:T(8,128)(2,1)S(1)}, f32[1,128]{1,0:T(1,128)S(1)}) custom-call(s32[1]{0:T(128)} %bitcast.core_ref, s32[1,256]{1,0:T(1,128)S(1)} %bitcast.26, f32[1,256]{1,0:T(1,128)S(1)} %copy-done.4, s32[1,32]{1,0:T(1,128)S(1)} %bitcast.27, bf16[3,28,2432]{2,1,0:T(8,128)(2,1)S(1)} %bitcast.22, ...), custom_call_target="tpu_custom_call" | custom-call | bytes 1048576 | tf_op jit(solution)/shard_map/pallas_call | solution.py:293
  28.2 0.0 collective-permute-done.1.sib1_hbm
  28.3 5.0 %all-to-all-done.tok_ref = bf16[16,152,128]{2,1,0:T(8,128)(2,1)S(1)} async-done(((bf16[16,152,128]{2,1,0:T(8,128)(2,1)}), bf16[16,152,128]{2,1,0:T(8,128)(2,1)S(1)}, u32[]{:S(2)}, u32[]{:S(2)}) %all-to-all-start) | async-done | bytes 622624 | tf_op jit(solution)/shard_map/all_to_all | solution.py:286
  33.3 3.7 %shard_map.84 = bf16[2,256,384]{2,1,0:T(8,128)(2,1)} custom-call(s32[1]{0:T(128)} %bitcast.core_ref, bf16[16,152,128]{2,1,0:T(8,128)(2,1)S(1)} %all-to-all-done.tok_ref, bf16[2,2432,128]{2,1,0:T(8,128)(2,1)} %get-tuple-element.39.mod_hbm, bf16[2432,128]{1,0:T(8,128)(2,1)S(1)} %get-tuple-element.40.own0_ref, ...), custom_call_target="tpu_custom_call" | custom-call | flops 478150656 | bytes 1048576 | tf_op jit(solution)/shard_map/pallas_call | solution.py:304
  37.1 10.3 %all-to-all-start.1 = ((bf16[64,8,384]{2,1,0:T(8,128)(2,1)}), bf16[64,8,384]{2,1,0:T(8,128)(2,1)S(1)}, u32[]{:S(2)}, u32[]{:S(2)}) async-start(bf16[64,8,384]{2,1,0:T(8,128)(2,1)} %bitcast.10), calls=%async_computation.1 | async-start | bytes 786432 | tf_op jit(solution)/shard_map/all_to_all | solution.py:319
  47.4 1.9 %collective-permute-start.4 = (bf16[128,2432]{1,0:T(8,128)(2,1)S(1)}, bf16[128,2432]{1,0:T(8,128)(2,1)S(1)}, u32[]{:S(2)}, u32[]{:S(2)}) collective-permute-start(bf16[128,2432]{1,0:T(8,128)(2,1)S(1)} %copy-done), channel_id=1, source_target_pairs={{0,2},{1,3},{2,0},{3,1},{4,6},{5,7},{6,4},{7,5},{8,10},{9,11},{10,... | collective-permute-start | bytes 1867784 | tf_op jit(solution)/shard_map/ppermute | solution.py:323
  49.3 3.9 %collective-permute-start.6 = (bf16[80,2432]{1,0:T(8,128)(2,1)}, bf16[80,2432]{1,0:T(8,128)(2,1)S(1)}, u32[]{:S(2)}, u32[]{:S(2)}) collective-permute-start(bf16[80,2432]{1,0:T(8,128)(2,1)} %slice.22), channel_id=1, source_target_pairs={{0,3},{1,2},{2,1},{3,0},{4,7},{5,6},{6,5},{7,4},{8,11},{9,10},{10,... | collective-permute-start | bytes 1167368 | tf_op jit(solution)/shard_map/ppermute | solution.py:324
  53.3 10.1 %all-to-all-done.1 = bf16[64,8,384]{2,1,0:T(8,128)(2,1)S(1)} async-done(((bf16[64,8,384]{2,1,0:T(8,128)(2,1)}), bf16[64,8,384]{2,1,0:T(8,128)(2,1)S(1)}, u32[]{:S(2)}, u32[]{:S(2)}) %all-to-all-start.1) | async-done | bytes 393248 | tf_op jit(solution)/shard_map/all_to_all | solution.py:319
  63.4 2.2 %shard_map.85 = bf16[512,128]{1,0:T(8,128)(2,1)} custom-call(bf16[512,384]{1,0:T(8,128)(2,1)S(1)} %bitcast.24, bf16[2,384,128]{2,1,0:T(8,128)(2,1)S(1)} %pad.4.ctx_ref), custom_call_target="tpu_custom_call" | custom-call | flops 469762048 | bytes 1048576 | tf_op jit(solution)/shard_map/pallas_call | solution.py:326
  65.7 7.0 %all-to-all-start.2 = ((bf16[128,4,128]{2,1,0:T(4,128)(2,1)}), bf16[128,4,128]{2,1,0:T(4,128)(2,1)S(1)}, u32[]{:S(2)}, u32[]{:S(2)}) async-start(bf16[128,4,128]{2,1,0:T(4,128)(2,1)} %bitcast.13), calls=%async_computation.2 | async-start | bytes 262144 | tf_op jit(solution)/shard_map/all_to_all | solution.py:333
  72.7 2.5 %collective-permute-start.5 = (bf16[48,2432]{1,0:T(8,128)(2,1)S(1)}, bf16[48,2432]{1,0:T(8,128)(2,1)S(1)}, u32[]{:S(2)}, u32[]{:S(2)}) collective-permute-start(bf16[48,2432]{1,0:T(8,128)(2,1)S(1)} %slice.24), channel_id=1, source_target_pairs={{0,1},{1,0},{2,3},{3,2},{4,5},{5,4},{6,7},{7,6},{8,9},{9,8},{10,11... | collective-permute-start | bytes 700424 | tf_op jit(solution)/shard_map/ppermute | solution.py:325
  75.2 1.1 %shard_map.86.refs_1_ = bf16[128,2432]{1,0:T(8,128)(2,1)S(1)} custom-call(bf16[128,2432]{1,0:T(8,128)(2,1)} %collective-permute-done.3.hbm), custom_call_target="tpu_custom_call" | custom-call | bytes 1048576 | tf_op jit(solution)/shard_map/pallas_call | solution.py:337
  76.3 0.0 copy-start.2
  76.3 7.0 %all-to-all-done.2 = bf16[128,4,128]{2,1,0:T(4,128)(2,1)S(1)} async-done(((bf16[128,4,128]{2,1,0:T(4,128)(2,1)}), bf16[128,4,128]{2,1,0:T(4,128)(2,1)S(1)}, u32[]{:S(2)}, u32[]{:S(2)}) %all-to-all-start.2) | async-done | bytes 131104 | tf_op jit(solution)/shard_map/all_to_all | solution.py:333
  83.3 0.8 shard_map.87
  84.1 16.5 %all_to_all.20.sums_ref = bf16[16,80,128]{2,1,0:T(8,128)(2,1)S(1)} all-to-all(bf16[16,80,128]{2,1,0:T(8,128)(2,1)S(1)} %shard_map.87), channel_id=1, replica_groups=mesh['dp'=32,'mp'=16] {'mp'}, dimensions={0} | all-to-all | bytes 655360 | tf_op jit(solution)/shard_map/all_to_all | solution.py:346
  100.6 0.9 shard_map.88
  (20 shorter events, 0.1 us)
Async XLA Ops:
  2.1 31.2 %all-to-all-start = ((bf16[16,152,128]{2,1,0:T(8,128)(2,1)}), bf16[16,152,128]{2,1,0:T(8,128)(2,1)S(1)}, u32[]{:S(2)}, u32[]{:S(2)}) async-start(bf16[16,152,128]{2,1,0:T(8,128)(2,1)} %get-tuple-element.31), calls=%async_computation | async-start | bytes 1245184 | tf_op jit(solution)/shard_map/all_to_all | solution.py:286
  14.0 8.1 %copy-start = (bf16[128,2432]{1,0:T(8,128)(2,1)S(1)}, bf16[128,2432]{1,0:T(8,128)(2,1)}, u32[]{:S(2)}) copy-start(bf16[128,2432]{1,0:T(8,128)(2,1)} %refs_0_) | copy-start | bytes 1867780
  14.0 11.2 %slice-start = ((bf16[28,3,2432]{2,0,1:T(8,128)(2,1)}), bf16[28,1,2432]{2,0,1:T(8,128)(2,1)S(1)}, s32[]{:S(2)}) async-start(bf16[28,3,2432]{2,0,1:T(8,128)(2,1)} %param.11), calls=%async_computation.4 | async-start | bytes 311296 | tf_op jit(solution)/shard_map/slice | solution.py:292
  14.0 11.3 %copy-start.3 = (s32[256,1]{0,1:T(1,128)S(1)}, s32[256,1]{0,1:T(1,128)}, u32[]{:S(2)}) copy-start(s32[256,1]{0,1:T(1,128)} %param.9) | copy-start | bytes 3076
  14.0 11.3 %copy-start.4 = (f32[1,256]{1,0:T(1,128)S(1)}, f32[1,256]{1,0:T(1,128)}, u32[]{:S(2)}) copy-start(f32[1,256]{1,0:T(1,128)} %get-tuple-element.34.pos_ref) | copy-start | bytes 3076
  14.0 11.2 %copy-start.6 = (s32[32]{0:T(128)S(1)}, s32[32]{0:T(128)}, u32[]{:S(2)}) copy-start(s32[32]{0:T(128)} %param.10) | copy-start | bytes 388
  14.0 19.3 %copy-start.5 = (f32[2,64]{1,0:T(2,128)S(1)}, f32[2,64]{1,0:T(2,128)}, u32[]{:S(2)}) copy-start(f32[2,64]{1,0:T(2,128)} %gain_ref.1) | copy-start | bytes 1540
  15.7 12.6 %collective-permute-start = (bf16[2432,128]{1,0:T(8,128)(2,1)S(1)}, bf16[2432,128]{1,0:T(8,128)(2,1)}, u32[]{:S(2)}, u32[]{:S(2)}) collective-permute-start(bf16[2432,128]{1,0:T(8,128)(2,1)S(1)} %get-tuple-element.40.own0_ref), channel_id=1, source_target_pairs={{0,1},{1,0},{2,3},{3,2},{4,5},{5,4},{6,7},{7,6},{8,9},{9,8},{10,11... | collective-permute-start | bytes 1867784 | tf_op jit(solution)/shard_map/ppermute | solution.py:289
  17.7 10.6 %collective-permute-start.1 = (bf16[2432,128]{1,0:T(8,128)(2,1)S(1)}, bf16[2432,128]{1,0:T(8,128)(2,1)}, u32[]{:S(2)}, u32[]{:S(2)}) collective-permute-start(bf16[2432,128]{1,0:T(8,128)(2,1)S(1)} %get-tuple-element.41.own1_ref), channel_id=1, source_target_pairs={{0,1},{1,0},{2,3},{3,2},{4,5},{5,4},{6,7},{7,6},{8,9},{9,8},{10,11... | collective-permute-start | bytes 1867784 | tf_op jit(solution)/shard_map/ppermute | solution.py:289
  20.0 8.3 %collective-permute-start.2 = (bf16[2432,128]{1,0:T(8,128)(2,1)S(1)}, bf16[2432,128]{1,0:T(8,128)(2,1)}, u32[]{:S(2)}, u32[]{:S(2)}) collective-permute-start(bf16[2432,128]{1,0:T(8,128)(2,1)S(1)} %get-tuple-element.42.own2_ref), channel_id=1, source_target_pairs={{0,1},{1,0},{2,3},{3,2},{4,5},{5,4},{6,7},{7,6},{8,9},{9,8},{10,11... | collective-permute-start | bytes 1867784 | tf_op jit(solution)/shard_map/ppermute | solution.py:289
  22.0 6.2 %collective-permute-start.3 = (bf16[128,2432]{1,0:T(8,128)(2,1)S(1)}, bf16[128,2432]{1,0:T(8,128)(2,1)}, u32[]{:S(2)}, u32[]{:S(2)}) collective-permute-start(bf16[128,2432]{1,0:T(8,128)(2,1)S(1)} %copy-done), channel_id=1, source_target_pairs={{0,1},{1,0},{2,3},{3,2},{4,5},{5,4},{6,7},{7,6},{8,9},{9,8},{10,11... | collective-permute-start | bytes 1867784 | tf_op jit(solution)/shard_map/ppermute | solution.py:290
  25.3 1.0 %copy-start.1 = (bf16[28,3,2432]{2,0,1:T(8,128)(2,1)S(1)}, bf16[28,3,2432]{2,0,1:T(8,128)(2,1)}, u32[]{:S(2)}) copy-start(bf16[28,3,2432]{2,0,1:T(8,128)(2,1)} %param.11) | copy-start | bytes 1225732
  33.3 19.9 %copy-start.7 = (bf16[1,2,333,128]{3,1,2,0:T(2,128)(2,1)S(1)}, bf16[1,2,333,128]{3,1,2,0:T(2,128)(2,1)}, u32[]{:S(2)}) copy-start(bf16[1,2,333,128]{3,1,2,0:T(2,128)(2,1)} %param.14) | copy-start | bytes 511492
  37.1 26.4 %all-to-all-start.1 = ((bf16[64,8,384]{2,1,0:T(8,128)(2,1)}), bf16[64,8,384]{2,1,0:T(8,128)(2,1)S(1)}, u32[]{:S(2)}, u32[]{:S(2)}) async-start(bf16[64,8,384]{2,1,0:T(8,128)(2,1)} %bitcast.10), calls=%async_computation.1 | async-start | bytes 786432 | tf_op jit(solution)/shard_map/all_to_all | solution.py:319
  47.4 25.2 %collective-permute-start.4 = (bf16[128,2432]{1,0:T(8,128)(2,1)S(1)}, bf16[128,2432]{1,0:T(8,128)(2,1)S(1)}, u32[]{:S(2)}, u32[]{:S(2)}) collective-permute-start(bf16[128,2432]{1,0:T(8,128)(2,1)S(1)} %copy-done), channel_id=1, source_target_pairs={{0,2},{1,3},{2,0},{3,1},{4,6},{5,7},{6,4},{7,5},{8,10},{9,11},{10,... | collective-permute-start | bytes 1867784 | tf_op jit(solution)/shard_map/ppermute | solution.py:323
  49.3 26.9 %collective-permute-start.6 = (bf16[80,2432]{1,0:T(8,128)(2,1)}, bf16[80,2432]{1,0:T(8,128)(2,1)S(1)}, u32[]{:S(2)}, u32[]{:S(2)}) collective-permute-start(bf16[80,2432]{1,0:T(8,128)(2,1)} %slice.22), channel_id=1, source_target_pairs={{0,3},{1,2},{2,1},{3,0},{4,7},{5,6},{6,5},{7,4},{8,11},{9,10},{10,... | collective-permute-start | bytes 1167368 | tf_op jit(solution)/shard_map/ppermute | solution.py:324
  65.7 17.6 %all-to-all-start.2 = ((bf16[128,4,128]{2,1,0:T(4,128)(2,1)}), bf16[128,4,128]{2,1,0:T(4,128)(2,1)S(1)}, u32[]{:S(2)}, u32[]{:S(2)}) async-start(bf16[128,4,128]{2,1,0:T(4,128)(2,1)} %bitcast.13), calls=%async_computation.2 | async-start | bytes 262144 | tf_op jit(solution)/shard_map/all_to_all | solution.py:333
  72.7 3.6 %collective-permute-start.5 = (bf16[48,2432]{1,0:T(8,128)(2,1)S(1)}, bf16[48,2432]{1,0:T(8,128)(2,1)S(1)}, u32[]{:S(2)}, u32[]{:S(2)}) collective-permute-start(bf16[48,2432]{1,0:T(8,128)(2,1)S(1)} %slice.24), channel_id=1, source_target_pairs={{0,1},{1,0},{2,3},{3,2},{4,5},{5,4},{6,7},{7,6},{8,9},{9,8},{10,11... | collective-permute-start | bytes 700424 | tf_op jit(solution)/shard_map/ppermute | solution.py:325
  76.3 24.3 %copy-start.2 = (bf16[152,256]{1,0:T(8,128)(2,1)S(1)}, bf16[152,256]{1,0:T(8,128)(2,1)}, u32[]{:S(2)}) copy-start(bf16[152,256]{1,0:T(8,128)(2,1)} %get-tuple-element.53.perm_ref) | copy-start | bytes 233476

commit v16 on v15

--- a/solution.py
+++ b/solution.py
@@ -112,8 +112,13 @@
     parts, width, rows = tok_ref.shape
     depth = parts * width
     inner = own0_ref.shape[1]
-    modulation = pltpu.make_async_copy(mod_hbm, mod_ref, sems.at[0])
-    modulation.start()
+    chunks = [pl.ds(i * (depth // 2), depth // 2) for i in range(2)]
+    modulation = [
+        pltpu.make_async_copy(mod_hbm.at[:, chunk], mod_ref.at[:, chunk], sems.at[4 * i])
+        for i, chunk in enumerate(chunks)
+    ]
+    for copy in modulation:
+        copy.start()
     weights = [
         pltpu.make_async_copy(source, w_ref.at[:, pl.ds(i * inner, inner)], sems.at[1 + i])
         for i, source in enumerate((sib0_hbm, sib1_hbm, sib2_hbm))
@@ -128,8 +133,9 @@
     mean = total * (1.0 / depth)
     square = sum(jnp.sum(jnp.square(tok_ref[m].astype(F32) - mean), axis=0, keepdims=True) for m in range(parts))
     inverse = lax.rsqrt(square * (1.0 / depth) + EPS)
-    modulation.wait()
     for m in range(0, parts, 2):
+        if m % (parts // 2) == 0:
+            modulation[m // (parts // 2)].wait()
         pair = jnp.concatenate([tok_ref[m].astype(F32), tok_ref[m + 1].astype(F32)], axis=0)
         lines = pl.ds(m * width, 2 * width)
         shift, scale = mod_ref[0, lines, :].astype(F32), mod_ref[1, lines, :].astype(F32)
@@ -310,7 +316,7 @@
             pltpu.VMEM((2, depth, half), BF16),
             pltpu.VMEM((depth, kinds * inner), BF16),
             pltpu.VMEM((depth, half), BF16),
-            pltpu.SemaphoreType.DMA((1 + kinds,)),
+            pltpu.SemaphoreType.DMA((2 + kinds,)),
         ],
         flops=4 * depth * half * kinds * inner,
     )(core, whole, in_hbm(mod), *[in_vmem(w) for w in w_own], *[in_hbm(w) for w in w_sib], qk_gain, slot)

time: 102 us -> 102 us (level)
  no operation moved by 1% of the time
where the time goes in v16:
time: 102 us; the launch traced here: 101 us
  starting transfers between devices  46.1 us (45%)
  waiting for transfers between devices  22.2 us (22%)
  blocking collectives  16.5 us (16%)
  Pallas kernels  12.7 us (12%)
  local copies, waits for them, and re-layouts  3.63 us (4%)
    all_to_all x1, blocking collectives, body(): sums = lax.all_to_all(partial, 'mp', 0, 0, tiled=True)  16.5 us
    all_to_all x1, starting transfers between devices, body(): whole = lax.all_to_all(spread, 'mp', 0, 0, tiled=True)  11.8 us
    all_to_all x1, starting transfers between devices, body(): lax.all_to_all(send.reshape(2 * requests, cap, kinds * inner), ('dp', 'mp...  10.3 us
    all_to_all x1, waiting for transfers between devices, body(): lax.all_to_all(send.reshape(2 * requests, cap, kinds * inner), ('dp', 'mp...  10.1 us
    all_to_all x1, waiting for transfers between devices, body(): lax.all_to_all(attn.reshape(4 * requests, cap // 2, inner), ('dp', 'mp'),...  6.96 us
    all_to_all x1, starting transfers between devices, body(): lax.all_to_all(attn.reshape(4 * requests, cap // 2, inner), ('dp', 'mp'),...  6.96 us
    ppermute x3, starting transfers between devices, body(): w_sib = [lax.ppermute(block, 'mp', sibling) for block in w_own]  6.34 us
    all_to_all x1, waiting for transfers between devices, body(): whole = lax.all_to_all(spread, 'mp', 0, 0, tiled=True)  5.04 us
  transfers between devices with their start and end apart: 10, of which 3 were waited for; matrix products, arithmetic and copies ran while one was open for 3% of the time, Pallas kernels for 5%

profile of v16, /device:TPU:1, one launch (start us, length us, event | category | flops | bytes accessed | tf_op | source)
XLA Modules:
  0.0 101.3 jit_solution(18446237861812573350)
XLA Ops:
  0.0 2.1 %shard_map.82 = (bf16[16,152,128]{2,1,0:T(8,128)(2,1)}, bf16[152,256]{1,0:T(8,128)(2,1)}, f32[1,256]{1,0:T(1,128)}) custom-call(bf16[152,256]{1,0:T(8,128)(2,1)} %bitcast.29, s32[1,256]{1,0:T(1,128)} %bitcast.25), custom_call_target="tpu_custom_call" | custom-call | bytes 1048576 | tf_op jit(solution)/shard_map/pallas_call | solution.py:284
  2.1 11.8 %all-to-all-start = ((bf16[16,152,128]{2,1,0:T(8,128)(2,1)}), bf16[16,152,128]{2,1,0:T(8,128)(2,1)S(1)}, u32[]{:S(2)}, u32[]{:S(2)}) async-start(bf16[16,152,128]{2,1,0:T(8,128)(2,1)} %get-tuple-element.31), calls=%async_computation | async-start | bytes 1245184 | tf_op jit(solution)/shard_map/all_to_all | solution.py:292
  14.0 0.0 slice-start
  14.0 0.0 copy-start.3
  14.0 0.0 copy-start.6
  14.0 0.0 copy-start.5
  14.0 1.6 %slice_bitcast_fusion = (bf16[2432,128]{1,0:T(8,128)(2,1)S(1)}, bf16[2432,128]{1,0:T(8,128)(2,1)S(1)}, bf16[2432,128]{1,0:T(8,128)(2,1)S(1)}) fusion(bf16[2432,3,128]{2,0,1:T(8,128)(2,1)} %param.12), kind=kLoop, calls=%fused_computation | loop fusion | bytes 3735552 | tf_op jit(solution)/shard_map/squeeze | solution.py:294
  15.7 2.0 %collective-permute-start = (bf16[2432,128]{1,0:T(8,128)(2,1)S(1)}, bf16[2432,128]{1,0:T(8,128)(2,1)}, u32[]{:S(2)}, u32[]{:S(2)}) collective-permute-start(bf16[2432,128]{1,0:T(8,128)(2,1)S(1)} %get-tuple-element.40.own0_ref), channel_id=1, source_target_pairs={{0,1},{1,0},{2,3},{3,2},{4,5},{5,4},{6,7},{7,6},{8,9},{9,8},{10,11... | collective-permute-start | bytes 1867784 | tf_op jit(solution)/shard_map/ppermute | solution.py:295
  17.7 2.3 %collective-permute-start.1 = (bf16[2432,128]{1,0:T(8,128)(2,1)S(1)}, bf16[2432,128]{1,0:T(8,128)(2,1)}, u32[]{:S(2)}, u32[]{:S(2)}) collective-permute-start(bf16[2432,128]{1,0:T(8,128)(2,1)S(1)} %get-tuple-element.41.own1_ref), channel_id=1, source_target_pairs={{0,1},{1,0},{2,3},{3,2},{4,5},{5,4},{6,7},{7,6},{8,9},{9,8},{10,11... | collective-permute-start | bytes 1867784 | tf_op jit(solution)/shard_map/ppermute | solution.py:295
  20.0 2.0 %collective-permute-start.2 = (bf16[2432,128]{1,0:T(8,128)(2,1)S(1)}, bf16[2432,128]{1,0:T(8,128)(2,1)}, u32[]{:S(2)}, u32[]{:S(2)}) collective-permute-start(bf16[2432,128]{1,0:T(8,128)(2,1)S(1)} %get-tuple-element.42.own2_ref), channel_id=1, source_target_pairs={{0,1},{1,0},{2,3},{3,2},{4,5},{5,4},{6,7},{7,6},{8,9},{9,8},{10,11... | collective-permute-start | bytes 1867784 | tf_op jit(solution)/shard_map/ppermute | solution.py:295
  22.0 2.3 %collective-permute-start.3 = (bf16[128,2432]{1,0:T(8,128)(2,1)S(1)}, bf16[128,2432]{1,0:T(8,128)(2,1)}, u32[]{:S(2)}, u32[]{:S(2)}) collective-permute-start(bf16[128,2432]{1,0:T(8,128)(2,1)S(1)} %copy-done), channel_id=1, source_target_pairs={{0,1},{1,0},{2,3},{3,2},{4,5},{5,4},{6,7},{7,6},{8,9},{9,8},{10,11... | collective-permute-start | bytes 1867784 | tf_op jit(solution)/shard_map/ppermute | solution.py:296
  24.4 0.8 slice.22
  25.2 0.1 dynamic-slice_bitcast_fusion.gate_ref
  25.3 0.0 copy-start.1
  25.3 1.0 copy-done.1
  26.3 1.9 %shard_map.83 = (bf16[2,2432,128]{2,1,0:T(8,128)(2,1)}, bf16[152,256]{1,0:T(8,128)(2,1)S(1)}, f32[1,128]{1,0:T(1,128)S(1)}) custom-call(s32[1]{0:T(128)} %bitcast.core_ref, s32[1,256]{1,0:T(1,128)S(1)} %bitcast.26, f32[1,256]{1,0:T(1,128)S(1)} %copy-done.4, s32[1,32]{1,0:T(1,128)S(1)} %bitcast.27, bf16[3,28,2432]{2,1,0:T(8,128)(2,1)S(1)} %bitcast.22, ...), custom_call_target="tpu_custom_call" | custom-call | bytes 1048576 | tf_op jit(solution)/shard_map/pallas_call | solution.py:299
  28.2 0.0 collective-permute-done.sib0_hbm
  28.3 5.0 %all-to-all-done.tok_ref = bf16[16,152,128]{2,1,0:T(8,128)(2,1)S(1)} async-done(((bf16[16,152,128]{2,1,0:T(8,128)(2,1)}), bf16[16,152,128]{2,1,0:T(8,128)(2,1)S(1)}, u32[]{:S(2)}, u32[]{:S(2)}) %all-to-all-start) | async-done | bytes 622624 | tf_op jit(solution)/shard_map/all_to_all | solution.py:292
  33.3 3.6 %shard_map.84 = bf16[2,256,384]{2,1,0:T(8,128)(2,1)} custom-call(s32[1]{0:T(128)} %bitcast.core_ref, bf16[16,152,128]{2,1,0:T(8,128)(2,1)S(1)} %all-to-all-done.tok_ref, bf16[2,2432,128]{2,1,0:T(8,128)(2,1)} %get-tuple-element.39.mod_hbm, bf16[2432,128]{1,0:T(8,128)(2,1)S(1)} %get-tuple-element.40.own0_ref, ...), custom_call_target="tpu_custom_call" | custom-call | flops 478150656 | bytes 1048576 | tf_op jit(solution)/shard_map/pallas_call | solution.py:310
  37.0 10.3 %all-to-all-start.1 = ((bf16[64,8,384]{2,1,0:T(8,128)(2,1)}), bf16[64,8,384]{2,1,0:T(8,128)(2,1)S(1)}, u32[]{:S(2)}, u32[]{:S(2)}) async-start(bf16[64,8,384]{2,1,0:T(8,128)(2,1)} %bitcast.10), calls=%async_computation.1 | async-start | bytes 786432 | tf_op jit(solution)/shard_map/all_to_all | solution.py:325
  47.3 1.9 %collective-permute-start.4 = (bf16[128,2432]{1,0:T(8,128)(2,1)S(1)}, bf16[128,2432]{1,0:T(8,128)(2,1)S(1)}, u32[]{:S(2)}, u32[]{:S(2)}) collective-permute-start(bf16[128,2432]{1,0:T(8,128)(2,1)S(1)} %copy-done), channel_id=1, source_target_pairs={{0,2},{1,3},{2,0},{3,1},{4,6},{5,7},{6,4},{7,5},{8,10},{9,11},{10,... | collective-permute-start | bytes 1867784 | tf_op jit(solution)/shard_map/ppermute | solution.py:329
  49.2 3.9 %collective-permute-start.6 = (bf16[80,2432]{1,0:T(8,128)(2,1)}, bf16[80,2432]{1,0:T(8,128)(2,1)S(1)}, u32[]{:S(2)}, u32[]{:S(2)}) collective-permute-start(bf16[80,2432]{1,0:T(8,128)(2,1)} %slice.22), channel_id=1, source_target_pairs={{0,3},{1,2},{2,1},{3,0},{4,7},{5,6},{6,5},{7,4},{8,11},{9,10},{10,... | collective-permute-start | bytes 1167368 | tf_op jit(solution)/shard_map/ppermute | solution.py:330
  53.2 10.1 %all-to-all-done.1 = bf16[64,8,384]{2,1,0:T(8,128)(2,1)S(1)} async-done(((bf16[64,8,384]{2,1,0:T(8,128)(2,1)}), bf16[64,8,384]{2,1,0:T(8,128)(2,1)S(1)}, u32[]{:S(2)}, u32[]{:S(2)}) %all-to-all-start.1) | async-done | bytes 393248 | tf_op jit(solution)/shard_map/all_to_all | solution.py:325
  63.3 2.2 %shard_map.85 = bf16[512,128]{1,0:T(8,128)(2,1)} custom-call(bf16[512,384]{1,0:T(8,128)(2,1)S(1)} %bitcast.24, bf16[2,384,128]{2,1,0:T(8,128)(2,1)S(1)} %pad.4.ctx_ref), custom_call_target="tpu_custom_call" | custom-call | flops 469762048 | bytes 1048576 | tf_op jit(solution)/shard_map/pallas_call | solution.py:332
  65.6 7.0 %all-to-all-start.2 = ((bf16[128,4,128]{2,1,0:T(4,128)(2,1)}), bf16[128,4,128]{2,1,0:T(4,128)(2,1)S(1)}, u32[]{:S(2)}, u32[]{:S(2)}) async-start(bf16[128,4,128]{2,1,0:T(4,128)(2,1)} %bitcast.13), calls=%async_computation.2 | async-start | bytes 262144 | tf_op jit(solution)/shard_map/all_to_all | solution.py:339
  72.6 2.5 %collective-permute-start.5 = (bf16[48,2432]{1,0:T(8,128)(2,1)S(1)}, bf16[48,2432]{1,0:T(8,128)(2,1)S(1)}, u32[]{:S(2)}, u32[]{:S(2)}) collective-permute-start(bf16[48,2432]{1,0:T(8,128)(2,1)S(1)} %slice.24), channel_id=1, source_target_pairs={{0,1},{1,0},{2,3},{3,2},{4,5},{5,4},{6,7},{7,6},{8,9},{9,8},{10,11... | collective-permute-start | bytes 700424 | tf_op jit(solution)/shard_map/ppermute | solution.py:331
  75.1 1.1 %shard_map.86.refs_1_ = bf16[128,2432]{1,0:T(8,128)(2,1)S(1)} custom-call(bf16[128,2432]{1,0:T(8,128)(2,1)} %collective-permute-done.3.hbm), custom_call_target="tpu_custom_call" | custom-call | bytes 1048576 | tf_op jit(solution)/shard_map/pallas_call | solution.py:343
  76.2 0.0 copy-start.2
  76.2 7.0 %all-to-all-done.2 = bf16[128,4,128]{2,1,0:T(4,128)(2,1)S(1)} async-done(((bf16[128,4,128]{2,1,0:T(4,128)(2,1)}), bf16[128,4,128]{2,1,0:T(4,128)(2,1)S(1)}, u32[]{:S(2)}, u32[]{:S(2)}) %all-to-all-start.2) | async-done | bytes 131104 | tf_op jit(solution)/shard_map/all_to_all | solution.py:339
  83.2 0.8 shard_map.87
  84.0 16.5 %all_to_all.20.sums_ref = bf16[16,80,128]{2,1,0:T(8,128)(2,1)S(1)} all-to-all(bf16[16,80,128]{2,1,0:T(8,128)(2,1)S(1)} %shard_map.87), channel_id=1, replica_groups=mesh['dp'=32,'mp'=16] {'mp'}, dimensions={0} | all-to-all | bytes 655360 | tf_op jit(solution)/shard_map/all_to_all | solution.py:352
  100.5 0.9 shard_map.88
  (20 shorter events, 0.1 us)
Async XLA Ops:
  2.1 31.2 %all-to-all-start = ((bf16[16,152,128]{2,1,0:T(8,128)(2,1)}), bf16[16,152,128]{2,1,0:T(8,128)(2,1)S(1)}, u32[]{:S(2)}, u32[]{:S(2)}) async-start(bf16[16,152,128]{2,1,0:T(8,128)(2,1)} %get-tuple-element.31), calls=%async_computation | async-start | bytes 1245184 | tf_op jit(solution)/shard_map/all_to_all | solution.py:292
  14.0 8.1 %copy-start = (bf16[128,2432]{1,0:T(8,128)(2,1)S(1)}, bf16[128,2432]{1,0:T(8,128)(2,1)}, u32[]{:S(2)}) copy-start(bf16[128,2432]{1,0:T(8,128)(2,1)} %refs_0_) | copy-start | bytes 1867780
  14.0 11.2 %slice-start = ((bf16[28,3,2432]{2,0,1:T(8,128)(2,1)}), bf16[28,1,2432]{2,0,1:T(8,128)(2,1)S(1)}, s32[]{:S(2)}) async-start(bf16[28,3,2432]{2,0,1:T(8,128)(2,1)} %param.11), calls=%async_computation.4 | async-start | bytes 311296 | tf_op jit(solution)/shard_map/slice | solution.py:298
  14.0 11.3 %copy-start.3 = (s32[256,1]{0,1:T(1,128)S(1)}, s32[256,1]{0,1:T(1,128)}, u32[]{:S(2)}) copy-start(s32[256,1]{0,1:T(1,128)} %param.9) | copy-start | bytes 3076
  14.0 11.3 %copy-start.4 = (f32[1,256]{1,0:T(1,128)S(1)}, f32[1,256]{1,0:T(1,128)}, u32[]{:S(2)}) copy-start(f32[1,256]{1,0:T(1,128)} %get-tuple-element.34.pos_ref) | copy-start | bytes 3076
  14.0 11.2 %copy-start.6 = (s32[32]{0:T(128)S(1)}, s32[32]{0:T(128)}, u32[]{:S(2)}) copy-start(s32[32]{0:T(128)} %param.10) | copy-start | bytes 388
  14.0 19.3 %copy-start.5 = (f32[2,64]{1,0:T(2,128)S(1)}, f32[2,64]{1,0:T(2,128)}, u32[]{:S(2)}) copy-start(f32[2,64]{1,0:T(2,128)} %gain_ref.1) | copy-start | bytes 1540
  15.7 12.6 %collective-permute-start = (bf16[2432,128]{1,0:T(8,128)(2,1)S(1)}, bf16[2432,128]{1,0:T(8,128)(2,1)}, u32[]{:S(2)}, u32[]{:S(2)}) collective-permute-start(bf16[2432,128]{1,0:T(8,128)(2,1)S(1)} %get-tuple-element.40.own0_ref), channel_id=1, source_target_pairs={{0,1},{1,0},{2,3},{3,2},{4,5},{5,4},{6,7},{7,6},{8,9},{9,8},{10,11... | collective-permute-start | bytes 1867784 | tf_op jit(solution)/shard_map/ppermute | solution.py:295
  17.7 10.6 %collective-permute-start.1 = (bf16[2432,128]{1,0:T(8,128)(2,1)S(1)}, bf16[2432,128]{1,0:T(8,128)(2,1)}, u32[]{:S(2)}, u32[]{:S(2)}) collective-permute-start(bf16[2432,128]{1,0:T(8,128)(2,1)S(1)} %get-tuple-element.41.own1_ref), channel_id=1, source_target_pairs={{0,1},{1,0},{2,3},{3,2},{4,5},{5,4},{6,7},{7,6},{8,9},{9,8},{10,11... | collective-permute-start | bytes 1867784 | tf_op jit(solution)/shard_map/ppermute | solution.py:295
  20.0 8.3 %collective-permute-start.2 = (bf16[2432,128]{1,0:T(8,128)(2,1)S(1)}, bf16[2432,128]{1,0:T(8,128)(2,1)}, u32[]{:S(2)}, u32[]{:S(2)}) collective-permute-start(bf16[2432,128]{1,0:T(8,128)(2,1)S(1)} %get-tuple-element.42.own2_ref), channel_id=1, source_target_pairs={{0,1},{1,0},{2,3},{3,2},{4,5},{5,4},{6,7},{7,6},{8,9},{9,8},{10,11... | collective-permute-start | bytes 1867784 | tf_op jit(solution)/shard_map/ppermute | solution.py:295
  22.0 6.2 %collective-permute-start.3 = (bf16[128,2432]{1,0:T(8,128)(2,1)S(1)}, bf16[128,2432]{1,0:T(8,128)(2,1)}, u32[]{:S(2)}, u32[]{:S(2)}) collective-permute-start(bf16[128,2432]{1,0:T(8,128)(2,1)S(1)} %copy-done), channel_id=1, source_target_pairs={{0,1},{1,0},{2,3},{3,2},{4,5},{5,4},{6,7},{7,6},{8,9},{9,8},{10,11... | collective-permute-start | bytes 1867784 | tf_op jit(solution)/shard_map/ppermute | solution.py:296
  25.3 1.0 %copy-start.1 = (bf16[28,3,2432]{2,0,1:T(8,128)(2,1)S(1)}, bf16[28,3,2432]{2,0,1:T(8,128)(2,1)}, u32[]{:S(2)}) copy-start(bf16[28,3,2432]{2,0,1:T(8,128)(2,1)} %param.11) | copy-start | bytes 1225732
  33.3 19.8 %copy-start.7 = (bf16[1,2,333,128]{3,1,2,0:T(2,128)(2,1)S(1)}, bf16[1,2,333,128]{3,1,2,0:T(2,128)(2,1)}, u32[]{:S(2)}) copy-start(bf16[1,2,333,128]{3,1,2,0:T(2,128)(2,1)} %param.14) | copy-start | bytes 511492
  37.0 26.4 %all-to-all-start.1 = ((bf16[64,8,384]{2,1,0:T(8,128)(2,1)}), bf16[64,8,384]{2,1,0:T(8,128)(2,1)S(1)}, u32[]{:S(2)}, u32[]{:S(2)}) async-start(bf16[64,8,384]{2,1,0:T(8,128)(2,1)} %bitcast.10), calls=%async_computation.1 | async-start | bytes 786432 | tf_op jit(solution)/shard_map/all_to_all | solution.py:325
  47.3 25.2 %collective-permute-start.4 = (bf16[128,2432]{1,0:T(8,128)(2,1)S(1)}, bf16[128,2432]{1,0:T(8,128)(2,1)S(1)}, u32[]{:S(2)}, u32[]{:S(2)}) collective-permute-start(bf16[128,2432]{1,0:T(8,128)(2,1)S(1)} %copy-done), channel_id=1, source_target_pairs={{0,2},{1,3},{2,0},{3,1},{4,6},{5,7},{6,4},{7,5},{8,10},{9,11},{10,... | collective-permute-start | bytes 1867784 | tf_op jit(solution)/shard_map/ppermute | solution.py:329
  49.2 26.9 %collective-permute-start.6 = (bf16[80,2432]{1,0:T(8,128)(2,1)}, bf16[80,2432]{1,0:T(8,128)(2,1)S(1)}, u32[]{:S(2)}, u32[]{:S(2)}) collective-permute-start(bf16[80,2432]{1,0:T(8,128)(2,1)} %slice.22), channel_id=1, source_target_pairs={{0,3},{1,2},{2,1},{3,0},{4,7},{5,6},{6,5},{7,4},{8,11},{9,10},{10,... | collective-permute-start | bytes 1167368 | tf_op jit(solution)/shard_map/ppermute | solution.py:330
  65.6 17.6 %all-to-all-start.2 = ((bf16[128,4,128]{2,1,0:T(4,128)(2,1)}), bf16[128,4,128]{2,1,0:T(4,128)(2,1)S(1)}, u32[]{:S(2)}, u32[]{:S(2)}) async-start(bf16[128,4,128]{2,1,0:T(4,128)(2,1)} %bitcast.13), calls=%async_computation.2 | async-start | bytes 262144 | tf_op jit(solution)/shard_map/all_to_all | solution.py:339
  72.6 3.6 %collective-permute-start.5 = (bf16[48,2432]{1,0:T(8,128)(2,1)S(1)}, bf16[48,2432]{1,0:T(8,128)(2,1)S(1)}, u32[]{:S(2)}, u32[]{:S(2)}) collective-permute-start(bf16[48,2432]{1,0:T(8,128)(2,1)S(1)} %slice.24), channel_id=1, source_target_pairs={{0,1},{1,0},{2,3},{3,2},{4,5},{5,4},{6,7},{7,6},{8,9},{9,8},{10,11... | collective-permute-start | bytes 700424 | tf_op jit(solution)/shard_map/ppermute | solution.py:331
  76.2 24.3 %copy-start.2 = (bf16[152,256]{1,0:T(8,128)(2,1)S(1)}, bf16[152,256]{1,0:T(8,128)(2,1)}, u32[]{:S(2)}) copy-start(bf16[152,256]{1,0:T(8,128)(2,1)} %get-tuple-element.53.perm_ref) | copy-start | bytes 233476

commit v17 on v15

--- a/solution.py
+++ b/solution.py
@@ -11,6 +11,7 @@
 EPS = 1e-06
 DEAD = 1e30
 MASKED = -1e30
+LOG2_E = 1.4426950408889634
 VMEM_LIMIT = 24 * 1024 * 1024
 VMEM_MOST = 60 * 1024 * 1024
 F32, BF16, I32 = jnp.float32, jnp.bfloat16, jnp.int32
@@ -137,7 +138,7 @@
     hidden = hid_ref[...].astype(F32).T.astype(BF16)
     normed = 2 * inner
     heads = one_hot(iota((normed, normed), 0) // HD == iota((normed, normed), 1) // HD)
-    gain = [gain_ref[0:1, :] * HD ** (-0.5)] * (inner // HD) + [gain_ref[1:2, :]] * (inner // HD)
+    gain = [gain_ref[0:1, :] * (HD ** (-0.5) * LOG2_E)] * (inner // HD) + [gain_ref[1:2, :]] * (inner // HD)
     gain = jnp.concatenate(gain, axis=1)
     own = jnp.concatenate([own0_ref[...], own1_ref[...], own2_ref[...]], axis=1)
     projected = [jnp.dot(hidden, own, preferred_element_type=F32)]
@@ -176,7 +177,7 @@
         query = queries[row : row + block]
         query = jnp.concatenate([jnp.where(first, query, zero), jnp.where(first, zero, query)], axis=0)
         scores = dot_nt(query, keys) + bias
-        weights = jnp.exp(scores - jnp.max(scores, axis=1, keepdims=True)).astype(BF16)
+        weights = jnp.exp2(scores - jnp.max(scores, axis=1, keepdims=True)).astype(BF16)
         upper = jnp.dot(weights[:block], jnp.where(first, values, one), preferred_element_type=F32)
         lower = jnp.dot(weights[block:], jnp.where(first, one, values), preferred_element_type=F32)
         sums = pltpu.roll(jnp.where(first, lower, upper), HD, 1)

time: 102 us -> 102 us (level)
  no operation moved by 1% of the time
where the time goes in v17:
time: 102 us; the launch traced here: 101 us
  starting transfers between devices  46.1 us (45%)
  waiting for transfers between devices  22.2 us (22%)
  blocking collectives  16.5 us (16%)
  Pallas kernels  12.8 us (13%)
  local copies, waits for them, and re-layouts  3.63 us (4%)
    all_to_all x1, blocking collectives, body(): sums = lax.all_to_all(partial, 'mp', 0, 0, tiled=True)  16.5 us
    all_to_all x1, starting transfers between devices, body(): whole = lax.all_to_all(spread, 'mp', 0, 0, tiled=True)  11.8 us
    all_to_all x1, starting transfers between devices, body(): lax.all_to_all(send.reshape(2 * requests, cap, kinds * inner), ('dp', 'mp...  10.3 us
    all_to_all x1, waiting for transfers between devices, body(): lax.all_to_all(send.reshape(2 * requests, cap, kinds * inner), ('dp', 'mp...  10.1 us
    all_to_all x1, waiting for transfers between devices, body(): lax.all_to_all(attn.reshape(4 * requests, cap // 2, inner), ('dp', 'mp'),...  6.96 us
    all_to_all x1, starting transfers between devices, body(): lax.all_to_all(attn.reshape(4 * requests, cap // 2, inner), ('dp', 'mp'),...  6.96 us
    ppermute x3, starting transfers between devices, body(): w_sib = [lax.ppermute(block, 'mp', sibling) for block in w_own]  6.34 us
    all_to_all x1, waiting for transfers between devices, body(): whole = lax.all_to_all(spread, 'mp', 0, 0, tiled=True)  5.04 us
  transfers between devices with their start and end apart: 10, of which 3 were waited for; matrix products, arithmetic and copies ran while one was open for 3% of the time, Pallas kernels for 5%

profile of v17, /device:TPU:1, one launch (start us, length us, event | category | flops | bytes accessed | tf_op | source)
XLA Modules:
  0.0 101.4 jit_solution(18222310677172592251)
XLA Ops:
  0.0 2.1 %shard_map.82 = (bf16[16,152,128]{2,1,0:T(8,128)(2,1)}, bf16[152,256]{1,0:T(8,128)(2,1)}, f32[1,256]{1,0:T(1,128)}) custom-call(bf16[152,256]{1,0:T(8,128)(2,1)} %bitcast.29, s32[1,256]{1,0:T(1,128)} %bitcast.25), custom_call_target="tpu_custom_call" | custom-call | bytes 1048576 | tf_op jit(solution)/shard_map/pallas_call | solution.py:279
  2.1 11.8 %all-to-all-start = ((bf16[16,152,128]{2,1,0:T(8,128)(2,1)}), bf16[16,152,128]{2,1,0:T(8,128)(2,1)S(1)}, u32[]{:S(2)}, u32[]{:S(2)}) async-start(bf16[16,152,128]{2,1,0:T(8,128)(2,1)} %get-tuple-element.31), calls=%async_computation | async-start | bytes 1245184 | tf_op jit(solution)/shard_map/all_to_all | solution.py:287
  14.0 0.0 slice-start
  14.0 0.0 copy-start.3
  14.0 0.0 copy-start.6
  14.0 0.0 copy-start.5
  14.0 1.6 %slice_bitcast_fusion = (bf16[2432,128]{1,0:T(8,128)(2,1)S(1)}, bf16[2432,128]{1,0:T(8,128)(2,1)S(1)}, bf16[2432,128]{1,0:T(8,128)(2,1)S(1)}) fusion(bf16[2432,3,128]{2,0,1:T(8,128)(2,1)} %param.12), kind=kLoop, calls=%fused_computation | loop fusion | bytes 3735552 | tf_op jit(solution)/shard_map/squeeze | solution.py:289
  15.7 2.0 %collective-permute-start = (bf16[2432,128]{1,0:T(8,128)(2,1)S(1)}, bf16[2432,128]{1,0:T(8,128)(2,1)}, u32[]{:S(2)}, u32[]{:S(2)}) collective-permute-start(bf16[2432,128]{1,0:T(8,128)(2,1)S(1)} %get-tuple-element.40.own0_ref), channel_id=1, source_target_pairs={{0,1},{1,0},{2,3},{3,2},{4,5},{5,4},{6,7},{7,6},{8,9},{9,8},{10,11... | collective-permute-start | bytes 1867784 | tf_op jit(solution)/shard_map/ppermute | solution.py:290
  17.7 2.3 %collective-permute-start.1 = (bf16[2432,128]{1,0:T(8,128)(2,1)S(1)}, bf16[2432,128]{1,0:T(8,128)(2,1)}, u32[]{:S(2)}, u32[]{:S(2)}) collective-permute-start(bf16[2432,128]{1,0:T(8,128)(2,1)S(1)} %get-tuple-element.41.own1_ref), channel_id=1, source_target_pairs={{0,1},{1,0},{2,3},{3,2},{4,5},{5,4},{6,7},{7,6},{8,9},{9,8},{10,11... | collective-permute-start | bytes 1867784 | tf_op jit(solution)/shard_map/ppermute | solution.py:290
  20.0 2.0 %collective-permute-start.2 = (bf16[2432,128]{1,0:T(8,128)(2,1)S(1)}, bf16[2432,128]{1,0:T(8,128)(2,1)}, u32[]{:S(2)}, u32[]{:S(2)}) collective-permute-start(bf16[2432,128]{1,0:T(8,128)(2,1)S(1)} %get-tuple-element.42.own2_ref), channel_id=1, source_target_pairs={{0,1},{1,0},{2,3},{3,2},{4,5},{5,4},{6,7},{7,6},{8,9},{9,8},{10,11... | collective-permute-start | bytes 1867784 | tf_op jit(solution)/shard_map/ppermute | solution.py:290
  22.0 2.3 %collective-permute-start.3 = (bf16[128,2432]{1,0:T(8,128)(2,1)S(1)}, bf16[128,2432]{1,0:T(8,128)(2,1)}, u32[]{:S(2)}, u32[]{:S(2)}) collective-permute-start(bf16[128,2432]{1,0:T(8,128)(2,1)S(1)} %copy-done), channel_id=1, source_target_pairs={{0,1},{1,0},{2,3},{3,2},{4,5},{5,4},{6,7},{7,6},{8,9},{9,8},{10,11... | collective-permute-start | bytes 1867784 | tf_op jit(solution)/shard_map/ppermute | solution.py:291
  24.4 0.8 slice.22
  25.2 0.1 dynamic-slice_bitcast_fusion.gate_ref
  25.3 0.0 copy-start.1
  25.3 1.0 copy-done.1
  26.3 1.9 %shard_map.83 = (bf16[2,2432,128]{2,1,0:T(8,128)(2,1)}, bf16[152,256]{1,0:T(8,128)(2,1)S(1)}, f32[1,128]{1,0:T(1,128)S(1)}) custom-call(s32[1]{0:T(128)} %bitcast.core_ref, s32[1,256]{1,0:T(1,128)S(1)} %bitcast.26, f32[1,256]{1,0:T(1,128)S(1)} %copy-done.4, s32[1,32]{1,0:T(1,128)S(1)} %bitcast.27, bf16[3,28,2432]{2,1,0:T(8,128)(2,1)S(1)} %bitcast.22, ...), custom_call_target="tpu_custom_call" | custom-call | bytes 1048576 | tf_op jit(solution)/shard_map/pallas_call | solution.py:294
  28.2 0.0 collective-permute-done.1.sib1_hbm
  28.3 5.0 %all-to-all-done.tok_ref = bf16[16,152,128]{2,1,0:T(8,128)(2,1)S(1)} async-done(((bf16[16,152,128]{2,1,0:T(8,128)(2,1)}), bf16[16,152,128]{2,1,0:T(8,128)(2,1)S(1)}, u32[]{:S(2)}, u32[]{:S(2)}) %all-to-all-start) | async-done | bytes 622624 | tf_op jit(solution)/shard_map/all_to_all | solution.py:287
  33.3 3.7 %shard_map.84 = bf16[2,256,384]{2,1,0:T(8,128)(2,1)} custom-call(s32[1]{0:T(128)} %bitcast.core_ref, bf16[16,152,128]{2,1,0:T(8,128)(2,1)S(1)} %all-to-all-done.tok_ref, bf16[2,2432,128]{2,1,0:T(8,128)(2,1)} %get-tuple-element.39.mod_hbm, bf16[2432,128]{1,0:T(8,128)(2,1)S(1)} %get-tuple-element.40.own0_ref, ...), custom_call_target="tpu_custom_call" | custom-call | flops 478150656 | bytes 1048576 | tf_op jit(solution)/shard_map/pallas_call | solution.py:305
  37.1 10.3 %all-to-all-start.1 = ((bf16[64,8,384]{2,1,0:T(8,128)(2,1)}), bf16[64,8,384]{2,1,0:T(8,128)(2,1)S(1)}, u32[]{:S(2)}, u32[]{:S(2)}) async-start(bf16[64,8,384]{2,1,0:T(8,128)(2,1)} %bitcast.10), calls=%async_computation.1 | async-start | bytes 786432 | tf_op jit(solution)/shard_map/all_to_all | solution.py:320
  47.4 1.9 %collective-permute-start.4 = (bf16[128,2432]{1,0:T(8,128)(2,1)S(1)}, bf16[128,2432]{1,0:T(8,128)(2,1)S(1)}, u32[]{:S(2)}, u32[]{:S(2)}) collective-permute-start(bf16[128,2432]{1,0:T(8,128)(2,1)S(1)} %copy-done), channel_id=1, source_target_pairs={{0,2},{1,3},{2,0},{3,1},{4,6},{5,7},{6,4},{7,5},{8,10},{9,11},{10,... | collective-permute-start | bytes 1867784 | tf_op jit(solution)/shard_map/ppermute | solution.py:324
  49.3 3.9 %collective-permute-start.6 = (bf16[80,2432]{1,0:T(8,128)(2,1)}, bf16[80,2432]{1,0:T(8,128)(2,1)S(1)}, u32[]{:S(2)}, u32[]{:S(2)}) collective-permute-start(bf16[80,2432]{1,0:T(8,128)(2,1)} %slice.22), channel_id=1, source_target_pairs={{0,3},{1,2},{2,1},{3,0},{4,7},{5,6},{6,5},{7,4},{8,11},{9,10},{10,... | collective-permute-start | bytes 1167368 | tf_op jit(solution)/shard_map/ppermute | solution.py:325
  53.3 10.1 %all-to-all-done.1 = bf16[64,8,384]{2,1,0:T(8,128)(2,1)S(1)} async-done(((bf16[64,8,384]{2,1,0:T(8,128)(2,1)}), bf16[64,8,384]{2,1,0:T(8,128)(2,1)S(1)}, u32[]{:S(2)}, u32[]{:S(2)}) %all-to-all-start.1) | async-done | bytes 393248 | tf_op jit(solution)/shard_map/all_to_all | solution.py:320
  63.4 2.2 %shard_map.85 = bf16[512,128]{1,0:T(8,128)(2,1)} custom-call(bf16[512,384]{1,0:T(8,128)(2,1)S(1)} %bitcast.24, bf16[2,384,128]{2,1,0:T(8,128)(2,1)S(1)} %pad.4.ctx_ref), custom_call_target="tpu_custom_call" | custom-call | flops 469762048 | bytes 1048576 | tf_op jit(solution)/shard_map/pallas_call | solution.py:327
  65.6 7.0 %all-to-all-start.2 = ((bf16[128,4,128]{2,1,0:T(4,128)(2,1)}), bf16[128,4,128]{2,1,0:T(4,128)(2,1)S(1)}, u32[]{:S(2)}, u32[]{:S(2)}) async-start(bf16[128,4,128]{2,1,0:T(4,128)(2,1)} %bitcast.13), calls=%async_computation.2 | async-start | bytes 262144 | tf_op jit(solution)/shard_map/all_to_all | solution.py:334
  72.6 2.5 %collective-permute-start.5 = (bf16[48,2432]{1,0:T(8,128)(2,1)S(1)}, bf16[48,2432]{1,0:T(8,128)(2,1)S(1)}, u32[]{:S(2)}, u32[]{:S(2)}) collective-permute-start(bf16[48,2432]{1,0:T(8,128)(2,1)S(1)} %slice.24), channel_id=1, source_target_pairs={{0,1},{1,0},{2,3},{3,2},{4,5},{5,4},{6,7},{7,6},{8,9},{9,8},{10,11... | collective-permute-start | bytes 700424 | tf_op jit(solution)/shard_map/ppermute | solution.py:326
  75.1 1.1 %shard_map.86.refs_1_ = bf16[128,2432]{1,0:T(8,128)(2,1)S(1)} custom-call(bf16[128,2432]{1,0:T(8,128)(2,1)} %collective-permute-done.3.hbm), custom_call_target="tpu_custom_call" | custom-call | bytes 1048576 | tf_op jit(solution)/shard_map/pallas_call | solution.py:338
  76.2 0.0 copy-start.2
  76.3 7.0 %all-to-all-done.2 = bf16[128,4,128]{2,1,0:T(4,128)(2,1)S(1)} async-done(((bf16[128,4,128]{2,1,0:T(4,128)(2,1)}), bf16[128,4,128]{2,1,0:T(4,128)(2,1)S(1)}, u32[]{:S(2)}, u32[]{:S(2)}) %all-to-all-start.2) | async-done | bytes 131104 | tf_op jit(solution)/shard_map/all_to_all | solution.py:334
  83.2 0.8 shard_map.87
  84.1 16.5 %all_to_all.20.sums_ref = bf16[16,80,128]{2,1,0:T(8,128)(2,1)S(1)} all-to-all(bf16[16,80,128]{2,1,0:T(8,128)(2,1)S(1)} %shard_map.87), channel_id=1, replica_groups=mesh['dp'=32,'mp'=16] {'mp'}, dimensions={0} | all-to-all | bytes 655360 | tf_op jit(solution)/shard_map/all_to_all | solution.py:347
  100.5 0.9 shard_map.88
  (20 shorter events, 0.1 us)
Async XLA Ops:
  2.1 31.2 %all-to-all-start = ((bf16[16,152,128]{2,1,0:T(8,128)(2,1)}), bf16[16,152,128]{2,1,0:T(8,128)(2,1)S(1)}, u32[]{:S(2)}, u32[]{:S(2)}) async-start(bf16[16,152,128]{2,1,0:T(8,128)(2,1)} %get-tuple-element.31), calls=%async_computation | async-start | bytes 1245184 | tf_op jit(solution)/shard_map/all_to_all | solution.py:287
  14.0 8.1 %copy-start = (bf16[128,2432]{1,0:T(8,128)(2,1)S(1)}, bf16[128,2432]{1,0:T(8,128)(2,1)}, u32[]{:S(2)}) copy-start(bf16[128,2432]{1,0:T(8,128)(2,1)} %refs_0_) | copy-start | bytes 1867780
  14.0 11.2 %slice-start = ((bf16[28,3,2432]{2,0,1:T(8,128)(2,1)}), bf16[28,1,2432]{2,0,1:T(8,128)(2,1)S(1)}, s32[]{:S(2)}) async-start(bf16[28,3,2432]{2,0,1:T(8,128)(2,1)} %param.11), calls=%async_computation.4 | async-start | bytes 311296 | tf_op jit(solution)/shard_map/slice | solution.py:293
  14.0 11.3 %copy-start.3 = (s32[256,1]{0,1:T(1,128)S(1)}, s32[256,1]{0,1:T(1,128)}, u32[]{:S(2)}) copy-start(s32[256,1]{0,1:T(1,128)} %param.9) | copy-start | bytes 3076
  14.0 11.3 %copy-start.4 = (f32[1,256]{1,0:T(1,128)S(1)}, f32[1,256]{1,0:T(1,128)}, u32[]{:S(2)}) copy-start(f32[1,256]{1,0:T(1,128)} %get-tuple-element.34.pos_ref) | copy-start | bytes 3076
  14.0 11.2 %copy-start.6 = (s32[32]{0:T(128)S(1)}, s32[32]{0:T(128)}, u32[]{:S(2)}) copy-start(s32[32]{0:T(128)} %param.10) | copy-start | bytes 388
  14.0 19.3 %copy-start.5 = (f32[2,64]{1,0:T(2,128)S(1)}, f32[2,64]{1,0:T(2,128)}, u32[]{:S(2)}) copy-start(f32[2,64]{1,0:T(2,128)} %gain_ref.1) | copy-start | bytes 1540
  15.7 12.6 %collective-permute-start = (bf16[2432,128]{1,0:T(8,128)(2,1)S(1)}, bf16[2432,128]{1,0:T(8,128)(2,1)}, u32[]{:S(2)}, u32[]{:S(2)}) collective-permute-start(bf16[2432,128]{1,0:T(8,128)(2,1)S(1)} %get-tuple-element.40.own0_ref), channel_id=1, source_target_pairs={{0,1},{1,0},{2,3},{3,2},{4,5},{5,4},{6,7},{7,6},{8,9},{9,8},{10,11... | collective-permute-start | bytes 1867784 | tf_op jit(solution)/shard_map/ppermute | solution.py:290
  17.7 10.6 %collective-permute-start.1 = (bf16[2432,128]{1,0:T(8,128)(2,1)S(1)}, bf16[2432,128]{1,0:T(8,128)(2,1)}, u32[]{:S(2)}, u32[]{:S(2)}) collective-permute-start(bf16[2432,128]{1,0:T(8,128)(2,1)S(1)} %get-tuple-element.41.own1_ref), channel_id=1, source_target_pairs={{0,1},{1,0},{2,3},{3,2},{4,5},{5,4},{6,7},{7,6},{8,9},{9,8},{10,11... | collective-permute-start | bytes 1867784 | tf_op jit(solution)/shard_map/ppermute | solution.py:290
  20.0 8.3 %collective-permute-start.2 = (bf16[2432,128]{1,0:T(8,128)(2,1)S(1)}, bf16[2432,128]{1,0:T(8,128)(2,1)}, u32[]{:S(2)}, u32[]{:S(2)}) collective-permute-start(bf16[2432,128]{1,0:T(8,128)(2,1)S(1)} %get-tuple-element.42.own2_ref), channel_id=1, source_target_pairs={{0,1},{1,0},{2,3},{3,2},{4,5},{5,4},{6,7},{7,6},{8,9},{9,8},{10,11... | collective-permute-start | bytes 1867784 | tf_op jit(solution)/shard_map/ppermute | solution.py:290
  22.0 6.2 %collective-permute-start.3 = (bf16[128,2432]{1,0:T(8,128)(2,1)S(1)}, bf16[128,2432]{1,0:T(8,128)(2,1)}, u32[]{:S(2)}, u32[]{:S(2)}) collective-permute-start(bf16[128,2432]{1,0:T(8,128)(2,1)S(1)} %copy-done), channel_id=1, source_target_pairs={{0,1},{1,0},{2,3},{3,2},{4,5},{5,4},{6,7},{7,6},{8,9},{9,8},{10,11... | collective-permute-start | bytes 1867784 | tf_op jit(solution)/shard_map/ppermute | solution.py:291
  25.3 1.0 %copy-start.1 = (bf16[28,3,2432]{2,0,1:T(8,128)(2,1)S(1)}, bf16[28,3,2432]{2,0,1:T(8,128)(2,1)}, u32[]{:S(2)}) copy-start(bf16[28,3,2432]{2,0,1:T(8,128)(2,1)} %param.11) | copy-start | bytes 1225732
  33.3 19.9 %copy-start.7 = (bf16[1,2,333,128]{3,1,2,0:T(2,128)(2,1)S(1)}, bf16[1,2,333,128]{3,1,2,0:T(2,128)(2,1)}, u32[]{:S(2)}) copy-start(bf16[1,2,333,128]{3,1,2,0:T(2,128)(2,1)} %param.14) | copy-start | bytes 511492
  37.1 26.4 %all-to-all-start.1 = ((bf16[64,8,384]{2,1,0:T(8,128)(2,1)}), bf16[64,8,384]{2,1,0:T(8,128)(2,1)S(1)}, u32[]{:S(2)}, u32[]{:S(2)}) async-start(bf16[64,8,384]{2,1,0:T(8,128)(2,1)} %bitcast.10), calls=%async_computation.1 | async-start | bytes 786432 | tf_op jit(solution)/shard_map/all_to_all | solution.py:320
  47.4 25.2 %collective-permute-start.4 = (bf16[128,2432]{1,0:T(8,128)(2,1)S(1)}, bf16[128,2432]{1,0:T(8,128)(2,1)S(1)}, u32[]{:S(2)}, u32[]{:S(2)}) collective-permute-start(bf16[128,2432]{1,0:T(8,128)(2,1)S(1)} %copy-done), channel_id=1, source_target_pairs={{0,2},{1,3},{2,0},{3,1},{4,6},{5,7},{6,4},{7,5},{8,10},{9,11},{10,... | collective-permute-start | bytes 1867784 | tf_op jit(solution)/shard_map/ppermute | solution.py:324
  49.3 26.9 %collective-permute-start.6 = (bf16[80,2432]{1,0:T(8,128)(2,1)}, bf16[80,2432]{1,0:T(8,128)(2,1)S(1)}, u32[]{:S(2)}, u32[]{:S(2)}) collective-permute-start(bf16[80,2432]{1,0:T(8,128)(2,1)} %slice.22), channel_id=1, source_target_pairs={{0,3},{1,2},{2,1},{3,0},{4,7},{5,6},{6,5},{7,4},{8,11},{9,10},{10,... | collective-permute-start | bytes 1167368 | tf_op jit(solution)/shard_map/ppermute | solution.py:325
  65.6 17.6 %all-to-all-start.2 = ((bf16[128,4,128]{2,1,0:T(4,128)(2,1)}), bf16[128,4,128]{2,1,0:T(4,128)(2,1)S(1)}, u32[]{:S(2)}, u32[]{:S(2)}) async-start(bf16[128,4,128]{2,1,0:T(4,128)(2,1)} %bitcast.13), calls=%async_computation.2 | async-start | bytes 262144 | tf_op jit(solution)/shard_map/all_to_all | solution.py:334
  72.6 3.6 %collective-permute-start.5 = (bf16[48,2432]{1,0:T(8,128)(2,1)S(1)}, bf16[48,2432]{1,0:T(8,128)(2,1)S(1)}, u32[]{:S(2)}, u32[]{:S(2)}) collective-permute-start(bf16[48,2432]{1,0:T(8,128)(2,1)S(1)} %slice.24), channel_id=1, source_target_pairs={{0,1},{1,0},{2,3},{3,2},{4,5},{5,4},{6,7},{7,6},{8,9},{9,8},{10,11... | collective-permute-start | bytes 700424 | tf_op jit(solution)/shard_map/ppermute | solution.py:326
  76.2 24.3 %copy-start.2 = (bf16[152,256]{1,0:T(8,128)(2,1)S(1)}, bf16[152,256]{1,0:T(8,128)(2,1)}, u32[]{:S(2)}) copy-start(bf16[152,256]{1,0:T(8,128)(2,1)} %get-tuple-element.53.perm_ref) | copy-start | bytes 233476
